TPU v7x, 32 devices: a whole 2x2x4 slice. The times are simulated.
32 devices in a mesh: groups: 2 (over x), row: 16 (over z, y, core).
Axes of the slice: x: 2, y: 2, z: 4, core: 2. Of those that a mesh axis runs over, the one named last changes fastest.
Arguments:
- pair: bfloat16 [1024, 512, 128], P(('groups', 'row')), parts along dimension 0, may hold values from -6 to 6
- window_rows: int32 [256], P(('groups', 'row')), parts along dimension 0, may hold values from 0 to 511, as said below
- token_mask: int32 [1024], P('groups'), parts along dimension 0, may hold values from 0 to 1, as said below
- chain_ids: int32 [1024], P('groups'), parts along dimension 0, may hold values from 0 to 3, never falling along the last dimension, each value on 1 to 256 neighbouring positions
- ln_gain: float32 [128], replicated, may hold values from 0.1 to 1.9
- ln_shift: float32 [128], replicated, may hold values from -3 to 3
- w_project: bfloat16 [128, 512], replicated, may hold values from -0.5 to 0.5
- gate_bias: float32 [128], replicated, may hold values from -4 to 4
- w_bias: bfloat16 [128, 4], replicated
- chain_bias: float32 [4], replicated, may hold values from -8 to 8
- w_out: bfloat16 [128, 128], replicated, may hold values from -0.5 to 0.5
Outputs:
- update: bfloat16 [256, 512, 128], P('groups', 'row'), parts along dimension 0
There are 2 independent parts, one for each index of `groups`. A program takes and returns all parts, laid end to end along the dimension named above; an argument that names none is the same for every part. Nothing has to cross between parts.
Inputs may be any that keep to these rules, and one draw needn't show every extreme that they name: `window_rows`: window slot w names a pair row from (w // 8) * 32 to (w // 8) * 32 + 31; the slots name distinct rows. `token_mask`: exactly 384 entries are 1. `chain_ids`: chain numbers never fall along the tokens.
All inputs are finite; a program needn't handle non-finite values.
Results may differ from a plain program's by a relative error of at most 0.0023.
The roundings to bfloat16 on the way count: a program that leaves them out, or rounds other values in their place, can miss the bound.
Values may be sent and summed in bfloat16 or wider, within the bound.
No kernel may reach another device: no remote copies, remote signals or barrier semaphores. Data moves between devices by JAX's collectives and lax.ppermute only.
A program may use at most 256 MiB of HBM per device.

v0:
```python
import jax
import jax.numpy as jnp
from jax import lax
from jax.sharding import PartitionSpec as P


def layer_norm(field, ln_gain, ln_shift):
    field = field.astype(jnp.float32)
    mean_value = jnp.mean(field, axis=-1, keepdims=True)
    variance = jnp.mean((field - mean_value) ** 2, axis=-1, keepdims=True)
    return ((field - mean_value) * lax.rsqrt(variance + 1e-05) * ln_gain + ln_shift).astype(
        jnp.bfloat16
    )


def local(
    pair,
    window_rows,
    token_mask,
    chain_ids,
    ln_gain,
    ln_shift,
    w_project,
    gate_bias,
    w_bias,
    chain_bias,
    w_out,
):
    rows_held, token_count, channels = pair.shape
    head_count = w_bias.shape[1]
    inner_width = w_out.shape[0]
    head_size = inner_width // head_count
    normed = layer_norm(pair, ln_gain, ln_shift)
    local_rows = window_rows % rows_held
    window = jnp.take(normed, local_rows, axis=0)
    win_rows = window.shape[0]
    projected = jnp.einsum("wjc,cf->wjf", window, w_project, preferred_element_type=jnp.float32)
    queries = (projected[..., :inner_width] * head_size ** (-0.5)).astype(jnp.bfloat16)
    key_rows = projected[..., inner_width : 2 * inner_width].astype(jnp.bfloat16)
    value_rows = projected[..., 2 * inner_width : 3 * inner_width].astype(jnp.bfloat16)
    gate_value = jax.nn.sigmoid(projected[..., 3 * inner_width :] + gate_bias)
    bias_panel = jnp.einsum(
        "jkc,ch->hjk", normed, w_bias, preferred_element_type=jnp.float32
    ).astype(jnp.bfloat16)
    key_live = token_mask == 1
    key_count = key_rows.shape[1]
    key_heads = key_rows.reshape(win_rows, key_count, head_count, head_size)
    value_heads = value_rows.reshape(win_rows, key_count, head_count, head_size)
    panel_piece = lax.all_gather(bias_panel, "row", axis=1, tiled=True)
    keep_part = token_mask.astype(jnp.float32)
    piece_rows = panel_piece.shape[1]
    q_part = queries.reshape(win_rows, piece_rows, head_count, head_size)
    same_chain = (chain_ids[:, None] == chain_ids[None, :]).astype(jnp.float32)
    added_bias = panel_piece.astype(jnp.float32) + chain_bias[:, None, None] * same_chain[None]
    scores = (
        jnp.einsum("wjhd,wkhd->whjk", q_part, key_heads, preferred_element_type=jnp.float32)
        + added_bias[None]
    )
    scores = jnp.where(key_live, scores, -jnp.inf)
    row_max = jnp.max(scores, axis=-1, keepdims=True)
    raised = jnp.where(key_live, jnp.exp(scores - row_max), 0.0)
    totals = jnp.sum(raised, axis=-1)
    weights = raised.astype(jnp.bfloat16)
    attended = jnp.einsum(
        "whjk,wkhd->wjhd", weights, value_heads, preferred_element_type=jnp.float32
    )
    attended = attended / jnp.transpose(totals, (0, 2, 1))[..., None]
    gated = (gate_value * attended.reshape(win_rows, piece_rows, inner_width)).astype(jnp.bfloat16)
    result = (
        jnp.einsum("wjf,fc->wjc", gated, w_out, preferred_element_type=jnp.float32)
        * keep_part[None, :, None]
    )
    updates = result.astype(jnp.bfloat16)
    return lax.all_to_all(updates, "row", split_axis=1, concat_axis=0, tiled=True)


def solution(mesh):
    placed = (
        P(("groups", "row"), None, None),
        P(("groups", "row")),
        P("groups"),
        P("groups"),
        P(),
        P(),
        P(),
        P(),
        P(),
        P(),
        P(),
    )
    return jax.shard_map(
        local, mesh=mesh, in_specs=placed, out_specs=P("groups", "row", None), check_vma=False
    )
```

profile of v0, /device:TPU:0, one launch (start us, length us, event | category | flops | bytes accessed | tf_op | source)
XLA Modules:
  0.0 149.8 jit_solution(9403630222805330227)
XLA Ops:
  6.5 0.0 copy-start
  6.5 0.0 copy-start.9
  6.5 0.0 copy-start.10
  6.5 0.0 all-gather.2.cloned.1.call-start
  6.5 0.0 copy-start.1
  6.6 3.5 %convert_reduce_fusion = f32[32,512]{1,0:T(8,128)S(1)} fusion(bf16[32,512,128]{2,1,0:T(8,128)(2,1)} %param.11), kind=kLoop, calls=%fused_computation.11 | loop fusion | flops 4177920 | bytes 4259840 | tf_op jit(solution)/shard_map/reduce_sum | solution.py:9
  10.1 0.0 copy-done.1
  10.1 4.8 %fusion.9 = f32[32,512]{1,0:T(8,128)S(1)} fusion(bf16[32,512,128]{2,1,0:T(8,128)(2,1)S(1)} %copy-done.1, f32[32,512]{1,0:T(8,128)S(1)} %broadcast_multiply_fusion), kind=kLoop, calls=%fused_computation.14 | loop fusion | flops 8372224 | bytes 4325376 | tf_op jit(solution)/shard_map/reduce_sum | solution.py:10
  14.9 0.0 copy-done.9
  14.9 0.0 copy-done.10
  14.9 0.0 copy-start.8
  14.9 5.0 %fusion.12 = bf16[32,512,128]{2,1,0:T(8,128)(2,1)S(1)} fusion(bf16[32,512,128]{2,1,0:T(8,128)(2,1)S(1)} %copy-done.1, f32[128]{0:T(128)S(1)} %copy-done.9, f32[128]{0:T(128)S(1)} %copy-done.10, f32[32,512]{1,0:T(8,128)S(1)} %add_rsqrt_fusion, f32[32,512]{1,0:T(8,128)S(1)} %broadcast_multiply_fusion), kind=kLoop, calls=%fused_computation.17 | loop fusion | flops 12582912 | bytes 8520704 | tf_op jit(solution)/shard_map/convert_element_type | solution.py:11
  19.9 0.0 copy-start.2
  19.9 1.9 %copy-done.2 = bf16[32,512,128]{2,1,0:T(8,128)(2,1)} copy-done((bf16[32,512,128]{2,1,0:T(8,128)(2,1)}, bf16[32,512,128]{2,1,0:T(8,128)(2,1)S(1)}, u32[]{:S(2)}) %copy-start.2) | copy-done | bytes 4194328
  21.9 0.0 copy-done.8
  21.9 0.0 copy-start.13
  21.9 0.0 copy-start.7
  21.9 0.0 copy-start.6
  21.9 1.9 %fusion.24 = bf16[4,32,512]{2,0,1:T(4,128)(2,1)} fusion(bf16[32,512,128]{2,1,0:T(8,128)(2,1)S(1)} %fusion.12, bf16[128,4]{0,1:T(4,128)(2,1)S(1)} %copy-done.8), kind=kOutput, calls=%fused_computation.32 | convolution fusion | flops 16842752 | bytes 4326400 | tf_op jit(solution)/shard_map/jkc,ch->hjk/dot_general | solution.py:42
  23.7 0.0 all-gather.2.cloned.1.call-update
  23.7 0.0 copy-done.13
  23.8 2.9 %gather_fusion = bf16[8,512,128]{2,1,0:T(8,128)(2,1)S(1)} fusion(bf16[32,512,128]{2,1,0:T(8,128)(2,1)} %copy-done.2, s32[1024]{0:T(1024)S(1)} %pad_clamp_fusion), kind=kCustom, calls=%fused_computation | custom fusion | bytes 2097184 | tf_op jit(solution)/shard_map/jit(_take)/gather | solution.py:35
  26.7 0.0 copy-done.7
  26.8 0.0 copy-done.6
  26.8 0.1 compare_convert_fusion
  26.9 0.0 copy-done
  26.9 1.3 fusion.43
  28.3 0.0 copy-start.3
  28.3 0.0 copy-start.12
  28.3 1.4 fusion.42
  29.6 0.0 copy-start.4
  29.6 2.1 %copy-done.3 = f32[8,512,512]{1,2,0:T(8,128)} copy-done((f32[8,512,512]{1,2,0:T(8,128)}, f32[8,512,512]{1,2,0:T(8,128)S(1)}, u32[]{:S(2)}) %copy-start.3) | copy-done | bytes 8388632
  31.8 0.3 fusion.15
  32.1 35.9 %all-gather.2.cloned.1.call-done = bf16[4,512,512]{2,0,1:T(4,128)(2,1)} async-done(((bf16[4,32,512]{2,0,1:T(4,128)(2,1)}), bf16[4,512,512]{2,0,1:T(4,128)(2,1)}) %all-gather.2.cloned.1.call-update) | async-done | bytes 2097168 | tf_op jit(solution)/shard_map/all_gather | solution.py:49
  68.0 0.0 copy-done.12
  68.0 4.7 %multiply_add_fusion = f32[4,512,512]{2,0,1:T(4,128)} fusion(bf16[4,512,512]{2,0,1:T(4,128)(2,1)} %all-gather.2.cloned.1.call-done, f32[512,512]{1,0:T(8,128)S(1)} %compare_convert_fusion, f32[4]{0:T(128)S(1)} %copy-done.12), kind=kLoop, calls=%fused_computation.18 | loop fusion | flops 3145728 | bytes 7340048 | tf_op jit(solution)/shard_map/add | solution.py:54
  72.7 5.3 %copy.18 = f32[4,512,512]{1,2,0:T(8,128)} copy(f32[4,512,512]{2,0,1:T(4,128)} %multiply_add_fusion) | data formatting | bytes 8388608 | tf_op jit(solution)/shard_map/add | solution.py:54
  77.9 0.0 copy-done.4
  77.9 15.1 %fusion.44 = f32[8,4,512]{2,1,0:T(4,128)S(1)} fusion(f32[4,512,512]{1,2,0:T(8,128)} %copy.18, pred[512]{0:T(512)(128)(4,1)S(1)} %broadcast_compare_fusion, bf16[8,512,4,32]{1,3,2,0:T(8,128)(2,1)S(1)} %bitcast.39, bf16[8,512,4,32]{1,3,2,0:T(8,128)(2,1)S(1)} %bitcast.41), kind=kOutput, calls=%fused_computation.57 | convolution fusion | flops 578814464 | bytes 6357504 | tf_op jit(solution)/shard_map/sub | solution.py:61
  93.0 0.0 copy-start.11
  93.0 17.0 %bitcast_divide_fusion = f32[8,512,4,32]{1,3,2,0:T(8,128)S(1)} fusion(bf16[8,512,4,32]{1,3,2,0:T(8,128)(2,1)} %bitcast.43, f32[8,512,4]{1,2,0:T(4,128)S(1)} %bitcast.44, f32[4,512,512]{1,2,0:T(8,128)} %copy.18, pred[512]{0:T(512)(128)(4,1)S(1)} %broadcast_compare_fusion, bf16[8,512,4,32]{1,3,2,0:T(8,128)(2,1)S(1)} %bitcast.40, ...), kind=kOutput, calls=%fused_computation.28 | convolution fusion | flops 1116226048 | bytes 9503232 | tf_op jit(solution)/shard_map/whjk,wkhd->wjhd/dot_general | solution.py:64
  110.0 0.0 copy-done.11
  110.0 0.0 copy-start.5
  110.0 2.4 %fusion.21 = bf16[8,512,128]{1,2,0:T(8,128)(2,1)S(1)} fusion(f32[8,512,4,32]{1,3,2,0:T(8,128)S(1)} %bitcast_divide_fusion, f32[8,512,512]{1,2,0:T(8,128)} %copy-done.3, f32[128]{0:T(128)S(1)} %copy-done.11), kind=kLoop, calls=%fused_computation.30 | loop fusion | flops 3145728 | bytes 5243392 | tf_op jit(solution)/shard_map/convert_element_type | solution.py:68
  112.4 0.0 copy-done.5
  112.4 0.5 multiply_convert_fusion
  112.9 0.7 copy.21
  113.6 28.1 %all_to_all.18 = bf16[8,512,128]{2,0,1:T(8,128)(2,1)S(1)} all-to-all(bf16[8,512,128]{2,0,1:T(8,128)(2,1)S(1)} %copy.21), channel_id=1, replica_groups=mesh['groups'=2,'row'=16] {'row'}, dimensions={1} | all-to-all | bytes 2097152 | tf_op jit(solution)/shard_map/all_to_all | solution.py:74
  141.7 1.2 copy.22
  (6 shorter events, 0.1 us)
Async XLA Ops:
  6.5 20.4 %copy-start = (bf16[128,512]{1,0:T(8,128)(2,1)S(1)}, bf16[128,512]{1,0:T(8,128)(2,1)}, u32[]{:S(2)}) copy-start(bf16[128,512]{1,0:T(8,128)(2,1)} %param.17) | copy-start | bytes 393220
  6.5 8.4 %copy-start.9 = (f32[128]{0:T(128)S(1)}, f32[128]{0:T(128)}, u32[]{:S(2)}) copy-start(f32[128]{0:T(128)} %param.16) | copy-start | bytes 1540
  6.5 8.4 %copy-start.10 = (f32[128]{0:T(128)S(1)}, f32[128]{0:T(128)}, u32[]{:S(2)}) copy-start(f32[128]{0:T(128)} %param.15) | copy-start | bytes 1540
  6.5 61.5 %all-gather.2.cloned.1.call-start = ((), (), s32[]{:S(2)}) async-start(), calls=%async_computation.1 | async-start | bytes 2228224 | tf_op jit(solution)/shard_map/all_gather | solution.py:49
  6.5 3.5 %copy-start.1 = (bf16[32,512,128]{2,1,0:T(8,128)(2,1)S(1)}, bf16[32,512,128]{2,1,0:T(8,128)(2,1)}, u32[]{:S(2)}) copy-start(bf16[32,512,128]{2,1,0:T(8,128)(2,1)} %param.11) | copy-start | bytes 12582916
  14.9 6.9 %copy-start.8 = (bf16[128,4]{0,1:T(4,128)(2,1)S(1)}, bf16[128,4]{0,1:T(4,128)(2,1)}, u32[]{:S(2)}) copy-start(bf16[128,4]{0,1:T(4,128)(2,1)} %param.19) | copy-start | bytes 3076
  19.9 1.9 %copy-start.2 = (bf16[32,512,128]{2,1,0:T(8,128)(2,1)}, bf16[32,512,128]{2,1,0:T(8,128)(2,1)S(1)}, u32[]{:S(2)}) copy-start(bf16[32,512,128]{2,1,0:T(8,128)(2,1)S(1)} %fusion.12) | copy-start | bytes 12582916
  21.9 1.9 %copy-start.13 = (s32[8]{0:T(128)S(1)}, s32[8]{0:T(128)}, u32[]{:S(2)}) copy-start(s32[8]{0:T(128)} %param.12) | copy-start | bytes 100
  21.9 4.9 %copy-start.7 = (s32[512]{0:T(512)S(1)}, s32[512]{0:T(512)}, u32[]{:S(2)}) copy-start(s32[512]{0:T(512)} %param.13) | copy-start | bytes 6148
  21.9 4.9 %copy-start.6 = (s32[512]{0:T(512)S(1)}, s32[512]{0:T(512)}, u32[]{:S(2)}) copy-start(s32[512]{0:T(512)} %param.14) | copy-start | bytes 6148
  28.3 3.5 %copy-start.3 = (f32[8,512,512]{1,2,0:T(8,128)}, f32[8,512,512]{1,2,0:T(8,128)S(1)}, u32[]{:S(2)}) copy-start(f32[8,512,512]{1,2,0:T(8,128)S(1)} %get-tuple-element.10) | copy-start | bytes 25165828
  28.3 39.7 %copy-start.12 = (f32[4]{0:T(128)S(1)}, f32[4]{0:T(128)}, u32[]{:S(2)}) copy-start(f32[4]{0:T(128)} %param.20) | copy-start | bytes 52
  29.6 48.3 %copy-start.4 = (bf16[8,512,128]{1,2,0:T(8,128)(2,1)}, bf16[8,512,128]{1,2,0:T(8,128)(2,1)S(1)}, u32[]{:S(2)}) copy-start(bf16[8,512,128]{1,2,0:T(8,128)(2,1)S(1)} %get-tuple-element.7) | copy-start | bytes 3145732
  93.0 17.0 %copy-start.11 = (f32[128]{0:T(128)S(1)}, f32[128]{0:T(128)}, u32[]{:S(2)}) copy-start(f32[128]{0:T(128)} %param.18) | copy-start | bytes 1540
  110.0 2.4 %copy-start.5 = (bf16[128,128]{1,0:T(8,128)(2,1)S(1)}, bf16[128,128]{1,0:T(8,128)(2,1)}, u32[]{:S(2)}) copy-start(bf16[128,128]{1,0:T(8,128)(2,1)} %param.21) | copy-start | bytes 98308
Sparse Core Ops, SparseCore 0:
  23.9 44.0 all-gather.1
where the time goes:
time: 150 us
  waiting for transfers between devices  35.9 us (24%)
  matrix products  35.7 us (24%)
  blocking collectives  28.1 us (19%)
  other arithmetic  20.8 us (14%)
  local copies, waits for them, and re-layouts  15.6 us (10%)
  between operations  13.7 us (9%)
    all_gather x1, waiting for transfers between devices, local(): panel_piece = lax.all_gather(bias_panel, 'row', axis=1, tiled=True)  35.9 us
    all_to_all x1, blocking collectives, local(): lax.all_to_all(updates, 'row', split_axis=1, concat_axis=0, tiled=True)  28.1 us
    dot_general x1, matrix products, local(): jnp.einsum('whjk,wkhd->wjhd', weights, value_heads, preferred_element_typ...  17 us
    sub x1, matrix products, local(): raised = jnp.where(key_live, jnp.exp(scores - row_max), 0.0)  15.1 us
    add x1, local copies, waits for them, and re-layouts, local(): panel_piece.astype(jnp.float32)  5.25 us
    convert_element_type x1, other arithmetic, layer_norm(): ((field - mean_value) * lax.rsqrt(variance + 1e-05) * ln_gain + ln_shift)...  4.99 us
    reduce_sum x1, other arithmetic, layer_norm(): variance = jnp.mean((field - mean_value) ** 2, axis=-1, keepdims=True)  4.76 us
    add x1, other arithmetic, local(): panel_piece.astype(jnp.float32)  4.68 us
  transfers between devices with their start and end apart: 1, of which 1 were waited for; matrix products, arithmetic and copies ran while one was open for 4% of the time, Pallas kernels for 0%

commit v1 on v0

v1 whole, which is shorter than its diff:
```python
import functools

import jax
import jax.numpy as jnp
from jax import lax
from jax.experimental import pallas as pl
from jax.experimental.pallas import tpu as pltpu
from jax.sharding import PartitionSpec as P

F32, BF16 = jnp.float32, jnp.bfloat16
VMEM = pl.BlockSpec(memory_space=pltpu.VMEM)
SMEM = pl.BlockSpec(memory_space=pltpu.SMEM)
ANY = pl.BlockSpec(memory_space=pl.ANY)
NT = (((1,), (1,)), ((), ()))
PARAMS = pltpu.CompilerParams(vmem_limit_bytes=48 * 1024 * 1024)


def normalised(rows, gain, shift):
    x = rows.astype(F32)
    mean = jnp.mean(x, axis=-1, keepdims=True)
    d = x - mean
    var = jnp.mean(d * d, axis=-1, keepdims=True)
    return (d * lax.rsqrt(var + 1e-05) * gain + shift).astype(BF16)


def live_ranks(mask_row):
    tokens = mask_row.shape[1]
    upper = lax.broadcasted_iota(jnp.int32, (tokens, tokens), 0) <= lax.broadcasted_iota(
        jnp.int32, (tokens, tokens), 1
    )
    ones = jnp.broadcast_to(mask_row.astype(F32), (8, tokens)).astype(BF16)
    running = jnp.dot(ones, upper.astype(F32).astype(BF16), preferred_element_type=F32)[0:1]
    return jnp.where(mask_row == 1, running - 1.0, -1.0)


def picking(mask_row, live):
    ranks = live_ranks(mask_row).astype(jnp.int32)
    wanted = lax.broadcasted_iota(jnp.int32, (live, mask_row.shape[1]), 0)
    return (wanted == ranks).astype(F32).astype(BF16)


def window_kernel(rows_ref, pair_ref, gain_ref, shift_ref, out_ref, held, sems):
    count = held.shape[0]
    rows_held = pair_ref.shape[0]
    copies = []
    for i in range(count):
        at = lax.rem(rows_ref[i], rows_held)
        copies.append(pltpu.make_async_copy(pair_ref.at[at], held.at[i], sems.at[i]))
        copies[-1].start()
    for i in range(count):
        copies[i].wait()
        out_ref[i] = normalised(held[i], gain_ref[...], shift_ref[...])


def bias_kernel(pair_ref, mask_ref, gain_ref, shift_ref, w_ref, out_ref, acc):
    step = pl.program_id(0)
    rows = pair_ref.shape[0]
    heads, held, tokens = acc.shape
    live = out_ref.shape[1]
    for i in range(rows):
        x = normalised(pair_ref[i], gain_ref[...], shift_ref[...])
        b = lax.dot_general(w_ref[...], x, NT, preferred_element_type=F32)
        for h in range(heads):
            acc[h, pl.ds(step * rows + i, 1), :] = b[h : h + 1]

    @pl.when(step == pl.num_programs(0) - 1)
    def _():
        full = acc[...].reshape(heads * held, tokens).astype(BF16)
        out_ref[...] = lax.dot_general(
            full, picking(mask_ref[...], live), NT, preferred_element_type=F32
        ).astype(BF16)


def key_value_kernel(own_ref, other_ref, mask_ref, w_ref, k_ref, v_ref, pick):
    count = own_ref.shape[0]
    live, inner = k_ref.shape[1:]
    pick[...] = picking(mask_ref[...], live)
    for i in range(count):
        both = jnp.concatenate([own_ref[i], other_ref[i]], axis=1)
        taken = jnp.dot(pick[...], both, preferred_element_type=F32).astype(BF16)
        c = own_ref.shape[2]
        for part in range(2):
            kv = jnp.dot(
                taken[:, part * c : (part + 1) * c],
                w_ref[:, inner : 3 * inner],
                preferred_element_type=F32,
            ).astype(BF16)
            k_ref[i + part * count] = kv[:, :inner]
            v_ref[i + part * count] = kv[:, inner:]


def attention_kernel(heads, blocks, place_ref, chain_bias_ref, *refs):
    bias_refs, refs = refs[:blocks], refs[blocks:]
    (own_ref, other_ref, k_ref, v_ref, mask_ref, chain_ref, w_ref, gate_bias_ref, w_out_ref), refs = (
        refs[:9],
        refs[9:],
    )
    out_refs, (q_s, gate_s, added_s, gated_s) = refs[:blocks], refs[blocks:]
    windows, live, inner = k_ref.shape
    half = windows // 2
    block = own_ref.shape[3]
    tokens = mask_ref.shape[1]
    size = inner // heads
    core = place_ref[0]
    chain_row = jnp.broadcast_to(chain_ref[...].astype(F32), (8, tokens)).astype(BF16)
    chain_live = lax.dot_general(
        chain_row, picking(mask_ref[...], live), NT, preferred_element_type=F32
    )[0:1]
    lane_head = lax.broadcasted_iota(jnp.int32, (block, inner), 1) // size
    w_q = w_ref[:, :inner]
    w_g = w_ref[:, 3 * inner :]
    for b in range(blocks):
        at = place_ref[1 + b]
        here = (
            lax.broadcasted_iota(jnp.int32, (block, tokens), 1)
            == (at * 2 + core) * block + lax.broadcasted_iota(jnp.int32, (block, tokens), 0)
        ).astype(F32)
        chain_here = jnp.sum(here * chain_ref[...].astype(F32), axis=1, keepdims=True)
        keep = jnp.sum(here * mask_ref[...].astype(F32), axis=1, keepdims=True)
        same = (chain_here == chain_live).astype(F32)
        for h in range(heads):
            rows = slice(h * block, (h + 1) * block)
            added_s[b, rows, :] = bias_refs[b][rows, :].astype(F32) + chain_bias_ref[h] * same
        for part, ref in enumerate((own_ref, other_ref)):
            x = ref[:, at, core].reshape(half * block, inner)
            span = pl.ds(part * half * block, half * block)
            q_s[b, span, :] = (
                jnp.dot(x, w_q, preferred_element_type=F32) * size ** (-0.5)
            ).astype(BF16)
            gate_s[b, span, :] = jax.nn.sigmoid(
                jnp.dot(x, w_g, preferred_element_type=F32) + gate_bias_ref[...]
            )

        def one_window(w, carry, b=b):
            span = pl.ds(pl.multiple_of(w * block, block), block)
            q = q_s[b, span, :].astype(F32)
            spread = jnp.concatenate(
                [jnp.where(lane_head == h, q, 0.0) for h in range(heads)], axis=0
            ).astype(BF16)
            scores = (
                lax.dot_general(spread, k_ref[w], NT, preferred_element_type=F32) + added_s[b]
            )
            top = jnp.max(scores, axis=1, keepdims=True)
            raised = jnp.exp(scores - top)
            totals = jnp.sum(raised, axis=1, keepdims=True)
            mixed = jnp.dot(raised.astype(BF16), v_ref[w], preferred_element_type=F32)
            mixed = mixed * (1.0 / totals)
            attended = mixed[0:block]
            for h in range(1, heads):
                attended = jnp.where(
                    lane_head == h, mixed[h * block : (h + 1) * block], attended
                )
            gated_s[b, span, :] = (gate_s[b, span, :] * attended).astype(BF16)
            return carry

        lax.fori_loop(0, windows, one_window, 0, unroll=4)
        result = jnp.dot(gated_s[b], w_out_ref[...], preferred_element_type=F32)
        result = result.reshape(windows, block, inner) * keep[None]
        result = result.astype(BF16)
        out_refs[b][pl.ds(core * half, half)] = result[:half]
        out_refs[b][pl.ds((1 - core) * half, half)] = result[half:]


def gather_kernel(place_ref, *refs):
    parts, out_ref, sems = refs[:-2], refs[-2], refs[-1]
    count = parts[0].shape[0]
    copies = []
    for i, part in enumerate(parts):
        at = place_ref[i] * count
        copies.append(pltpu.make_async_copy(part, out_ref.at[pl.ds(at, count)], sems.at[i]))
        copies[-1].start()
    for copy in copies:
        copy.wait()


def local(
    devices,
    pair,
    window_rows,
    token_mask,
    chain_ids,
    ln_gain,
    ln_shift,
    w_project,
    gate_bias,
    w_bias,
    chain_bias,
    w_out,
):
    rows_held, tokens, channels = pair.shape
    heads = w_bias.shape[1]
    inner = w_out.shape[0]
    count = window_rows.shape[0]
    live = tokens * 3 // 4
    owners = devices // 2
    me = lax.axis_index("row")
    core, chip = me % 2, me // 2
    mask_row = token_mask.reshape(1, tokens)
    chain_row = chain_ids.reshape(1, tokens)
    gain = ln_gain.reshape(1, channels)
    shift = ln_shift.reshape(1, channels)

    def swap(x, bits):
        return lax.ppermute(x, "row", [(i, i ^ bits) for i in range(devices)])

    own = pl.pallas_call(
        window_kernel,
        out_shape=jax.ShapeDtypeStruct((count, tokens, channels), BF16),
        in_specs=[SMEM, ANY, VMEM, VMEM],
        out_specs=VMEM,
        scratch_shapes=[
            pltpu.VMEM((count, tokens, channels), BF16),
            pltpu.SemaphoreType.DMA((count,)),
        ],
        compiler_params=PARAMS,
    )(window_rows, pair, gain, shift)
    other = swap(own, 1)

    step_rows = 4
    w_bias_t = jnp.pad(w_bias.T, ((0, 8 - heads), (0, 0)))
    bias = pl.pallas_call(
        bias_kernel,
        grid=(rows_held // step_rows,),
        out_shape=jax.ShapeDtypeStruct((heads * rows_held, live), BF16),
        in_specs=[
            pl.BlockSpec((step_rows, tokens, channels), lambda i: (i, 0, 0)),
            pl.BlockSpec((1, tokens), lambda i: (0, 0)),
            pl.BlockSpec((1, channels), lambda i: (0, 0)),
            pl.BlockSpec((1, channels), lambda i: (0, 0)),
            pl.BlockSpec((8, channels), lambda i: (0, 0)),
        ],
        out_specs=pl.BlockSpec((heads * rows_held, live), lambda i: (0, 0)),
        scratch_shapes=[pltpu.VMEM((heads, rows_held, tokens), F32)],
        compiler_params=PARAMS,
    )(pair, mask_row, gain, shift, w_bias_t)
    biases = [bias] + [swap(bias, 2 * m) for m in range(1, owners)]

    keys, values = pl.pallas_call(
        key_value_kernel,
        out_shape=[jax.ShapeDtypeStruct((2 * count, live, inner), BF16)] * 2,
        in_specs=[VMEM] * 4,
        out_specs=[VMEM] * 2,
        scratch_shapes=[pltpu.VMEM((live, tokens), BF16)],
        compiler_params=PARAMS,
    )(own, other, mask_row, w_project)

    split = (count, owners, 2, rows_held, channels)
    own, other = own.reshape(split), other.reshape(split)

    def attend(ms):
        blocks = len(ms)
        place = jnp.stack([core] + [chip ^ m for m in ms]).astype(jnp.int32)
        rows = 2 * count * rows_held
        return pl.pallas_call(
            functools.partial(attention_kernel, heads, blocks),
            out_shape=[jax.ShapeDtypeStruct((2 * count, rows_held, channels), BF16)] * blocks,
            in_specs=[SMEM, SMEM] + [VMEM] * (blocks + 9),
            out_specs=[VMEM] * blocks,
            scratch_shapes=[
                pltpu.VMEM((blocks, rows, inner), BF16),
                pltpu.VMEM((blocks, rows, inner), F32),
                pltpu.VMEM((blocks, heads * rows_held, live), F32),
                pltpu.VMEM((blocks, rows, inner), BF16),
            ],
            compiler_params=PARAMS,
        )(
            place,
            chain_bias,
            *[biases[m] for m in ms],
            own,
            other,
            keys,
            values,
            mask_row,
            chain_row,
            w_project,
            gate_bias.reshape(1, inner),
            w_out,
        )

    ms = list(range(owners))
    updates = attend(ms)
    received = [u if m == 0 else swap(u, 2 * m) for m, u in zip(ms, updates)]
    place = jnp.stack([chip ^ m for m in ms]).astype(jnp.int32)
    return pl.pallas_call(
        gather_kernel,
        out_shape=jax.ShapeDtypeStruct((owners * 2 * count, rows_held, channels), BF16),
        in_specs=[SMEM] + [ANY] * owners,
        out_specs=ANY,
        scratch_shapes=[pltpu.SemaphoreType.DMA((owners,))],
        compiler_params=PARAMS,
    )(place, *received)


def solution(mesh):
    placed = (
        P(("groups", "row"), None, None),
        P(("groups", "row")),
        P("groups"),
        P("groups"),
        P(),
        P(),
        P(),
        P(),
        P(),
        P(),
        P(),
    )
    return jax.shard_map(
        functools.partial(local, mesh.shape["row"]),
        mesh=mesh,
        in_specs=placed,
        out_specs=P("groups", "row", None),
        check_vma=False,
    )
```

time: 150 us -> 112 us (0.75); the launches traced: 150 us -> 110 us
  Pallas kernels: 0 us -> 56.5 us
  matrix products: 35.7 us -> 0 us
  starting transfers between devices: 0.01 us -> 33 us
  blocking collectives: 28.1 us -> 0 us
  waiting for transfers between devices: 35.9 us -> 14.8 us
  other arithmetic: 20.8 us -> 0 us
  between operations: 13.7 us -> 0.13 us
  local copies, waits for them, and re-layouts: 15.6 us -> 5.55 us
    pallas_call x0 -> x5, Pallas kernels: none -> 56.5 us  [the longest x1 42.2 us: attend(): pl.pallas_call(functools.partial(attention_kernel, heads, blocks), out_sh...]
    all_gather x1 -> x0, waiting for transfers between devices: 35.9 us -> none  [local(): panel_piece = lax.all_gather(bias_panel, 'row', axis=1, tiled=True)]
    ppermute x0 -> x15, starting transfers between devices: none -> 33 us  [swap(): return lax.ppermute(x, 'row', [(i, i ^ bits) for i in range(devices)])]
    all_to_all x1 -> x0, blocking collectives: 28.1 us -> none  [local(): lax.all_to_all(updates, 'row', split_axis=1, concat_axis=0, tiled=True)]
    dot_general x4 -> x0, matrix products: 20.7 us -> none  [the longest x1 17 us: local(): jnp.einsum('whjk,wkhd->wjhd', weights, value_heads, preferred_element_typ...]
    sub x1 -> x0, matrix products: 15.1 us -> none  [local(): raised = jnp.where(key_live, jnp.exp(scores - row_max), 0.0)]
    ppermute x0 -> x15, waiting for transfers between devices: none -> 14.8 us  [swap(): return lax.ppermute(x, 'row', [(i, i ^ bits) for i in range(devices)])]
    reduce_sum x2 -> x0, other arithmetic: 8.27 us -> none  [the longest x1 4.76 us: layer_norm(): variance = jnp.mean((field - mean_value) ** 2, axis=-1, keepdims=True)]
  transfers between devices with their start and end apart: 1 -> 15, of which waited for: 1 -> 5; matrix products, arithmetic and copies ran while one was open for 4% -> 0% of each run, Pallas kernels for 0% -> 8%
where the time goes in v1:
time: 112 us; the launch traced here: 110 us
  Pallas kernels  56.5 us (50%)
  starting transfers between devices  33 us (29%)
  waiting for transfers between devices  14.8 us (13%)
  local copies, waits for them, and re-layouts  5.55 us (5%)
    pallas_call x1, Pallas kernels, attend(): pl.pallas_call(functools.partial(attention_kernel, heads, blocks), out_sh...  42.2 us
    ppermute x15, starting transfers between devices, swap(): return lax.ppermute(x, 'row', [(i, i ^ bits) for i in range(devices)])  33 us
    ppermute x15, waiting for transfers between devices, swap(): return lax.ppermute(x, 'row', [(i, i ^ bits) for i in range(devices)])  14.8 us
    pallas_call x1, Pallas kernels, local(): pl.pallas_call(bias_kernel, grid=(rows_held // step_rows,), out_shape=jax...  6.72 us
    unnamed x26, local copies, waits for them, and re-layouts  5.37 us
    pallas_call x1, Pallas kernels, local(): pl.pallas_call(window_kernel, out_shape=jax.ShapeDtypeStruct((count, toke...  3.89 us
  transfers between devices with their start and end apart: 15, of which 5 were waited for; matrix products, arithmetic and copies ran while one was open for 0% of the time, Pallas kernels for 8%

profile of v1, /device:TPU:0, one launch (start us, length us, event | category | flops | bytes accessed | tf_op | source)
XLA Modules:
  0.0 110.0 jit_solution(4931628726508193768)
XLA Ops:
  0.0 0.0 copy-start
  0.0 2.2 %copy-done = bf16[32,512,128]{2,1,0:T(8,128)(2,1)S(1)} copy-done((bf16[32,512,128]{2,1,0:T(8,128)(2,1)S(1)}, bf16[32,512,128]{2,1,0:T(8,128)(2,1)}, u32[]{:S(2)}) %copy-start) | copy-done | bytes 4194328
  2.2 0.0 copy-start.6
  2.2 0.7 copy-done.6
  2.8 0.0 copy-start.8
  2.8 0.7 copy-done.8
  3.5 0.0 copy-start.9
  3.5 0.7 copy-done.9
  4.2 0.0 copy-start.12
  4.2 0.0 copy-start.4
  4.2 0.0 copy-start.7
  4.2 3.9 %shard_map.110.own_ref = bf16[8,512,128]{2,1,0:T(8,128)(2,1)S(1)} custom-call(s32[8]{0:T(128)S(1)} %copy-done.9, bf16[32,512,128]{2,1,0:T(8,128)(2,1)S(1)} %copy-done, f32[1,128]{1,0:T(1,128)S(1)} %bitcast.23, f32[1,128]{1,0:T(1,128)S(1)} %bitcast.25), custom_call_target="tpu_custom_call" | custom-call | tf_op jit(solution)/shard_map/pallas_call | solution.py:206
  8.1 0.5 collective-permute-start.7
  8.6 0.0 copy-done.12
  8.6 0.0 copy-done.4
  8.6 0.0 copy-done.7
  8.6 0.0 copy-start.2
  8.6 6.7 %shard_map.109.refs_0_ = bf16[128,384]{1,0:T(8,128)(2,1)S(1)} custom-call(bf16[32,512,128]{2,1,0:T(8,128)(2,1)S(1)} %copy-done, s32[1,512]{1,0:T(1,128)S(1)} %bitcast.19, f32[1,128]{1,0:T(1,128)S(1)} %bitcast.24, f32[1,128]{1,0:T(1,128)S(1)} %bitcast.26, bf16[8,128]{1,0:T(8,128)(2,1)S(1)} %pad.4.w_ref), custom_call_target="tpu_custom_call" | custom-call | tf_op jit(solution)/shard_map/pallas_call | solution.py:221
  15.3 0.0 copy-start.3
  15.4 0.0 copy-start.5
  15.4 0.0 copy-start.10
  15.4 0.0 copy-start.11
  15.4 5.7 %collective-permute-start.6 = (bf16[128,384]{1,0:T(8,128)(2,1)S(1)}, bf16[128,384]{1,0:T(8,128)(2,1)S(1)}, u32[]{:S(2)}, u32[]{:S(2)}) collective-permute-start(bf16[128,384]{1,0:T(8,128)(2,1)S(1)} %shard_map.109.refs_0_), channel_id=1, source_target_pairs={{0,14},{1,15},{2,12},{3,13},{4,10},{5,11},{6,8},{7,9},{8,6},{9,7},... | collective-permute-start | bytes 294920 | tf_op jit(solution)/shard_map/ppermute | solution.py:204
  21.0 0.2 collective-permute-start.5
  21.3 0.7 collective-permute-start.4
  22.0 2.0 %collective-permute-start.3 = (bf16[128,384]{1,0:T(8,128)(2,1)S(1)}, bf16[128,384]{1,0:T(8,128)(2,1)S(1)}, u32[]{:S(2)}, u32[]{:S(2)}) collective-permute-start(bf16[128,384]{1,0:T(8,128)(2,1)S(1)} %shard_map.109.refs_0_), channel_id=1, source_target_pairs={{0,8},{1,9},{2,10},{3,11},{4,12},{5,13},{6,14},{7,15},{8,0},{9,1},... | collective-permute-start | bytes 294920 | tf_op jit(solution)/shard_map/ppermute | solution.py:204
  24.0 0.5 collective-permute-done.6.refs_7_
  24.6 9.1 %collective-permute-start.2 = (bf16[128,384]{1,0:T(8,128)(2,1)S(1)}, bf16[128,384]{1,0:T(8,128)(2,1)S(1)}, u32[]{:S(2)}, u32[]{:S(2)}) collective-permute-start(bf16[128,384]{1,0:T(8,128)(2,1)S(1)} %shard_map.109.refs_0_), channel_id=1, source_target_pairs={{0,6},{1,7},{2,4},{3,5},{4,2},{5,3},{6,0},{7,1},{8,14},{9,15},{10,... | collective-permute-start | bytes 294920 | tf_op jit(solution)/shard_map/ppermute | solution.py:204
  33.7 0.0 collective-permute-done.5.refs_6_
  33.7 1.5 %collective-permute-start.1 = (bf16[128,384]{1,0:T(8,128)(2,1)S(1)}, bf16[128,384]{1,0:T(8,128)(2,1)S(1)}, u32[]{:S(2)}, u32[]{:S(2)}) collective-permute-start(bf16[128,384]{1,0:T(8,128)(2,1)S(1)} %shard_map.109.refs_0_), channel_id=1, source_target_pairs={{0,4},{1,5},{2,6},{3,7},{4,0},{5,1},{6,2},{7,3},{8,12},{9,13},{10,... | collective-permute-start | bytes 294920 | tf_op jit(solution)/shard_map/ppermute | solution.py:204
  35.1 0.0 collective-permute-done.7.other_ref
  35.1 0.5 collective-permute-start
  35.7 0.1 stack.51.place_ref
  35.7 0.0 copy-done.2
  35.7 2.2 %shard_map.111 = (bf16[16,384,128]{2,1,0:T(8,128)(2,1)S(1)}, bf16[16,384,128]{2,1,0:T(8,128)(2,1)S(1)}) custom-call(bf16[8,512,128]{2,1,0:T(8,128)(2,1)S(1)} %shard_map.110.own_ref, bf16[8,512,128]{2,1,0:T(8,128)(2,1)S(1)} %collective-permute-done.7.other_ref, s32[1,512]{1,0:T(1,128)S(1)} %bitcast.20, bf16[128,512]{1,0:T(8,128)(2,1)S(1)} %copy-done.2), custom_call_target="tpu_custom_call" | custom-call | tf_op jit(solution)/shard_map/pallas_call | solution.py:238
  37.9 0.0 copy-start.1
  37.9 1.2 %copy-done.1 = bf16[16,384,128]{2,1,0:T(8,128)(2,1)} copy-done((bf16[16,384,128]{2,1,0:T(8,128)(2,1)}, bf16[16,384,128]{2,1,0:T(8,128)(2,1)S(1)}, u32[]{:S(2)}) %copy-start.1) | copy-done | bytes 1572888
  39.1 0.0 collective-permute-done.4.refs_5_
  39.1 0.0 collective-permute-done.3.refs_4_
  39.1 1.3 %collective-permute-done.2.refs_3_ = bf16[128,384]{1,0:T(8,128)(2,1)S(1)} collective-permute-done((bf16[128,384]{1,0:T(8,128)(2,1)S(1)}, bf16[128,384]{1,0:T(8,128)(2,1)S(1)}, u32[]{:S(2)}, u32[]{:S(2)}) %collective-permute-start.2) | collective-permute-done | bytes 98336 | tf_op jit(solution)/shard_map/ppermute | solution.py:204
  40.4 0.9 collective-permute-done.1.refs_2_
  41.4 0.0 collective-permute-done.refs_1_
  41.4 0.0 copy-done.3
  41.4 0.0 copy-done.5
  41.4 0.0 copy-done.10
  41.4 0.0 copy-done.11
  41.4 42.2 %shard_map.112 = (bf16[16,32,128]{2,1,0:T(8,128)(2,1)S(1)}, bf16[16,32,128]{2,1,0:T(8,128)(2,1)S(1)}, bf16[16,32,128]{2,1,0:T(8,128)(2,1)S(1)}, bf16[16,32,128]{...) custom-call(s32[9]{0:T(128)S(1)} %stack.51.place_ref, ...), custom_call_target="tpu_custom_call" | custom-call | tf_op jit(solution)/shard_map/pallas_call | solution.py:254
  83.6 0.7 collective-permute-start.8
  84.2 0.0 collective-permute-start.9
  84.2 2.8 %collective-permute-start.10 = (bf16[16,32,128]{2,1,0:T(8,128)(2,1)}, bf16[16,32,128]{2,1,0:T(8,128)(2,1)S(1)}, u32[]{:S(2)}, u32[]{:S(2)}) collective-permute-start(bf16[16,32,128]{2,1,0:T(8,128)(2,1)} %get-tuple-element.20), channel_id=1, source_target_pairs={{0,6},{1,7},{2,4},{3,5},{4,2},{5,3},{6,0},{7,1},{8,14},{9,15},{10,... | collective-permute-start | bytes 393224 | tf_op jit(solution)/shard_map/ppermute | solution.py:204
  87.1 1.2 %collective-permute-start.11 = (bf16[16,32,128]{2,1,0:T(8,128)(2,1)}, bf16[16,32,128]{2,1,0:T(8,128)(2,1)S(1)}, u32[]{:S(2)}, u32[]{:S(2)}) collective-permute-start(bf16[16,32,128]{2,1,0:T(8,128)(2,1)} %get-tuple-element.21), channel_id=1, source_target_pairs={{0,8},{1,9},{2,10},{3,11},{4,12},{5,13},{6,14},{7,15},{8,0},{9,1},... | collective-permute-start | bytes 393224 | tf_op jit(solution)/shard_map/ppermute | solution.py:204
  88.2 1.9 %collective-permute-start.12 = (bf16[16,32,128]{2,1,0:T(8,128)(2,1)}, bf16[16,32,128]{2,1,0:T(8,128)(2,1)S(1)}, u32[]{:S(2)}, u32[]{:S(2)}) collective-permute-start(bf16[16,32,128]{2,1,0:T(8,128)(2,1)} %get-tuple-element.22), channel_id=1, source_target_pairs={{0,10},{1,11},{2,8},{3,9},{4,14},{5,15},{6,12},{7,13},{8,2},{9,3},... | collective-permute-start | bytes 393224 | tf_op jit(solution)/shard_map/ppermute | solution.py:204
  90.1 0.0 collective-permute-done.8.refs_1_
  90.1 2.5 %collective-permute-start.13 = (bf16[16,32,128]{2,1,0:T(8,128)(2,1)S(1)}, bf16[16,32,128]{2,1,0:T(8,128)(2,1)S(1)}, u32[]{:S(2)}, u32[]{:S(2)}) collective-permute-start(bf16[16,32,128]{2,1,0:T(8,128)(2,1)S(1)} %get-tuple-element.23), channel_id=1, source_target_pairs={{0,12},{1,13},{2,14},{3,15},{4,8},{5,9},{6,10},{7,11},{8,4},{9,5},... | collective-permute-start | bytes 393224 | tf_op jit(solution)/shard_map/ppermute | solution.py:204
  92.6 0.0 collective-permute-done.9.refs_2_
  92.6 3.8 %collective-permute-start.14 = (bf16[16,32,128]{2,1,0:T(8,128)(2,1)S(1)}, bf16[16,32,128]{2,1,0:T(8,128)(2,1)S(1)}, u32[]{:S(2)}, u32[]{:S(2)}) collective-permute-start(bf16[16,32,128]{2,1,0:T(8,128)(2,1)S(1)} %get-tuple-element.24), channel_id=1, source_target_pairs={{0,14},{1,15},{2,12},{3,13},{4,10},{5,11},{6,8},{7,9},{8,6},{9,7},... | collective-permute-start | bytes 393224 | tf_op jit(solution)/shard_map/ppermute | solution.py:204
  96.3 0.1 stack.49.place_ref
  96.4 0.0 collective-permute-done.10.refs_3_
  96.4 8.9 %collective-permute-done.11.refs_4_ = bf16[16,32,128]{2,1,0:T(8,128)(2,1)S(1)} collective-permute-done((bf16[16,32,128]{2,1,0:T(8,128)(2,1)}, bf16[16,32,128]{2,1,0:T(8,128)(2,1)S(1)}, u32[]{:S(2)}, u32[]{:S(2)}) %collective-permute-start.11) | collective-permute-done | bytes 131104 | tf_op jit(solution)/shard_map/ppermute | solution.py:204
  105.3 3.1 %collective-permute-done.12.refs_5_ = bf16[16,32,128]{2,1,0:T(8,128)(2,1)S(1)} collective-permute-done((bf16[16,32,128]{2,1,0:T(8,128)(2,1)}, bf16[16,32,128]{2,1,0:T(8,128)(2,1)S(1)}, u32[]{:S(2)}, u32[]{:S(2)}) %collective-permute-start.12) | collective-permute-done | bytes 131104 | tf_op jit(solution)/shard_map/ppermute | solution.py:204
  108.4 0.0 collective-permute-done.13.refs_6_
  108.4 0.0 collective-permute-done.14.refs_7_
  108.4 1.6 %shard_map.113 = bf16[128,32,128]{2,1,0:T(8,128)(2,1)} custom-call(s32[8]{0:T(128)S(1)} %stack.49.place_ref, bf16[16,32,128]{2,1,0:T(8,128)(2,1)S(1)} %get-tuple-element.17.refs_0_, bf16[16,32,128]{2,1,0:T(8,128)(2,1)S(1)} %collective-permute-done.8.refs_1_, bf16[16,32,128]{2,1,0:T(8,128)(2,1)S(1)} %collective-permute-done.9.refs_2_, ...), custom_call_target="tpu_custom_call" | custom-call | tf_op jit(solution)/shard_map/pallas_call | solution.py:285
  (1 shorter events, 0.0 us)
Async XLA Ops:
  0.0 2.2 %copy-start = (bf16[32,512,128]{2,1,0:T(8,128)(2,1)S(1)}, bf16[32,512,128]{2,1,0:T(8,128)(2,1)}, u32[]{:S(2)}) copy-start(bf16[32,512,128]{2,1,0:T(8,128)(2,1)} %pair_ref.3) | copy-start | bytes 12582916
  2.2 0.7 copy-start.6
  2.8 0.7 copy-start.8
  3.5 0.7 copy-start.9
  4.2 4.4 %copy-start.12 = (bf16[128,4]{0,1:T(4,128)(2,1)S(1)}, bf16[128,4]{0,1:T(4,128)(2,1)}, u32[]{:S(2)}) copy-start(bf16[128,4]{0,1:T(4,128)(2,1)} %param.19) | copy-start | bytes 3076
  4.2 4.4 %copy-start.4 = (s32[512]{0:T(512)S(1)}, s32[512]{0:T(512)}, u32[]{:S(2)}) copy-start(s32[512]{0:T(512)} %param.13) | copy-start | bytes 6148
  4.2 4.4 %copy-start.7 = (f32[128]{0:T(128)S(1)}, f32[128]{0:T(128)}, u32[]{:S(2)}) copy-start(f32[128]{0:T(128)} %param.15) | copy-start | bytes 1540
  8.1 27.1 %collective-permute-start.7 = (bf16[8,512,128]{2,1,0:T(8,128)(2,1)S(1)}, bf16[8,512,128]{2,1,0:T(8,128)(2,1)S(1)}, u32[]{:S(2)}, u32[]{:S(2)}) collective-permute-start(bf16[8,512,128]{2,1,0:T(8,128)(2,1)S(1)} %shard_map.110.own_ref), channel_id=1, source_target_pairs={{0,1},{1,0},{2,3},{3,2},{4,5},{5,4},{6,7},{7,6},{8,9},{9,8},{10,11... | collective-permute-start | bytes 3145736 | tf_op jit(solution)/shard_map/ppermute | solution.py:204
  8.6 27.1 %copy-start.2 = (bf16[128,512]{1,0:T(8,128)(2,1)S(1)}, bf16[128,512]{1,0:T(8,128)(2,1)}, u32[]{:S(2)}) copy-start(bf16[128,512]{1,0:T(8,128)(2,1)} %refs_14_.1) | copy-start | bytes 393220
  15.3 26.0 %copy-start.3 = (bf16[128,128]{1,0:T(8,128)(2,1)S(1)}, bf16[128,128]{1,0:T(8,128)(2,1)}, u32[]{:S(2)}) copy-start(bf16[128,128]{1,0:T(8,128)(2,1)} %refs_16_.1) | copy-start | bytes 98308
  15.4 26.0 %copy-start.5 = (s32[512]{0:T(512)S(1)}, s32[512]{0:T(512)}, u32[]{:S(2)}) copy-start(s32[512]{0:T(512)} %param.14) | copy-start | bytes 6148
  15.4 26.0 %copy-start.10 = (f32[4]{0:T(128)S(1)}, f32[4]{0:T(128)}, u32[]{:S(2)}) copy-start(f32[4]{0:T(128)} %chain_bias_ref.1) | copy-start | bytes 52
  15.4 26.0 %copy-start.11 = (f32[128]{0:T(128)S(1)}, f32[128]{0:T(128)}, u32[]{:S(2)}) copy-start(f32[128]{0:T(128)} %param.18) | copy-start | bytes 1540
  15.4 9.2 %collective-permute-start.6 = (bf16[128,384]{1,0:T(8,128)(2,1)S(1)}, bf16[128,384]{1,0:T(8,128)(2,1)S(1)}, u32[]{:S(2)}, u32[]{:S(2)}) collective-permute-start(bf16[128,384]{1,0:T(8,128)(2,1)S(1)} %shard_map.109.refs_0_), channel_id=1, source_target_pairs={{0,14},{1,15},{2,12},{3,13},{4,10},{5,11},{6,8},{7,9},{8,6},{9,7},... | collective-permute-start | bytes 294920 | tf_op jit(solution)/shard_map/ppermute | solution.py:204
  21.0 12.6 %collective-permute-start.5 = (bf16[128,384]{1,0:T(8,128)(2,1)S(1)}, bf16[128,384]{1,0:T(8,128)(2,1)S(1)}, u32[]{:S(2)}, u32[]{:S(2)}) collective-permute-start(bf16[128,384]{1,0:T(8,128)(2,1)S(1)} %shard_map.109.refs_0_), channel_id=1, source_target_pairs={{0,12},{1,13},{2,14},{3,15},{4,8},{5,9},{6,10},{7,11},{8,4},{9,5},... | collective-permute-start | bytes 294920 | tf_op jit(solution)/shard_map/ppermute | solution.py:204
  21.3 17.8 %collective-permute-start.4 = (bf16[128,384]{1,0:T(8,128)(2,1)S(1)}, bf16[128,384]{1,0:T(8,128)(2,1)S(1)}, u32[]{:S(2)}, u32[]{:S(2)}) collective-permute-start(bf16[128,384]{1,0:T(8,128)(2,1)S(1)} %shard_map.109.refs_0_), channel_id=1, source_target_pairs={{0,10},{1,11},{2,8},{3,9},{4,14},{5,15},{6,12},{7,13},{8,2},{9,3},... | collective-permute-start | bytes 294920 | tf_op jit(solution)/shard_map/ppermute | solution.py:204
  22.0 17.1 %collective-permute-start.3 = (bf16[128,384]{1,0:T(8,128)(2,1)S(1)}, bf16[128,384]{1,0:T(8,128)(2,1)S(1)}, u32[]{:S(2)}, u32[]{:S(2)}) collective-permute-start(bf16[128,384]{1,0:T(8,128)(2,1)S(1)} %shard_map.109.refs_0_), channel_id=1, source_target_pairs={{0,8},{1,9},{2,10},{3,11},{4,12},{5,13},{6,14},{7,15},{8,0},{9,1},... | collective-permute-start | bytes 294920 | tf_op jit(solution)/shard_map/ppermute | solution.py:204
  24.6 15.8 %collective-permute-start.2 = (bf16[128,384]{1,0:T(8,128)(2,1)S(1)}, bf16[128,384]{1,0:T(8,128)(2,1)S(1)}, u32[]{:S(2)}, u32[]{:S(2)}) collective-permute-start(bf16[128,384]{1,0:T(8,128)(2,1)S(1)} %shard_map.109.refs_0_), channel_id=1, source_target_pairs={{0,6},{1,7},{2,4},{3,5},{4,2},{5,3},{6,0},{7,1},{8,14},{9,15},{10,... | collective-permute-start | bytes 294920 | tf_op jit(solution)/shard_map/ppermute | solution.py:204
  33.7 7.7 %collective-permute-start.1 = (bf16[128,384]{1,0:T(8,128)(2,1)S(1)}, bf16[128,384]{1,0:T(8,128)(2,1)S(1)}, u32[]{:S(2)}, u32[]{:S(2)}) collective-permute-start(bf16[128,384]{1,0:T(8,128)(2,1)S(1)} %shard_map.109.refs_0_), channel_id=1, source_target_pairs={{0,4},{1,5},{2,6},{3,7},{4,0},{5,1},{6,2},{7,3},{8,12},{9,13},{10,... | collective-permute-start | bytes 294920 | tf_op jit(solution)/shard_map/ppermute | solution.py:204
  35.1 6.2 %collective-permute-start = (bf16[128,384]{1,0:T(8,128)(2,1)S(1)}, bf16[128,384]{1,0:T(8,128)(2,1)S(1)}, u32[]{:S(2)}, u32[]{:S(2)}) collective-permute-start(bf16[128,384]{1,0:T(8,128)(2,1)S(1)} %shard_map.109.refs_0_), channel_id=1, source_target_pairs={{0,2},{1,3},{2,0},{3,1},{4,6},{5,7},{6,4},{7,5},{8,10},{9,11},{10,... | collective-permute-start | bytes 294920 | tf_op jit(solution)/shard_map/ppermute | solution.py:204
  37.9 1.2 %copy-start.1 = (bf16[16,384,128]{2,1,0:T(8,128)(2,1)}, bf16[16,384,128]{2,1,0:T(8,128)(2,1)S(1)}, u32[]{:S(2)}) copy-start(bf16[16,384,128]{2,1,0:T(8,128)(2,1)S(1)} %get-tuple-element.16.refs_11_) | copy-start | bytes 4718596
  83.6 6.5 %collective-permute-start.8 = (bf16[16,32,128]{2,1,0:T(8,128)(2,1)S(1)}, bf16[16,32,128]{2,1,0:T(8,128)(2,1)S(1)}, u32[]{:S(2)}, u32[]{:S(2)}) collective-permute-start(bf16[16,32,128]{2,1,0:T(8,128)(2,1)S(1)} %get-tuple-element.18), channel_id=1, source_target_pairs={{0,2},{1,3},{2,0},{3,1},{4,6},{5,7},{6,4},{7,5},{8,10},{9,11},{10,... | collective-permute-start | bytes 393224 | tf_op jit(solution)/shard_map/ppermute | solution.py:204
  84.2 8.3 %collective-permute-start.9 = (bf16[16,32,128]{2,1,0:T(8,128)(2,1)S(1)}, bf16[16,32,128]{2,1,0:T(8,128)(2,1)S(1)}, u32[]{:S(2)}, u32[]{:S(2)}) collective-permute-start(bf16[16,32,128]{2,1,0:T(8,128)(2,1)S(1)} %get-tuple-element.19), channel_id=1, source_target_pairs={{0,4},{1,5},{2,6},{3,7},{4,0},{5,1},{6,2},{7,3},{8,12},{9,13},{10,... | collective-permute-start | bytes 393224 | tf_op jit(solution)/shard_map/ppermute | solution.py:204
  84.2 12.2 %collective-permute-start.10 = (bf16[16,32,128]{2,1,0:T(8,128)(2,1)}, bf16[16,32,128]{2,1,0:T(8,128)(2,1)S(1)}, u32[]{:S(2)}, u32[]{:S(2)}) collective-permute-start(bf16[16,32,128]{2,1,0:T(8,128)(2,1)} %get-tuple-element.20), channel_id=1, source_target_pairs={{0,6},{1,7},{2,4},{3,5},{4,2},{5,3},{6,0},{7,1},{8,14},{9,15},{10,... | collective-permute-start | bytes 393224 | tf_op jit(solution)/shard_map/ppermute | solution.py:204
  87.1 18.2 %collective-permute-start.11 = (bf16[16,32,128]{2,1,0:T(8,128)(2,1)}, bf16[16,32,128]{2,1,0:T(8,128)(2,1)S(1)}, u32[]{:S(2)}, u32[]{:S(2)}) collective-permute-start(bf16[16,32,128]{2,1,0:T(8,128)(2,1)} %get-tuple-element.21), channel_id=1, source_target_pairs={{0,8},{1,9},{2,10},{3,11},{4,12},{5,13},{6,14},{7,15},{8,0},{9,1},... | collective-permute-start | bytes 393224 | tf_op jit(solution)/shard_map/ppermute | solution.py:204
  88.2 20.2 %collective-permute-start.12 = (bf16[16,32,128]{2,1,0:T(8,128)(2,1)}, bf16[16,32,128]{2,1,0:T(8,128)(2,1)S(1)}, u32[]{:S(2)}, u32[]{:S(2)}) collective-permute-start(bf16[16,32,128]{2,1,0:T(8,128)(2,1)} %get-tuple-element.22), channel_id=1, source_target_pairs={{0,10},{1,11},{2,8},{3,9},{4,14},{5,15},{6,12},{7,13},{8,2},{9,3},... | collective-permute-start | bytes 393224 | tf_op jit(solution)/shard_map/ppermute | solution.py:204
  90.1 18.3 %collective-permute-start.13 = (bf16[16,32,128]{2,1,0:T(8,128)(2,1)S(1)}, bf16[16,32,128]{2,1,0:T(8,128)(2,1)S(1)}, u32[]{:S(2)}, u32[]{:S(2)}) collective-permute-start(bf16[16,32,128]{2,1,0:T(8,128)(2,1)S(1)} %get-tuple-element.23), channel_id=1, source_target_pairs={{0,12},{1,13},{2,14},{3,15},{4,8},{5,9},{6,10},{7,11},{8,4},{9,5},... | collective-permute-start | bytes 393224 | tf_op jit(solution)/shard_map/ppermute | solution.py:204
  92.6 15.9 %collective-permute-start.14 = (bf16[16,32,128]{2,1,0:T(8,128)(2,1)S(1)}, bf16[16,32,128]{2,1,0:T(8,128)(2,1)S(1)}, u32[]{:S(2)}, u32[]{:S(2)}) collective-permute-start(bf16[16,32,128]{2,1,0:T(8,128)(2,1)S(1)} %get-tuple-element.24), channel_id=1, source_target_pairs={{0,14},{1,15},{2,12},{3,13},{4,10},{5,11},{6,8},{7,9},{8,6},{9,7},... | collective-permute-start | bytes 393224 | tf_op jit(solution)/shard_map/ppermute | solution.py:204

commit v2 on v1

v2 whole, which is shorter than its diff:
```python
import functools

import jax
import jax.numpy as jnp
from jax import lax
from jax.experimental import pallas as pl
from jax.experimental.pallas import tpu as pltpu
from jax.sharding import PartitionSpec as P

F32, BF16 = jnp.float32, jnp.bfloat16
VMEM = pl.BlockSpec(memory_space=pltpu.VMEM)
SMEM = pl.BlockSpec(memory_space=pltpu.SMEM)
ANY = pl.BlockSpec(memory_space=pl.ANY)
NT = (((1,), (1,)), ((), ()))
PARAMS = pltpu.CompilerParams(vmem_limit_bytes=32 * 1024 * 1024)


def normalised(rows, gain, shift):
    channels = rows.shape[-1]
    x = rows.astype(F32)
    mean = jnp.dot(
        rows, jnp.full((channels, channels), 1.0 / channels, BF16), preferred_element_type=F32
    )
    d = x - mean
    var = jnp.mean(d * d, axis=-1, keepdims=True)
    return (d * lax.rsqrt(var + 1e-05) * gain + shift).astype(BF16)


def live_ranks(mask_row):
    tokens = mask_row.shape[1]
    upper = lax.broadcasted_iota(jnp.int32, (tokens, tokens), 0) <= lax.broadcasted_iota(
        jnp.int32, (tokens, tokens), 1
    )
    ones = jnp.broadcast_to(mask_row.astype(F32), (8, tokens)).astype(BF16)
    running = jnp.dot(ones, upper.astype(F32).astype(BF16), preferred_element_type=F32)[0:1]
    return jnp.where(mask_row == 1, running - 1.0, -1.0)


def picking(mask_row, live):
    ranks = live_ranks(mask_row).astype(jnp.int32)
    wanted = lax.broadcasted_iota(jnp.int32, (live, mask_row.shape[1]), 0)
    return (wanted == ranks).astype(F32).astype(BF16)


def window_kernel(rows_ref, after_ref, pair_ref, gain_ref, shift_ref, out_ref, held, sems):
    count = held.shape[0]
    rows_held = pair_ref.shape[0]
    copies = []
    for i in range(count):
        at = lax.rem(rows_ref[i], rows_held)
        copies.append(pltpu.make_async_copy(pair_ref.at[at], held.at[i], sems.at[i]))
        copies[-1].start()
    for i in range(count):
        copies[i].wait()
        out_ref[i] = normalised(held[i], gain_ref[...], shift_ref[...])


def bias_kernel(pair_ref, mask_ref, gain_ref, shift_ref, w_ref, out_ref, acc):
    step = pl.program_id(0)
    rows, tokens, channels = pair_ref.shape
    columns, live = out_ref.shape
    held = rows * pl.num_programs(0)
    heads = w_ref.shape[0]
    row_of = columns // heads
    column = lax.broadcasted_iota(jnp.int32, (heads, columns), 1)
    spread = (column // row_of == lax.broadcasted_iota(jnp.int32, (heads, columns), 0)).astype(F32)
    w = lax.dot_general(
        w_ref[...], spread.astype(BF16), (((0,), (0,)), ((), ())), preferred_element_type=F32
    )
    row_column = lax.broadcasted_iota(jnp.int32, (channels, columns), 1) % row_of
    xs, ws = [], []
    for i in range(rows):
        xs.append(normalised(pair_ref[i], gain_ref[...], shift_ref[...]))
        ws.append(jnp.where(row_column == step * rows + i, w, 0.0).astype(BF16))
    part = jnp.dot(
        jnp.concatenate(xs, axis=1), jnp.concatenate(ws, axis=0), preferred_element_type=F32
    )

    @pl.when(step == 0)
    def _():
        acc[...] = part

    @pl.when(step > 0)
    def _():
        acc[...] += part

    @pl.when(step == pl.num_programs(0) - 1)
    def _():
        full = acc[...].astype(BF16)
        taken = jnp.dot(picking(mask_ref[...], live), full, preferred_element_type=F32)
        out_ref[...] = taken.T.astype(BF16)


def key_value_kernel(own_ref, other_ref, mask_ref, w_ref, k_ref, v_ref, pick):
    count = own_ref.shape[0]
    live, inner = v_ref.shape[1:]
    pick[...] = picking(mask_ref[...], live)
    for i in range(count):
        both = jnp.concatenate([own_ref[i], other_ref[i]], axis=1)
        taken = jnp.dot(pick[...], both, preferred_element_type=F32).astype(BF16)
        c = own_ref.shape[2]
        for part in range(2):
            kv = jnp.dot(
                taken[:, part * c : (part + 1) * c],
                w_ref[:, inner : 3 * inner],
                preferred_element_type=F32,
            ).astype(BF16)
            k_ref[i + part * count] = kv[:, :inner].T
            v_ref[i + part * count] = kv[:, inner:]


def attention_kernel(heads, ms, me_ref, chain_bias_ref, *refs):
    blocks = len(ms)
    bias_refs, refs = refs[:blocks], refs[blocks:]
    own_ref, other_ref, k_ref, v_ref, mask_ref, chain_ref, w_ref, gate_bias_ref, w_out_ref = refs[:9]
    out_refs, (q_s, gate_s, added_s, gated_s) = refs[-4 - blocks : -4], refs[-4:]
    windows, inner, live = k_ref.shape
    half = windows // 2
    block = own_ref.shape[3]
    tokens = mask_ref.shape[1]
    size = inner // heads
    core, chip = lax.rem(me_ref[0], 2), lax.div(me_ref[0], 2)
    chain_row = jnp.broadcast_to(chain_ref[...].astype(F32), (8, tokens)).astype(BF16)
    chain_live = lax.dot_general(
        chain_row, picking(mask_ref[...], live), NT, preferred_element_type=F32
    )[0:1]
    lane_head = lax.broadcasted_iota(jnp.int32, (block, inner), 1) // size
    w_q = w_ref[:, :inner]
    w_g = w_ref[:, 3 * inner :]
    for b in range(blocks):
        at = lax.bitwise_xor(chip, ms[b])
        here = (
            lax.broadcasted_iota(jnp.int32, (block, tokens), 1)
            == (at * 2 + core) * block + lax.broadcasted_iota(jnp.int32, (block, tokens), 0)
        ).astype(F32)
        chain_here = jnp.sum(here * chain_ref[...].astype(F32), axis=1, keepdims=True)
        keep = jnp.sum(here * mask_ref[...].astype(F32), axis=1, keepdims=True)
        same = (chain_here == chain_live).astype(F32)
        for h in range(heads):
            rows = slice(h * block, (h + 1) * block)
            added_s[rows, :] = bias_refs[b][rows, :].astype(F32) + chain_bias_ref[h] * same
        for part, ref in enumerate((own_ref, other_ref)):
            x = ref[:, at, core].reshape(half * block, inner)
            span = pl.ds(part * half * block, half * block)
            q_s[span, :] = (
                jnp.dot(x, w_q, preferred_element_type=F32) * size ** (-0.5)
            ).astype(BF16)
            gate_s[span, :] = jax.nn.sigmoid(
                jnp.dot(x, w_g, preferred_element_type=F32) + gate_bias_ref[...]
            )

        def some_windows(g, carry):
            spans = [
                pl.ds(pl.multiple_of((g * half + i) * block, block), block) for i in range(half)
            ]
            scores = []
            for i in range(half):
                q = q_s[spans[i], :].astype(F32)
                spread = jnp.concatenate(
                    [jnp.where(lane_head == h, q, 0.0) for h in range(heads)], axis=0
                ).astype(BF16)
                scores.append(
                    jnp.dot(spread, k_ref[g * half + i], preferred_element_type=F32) + added_s[...]
                )
            tops = [jnp.max(s, axis=1, keepdims=True) for s in scores]
            raised = [jnp.exp(s - top) for s, top in zip(scores, tops)]
            shares = [1.0 / jnp.sum(r, axis=1, keepdims=True) for r in raised]
            mixed = [
                jnp.dot(r.astype(BF16), v_ref[g * half + i], preferred_element_type=F32)
                for i, r in enumerate(raised)
            ]
            for i in range(half):
                m = mixed[i] * shares[i]
                attended = m[0:block]
                for h in range(1, heads):
                    attended = jnp.where(lane_head == h, m[h * block : (h + 1) * block], attended)
                gated_s[spans[i], :] = (gate_s[spans[i], :] * attended).astype(BF16)
            return carry

        lax.fori_loop(0, 2, some_windows, 0)
        result = jnp.dot(gated_s[...], w_out_ref[...], preferred_element_type=F32)
        result = (result.reshape(windows, block, inner) * keep[None]).astype(BF16)
        out_refs[b][pl.ds(core * half, half)] = result[:half]
        out_refs[b][pl.ds((1 - core) * half, half)] = result[half:]


def gather_kernel(me_ref, *refs):
    parts, out_ref, sems = refs[:-2], refs[-2], refs[-1]
    count = parts[0].shape[0]
    chip = lax.div(me_ref[0], 2)
    copies = []
    for m, part in enumerate(parts):
        at = lax.bitwise_xor(chip, m) * count
        copies.append(pltpu.make_async_copy(part, out_ref.at[pl.ds(at, count)], sems.at[m]))
        copies[-1].start()
    for copy in copies:
        copy.wait()


def local(
    devices,
    pair,
    window_rows,
    token_mask,
    chain_ids,
    ln_gain,
    ln_shift,
    w_project,
    gate_bias,
    w_bias,
    chain_bias,
    w_out,
):
    rows_held, tokens, channels = pair.shape
    heads = w_bias.shape[1]
    inner = w_out.shape[0]
    count = window_rows.shape[0]
    live = tokens * 3 // 4
    owners = devices // 2
    me = lax.axis_index("row").astype(jnp.int32).reshape(1)
    mask_row = token_mask.reshape(1, tokens)
    chain_row = chain_ids.reshape(1, tokens)
    gain = ln_gain.reshape(1, channels)
    shift = ln_shift.reshape(1, channels)

    def swap(x, bits):
        return lax.ppermute(x, "row", [(i, i ^ bits) for i in range(devices)])

    step_rows = 8
    bias = pl.pallas_call(
        bias_kernel,
        grid=(rows_held // step_rows,),
        out_shape=jax.ShapeDtypeStruct((heads * rows_held, live), BF16),
        in_specs=[
            pl.BlockSpec((step_rows, tokens, channels), lambda i: (i, 0, 0)),
            pl.BlockSpec((1, tokens), lambda i: (0, 0)),
            pl.BlockSpec((1, channels), lambda i: (0, 0)),
            pl.BlockSpec((1, channels), lambda i: (0, 0)),
            pl.BlockSpec((heads, channels), lambda i: (0, 0)),
        ],
        out_specs=pl.BlockSpec((heads * rows_held, live), lambda i: (0, 0)),
        scratch_shapes=[pltpu.VMEM((tokens, heads * rows_held), F32)],
    )(pair, mask_row, gain, shift, w_bias.T)

    far = [m for m in range(owners // 2, owners) if m % 2 == 0]
    passed = [m + 1 for m in far]
    near = list(range(1, owners // 2))
    biases = {0: bias}
    for m in far[::-1] + near[::-1]:
        biases[m] = swap(bias, 2 * m)
    for m in passed:
        biases[m] = swap(biases[m - 1], 2)

    own = pl.pallas_call(
        window_kernel,
        out_shape=jax.ShapeDtypeStruct((count, tokens, channels), BF16),
        in_specs=[SMEM, ANY, ANY, VMEM, VMEM],
        out_specs=VMEM,
        scratch_shapes=[
            pltpu.VMEM((count, tokens, channels), BF16),
            pltpu.SemaphoreType.DMA((count,)),
        ],
        compiler_params=PARAMS,
    )(window_rows, bias, pair, gain, shift)
    other = swap(own, 1)

    keys, values = pl.pallas_call(
        key_value_kernel,
        out_shape=[
            jax.ShapeDtypeStruct((2 * count, inner, live), BF16),
            jax.ShapeDtypeStruct((2 * count, live, inner), BF16),
        ],
        in_specs=[VMEM] * 4,
        out_specs=[VMEM] * 2,
        scratch_shapes=[pltpu.VMEM((live, tokens), BF16)],
        compiler_params=PARAMS,
    )(own, other, mask_row, w_project)

    split = (count, owners, 2, rows_held, channels)
    own, other = own.reshape(split), other.reshape(split)
    updates = {}
    after = bias
    for ms in (far, [0] + near, passed):
        blocks = len(ms)
        rows = 2 * count * rows_held
        outs = pl.pallas_call(
            functools.partial(attention_kernel, heads, ms),
            out_shape=[jax.ShapeDtypeStruct((2 * count, rows_held, channels), BF16)] * blocks,
            in_specs=[SMEM, SMEM] + [VMEM] * (blocks + 9) + [ANY],
            out_specs=[VMEM] * blocks,
            scratch_shapes=[
                pltpu.VMEM((rows, inner), BF16),
                pltpu.VMEM((rows, inner), F32),
                pltpu.VMEM((heads * rows_held, live), F32),
                pltpu.VMEM((rows, inner), BF16),
            ],
            compiler_params=PARAMS,
        )(
            me,
            chain_bias,
            *[biases[m] for m in ms],
            own,
            other,
            keys,
            values,
            mask_row,
            chain_row,
            w_project,
            gate_bias.reshape(1, inner),
            w_out,
            after,
        )
        after = outs[0]
        for m, out in zip(ms, outs):
            updates[m] = out if m == 0 else swap(out, 2 * m)

    return pl.pallas_call(
        gather_kernel,
        out_shape=jax.ShapeDtypeStruct((owners * 2 * count, rows_held, channels), BF16),
        in_specs=[SMEM] + [ANY] * owners,
        out_specs=ANY,
        scratch_shapes=[pltpu.SemaphoreType.DMA((owners,))],
        compiler_params=PARAMS,
    )(me, *[updates[m] for m in range(owners)])


def solution(mesh):
    placed = (
        P(("groups", "row"), None, None),
        P(("groups", "row")),
        P("groups"),
        P("groups"),
        P(),
        P(),
        P(),
        P(),
        P(),
        P(),
        P(),
    )
    return jax.shard_map(
        functools.partial(local, mesh.shape["row"]),
        mesh=mesh,
        in_specs=placed,
        out_specs=P("groups", "row", None),
        check_vma=False,
    )
```

time: 112 us -> 83.1 us (0.74); the launches traced: 110 us -> 82.9 us
  Pallas kernels: 56.5 us -> 31.7 us
  waiting for transfers between devices: 14.8 us -> 28.6 us
  starting transfers between devices: 33 us -> 20.2 us
  local copies, waits for them, and re-layouts: 5.55 us -> 2.23 us
    pallas_call x1 -> x3, Pallas kernels: 42.2 us -> 17.3 us  [local(): pl.pallas_call(functools.partial(attention_kernel, heads, ms), out_shape=...]
    ppermute x15, waiting for transfers between devices: 14.8 us -> 28.6 us  [swap(): return lax.ppermute(x, 'row', [(i, i ^ bits) for i in range(devices)])]
    ppermute x15, starting transfers between devices: 33 us -> 20.2 us  [swap(): return lax.ppermute(x, 'row', [(i, i ^ bits) for i in range(devices)])]
    unnamed x26 -> x20, local copies, waits for them, and re-layouts: 5.37 us -> 2.23 us
  transfers between devices with their start and end apart: 15 -> 15, of which waited for: 5 -> 5; matrix products, arithmetic and copies ran while one was open for 0% -> 0% of each run, Pallas kernels for 8% -> 13%
where the time goes in v2:
time: 83.1 us; the launch traced here: 82.9 us
  Pallas kernels  31.7 us (38%)
  waiting for transfers between devices  28.6 us (34%)
  starting transfers between devices  20.2 us (24%)
  local copies, waits for them, and re-layouts  2.23 us (3%)
    ppermute x15, waiting for transfers between devices, swap(): return lax.ppermute(x, 'row', [(i, i ^ bits) for i in range(devices)])  28.6 us
    ppermute x15, starting transfers between devices, swap(): return lax.ppermute(x, 'row', [(i, i ^ bits) for i in range(devices)])  20.2 us
    pallas_call x3, Pallas kernels, local(): pl.pallas_call(functools.partial(attention_kernel, heads, ms), out_shape=...  17.3 us
    pallas_call x1, Pallas kernels, local(): pl.pallas_call(bias_kernel, grid=(rows_held // step_rows,), out_shape=jax...  6.79 us
    pallas_call x1, Pallas kernels, local(): pl.pallas_call(window_kernel, out_shape=jax.ShapeDtypeStruct((count, toke...  4.32 us
    unnamed x20, local copies, waits for them, and re-layouts  2.23 us
    pallas_call x1, Pallas kernels, local(): pl.pallas_call(key_value_kernel, out_shape=[jax.ShapeDtypeStruct((2 * cou...  2.22 us
  transfers between devices with their start and end apart: 15, of which 5 were waited for; matrix products, arithmetic and copies ran while one was open for 0% of the time, Pallas kernels for 13%

profile of v2, /device:TPU:0, one launch (start us, length us, event | category | flops | bytes accessed | tf_op | source)
XLA Modules:
  0.0 82.9 jit_solution(8205626179094637252)
XLA Ops:
  0.0 0.0 copy-start.7
  0.0 0.0 copy-start.8
  0.0 0.0 copy-start.9
  0.0 6.8 %shard_map.109.after_ref.refs_11_.refs_0_ = bf16[128,384]{1,0:T(8,128)(2,1)} custom-call(bf16[32,512,128]{2,1,0:T(8,128)(2,1)} %pair_ref.3, s32[1,512]{1,0:T(1,128)} %bitcast.15, f32[1,128]{1,0:T(1,128)} %bitcast.26, f32[1,128]{1,0:T(1,128)} %bitcast.28, bf16[4,128]{1,0:T(4,128)(2,1)} %bitcast.30), custom_call_target="tpu_custom_call" | custom-call | tf_op jit(solution)/shard_map/pallas_call | solution.py:230
  6.8 0.0 copy-done.7
  6.8 0.0 copy-done.8
  6.8 0.0 copy-done.9
  6.8 0.0 copy-start
  6.8 2.2 %copy-done = bf16[32,512,128]{2,1,0:T(8,128)(2,1)S(1)} copy-done((bf16[32,512,128]{2,1,0:T(8,128)(2,1)S(1)}, bf16[32,512,128]{2,1,0:T(8,128)(2,1)}, u32[]{:S(2)}) %copy-start) | copy-done | bytes 4194328
  9.0 0.0 copy-start.1
  9.0 0.0 copy-start.3
  9.0 4.3 %shard_map.110.own_ref = bf16[8,512,128]{2,1,0:T(8,128)(2,1)S(1)} custom-call(s32[8]{0:T(128)S(1)} %copy-done.9, bf16[128,384]{1,0:T(8,128)(2,1)} %shard_map.109.after_ref.refs_11_.refs_0_, bf16[32,512,128]{2,1,0:T(8,128)(2,1)S(1)} %copy-done, f32[1,128]{1,0:T(1,128)S(1)} %bitcast.27, f32[1,128]{1,0:T(1,128)S(1)} %bitcast.29), custom_call_target="tpu_custom_call" | custom-call | tf_op jit(solution)/shard_map/pallas_call | solution.py:254
  13.3 0.0 copy-start.2
  13.4 0.0 copy-start.4
  13.4 0.0 copy-start.5
  13.4 0.0 copy-start.6
  13.4 0.5 collective-permute-start.3
  13.9 4.7 %collective-permute-start.5 = (bf16[128,384]{1,0:T(8,128)(2,1)}, bf16[128,384]{1,0:T(8,128)(2,1)S(1)}, u32[]{:S(2)}, u32[]{:S(2)}) collective-permute-start(bf16[128,384]{1,0:T(8,128)(2,1)} %shard_map.109.after_ref.refs_11_.refs_0_), channel_id=1, source_target_pairs={{0,12},{1,13},{2,14},{3,15},{4,8},{5,9},{6,10},{7,11},{8,4},{9,5},... | collective-permute-start | bytes 294920 | tf_op jit(solution)/shard_map/ppermute | solution.py:227
  18.6 0.0 collective-permute-start.4
  18.6 1.7 %collective-permute-start.2 = (bf16[128,384]{1,0:T(8,128)(2,1)}, bf16[128,384]{1,0:T(8,128)(2,1)S(1)}, u32[]{:S(2)}, u32[]{:S(2)}) collective-permute-start(bf16[128,384]{1,0:T(8,128)(2,1)} %shard_map.109.after_ref.refs_11_.refs_0_), channel_id=1, source_target_pairs={{0,6},{1,7},{2,4},{3,5},{4,2},{5,3},{6,0},{7,1},{8,14},{9,15},{10,... | collective-permute-start | bytes 294920 | tf_op jit(solution)/shard_map/ppermute | solution.py:227
  20.3 1.2 %collective-permute-start.1 = (bf16[128,384]{1,0:T(8,128)(2,1)}, bf16[128,384]{1,0:T(8,128)(2,1)S(1)}, u32[]{:S(2)}, u32[]{:S(2)}) collective-permute-start(bf16[128,384]{1,0:T(8,128)(2,1)} %shard_map.109.after_ref.refs_11_.refs_0_), channel_id=1, source_target_pairs={{0,4},{1,5},{2,6},{3,7},{4,0},{5,1},{6,2},{7,3},{8,12},{9,13},{10,... | collective-permute-start | bytes 294920 | tf_op jit(solution)/shard_map/ppermute | solution.py:227
  21.6 0.0 collective-permute-done.3.other_ref
  21.6 0.5 collective-permute-start
  22.1 0.0 copy-done.1
  22.1 0.0 copy-done.3
  22.1 2.2 %shard_map.111 = (bf16[16,128,384]{2,1,0:T(8,128)(2,1)S(1)}, bf16[16,384,128]{2,1,0:T(8,128)(2,1)S(1)}) custom-call(bf16[8,512,128]{2,1,0:T(8,128)(2,1)S(1)} %shard_map.110.own_ref, bf16[8,512,128]{2,1,0:T(8,128)(2,1)S(1)} %collective-permute-done.3.other_ref, s32[1,512]{1,0:T(1,128)S(1)} %bitcast.16, bf16[128,512]{1,0:T(8,128)(2,1)S(1)} %copy-done.1), custom_call_target="tpu_custom_call" | custom-call | tf_op jit(solution)/shard_map/pallas_call | solution.py:267
  24.3 0.0 collective-permute-done.5.refs_1_
  24.3 3.5 %collective-permute-done.4.refs_0_ = bf16[128,384]{1,0:T(8,128)(2,1)S(1)} collective-permute-done((bf16[128,384]{1,0:T(8,128)(2,1)}, bf16[128,384]{1,0:T(8,128)(2,1)S(1)}, u32[]{:S(2)}, u32[]{:S(2)}) %collective-permute-start.4) | collective-permute-done | bytes 98336 | tf_op jit(solution)/shard_map/ppermute | solution.py:227
  27.8 0.0 copy-done.2
  27.8 0.0 copy-done.4
  27.8 0.0 copy-done.5
  27.8 0.0 copy-done.6
  27.8 4.5 %shard_map.112 = (bf16[16,32,128]{2,1,0:T(8,128)(2,1)S(1)}, bf16[16,32,128]{2,1,0:T(8,128)(2,1)S(1)}) custom-call(s32[1]{0:T(128)} %bitcast.me_ref, f32[4]{0:T(128)S(1)} %copy-done.5, bf16[128,384]{1,0:T(8,128)(2,1)S(1)} %collective-permute-done.4.refs_0_, bf16[128,384]{1,0:T(8,128)(2,1)S(1)} %collective-permute-done.5.refs_1_, ...), custom_call_target="tpu_custom_call" | custom-call | tf_op jit(solution)/shard_map/pallas_call | solution.py:286
  32.3 0.0 collective-permute-done.2.refs_3_
  32.3 0.0 collective-permute-done.1.refs_2_
  32.3 0.0 collective-permute-done.refs_1_
  32.3 8.4 %shard_map.113 = (bf16[16,32,128]{2,1,0:T(8,128)(2,1)S(1)}, bf16[16,32,128]{2,1,0:T(8,128)(2,1)S(1)}, bf16[16,32,128]{2,1,0:T(8,128)(2,1)S(1)}, bf16[16,32,128]{2,1,0:T(8,128)(2,1)S(1)}) custom-call(s32[1]{0:T(128)} %bitcast.me_ref, f32[4]{0:T(128)S(1)} %copy-done.5, bf16[128,384]{1,0:T(8,128)(2,1)} %shard_map.109.after_ref.refs_11_.refs_0_, ...), custom_call_target="tpu_custom_call" | custom-call | tf_op jit(solution)/shard_map/pallas_call | solution.py:286
  40.7 1.6 %collective-permute-start.6 = (bf16[16,32,128]{2,1,0:T(8,128)(2,1)S(1)}, bf16[16,32,128]{2,1,0:T(8,128)(2,1)S(1)}, u32[]{:S(2)}, u32[]{:S(2)}) collective-permute-start(bf16[16,32,128]{2,1,0:T(8,128)(2,1)S(1)} %get-tuple-element.19), channel_id=1, source_target_pairs={{0,2},{1,3},{2,0},{3,1},{4,6},{5,7},{6,4},{7,5},{8,10},{9,11},{10,... | collective-permute-start | bytes 393224 | tf_op jit(solution)/shard_map/ppermute | solution.py:227
  42.3 0.0 collective-permute-start.7
  42.3 0.5 collective-permute-start.11
  42.8 1.5 %collective-permute-start.10 = (bf16[128,384]{1,0:T(8,128)(2,1)S(1)}, bf16[128,384]{1,0:T(8,128)(2,1)S(1)}, u32[]{:S(2)}, u32[]{:S(2)}) collective-permute-start(bf16[128,384]{1,0:T(8,128)(2,1)S(1)} %collective-permute-done.4.refs_0_), channel_id=1, source_target_pairs={{0,2},{1,3},{2,0},{3,1},{4,6},{5,7},{6,4},{7,5},{8,10},{9,11},{10,... | collective-permute-start | bytes 294920 | tf_op jit(solution)/shard_map/ppermute | solution.py:227
  44.3 2.0 %collective-permute-start.8 = (bf16[16,32,128]{2,1,0:T(8,128)(2,1)S(1)}, bf16[16,32,128]{2,1,0:T(8,128)(2,1)S(1)}, u32[]{:S(2)}, u32[]{:S(2)}) collective-permute-start(bf16[16,32,128]{2,1,0:T(8,128)(2,1)S(1)} %get-tuple-element.21), channel_id=1, source_target_pairs={{0,6},{1,7},{2,4},{3,5},{4,2},{5,3},{6,0},{7,1},{8,14},{9,15},{10,... | collective-permute-start | bytes 393224 | tf_op jit(solution)/shard_map/ppermute | solution.py:227
  46.3 5.5 %collective-permute-done.11.refs_1_ = bf16[128,384]{1,0:T(8,128)(2,1)S(1)} collective-permute-done((bf16[128,384]{1,0:T(8,128)(2,1)S(1)}, bf16[128,384]{1,0:T(8,128)(2,1)S(1)}, u32[]{:S(2)}, u32[]{:S(2)}) %collective-permute-start.11) | collective-permute-done | bytes 98336 | tf_op jit(solution)/shard_map/ppermute | solution.py:227
  51.7 1.1 %collective-permute-done.10.refs_0_ = bf16[128,384]{1,0:T(8,128)(2,1)S(1)} collective-permute-done((bf16[128,384]{1,0:T(8,128)(2,1)S(1)}, bf16[128,384]{1,0:T(8,128)(2,1)S(1)}, u32[]{:S(2)}, u32[]{:S(2)}) %collective-permute-start.10) | collective-permute-done | bytes 98336 | tf_op jit(solution)/shard_map/ppermute | solution.py:227
  52.8 4.5 %shard_map.114 = (bf16[16,32,128]{2,1,0:T(8,128)(2,1)S(1)}, bf16[16,32,128]{2,1,0:T(8,128)(2,1)S(1)}) custom-call(s32[1]{0:T(128)} %bitcast.me_ref, f32[4]{0:T(128)S(1)} %copy-done.5, bf16[128,384]{1,0:T(8,128)(2,1)S(1)} %collective-permute-done.10.refs_0_, bf16[128,384]{1,0:T(8,128)(2,1)S(1)} %collective-permute-done.11.refs_1_, ...), custom_call_target="tpu_custom_call" | custom-call | tf_op jit(solution)/shard_map/pallas_call | solution.py:286
  57.3 1.4 %collective-permute-start.12 = (bf16[16,32,128]{2,1,0:T(8,128)(2,1)S(1)}, bf16[16,32,128]{2,1,0:T(8,128)(2,1)S(1)}, u32[]{:S(2)}, u32[]{:S(2)}) collective-permute-start(bf16[16,32,128]{2,1,0:T(8,128)(2,1)S(1)} %get-tuple-element.22), channel_id=1, source_target_pairs={{0,10},{1,11},{2,8},{3,9},{4,14},{5,15},{6,12},{7,13},{8,2},{9,3},... | collective-permute-start | bytes 393224 | tf_op jit(solution)/shard_map/ppermute | solution.py:227
  58.6 2.2 %collective-permute-start.14 = (bf16[16,32,128]{2,1,0:T(8,128)(2,1)S(1)}, bf16[16,32,128]{2,1,0:T(8,128)(2,1)S(1)}, u32[]{:S(2)}, u32[]{:S(2)}) collective-permute-start(bf16[16,32,128]{2,1,0:T(8,128)(2,1)S(1)} %get-tuple-element.24), channel_id=1, source_target_pairs={{0,14},{1,15},{2,12},{3,13},{4,10},{5,11},{6,8},{7,9},{8,6},{9,7},... | collective-permute-start | bytes 393224 | tf_op jit(solution)/shard_map/ppermute | solution.py:227
  60.9 0.0 collective-permute-done.6.refs_1_
  60.9 2.4 %collective-permute-start.13 = (bf16[16,32,128]{2,1,0:T(8,128)(2,1)S(1)}, bf16[16,32,128]{2,1,0:T(8,128)(2,1)S(1)}, u32[]{:S(2)}, u32[]{:S(2)}) collective-permute-start(bf16[16,32,128]{2,1,0:T(8,128)(2,1)S(1)} %get-tuple-element.23), channel_id=1, source_target_pairs={{0,12},{1,13},{2,14},{3,15},{4,8},{5,9},{6,10},{7,11},{8,4},{9,5},... | collective-permute-start | bytes 393224 | tf_op jit(solution)/shard_map/ppermute | solution.py:227
  63.3 0.0 collective-permute-done.7.refs_2_
  63.3 0.0 collective-permute-start.9
  63.3 0.0 collective-permute-done.8.refs_3_
  63.3 11.2 %collective-permute-done.12.refs_5_ = bf16[16,32,128]{2,1,0:T(8,128)(2,1)S(1)} collective-permute-done((bf16[16,32,128]{2,1,0:T(8,128)(2,1)S(1)}, bf16[16,32,128]{2,1,0:T(8,128)(2,1)S(1)}, u32[]{:S(2)}, u32[]{:S(2)}) %collective-permute-start.12) | collective-permute-done | bytes 131104 | tf_op jit(solution)/shard_map/ppermute | solution.py:227
  74.5 0.0 collective-permute-done.14.refs_7_
  74.5 0.0 collective-permute-done.13.refs_6_
  74.5 7.4 %collective-permute-done.9.refs_4_ = bf16[16,32,128]{2,1,0:T(8,128)(2,1)S(1)} collective-permute-done((bf16[16,32,128]{2,1,0:T(8,128)(2,1)S(1)}, bf16[16,32,128]{2,1,0:T(8,128)(2,1)S(1)}, u32[]{:S(2)}, u32[]{:S(2)}) %collective-permute-start.9) | collective-permute-done | bytes 131104 | tf_op jit(solution)/shard_map/ppermute | solution.py:227
  81.9 1.0 %shard_map.115 = bf16[128,32,128]{2,1,0:T(8,128)(2,1)} custom-call(s32[1]{0:T(128)} %bitcast.me_ref, bf16[16,32,128]{2,1,0:T(8,128)(2,1)S(1)} %get-tuple-element.18.refs_11_.refs_0_, bf16[16,32,128]{2,1,0:T(8,128)(2,1)S(1)} %collective-permute-done.6.refs_1_, bf16[16,32,128]{2,1,0:T(8,128)(2,1)S(1)} %collective-permute-done.7.refs_2_, ...), custom_call_target="tpu_custom_call" | custom-call | tf_op jit(solution)/shard_map/pallas_call | solution.py:317
Async XLA Ops:
  0.0 6.8 %copy-start.7 = (f32[128]{0:T(128)S(1)}, f32[128]{0:T(128)}, u32[]{:S(2)}) copy-start(f32[128]{0:T(128)} %param.15) | copy-start | bytes 1540
  0.0 6.8 %copy-start.8 = (f32[128]{0:T(128)S(1)}, f32[128]{0:T(128)}, u32[]{:S(2)}) copy-start(f32[128]{0:T(128)} %param.16) | copy-start | bytes 1540
  0.0 6.8 %copy-start.9 = (s32[8]{0:T(128)S(1)}, s32[8]{0:T(128)}, u32[]{:S(2)}) copy-start(s32[8]{0:T(128)} %rows_ref.1) | copy-start | bytes 100
  6.8 2.2 %copy-start = (bf16[32,512,128]{2,1,0:T(8,128)(2,1)S(1)}, bf16[32,512,128]{2,1,0:T(8,128)(2,1)}, u32[]{:S(2)}) copy-start(bf16[32,512,128]{2,1,0:T(8,128)(2,1)} %pair_ref.3) | copy-start | bytes 12582916
  9.0 13.1 %copy-start.1 = (bf16[128,512]{1,0:T(8,128)(2,1)S(1)}, bf16[128,512]{1,0:T(8,128)(2,1)}, u32[]{:S(2)}) copy-start(bf16[128,512]{1,0:T(8,128)(2,1)} %refs_8_.3) | copy-start | bytes 393220
  9.0 13.1 %copy-start.3 = (s32[512]{0:T(512)S(1)}, s32[512]{0:T(512)}, u32[]{:S(2)}) copy-start(s32[512]{0:T(512)} %param.13) | copy-start | bytes 6148
  13.3 14.4 %copy-start.2 = (bf16[128,128]{1,0:T(8,128)(2,1)S(1)}, bf16[128,128]{1,0:T(8,128)(2,1)}, u32[]{:S(2)}) copy-start(bf16[128,128]{1,0:T(8,128)(2,1)} %refs_10_.5) | copy-start | bytes 98308
  13.4 14.4 %copy-start.4 = (s32[512]{0:T(512)S(1)}, s32[512]{0:T(512)}, u32[]{:S(2)}) copy-start(s32[512]{0:T(512)} %param.14) | copy-start | bytes 6148
  13.4 14.4 %copy-start.5 = (f32[4]{0:T(128)S(1)}, f32[4]{0:T(128)}, u32[]{:S(2)}) copy-start(f32[4]{0:T(128)} %chain_bias_ref.5) | copy-start | bytes 52
  13.4 14.4 %copy-start.6 = (f32[128]{0:T(128)S(1)}, f32[128]{0:T(128)}, u32[]{:S(2)}) copy-start(f32[128]{0:T(128)} %param.18) | copy-start | bytes 1540
  13.4 8.2 %collective-permute-start.3 = (bf16[8,512,128]{2,1,0:T(8,128)(2,1)S(1)}, bf16[8,512,128]{2,1,0:T(8,128)(2,1)S(1)}, u32[]{:S(2)}, u32[]{:S(2)}) collective-permute-start(bf16[8,512,128]{2,1,0:T(8,128)(2,1)S(1)} %shard_map.110.own_ref), channel_id=1, source_target_pairs={{0,1},{1,0},{2,3},{3,2},{4,5},{5,4},{6,7},{7,6},{8,9},{9,8},{10,11... | collective-permute-start | bytes 3145736 | tf_op jit(solution)/shard_map/ppermute | solution.py:227
  13.9 10.4 %collective-permute-start.5 = (bf16[128,384]{1,0:T(8,128)(2,1)}, bf16[128,384]{1,0:T(8,128)(2,1)S(1)}, u32[]{:S(2)}, u32[]{:S(2)}) collective-permute-start(bf16[128,384]{1,0:T(8,128)(2,1)} %shard_map.109.after_ref.refs_11_.refs_0_), channel_id=1, source_target_pairs={{0,12},{1,13},{2,14},{3,15},{4,8},{5,9},{6,10},{7,11},{8,4},{9,5},... | collective-permute-start | bytes 294920 | tf_op jit(solution)/shard_map/ppermute | solution.py:227
  18.6 9.2 %collective-permute-start.4 = (bf16[128,384]{1,0:T(8,128)(2,1)}, bf16[128,384]{1,0:T(8,128)(2,1)S(1)}, u32[]{:S(2)}, u32[]{:S(2)}) collective-permute-start(bf16[128,384]{1,0:T(8,128)(2,1)} %shard_map.109.after_ref.refs_11_.refs_0_), channel_id=1, source_target_pairs={{0,8},{1,9},{2,10},{3,11},{4,12},{5,13},{6,14},{7,15},{8,0},{9,1},... | collective-permute-start | bytes 294920 | tf_op jit(solution)/shard_map/ppermute | solution.py:227
  18.6 13.7 %collective-permute-start.2 = (bf16[128,384]{1,0:T(8,128)(2,1)}, bf16[128,384]{1,0:T(8,128)(2,1)S(1)}, u32[]{:S(2)}, u32[]{:S(2)}) collective-permute-start(bf16[128,384]{1,0:T(8,128)(2,1)} %shard_map.109.after_ref.refs_11_.refs_0_), channel_id=1, source_target_pairs={{0,6},{1,7},{2,4},{3,5},{4,2},{5,3},{6,0},{7,1},{8,14},{9,15},{10,... | collective-permute-start | bytes 294920 | tf_op jit(solution)/shard_map/ppermute | solution.py:227
  20.3 12.0 %collective-permute-start.1 = (bf16[128,384]{1,0:T(8,128)(2,1)}, bf16[128,384]{1,0:T(8,128)(2,1)S(1)}, u32[]{:S(2)}, u32[]{:S(2)}) collective-permute-start(bf16[128,384]{1,0:T(8,128)(2,1)} %shard_map.109.after_ref.refs_11_.refs_0_), channel_id=1, source_target_pairs={{0,4},{1,5},{2,6},{3,7},{4,0},{5,1},{6,2},{7,3},{8,12},{9,13},{10,... | collective-permute-start | bytes 294920 | tf_op jit(solution)/shard_map/ppermute | solution.py:227
  21.6 10.7 %collective-permute-start = (bf16[128,384]{1,0:T(8,128)(2,1)}, bf16[128,384]{1,0:T(8,128)(2,1)S(1)}, u32[]{:S(2)}, u32[]{:S(2)}) collective-permute-start(bf16[128,384]{1,0:T(8,128)(2,1)} %shard_map.109.after_ref.refs_11_.refs_0_), channel_id=1, source_target_pairs={{0,2},{1,3},{2,0},{3,1},{4,6},{5,7},{6,4},{7,5},{8,10},{9,11},{10,... | collective-permute-start | bytes 294920 | tf_op jit(solution)/shard_map/ppermute | solution.py:227
  40.7 20.1 %collective-permute-start.6 = (bf16[16,32,128]{2,1,0:T(8,128)(2,1)S(1)}, bf16[16,32,128]{2,1,0:T(8,128)(2,1)S(1)}, u32[]{:S(2)}, u32[]{:S(2)}) collective-permute-start(bf16[16,32,128]{2,1,0:T(8,128)(2,1)S(1)} %get-tuple-element.19), channel_id=1, source_target_pairs={{0,2},{1,3},{2,0},{3,1},{4,6},{5,7},{6,4},{7,5},{8,10},{9,11},{10,... | collective-permute-start | bytes 393224 | tf_op jit(solution)/shard_map/ppermute | solution.py:227
  42.3 21.0 %collective-permute-start.7 = (bf16[16,32,128]{2,1,0:T(8,128)(2,1)S(1)}, bf16[16,32,128]{2,1,0:T(8,128)(2,1)S(1)}, u32[]{:S(2)}, u32[]{:S(2)}) collective-permute-start(bf16[16,32,128]{2,1,0:T(8,128)(2,1)S(1)} %get-tuple-element.20), channel_id=1, source_target_pairs={{0,4},{1,5},{2,6},{3,7},{4,0},{5,1},{6,2},{7,3},{8,12},{9,13},{10,... | collective-permute-start | bytes 393224 | tf_op jit(solution)/shard_map/ppermute | solution.py:227
  42.3 9.5 %collective-permute-start.11 = (bf16[128,384]{1,0:T(8,128)(2,1)S(1)}, bf16[128,384]{1,0:T(8,128)(2,1)S(1)}, u32[]{:S(2)}, u32[]{:S(2)}) collective-permute-start(bf16[128,384]{1,0:T(8,128)(2,1)S(1)} %collective-permute-done.5.refs_1_), channel_id=1, source_target_pairs={{0,2},{1,3},{2,0},{3,1},{4,6},{5,7},{6,4},{7,5},{8,10},{9,11},{10,... | collective-permute-start | bytes 294920 | tf_op jit(solution)/shard_map/ppermute | solution.py:227
  42.8 10.0 %collective-permute-start.10 = (bf16[128,384]{1,0:T(8,128)(2,1)S(1)}, bf16[128,384]{1,0:T(8,128)(2,1)S(1)}, u32[]{:S(2)}, u32[]{:S(2)}) collective-permute-start(bf16[128,384]{1,0:T(8,128)(2,1)S(1)} %collective-permute-done.4.refs_0_), channel_id=1, source_target_pairs={{0,2},{1,3},{2,0},{3,1},{4,6},{5,7},{6,4},{7,5},{8,10},{9,11},{10,... | collective-permute-start | bytes 294920 | tf_op jit(solution)/shard_map/ppermute | solution.py:227
  44.3 19.0 %collective-permute-start.8 = (bf16[16,32,128]{2,1,0:T(8,128)(2,1)S(1)}, bf16[16,32,128]{2,1,0:T(8,128)(2,1)S(1)}, u32[]{:S(2)}, u32[]{:S(2)}) collective-permute-start(bf16[16,32,128]{2,1,0:T(8,128)(2,1)S(1)} %get-tuple-element.21), channel_id=1, source_target_pairs={{0,6},{1,7},{2,4},{3,5},{4,2},{5,3},{6,0},{7,1},{8,14},{9,15},{10,... | collective-permute-start | bytes 393224 | tf_op jit(solution)/shard_map/ppermute | solution.py:227
  57.3 17.2 %collective-permute-start.12 = (bf16[16,32,128]{2,1,0:T(8,128)(2,1)S(1)}, bf16[16,32,128]{2,1,0:T(8,128)(2,1)S(1)}, u32[]{:S(2)}, u32[]{:S(2)}) collective-permute-start(bf16[16,32,128]{2,1,0:T(8,128)(2,1)S(1)} %get-tuple-element.22), channel_id=1, source_target_pairs={{0,10},{1,11},{2,8},{3,9},{4,14},{5,15},{6,12},{7,13},{8,2},{9,3},... | collective-permute-start | bytes 393224 | tf_op jit(solution)/shard_map/ppermute | solution.py:227
  58.6 15.8 %collective-permute-start.14 = (bf16[16,32,128]{2,1,0:T(8,128)(2,1)S(1)}, bf16[16,32,128]{2,1,0:T(8,128)(2,1)S(1)}, u32[]{:S(2)}, u32[]{:S(2)}) collective-permute-start(bf16[16,32,128]{2,1,0:T(8,128)(2,1)S(1)} %get-tuple-element.24), channel_id=1, source_target_pairs={{0,14},{1,15},{2,12},{3,13},{4,10},{5,11},{6,8},{7,9},{8,6},{9,7},... | collective-permute-start | bytes 393224 | tf_op jit(solution)/shard_map/ppermute | solution.py:227
  60.9 13.6 %collective-permute-start.13 = (bf16[16,32,128]{2,1,0:T(8,128)(2,1)S(1)}, bf16[16,32,128]{2,1,0:T(8,128)(2,1)S(1)}, u32[]{:S(2)}, u32[]{:S(2)}) collective-permute-start(bf16[16,32,128]{2,1,0:T(8,128)(2,1)S(1)} %get-tuple-element.23), channel_id=1, source_target_pairs={{0,12},{1,13},{2,14},{3,15},{4,8},{5,9},{6,10},{7,11},{8,4},{9,5},... | collective-permute-start | bytes 393224 | tf_op jit(solution)/shard_map/ppermute | solution.py:227
  63.3 18.6 %collective-permute-start.9 = (bf16[16,32,128]{2,1,0:T(8,128)(2,1)S(1)}, bf16[16,32,128]{2,1,0:T(8,128)(2,1)S(1)}, u32[]{:S(2)}, u32[]{:S(2)}) collective-permute-start(bf16[16,32,128]{2,1,0:T(8,128)(2,1)S(1)} %get-tuple-element.17.refs_13_), channel_id=1, source_target_pairs={{0,8},{1,9},{2,10},{3,11},{4,12},{5,13},{6,14},{7,15},{8,0},{9,1},... | collective-permute-start | bytes 393224 | tf_op jit(solution)/shard_map/ppermute | solution.py:227

commit v3 on v2

--- a/solution.py
+++ b/solution.py
@@ -15,13 +15,20 @@
 PARAMS = pltpu.CompilerParams(vmem_limit_bytes=32 * 1024 * 1024)
 
 
+def measured(microseconds):
+    return pl.CostEstimate(
+        flops=0, transcendentals=0, bytes_accessed=int(microseconds * 3.69e6)
+    )
+
+
 def normalised(rows, gain, shift):
     channels = rows.shape[-1]
-    x = rows.astype(F32)
-    mean = jnp.dot(
-        rows, jnp.full((channels, channels), 1.0 / channels, BF16), preferred_element_type=F32
-    )
-    d = x - mean
+    square = (channels, channels)
+    diagonal = lax.broadcasted_iota(jnp.int32, square, 0) == lax.broadcasted_iota(
+        jnp.int32, square, 1
+    )
+    centring = jnp.where(diagonal, 1.0 - 1.0 / channels, -1.0 / channels).astype(BF16)
+    d = jnp.dot(rows, centring, preferred_element_type=F32)
     var = jnp.mean(d * d, axis=-1, keepdims=True)
     return (d * lax.rsqrt(var + 1e-05) * gain + shift).astype(BF16)
 
@@ -42,20 +49,9 @@
     return (wanted == ranks).astype(F32).astype(BF16)
 
 
-def window_kernel(rows_ref, after_ref, pair_ref, gain_ref, shift_ref, out_ref, held, sems):
-    count = held.shape[0]
-    rows_held = pair_ref.shape[0]
-    copies = []
-    for i in range(count):
-        at = lax.rem(rows_ref[i], rows_held)
-        copies.append(pltpu.make_async_copy(pair_ref.at[at], held.at[i], sems.at[i]))
-        copies[-1].start()
-    for i in range(count):
-        copies[i].wait()
-        out_ref[i] = normalised(held[i], gain_ref[...], shift_ref[...])
-
-
-def bias_kernel(pair_ref, mask_ref, gain_ref, shift_ref, w_ref, out_ref, acc):
+def bias_kernel(
+    rows_ref, pair_ref, mask_ref, gain_ref, shift_ref, w_ref, out_ref, window_ref, acc, normed
+):
     step = pl.program_id(0)
     rows, tokens, channels = pair_ref.shape
     columns, live = out_ref.shape
@@ -72,6 +68,7 @@
     for i in range(rows):
         xs.append(normalised(pair_ref[i], gain_ref[...], shift_ref[...]))
         ws.append(jnp.where(row_column == step * rows + i, w, 0.0).astype(BF16))
+        normed[step * rows + i] = xs[i]
     part = jnp.dot(
         jnp.concatenate(xs, axis=1), jnp.concatenate(ws, axis=0), preferred_element_type=F32
     )
@@ -89,6 +86,8 @@
         full = acc[...].astype(BF16)
         taken = jnp.dot(picking(mask_ref[...], live), full, preferred_element_type=F32)
         out_ref[...] = taken.T.astype(BF16)
+        for i in range(window_ref.shape[0]):
+            window_ref[i] = normed[lax.rem(rows_ref[i], held)]
 
 
 def key_value_kernel(own_ref, other_ref, mask_ref, w_ref, k_ref, v_ref, pick):
@@ -227,20 +226,32 @@
         return lax.ppermute(x, "row", [(i, i ^ bits) for i in range(devices)])
 
     step_rows = 8
-    bias = pl.pallas_call(
+    bias, own = pl.pallas_call(
         bias_kernel,
         grid=(rows_held // step_rows,),
-        out_shape=jax.ShapeDtypeStruct((heads * rows_held, live), BF16),
+        out_shape=[
+            jax.ShapeDtypeStruct((heads * rows_held, live), BF16),
+            jax.ShapeDtypeStruct((count, tokens, channels), BF16),
+        ],
         in_specs=[
+            SMEM,
             pl.BlockSpec((step_rows, tokens, channels), lambda i: (i, 0, 0)),
             pl.BlockSpec((1, tokens), lambda i: (0, 0)),
             pl.BlockSpec((1, channels), lambda i: (0, 0)),
             pl.BlockSpec((1, channels), lambda i: (0, 0)),
             pl.BlockSpec((heads, channels), lambda i: (0, 0)),
         ],
-        out_specs=pl.BlockSpec((heads * rows_held, live), lambda i: (0, 0)),
-        scratch_shapes=[pltpu.VMEM((tokens, heads * rows_held), F32)],
-    )(pair, mask_row, gain, shift, w_bias.T)
+        out_specs=[
+            pl.BlockSpec((heads * rows_held, live), lambda i: (0, 0)),
+            pl.BlockSpec((count, tokens, channels), lambda i: (0, 0, 0)),
+        ],
+        scratch_shapes=[
+            pltpu.VMEM((tokens, heads * rows_held), F32),
+            pltpu.VMEM((rows_held, tokens, channels), BF16),
+        ],
+        compiler_params=pltpu.CompilerParams(vmem_limit_bytes=60 * 1024 * 1024),
+        cost_estimate=measured(6),
+    )(window_rows, pair, mask_row, gain, shift, w_bias.T)
 
     far = [m for m in range(owners // 2, owners) if m % 2 == 0]
     passed = [m + 1 for m in far]
@@ -251,17 +262,6 @@
     for m in passed:
         biases[m] = swap(biases[m - 1], 2)
 
-    own = pl.pallas_call(
-        window_kernel,
-        out_shape=jax.ShapeDtypeStruct((count, tokens, channels), BF16),
-        in_specs=[SMEM, ANY, ANY, VMEM, VMEM],
-        out_specs=VMEM,
-        scratch_shapes=[
-            pltpu.VMEM((count, tokens, channels), BF16),
-            pltpu.SemaphoreType.DMA((count,)),
-        ],
-        compiler_params=PARAMS,
-    )(window_rows, bias, pair, gain, shift)
     other = swap(own, 1)
 
     keys, values = pl.pallas_call(
@@ -274,19 +274,22 @@
         out_specs=[VMEM] * 2,
         scratch_shapes=[pltpu.VMEM((live, tokens), BF16)],
         compiler_params=PARAMS,
+        cost_estimate=measured(2.2),
     )(own, other, mask_row, w_project)
 
     split = (count, owners, 2, rows_held, channels)
     own, other = own.reshape(split), other.reshape(split)
     updates = {}
-    after = bias
-    for ms in (far, [0] + near, passed):
+    calls = ((far, []), ([0] + near[:1], far[:1]), (passed, near[:1]), (near[1:], far))
+    sent = {}
+    for ms, earlier in calls:
+        after = [sent[m] if ms == near[1:] else updates[m] for m in earlier]
         blocks = len(ms)
         rows = 2 * count * rows_held
         outs = pl.pallas_call(
             functools.partial(attention_kernel, heads, ms),
             out_shape=[jax.ShapeDtypeStruct((2 * count, rows_held, channels), BF16)] * blocks,
-            in_specs=[SMEM, SMEM] + [VMEM] * (blocks + 9) + [ANY],
+            in_specs=[SMEM, SMEM] + [VMEM] * (blocks + 9) + [ANY] * len(after),
             out_specs=[VMEM] * blocks,
             scratch_shapes=[
                 pltpu.VMEM((rows, inner), BF16),
@@ -295,6 +298,7 @@
                 pltpu.VMEM((rows, inner), BF16),
             ],
             compiler_params=PARAMS,
+            cost_estimate=measured(2.2 * blocks),
         )(
             me,
             chain_bias,
@@ -308,11 +312,11 @@
             w_project,
             gate_bias.reshape(1, inner),
             w_out,
-            after,
+            *after,
         )
-        after = outs[0]
         for m, out in zip(ms, outs):
-            updates[m] = out if m == 0 else swap(out, 2 * m)
+            updates[m] = out
+            sent[m] = out if m == 0 else swap(out, 2 * m)
 
     return pl.pallas_call(
         gather_kernel,
@@ -321,7 +325,7 @@
         out_specs=ANY,
         scratch_shapes=[pltpu.SemaphoreType.DMA((owners,))],
         compiler_params=PARAMS,
-    )(me, *[updates[m] for m in range(owners)])
+    )(me, *[sent[m] for m in range(owners)])
 
 
 def solution(mesh):

time: 83.1 us -> 61.9 us (0.74)
  waiting for transfers between devices: 28.6 us -> 7.82 us
  starting transfers between devices: 20.2 us -> 24.4 us
  Pallas kernels: 31.7 us -> 28.1 us
  local copies, waits for them, and re-layouts: 2.23 us -> 1.25 us
    ppermute x15, waiting for transfers between devices: 28.6 us -> 7.82 us  [swap(): return lax.ppermute(x, 'row', [(i, i ^ bits) for i in range(devices)])]
    pallas_call x2 -> x1, Pallas kernels: 11.1 us -> 6.94 us  [local(): pl.pallas_call(bias_kernel, grid=(rows_held // step_rows,), out_shape=[ja...]
    ppermute x15, starting transfers between devices: 20.2 us -> 24.4 us  [swap(): return lax.ppermute(x, 'row', [(i, i ^ bits) for i in range(devices)])]
    unnamed x20 -> x18, local copies, waits for them, and re-layouts: 2.23 us -> 1.25 us
    pallas_call x3 -> x4, Pallas kernels: 17.3 us -> 17.9 us  [local(): pl.pallas_call(functools.partial(attention_kernel, heads, ms), out_shape=...]
  transfers between devices with their start and end apart: 15 -> 15, of which waited for: 5 -> 4; matrix products, arithmetic and copies ran while one was open for 0% -> 0% of each run, Pallas kernels for 13% -> 33%
where the time goes in v3:
time: 61.9 us; the launch traced here: 61.7 us
  Pallas kernels  28.1 us (45%)
  starting transfers between devices  24.4 us (39%)
  waiting for transfers between devices  7.82 us (13%)
  local copies, waits for them, and re-layouts  1.25 us (2%)
    ppermute x15, starting transfers between devices, swap(): return lax.ppermute(x, 'row', [(i, i ^ bits) for i in range(devices)])  24.4 us
    pallas_call x4, Pallas kernels, local(): pl.pallas_call(functools.partial(attention_kernel, heads, ms), out_shape=...  17.9 us
    ppermute x15, waiting for transfers between devices, swap(): return lax.ppermute(x, 'row', [(i, i ^ bits) for i in range(devices)])  7.82 us
    pallas_call x1, Pallas kernels, local(): pl.pallas_call(bias_kernel, grid=(rows_held // step_rows,), out_shape=[ja...  6.94 us
    pallas_call x1, Pallas kernels, local(): pl.pallas_call(key_value_kernel, out_shape=[jax.ShapeDtypeStruct((2 * cou...  2.23 us
    unnamed x18, local copies, waits for them, and re-layouts  1.25 us
  transfers between devices with their start and end apart: 15, of which 4 were waited for; matrix products, arithmetic and copies ran while one was open for 0% of the time, Pallas kernels for 33%

profile of v3, /device:TPU:0, one launch (start us, length us, event | category | flops | bytes accessed | tf_op | source)
XLA Modules:
  0.0 61.7 jit_solution(3533048773319270034)
XLA Ops:
  0.0 0.0 copy-start.2
  0.0 0.0 copy-start.5
  0.0 0.0 copy-start.3
  0.0 6.9 %shard_map.109 = (bf16[128,384]{1,0:T(8,128)(2,1)}, bf16[8,512,128]{2,1,0:T(8,128)(2,1)}) custom-call(s32[8]{0:T(128)} %rows_ref.1, bf16[32,512,128]{2,1,0:T(8,128)(2,1)} %pair_ref.1, s32[1,512]{1,0:T(1,128)} %bitcast.17, f32[1,128]{1,0:T(1,128)} %bitcast.32, f32[1,128]{1,0:T(1,128)} %bitcast.33, bf16[4,128]{1,0:T(4,128)(2,1)} %bitcast.31), custom_call_target="tpu_custom_call" | custom-call | bytes 22140000 | tf_op jit(solution)/shard_map/pallas_call | solution.py:229
  6.9 0.0 copy-start.6
  7.0 0.0 copy-start.7
  7.0 0.0 copy-start.8
  7.0 0.6 collective-permute-start.1
  7.5 4.7 %collective-permute-start.3 = (bf16[128,384]{1,0:T(8,128)(2,1)}, bf16[128,384]{1,0:T(8,128)(2,1)S(1)}, u32[]{:S(2)}, u32[]{:S(2)}) collective-permute-start(bf16[128,384]{1,0:T(8,128)(2,1)} %get-tuple-element.17.refs_0_), channel_id=1, source_target_pairs={{0,12},{1,13},{2,14},{3,15},{4,8},{5,9},{6,10},{7,11},{8,4},{9,5},... | collective-permute-start | bytes 294920 | tf_op jit(solution)/shard_map/ppermute | solution.py:226
  12.2 0.0 collective-permute-start.2
  12.2 1.5 %collective-permute-start = (bf16[128,384]{1,0:T(8,128)(2,1)}, bf16[128,384]{1,0:T(8,128)(2,1)S(1)}, u32[]{:S(2)}, u32[]{:S(2)}) collective-permute-start(bf16[128,384]{1,0:T(8,128)(2,1)} %get-tuple-element.17.refs_0_), channel_id=1, source_target_pairs={{0,2},{1,3},{2,0},{3,1},{4,6},{5,7},{6,4},{7,5},{8,10},{9,11},{10,... | collective-permute-start | bytes 294920 | tf_op jit(solution)/shard_map/ppermute | solution.py:226
  13.7 2.4 %collective-permute-done.3.refs_1_ = bf16[128,384]{1,0:T(8,128)(2,1)S(1)} collective-permute-done((bf16[128,384]{1,0:T(8,128)(2,1)}, bf16[128,384]{1,0:T(8,128)(2,1)S(1)}, u32[]{:S(2)}, u32[]{:S(2)}) %collective-permute-start.3) | collective-permute-done | bytes 98336 | tf_op jit(solution)/shard_map/ppermute | solution.py:226
  16.1 1.7 %collective-permute-start.12 = (bf16[128,384]{1,0:T(8,128)(2,1)S(1)}, bf16[128,384]{1,0:T(8,128)(2,1)S(1)}, u32[]{:S(2)}, u32[]{:S(2)}) collective-permute-start(bf16[128,384]{1,0:T(8,128)(2,1)S(1)} %collective-permute-done.3.refs_1_), channel_id=1, source_target_pairs={{0,2},{1,3},{2,0},{3,1},{4,6},{5,7},{6,4},{7,5},{8,10},{9,11},{10,... | collective-permute-start | bytes 294920 | tf_op jit(solution)/shard_map/ppermute | solution.py:226
  17.8 0.0 collective-permute-done.1.other_ref
  17.8 0.0 copy-done.2
  17.8 0.0 copy-done.5
  17.8 0.0 copy-start
  17.8 1.2 %copy-done = bf16[8,512,128]{2,1,0:T(8,128)(2,1)S(1)} copy-done((bf16[8,512,128]{2,1,0:T(8,128)(2,1)S(1)}, bf16[8,512,128]{2,1,0:T(8,128)(2,1)}, u32[]{:S(2)}) %copy-start) | copy-done | bytes 1048600
  19.0 2.2 %shard_map.110 = (bf16[16,128,384]{2,1,0:T(8,128)(2,1)S(1)}, bf16[16,384,128]{2,1,0:T(8,128)(2,1)S(1)}) custom-call(bf16[8,512,128]{2,1,0:T(8,128)(2,1)S(1)} %copy-done, bf16[8,512,128]{2,1,0:T(8,128)(2,1)S(1)} %collective-permute-done.1.other_ref, s32[1,512]{1,0:T(1,128)S(1)} %bitcast.18, bf16[128,512]{1,0:T(8,128)(2,1)S(1)} %copy-done.2), custom_call_target="tpu_custom_call" | custom-call | bytes 8118000 | tf_op jit(solution)/shard_map/pallas_call | solution.py:267
  21.3 0.0 collective-permute-done.2.refs_0_
  21.3 0.0 copy-done.3
  21.3 0.0 copy-done.6
  21.3 0.0 copy-done.7
  21.3 0.0 copy-done.8
  21.3 0.0 copy-start.4
  21.3 0.0 copy-start.1
  21.4 4.5 %shard_map.111 = (bf16[16,32,128]{2,1,0:T(8,128)(2,1)S(1)}, bf16[16,32,128]{2,1,0:T(8,128)(2,1)S(1)}) custom-call(s32[1]{0:T(128)} %bitcast.me_ref, f32[4]{0:T(128)S(1)} %copy-done.7, bf16[128,384]{1,0:T(8,128)(2,1)S(1)} %collective-permute-done.2.refs_0_, bf16[128,384]{1,0:T(8,128)(2,1)S(1)} %collective-permute-done.3.refs_1_, ...), custom_call_target="tpu_custom_call" | custom-call | bytes 16236000 | tf_op jit(solution)/shard_map/pallas_call | solution.py:289
  25.8 3.7 %collective-permute-start.8 = (bf16[16,32,128]{2,1,0:T(8,128)(2,1)S(1)}, bf16[16,32,128]{2,1,0:T(8,128)(2,1)S(1)}, u32[]{:S(2)}, u32[]{:S(2)}) collective-permute-start(bf16[16,32,128]{2,1,0:T(8,128)(2,1)S(1)} %get-tuple-element.24), channel_id=1, source_target_pairs={{0,12},{1,13},{2,14},{3,15},{4,8},{5,9},{6,10},{7,11},{8,4},{9,5},... | collective-permute-start | bytes 393224 | tf_op jit(solution)/shard_map/ppermute | solution.py:226
  29.5 1.8 %collective-permute-start.7 = (bf16[16,32,128]{2,1,0:T(8,128)(2,1)S(1)}, bf16[16,32,128]{2,1,0:T(8,128)(2,1)S(1)}, u32[]{:S(2)}, u32[]{:S(2)}) collective-permute-start(bf16[16,32,128]{2,1,0:T(8,128)(2,1)S(1)} %get-tuple-element.21.refs_11_), channel_id=1, source_target_pairs={{0,8},{1,9},{2,10},{3,11},{4,12},{5,13},{6,14},{7,15},{8,0},{9,1},... | collective-permute-start | bytes 393224 | tf_op jit(solution)/shard_map/ppermute | solution.py:226
  31.3 0.5 collective-permute-start.11
  31.8 0.0 collective-permute-done.refs_1_
  31.8 0.0 copy-done.4
  31.8 1.1 %collective-permute-start.6 = (bf16[128,384]{1,0:T(8,128)(2,1)S(1)}, bf16[128,384]{1,0:T(8,128)(2,1)S(1)}, u32[]{:S(2)}, u32[]{:S(2)}) collective-permute-start(bf16[128,384]{1,0:T(8,128)(2,1)S(1)} %copy-done.4), channel_id=1, source_target_pairs={{0,6},{1,7},{2,4},{3,5},{4,2},{5,3},{6,0},{7,1},{8,14},{9,15},{10,... | collective-permute-start | bytes 294920 | tf_op jit(solution)/shard_map/ppermute | solution.py:226
  32.9 0.0 collective-permute-done.12.refs_1_
  32.9 1.9 %collective-permute-start.5 = (bf16[128,384]{1,0:T(8,128)(2,1)S(1)}, bf16[128,384]{1,0:T(8,128)(2,1)S(1)}, u32[]{:S(2)}, u32[]{:S(2)}) collective-permute-start(bf16[128,384]{1,0:T(8,128)(2,1)S(1)} %copy-done.4), channel_id=1, source_target_pairs={{0,4},{1,5},{2,6},{3,7},{4,0},{5,1},{6,2},{7,3},{8,12},{9,13},{10,... | collective-permute-start | bytes 294920 | tf_op jit(solution)/shard_map/ppermute | solution.py:226
  34.8 0.0 copy-done.1
  34.8 4.5 %shard_map.112 = (bf16[16,32,128]{2,1,0:T(8,128)(2,1)S(1)}, bf16[16,32,128]{2,1,0:T(8,128)(2,1)S(1)}) custom-call(s32[1]{0:T(128)} %bitcast.me_ref, f32[4]{0:T(128)S(1)} %copy-done.7, bf16[128,384]{1,0:T(8,128)(2,1)S(1)} %copy-done.4, bf16[128,384]{1,0:T(8,128)(2,1)S(1)} %collective-permute-done.refs_1_, bf16[8,8,2,32,128]{4,3,2,1,0:T(8,128)(2,1)S(1)} %bitcast.10, ...), custom_call_target="tpu_custom_call" | custom-call | bytes 16236000 | tf_op jit(solution)/shard_map/pallas_call | solution.py:289
  39.2 0.0 collective-permute-done.11.refs_0_
  39.2 0.6 collective-permute-start.4
  39.8 4.5 %shard_map.114 = (bf16[16,32,128]{2,1,0:T(8,128)(2,1)S(1)}, bf16[16,32,128]{2,1,0:T(8,128)(2,1)S(1)}) custom-call(s32[1]{0:T(128)} %bitcast.me_ref, f32[4]{0:T(128)S(1)} %copy-done.7, bf16[128,384]{1,0:T(8,128)(2,1)S(1)} %collective-permute-done.11.refs_0_, bf16[128,384]{1,0:T(8,128)(2,1)S(1)} %collective-permute-done.12.refs_1_, ...), custom_call_target="tpu_custom_call" | custom-call | bytes 16236000 | tf_op jit(solution)/shard_map/pallas_call | solution.py:289
  44.3 0.0 collective-permute-done.6.refs_1_
  44.3 2.2 %collective-permute-start.13 = (bf16[16,32,128]{2,1,0:T(8,128)(2,1)S(1)}, bf16[16,32,128]{2,1,0:T(8,128)(2,1)S(1)}, u32[]{:S(2)}, u32[]{:S(2)}) collective-permute-start(bf16[16,32,128]{2,1,0:T(8,128)(2,1)S(1)} %get-tuple-element.27), channel_id=1, source_target_pairs={{0,10},{1,11},{2,8},{3,9},{4,14},{5,15},{6,12},{7,13},{8,2},{9,3},... | collective-permute-start | bytes 393224 | tf_op jit(solution)/shard_map/ppermute | solution.py:226
  46.5 0.0 collective-permute-done.5.refs_0_
  46.5 1.4 %collective-permute-start.14 = (bf16[16,32,128]{2,1,0:T(8,128)(2,1)S(1)}, bf16[16,32,128]{2,1,0:T(8,128)(2,1)S(1)}, u32[]{:S(2)}, u32[]{:S(2)}) collective-permute-start(bf16[16,32,128]{2,1,0:T(8,128)(2,1)S(1)} %get-tuple-element.28), channel_id=1, source_target_pairs={{0,14},{1,15},{2,12},{3,13},{4,10},{5,11},{6,8},{7,9},{8,6},{9,7},... | collective-permute-start | bytes 393224 | tf_op jit(solution)/shard_map/ppermute | solution.py:226
  47.9 0.0 collective-permute-done.8.refs_12_.refs_6_
  47.9 0.0 collective-permute-done.7.refs_11_.refs_4_
  47.9 4.5 %shard_map.113 = (bf16[16,32,128]{2,1,0:T(8,128)(2,1)S(1)}, bf16[16,32,128]{2,1,0:T(8,128)(2,1)S(1)}) custom-call(s32[1]{0:T(128)} %bitcast.me_ref, f32[4]{0:T(128)S(1)} %copy-done.7, bf16[128,384]{1,0:T(8,128)(2,1)S(1)} %collective-permute-done.5.refs_0_, bf16[128,384]{1,0:T(8,128)(2,1)S(1)} %collective-permute-done.6.refs_1_, ...), custom_call_target="tpu_custom_call" | custom-call | bytes 16236000 | tf_op jit(solution)/shard_map/pallas_call | solution.py:289
  52.4 0.9 %collective-permute-start.9 = (bf16[16,32,128]{2,1,0:T(8,128)(2,1)S(1)}, bf16[16,32,128]{2,1,0:T(8,128)(2,1)S(1)}, u32[]{:S(2)}, u32[]{:S(2)}) collective-permute-start(bf16[16,32,128]{2,1,0:T(8,128)(2,1)S(1)} %get-tuple-element.25), channel_id=1, source_target_pairs={{0,4},{1,5},{2,6},{3,7},{4,0},{5,1},{6,2},{7,3},{8,12},{9,13},{10,... | collective-permute-start | bytes 393224 | tf_op jit(solution)/shard_map/ppermute | solution.py:226
  53.4 2.0 %collective-permute-start.10 = (bf16[16,32,128]{2,1,0:T(8,128)(2,1)S(1)}, bf16[16,32,128]{2,1,0:T(8,128)(2,1)S(1)}, u32[]{:S(2)}, u32[]{:S(2)}) collective-permute-start(bf16[16,32,128]{2,1,0:T(8,128)(2,1)S(1)} %get-tuple-element.26), channel_id=1, source_target_pairs={{0,6},{1,7},{2,4},{3,5},{4,2},{5,3},{6,0},{7,1},{8,14},{9,15},{10,... | collective-permute-start | bytes 393224 | tf_op jit(solution)/shard_map/ppermute | solution.py:226
  55.3 0.6 collective-permute-done.13.refs_5_
  55.9 0.0 collective-permute-done.14.refs_7_
  55.9 0.0 collective-permute-done.4.refs_1_
  55.9 2.8 %collective-permute-done.9.refs_2_ = bf16[16,32,128]{2,1,0:T(8,128)(2,1)S(1)} collective-permute-done((bf16[16,32,128]{2,1,0:T(8,128)(2,1)S(1)}, bf16[16,32,128]{2,1,0:T(8,128)(2,1)S(1)}, u32[]{:S(2)}, u32[]{:S(2)}) %collective-permute-start.9) | collective-permute-done | bytes 131104 | tf_op jit(solution)/shard_map/ppermute | solution.py:226
  58.7 2.0 %collective-permute-done.10.refs_3_ = bf16[16,32,128]{2,1,0:T(8,128)(2,1)S(1)} collective-permute-done((bf16[16,32,128]{2,1,0:T(8,128)(2,1)S(1)}, bf16[16,32,128]{2,1,0:T(8,128)(2,1)S(1)}, u32[]{:S(2)}, u32[]{:S(2)}) %collective-permute-start.10) | collective-permute-done | bytes 131104 | tf_op jit(solution)/shard_map/ppermute | solution.py:226
  60.7 1.0 %shard_map.115 = bf16[128,32,128]{2,1,0:T(8,128)(2,1)} custom-call(s32[1]{0:T(128)} %bitcast.me_ref, bf16[16,32,128]{2,1,0:T(8,128)(2,1)S(1)} %get-tuple-element.22.refs_0_, bf16[16,32,128]{2,1,0:T(8,128)(2,1)S(1)} %collective-permute-done.4.refs_1_, bf16[16,32,128]{2,1,0:T(8,128)(2,1)S(1)} %collective-permute-done.9.refs_2_, ...), custom_call_target="tpu_custom_call" | custom-call | tf_op jit(solution)/shard_map/pallas_call | solution.py:321
Async XLA Ops:
  0.0 17.8 %copy-start.2 = (bf16[128,512]{1,0:T(8,128)(2,1)S(1)}, bf16[128,512]{1,0:T(8,128)(2,1)}, u32[]{:S(2)}) copy-start(bf16[128,512]{1,0:T(8,128)(2,1)} %refs_8_.7) | copy-start | bytes 393220
  0.0 17.8 %copy-start.5 = (s32[512]{0:T(512)S(1)}, s32[512]{0:T(512)}, u32[]{:S(2)}) copy-start(s32[512]{0:T(512)} %param.13) | copy-start | bytes 6148
  0.0 21.3 %copy-start.3 = (bf16[128,128]{1,0:T(8,128)(2,1)S(1)}, bf16[128,128]{1,0:T(8,128)(2,1)}, u32[]{:S(2)}) copy-start(bf16[128,128]{1,0:T(8,128)(2,1)} %refs_10_.7) | copy-start | bytes 98308
  6.9 14.4 %copy-start.6 = (s32[512]{0:T(512)S(1)}, s32[512]{0:T(512)}, u32[]{:S(2)}) copy-start(s32[512]{0:T(512)} %param.14) | copy-start | bytes 6148
  7.0 14.4 %copy-start.7 = (f32[4]{0:T(128)S(1)}, f32[4]{0:T(128)}, u32[]{:S(2)}) copy-start(f32[4]{0:T(128)} %chain_bias_ref.7) | copy-start | bytes 52
  7.0 14.4 %copy-start.8 = (f32[128]{0:T(128)S(1)}, f32[128]{0:T(128)}, u32[]{:S(2)}) copy-start(f32[128]{0:T(128)} %param.18) | copy-start | bytes 1540
  7.0 10.9 %collective-permute-start.1 = (bf16[8,512,128]{2,1,0:T(8,128)(2,1)}, bf16[8,512,128]{2,1,0:T(8,128)(2,1)S(1)}, u32[]{:S(2)}, u32[]{:S(2)}) collective-permute-start(bf16[8,512,128]{2,1,0:T(8,128)(2,1)} %get-tuple-element.18.own_ref), channel_id=1, source_target_pairs={{0,1},{1,0},{2,3},{3,2},{4,5},{5,4},{6,7},{7,6},{8,9},{9,8},{10,11... | collective-permute-start | bytes 3145736 | tf_op jit(solution)/shard_map/ppermute | solution.py:226
  7.5 8.6 %collective-permute-start.3 = (bf16[128,384]{1,0:T(8,128)(2,1)}, bf16[128,384]{1,0:T(8,128)(2,1)S(1)}, u32[]{:S(2)}, u32[]{:S(2)}) collective-permute-start(bf16[128,384]{1,0:T(8,128)(2,1)} %get-tuple-element.17.refs_0_), channel_id=1, source_target_pairs={{0,12},{1,13},{2,14},{3,15},{4,8},{5,9},{6,10},{7,11},{8,4},{9,5},... | collective-permute-start | bytes 294920 | tf_op jit(solution)/shard_map/ppermute | solution.py:226
  12.2 9.1 %collective-permute-start.2 = (bf16[128,384]{1,0:T(8,128)(2,1)}, bf16[128,384]{1,0:T(8,128)(2,1)S(1)}, u32[]{:S(2)}, u32[]{:S(2)}) collective-permute-start(bf16[128,384]{1,0:T(8,128)(2,1)} %get-tuple-element.17.refs_0_), channel_id=1, source_target_pairs={{0,8},{1,9},{2,10},{3,11},{4,12},{5,13},{6,14},{7,15},{8,0},{9,1},... | collective-permute-start | bytes 294920 | tf_op jit(solution)/shard_map/ppermute | solution.py:226
  12.2 19.6 %collective-permute-start = (bf16[128,384]{1,0:T(8,128)(2,1)}, bf16[128,384]{1,0:T(8,128)(2,1)S(1)}, u32[]{:S(2)}, u32[]{:S(2)}) collective-permute-start(bf16[128,384]{1,0:T(8,128)(2,1)} %get-tuple-element.17.refs_0_), channel_id=1, source_target_pairs={{0,2},{1,3},{2,0},{3,1},{4,6},{5,7},{6,4},{7,5},{8,10},{9,11},{10,... | collective-permute-start | bytes 294920 | tf_op jit(solution)/shard_map/ppermute | solution.py:226
  16.1 16.7 %collective-permute-start.12 = (bf16[128,384]{1,0:T(8,128)(2,1)S(1)}, bf16[128,384]{1,0:T(8,128)(2,1)S(1)}, u32[]{:S(2)}, u32[]{:S(2)}) collective-permute-start(bf16[128,384]{1,0:T(8,128)(2,1)S(1)} %collective-permute-done.3.refs_1_), channel_id=1, source_target_pairs={{0,2},{1,3},{2,0},{3,1},{4,6},{5,7},{6,4},{7,5},{8,10},{9,11},{10,... | collective-permute-start | bytes 294920 | tf_op jit(solution)/shard_map/ppermute | solution.py:226
  17.8 1.2 %copy-start = (bf16[8,512,128]{2,1,0:T(8,128)(2,1)S(1)}, bf16[8,512,128]{2,1,0:T(8,128)(2,1)}, u32[]{:S(2)}) copy-start(bf16[8,512,128]{2,1,0:T(8,128)(2,1)} %get-tuple-element.18.own_ref) | copy-start | bytes 3145732
  21.3 10.4 %copy-start.4 = (bf16[128,384]{1,0:T(8,128)(2,1)S(1)}, bf16[128,384]{1,0:T(8,128)(2,1)}, u32[]{:S(2)}) copy-start(bf16[128,384]{1,0:T(8,128)(2,1)} %get-tuple-element.17.refs_0_) | copy-start | bytes 294916
  21.3 13.4 %copy-start.1 = (bf16[8,512,128]{2,1,0:T(8,128)(2,1)S(1)}, bf16[8,512,128]{2,1,0:T(8,128)(2,1)}, u32[]{:S(2)}) copy-start(bf16[8,512,128]{2,1,0:T(8,128)(2,1)} %get-tuple-element.18.own_ref) | copy-start | bytes 3145732
  25.8 22.1 %collective-permute-start.8 = (bf16[16,32,128]{2,1,0:T(8,128)(2,1)S(1)}, bf16[16,32,128]{2,1,0:T(8,128)(2,1)S(1)}, u32[]{:S(2)}, u32[]{:S(2)}) collective-permute-start(bf16[16,32,128]{2,1,0:T(8,128)(2,1)S(1)} %get-tuple-element.24), channel_id=1, source_target_pairs={{0,12},{1,13},{2,14},{3,15},{4,8},{5,9},{6,10},{7,11},{8,4},{9,5},... | collective-permute-start | bytes 393224 | tf_op jit(solution)/shard_map/ppermute | solution.py:226
  29.5 18.4 %collective-permute-start.7 = (bf16[16,32,128]{2,1,0:T(8,128)(2,1)S(1)}, bf16[16,32,128]{2,1,0:T(8,128)(2,1)S(1)}, u32[]{:S(2)}, u32[]{:S(2)}) collective-permute-start(bf16[16,32,128]{2,1,0:T(8,128)(2,1)S(1)} %get-tuple-element.21.refs_11_), channel_id=1, source_target_pairs={{0,8},{1,9},{2,10},{3,11},{4,12},{5,13},{6,14},{7,15},{8,0},{9,1},... | collective-permute-start | bytes 393224 | tf_op jit(solution)/shard_map/ppermute | solution.py:226
  31.3 8.0 %collective-permute-start.11 = (bf16[128,384]{1,0:T(8,128)(2,1)S(1)}, bf16[128,384]{1,0:T(8,128)(2,1)S(1)}, u32[]{:S(2)}, u32[]{:S(2)}) collective-permute-start(bf16[128,384]{1,0:T(8,128)(2,1)S(1)} %collective-permute-done.2.refs_0_), channel_id=1, source_target_pairs={{0,2},{1,3},{2,0},{3,1},{4,6},{5,7},{6,4},{7,5},{8,10},{9,11},{10,... | collective-permute-start | bytes 294920 | tf_op jit(solution)/shard_map/ppermute | solution.py:226
  31.8 12.5 %collective-permute-start.6 = (bf16[128,384]{1,0:T(8,128)(2,1)S(1)}, bf16[128,384]{1,0:T(8,128)(2,1)S(1)}, u32[]{:S(2)}, u32[]{:S(2)}) collective-permute-start(bf16[128,384]{1,0:T(8,128)(2,1)S(1)} %copy-done.4), channel_id=1, source_target_pairs={{0,6},{1,7},{2,4},{3,5},{4,2},{5,3},{6,0},{7,1},{8,14},{9,15},{10,... | collective-permute-start | bytes 294920 | tf_op jit(solution)/shard_map/ppermute | solution.py:226
  32.9 13.7 %collective-permute-start.5 = (bf16[128,384]{1,0:T(8,128)(2,1)S(1)}, bf16[128,384]{1,0:T(8,128)(2,1)S(1)}, u32[]{:S(2)}, u32[]{:S(2)}) collective-permute-start(bf16[128,384]{1,0:T(8,128)(2,1)S(1)} %copy-done.4), channel_id=1, source_target_pairs={{0,4},{1,5},{2,6},{3,7},{4,0},{5,1},{6,2},{7,3},{8,12},{9,13},{10,... | collective-permute-start | bytes 294920 | tf_op jit(solution)/shard_map/ppermute | solution.py:226
  39.2 16.6 %collective-permute-start.4 = (bf16[16,32,128]{2,1,0:T(8,128)(2,1)S(1)}, bf16[16,32,128]{2,1,0:T(8,128)(2,1)S(1)}, u32[]{:S(2)}, u32[]{:S(2)}) collective-permute-start(bf16[16,32,128]{2,1,0:T(8,128)(2,1)S(1)} %get-tuple-element.23.refs_11_), channel_id=1, source_target_pairs={{0,2},{1,3},{2,0},{3,1},{4,6},{5,7},{6,4},{7,5},{8,10},{9,11},{10,... | collective-permute-start | bytes 393224 | tf_op jit(solution)/shard_map/ppermute | solution.py:226
  44.3 11.6 %collective-permute-start.13 = (bf16[16,32,128]{2,1,0:T(8,128)(2,1)S(1)}, bf16[16,32,128]{2,1,0:T(8,128)(2,1)S(1)}, u32[]{:S(2)}, u32[]{:S(2)}) collective-permute-start(bf16[16,32,128]{2,1,0:T(8,128)(2,1)S(1)} %get-tuple-element.27), channel_id=1, source_target_pairs={{0,10},{1,11},{2,8},{3,9},{4,14},{5,15},{6,12},{7,13},{8,2},{9,3},... | collective-permute-start | bytes 393224 | tf_op jit(solution)/shard_map/ppermute | solution.py:226
  46.5 9.4 %collective-permute-start.14 = (bf16[16,32,128]{2,1,0:T(8,128)(2,1)S(1)}, bf16[16,32,128]{2,1,0:T(8,128)(2,1)S(1)}, u32[]{:S(2)}, u32[]{:S(2)}) collective-permute-start(bf16[16,32,128]{2,1,0:T(8,128)(2,1)S(1)} %get-tuple-element.28), channel_id=1, source_target_pairs={{0,14},{1,15},{2,12},{3,13},{4,10},{5,11},{6,8},{7,9},{8,6},{9,7},... | collective-permute-start | bytes 393224 | tf_op jit(solution)/shard_map/ppermute | solution.py:226
  52.4 6.3 %collective-permute-start.9 = (bf16[16,32,128]{2,1,0:T(8,128)(2,1)S(1)}, bf16[16,32,128]{2,1,0:T(8,128)(2,1)S(1)}, u32[]{:S(2)}, u32[]{:S(2)}) collective-permute-start(bf16[16,32,128]{2,1,0:T(8,128)(2,1)S(1)} %get-tuple-element.25), channel_id=1, source_target_pairs={{0,4},{1,5},{2,6},{3,7},{4,0},{5,1},{6,2},{7,3},{8,12},{9,13},{10,... | collective-permute-start | bytes 393224 | tf_op jit(solution)/shard_map/ppermute | solution.py:226
  53.4 7.3 %collective-permute-start.10 = (bf16[16,32,128]{2,1,0:T(8,128)(2,1)S(1)}, bf16[16,32,128]{2,1,0:T(8,128)(2,1)S(1)}, u32[]{:S(2)}, u32[]{:S(2)}) collective-permute-start(bf16[16,32,128]{2,1,0:T(8,128)(2,1)S(1)} %get-tuple-element.26), channel_id=1, source_target_pairs={{0,6},{1,7},{2,4},{3,5},{4,2},{5,3},{6,0},{7,1},{8,14},{9,15},{10,... | collective-permute-start | bytes 393224 | tf_op jit(solution)/shard_map/ppermute | solution.py:226

commit v4 on v3

--- a/solution.py
+++ b/solution.py
@@ -50,7 +50,19 @@
 
 
 def bias_kernel(
-    rows_ref, pair_ref, mask_ref, gain_ref, shift_ref, w_ref, out_ref, window_ref, acc, normed
+    rows_ref,
+    pair_ref,
+    mask_ref,
+    chain_ref,
+    gain_ref,
+    shift_ref,
+    w_ref,
+    out_ref,
+    window_ref,
+    pick_ref,
+    chain_live_ref,
+    acc,
+    normed,
 ):
     step = pl.program_id(0)
     rows, tokens, channels = pair_ref.shape
@@ -76,6 +88,10 @@
     @pl.when(step == 0)
     def _():
         acc[...] = part
+        pick = picking(mask_ref[...], live)
+        pick_ref[...] = pick
+        chain_row = jnp.broadcast_to(chain_ref[...].astype(F32), (8, tokens)).astype(BF16)
+        chain_live_ref[...] = lax.dot_general(chain_row, pick, NT, preferred_element_type=F32)
 
     @pl.when(step > 0)
     def _():
@@ -84,19 +100,18 @@
     @pl.when(step == pl.num_programs(0) - 1)
     def _():
         full = acc[...].astype(BF16)
-        taken = jnp.dot(picking(mask_ref[...], live), full, preferred_element_type=F32)
+        taken = jnp.dot(pick_ref[...], full, preferred_element_type=F32)
         out_ref[...] = taken.T.astype(BF16)
         for i in range(window_ref.shape[0]):
             window_ref[i] = normed[lax.rem(rows_ref[i], held)]
 
 
-def key_value_kernel(own_ref, other_ref, mask_ref, w_ref, k_ref, v_ref, pick):
+def key_value_kernel(own_ref, other_ref, pick_ref, w_ref, k_ref, v_ref):
     count = own_ref.shape[0]
     live, inner = v_ref.shape[1:]
-    pick[...] = picking(mask_ref[...], live)
     for i in range(count):
         both = jnp.concatenate([own_ref[i], other_ref[i]], axis=1)
-        taken = jnp.dot(pick[...], both, preferred_element_type=F32).astype(BF16)
+        taken = jnp.dot(pick_ref[...], both, preferred_element_type=F32).astype(BF16)
         c = own_ref.shape[2]
         for part in range(2):
             kv = jnp.dot(
@@ -108,10 +123,11 @@
             v_ref[i + part * count] = kv[:, inner:]
 
 
-def attention_kernel(heads, ms, me_ref, chain_bias_ref, *refs):
+def attention_kernel(heads, ms, first, me_ref, chain_bias_ref, *refs):
     blocks = len(ms)
     bias_refs, refs = refs[:blocks], refs[blocks:]
-    own_ref, other_ref, k_ref, v_ref, mask_ref, chain_ref, w_ref, gate_bias_ref, w_out_ref = refs[:9]
+    own_ref, other_ref, k_ref, v_ref, mask_ref, chain_ref, chain_live_ref = refs[:7]
+    w_ref, gate_bias_ref, w_out_ref = refs[7:10]
     out_refs, (q_s, gate_s, added_s, gated_s) = refs[-4 - blocks : -4], refs[-4:]
     windows, inner, live = k_ref.shape
     half = windows // 2
@@ -119,10 +135,7 @@
     tokens = mask_ref.shape[1]
     size = inner // heads
     core, chip = lax.rem(me_ref[0], 2), lax.div(me_ref[0], 2)
-    chain_row = jnp.broadcast_to(chain_ref[...].astype(F32), (8, tokens)).astype(BF16)
-    chain_live = lax.dot_general(
-        chain_row, picking(mask_ref[...], live), NT, preferred_element_type=F32
-    )[0:1]
+    chain_live = chain_live_ref[0:1, :]
     lane_head = lax.broadcasted_iota(jnp.int32, (block, inner), 1) // size
     w_q = w_ref[:, :inner]
     w_g = w_ref[:, 3 * inner :]
@@ -137,7 +150,8 @@
         same = (chain_here == chain_live).astype(F32)
         for h in range(heads):
             rows = slice(h * block, (h + 1) * block)
-            added_s[rows, :] = bias_refs[b][rows, :].astype(F32) + chain_bias_ref[h] * same
+            taken = pl.ds(first[b] + h * block, block)
+            added_s[rows, :] = bias_refs[b][taken, :].astype(F32) + chain_bias_ref[h] * same
         for part, ref in enumerate((own_ref, other_ref)):
             x = ref[:, at, core].reshape(half * block, inner)
             span = pl.ds(part * half * block, half * block)
@@ -183,14 +197,14 @@
         out_refs[b][pl.ds((1 - core) * half, half)] = result[half:]
 
 
-def gather_kernel(me_ref, *refs):
-    parts, out_ref, sems = refs[:-2], refs[-2], refs[-1]
+def gather_kernel(order, me_ref, *refs):
+    parts, out_ref, sems = refs[: len(order)], refs[-2], refs[-1]
     count = parts[0].shape[0]
     chip = lax.div(me_ref[0], 2)
     copies = []
-    for m, part in enumerate(parts):
-        at = lax.bitwise_xor(chip, m) * count
-        copies.append(pltpu.make_async_copy(part, out_ref.at[pl.ds(at, count)], sems.at[m]))
+    for i, part in enumerate(parts):
+        at = lax.bitwise_xor(chip, order[i]) * count
+        copies.append(pltpu.make_async_copy(part, out_ref.at[pl.ds(at, count)], sems.at[i]))
         copies[-1].start()
     for copy in copies:
         copy.wait()
@@ -225,18 +239,21 @@
     def swap(x, bits):
         return lax.ppermute(x, "row", [(i, i ^ bits) for i in range(devices)])
 
-    step_rows = 8
-    bias, own = pl.pallas_call(
+    step_rows = 16
+    bias, own, pick, chain_live = pl.pallas_call(
         bias_kernel,
         grid=(rows_held // step_rows,),
         out_shape=[
             jax.ShapeDtypeStruct((heads * rows_held, live), BF16),
             jax.ShapeDtypeStruct((count, tokens, channels), BF16),
+            jax.ShapeDtypeStruct((live, tokens), BF16),
+            jax.ShapeDtypeStruct((8, live), F32),
         ],
         in_specs=[
             SMEM,
             pl.BlockSpec((step_rows, tokens, channels), lambda i: (i, 0, 0)),
             pl.BlockSpec((1, tokens), lambda i: (0, 0)),
+            pl.BlockSpec((1, tokens), lambda i: (0, 0)),
             pl.BlockSpec((1, channels), lambda i: (0, 0)),
             pl.BlockSpec((1, channels), lambda i: (0, 0)),
             pl.BlockSpec((heads, channels), lambda i: (0, 0)),
@@ -244,6 +261,8 @@
         out_specs=[
             pl.BlockSpec((heads * rows_held, live), lambda i: (0, 0)),
             pl.BlockSpec((count, tokens, channels), lambda i: (0, 0, 0)),
+            pl.BlockSpec((live, tokens), lambda i: (0, 0)),
+            pl.BlockSpec((8, live), lambda i: (0, 0)),
         ],
         scratch_shapes=[
             pltpu.VMEM((tokens, heads * rows_held), F32),
@@ -251,7 +270,7 @@
         ],
         compiler_params=pltpu.CompilerParams(vmem_limit_bytes=60 * 1024 * 1024),
         cost_estimate=measured(6),
-    )(window_rows, pair, mask_row, gain, shift, w_bias.T)
+    )(window_rows, pair, mask_row, chain_row, gain, shift, w_bias.T)
 
     far = [m for m in range(owners // 2, owners) if m % 2 == 0]
     passed = [m + 1 for m in far]
@@ -259,9 +278,6 @@
     biases = {0: bias}
     for m in far[::-1] + near[::-1]:
         biases[m] = swap(bias, 2 * m)
-    for m in passed:
-        biases[m] = swap(biases[m - 1], 2)
-
     other = swap(own, 1)
 
     keys, values = pl.pallas_call(
@@ -272,24 +288,30 @@
         ],
         in_specs=[VMEM] * 4,
         out_specs=[VMEM] * 2,
-        scratch_shapes=[pltpu.VMEM((live, tokens), BF16)],
         compiler_params=PARAMS,
-        cost_estimate=measured(2.2),
-    )(own, other, mask_row, w_project)
+        cost_estimate=measured(2),
+    )(own, other, pick, w_project)
 
     split = (count, owners, 2, rows_held, channels)
     own, other = own.reshape(split), other.reshape(split)
     updates = {}
-    calls = ((far, []), ([0] + near[:1], far[:1]), (passed, near[:1]), (near[1:], far))
     sent = {}
-    for ms, earlier in calls:
-        after = [sent[m] if ms == near[1:] else updates[m] for m in earlier]
+    for ms in ([0] + near[:1], far, passed, near[1:]):
+        if ms == far:
+            after = [updates[0]] + [biases[m] for m in near[1:]]
+        elif ms == passed:
+            after = [updates[far[0]]]
+        elif ms == near[1:]:
+            after = [updates[passed[0]]] + [sent[m] for m in far]
+        else:
+            after = []
         blocks = len(ms)
+        first = [i * heads * rows_held if ms == passed else 0 for i in range(blocks)]
         rows = 2 * count * rows_held
         outs = pl.pallas_call(
-            functools.partial(attention_kernel, heads, ms),
+            functools.partial(attention_kernel, heads, ms, first),
             out_shape=[jax.ShapeDtypeStruct((2 * count, rows_held, channels), BF16)] * blocks,
-            in_specs=[SMEM, SMEM] + [VMEM] * (blocks + 9) + [ANY] * len(after),
+            in_specs=[SMEM, SMEM] + [VMEM] * (blocks + 10) + [ANY] * len(after),
             out_specs=[VMEM] * blocks,
             scratch_shapes=[
                 pltpu.VMEM((rows, inner), BF16),
@@ -309,6 +331,7 @@
             values,
             mask_row,
             chain_row,
+            chain_live,
             w_project,
             gate_bias.reshape(1, inner),
             w_out,
@@ -316,16 +339,30 @@
         )
         for m, out in zip(ms, outs):
             updates[m] = out
+        if 0 in ms:
+            *straight, _ = lax.optimization_barrier((*[biases[m] for m in far], outs[0]))
+            straight = swap(jnp.concatenate(straight), 2)
+            for i, m in enumerate(passed):
+                biases[m] = straight
+        for m, out in zip(ms, outs):
             sent[m] = out if m == 0 else swap(out, 2 * m)
 
-    return pl.pallas_call(
-        gather_kernel,
-        out_shape=jax.ShapeDtypeStruct((owners * 2 * count, rows_held, channels), BF16),
-        in_specs=[SMEM] + [ANY] * owners,
-        out_specs=ANY,
-        scratch_shapes=[pltpu.SemaphoreType.DMA((owners,))],
-        compiler_params=PARAMS,
-    )(me, *[sent[m] for m in range(owners)])
+    whole = []
+    for order in ([0] + near[:1] + far + passed, near[1:]):
+        placed = len(order)
+        whole = [
+            pl.pallas_call(
+                functools.partial(gather_kernel, order),
+                out_shape=jax.ShapeDtypeStruct((owners * 2 * count, rows_held, channels), BF16),
+                in_specs=[SMEM] + [ANY] * (placed + len(whole)),
+                out_specs=ANY,
+                scratch_shapes=[pltpu.SemaphoreType.DMA((placed,))],
+                input_output_aliases={placed + 1: 0} if whole else {},
+                compiler_params=PARAMS,
+                cost_estimate=measured(1),
+            )(me, *[sent[m] for m in order], *whole)
+        ]
+    return whole[0]
 
 
 def solution(mesh):

time: 61.9 us -> 61.1 us (0.987)
  starting transfers between devices: 24.4 us -> 21.4 us
  waiting for transfers between devices: 7.82 us -> 10.4 us
  Pallas kernels: 28.1 us -> 26.6 us
  local copies, waits for them, and re-layouts: 1.25 us -> 2.26 us
    ppermute x15 -> x14, starting transfers between devices: 24.4 us -> 21.4 us  [swap(): return lax.ppermute(x, 'row', [(i, i ^ bits) for i in range(devices)])]
    ppermute x15 -> x14, waiting for transfers between devices: 7.82 us -> 10.4 us  [swap(): return lax.ppermute(x, 'row', [(i, i ^ bits) for i in range(devices)])]
    pallas_call x5 -> x6, Pallas kernels: 18.9 us -> 17.7 us  [the longest x4 16 us: local(): pl.pallas_call(functools.partial(attention_kernel, heads, ms, first), out...]
    unnamed x18 -> x22, local copies, waits for them, and re-layouts: 1.25 us -> 2.26 us
  transfers between devices with their start and end apart: 15 -> 14, of which waited for: 4 -> 3; matrix products, arithmetic and copies ran while one was open for 0% -> 0% of each run, Pallas kernels for 33% -> 32%
where the time goes in v4:
time: 61.1 us; the launch traced here: 60.9 us
  Pallas kernels  26.6 us (44%)
  starting transfers between devices  21.4 us (35%)
  waiting for transfers between devices  10.4 us (17%)
  local copies, waits for them, and re-layouts  2.26 us (4%)
    ppermute x14, starting transfers between devices, swap(): return lax.ppermute(x, 'row', [(i, i ^ bits) for i in range(devices)])  21.4 us
    pallas_call x4, Pallas kernels, local(): pl.pallas_call(functools.partial(attention_kernel, heads, ms, first), out...  16 us
    ppermute x14, waiting for transfers between devices, swap(): return lax.ppermute(x, 'row', [(i, i ^ bits) for i in range(devices)])  10.4 us
    pallas_call x1, Pallas kernels, local(): pl.pallas_call(bias_kernel, grid=(rows_held // step_rows,), out_shape=[ja...  6.64 us
    pallas_call x1, Pallas kernels, local(): pl.pallas_call(key_value_kernel, out_shape=[jax.ShapeDtypeStruct((2 * cou...  2.27 us
    unnamed x22, local copies, waits for them, and re-layouts  2.26 us
    pallas_call x2, Pallas kernels, local(): pl.pallas_call(functools.partial(gather_kernel, order), out_shape=jax.Sha...  1.64 us
  transfers between devices with their start and end apart: 14, of which 3 were waited for; matrix products, arithmetic and copies ran while one was open for 0% of the time, Pallas kernels for 32%

profile of v4, /device:TPU:0, one launch (start us, length us, event | category | flops | bytes accessed | tf_op | source)
XLA Modules:
  0.0 60.9 jit_solution(4988200397788949444)
XLA Ops:
  0.0 0.0 copy-start.2
  0.0 0.0 copy-start.3
  0.0 6.6 %shard_map.109 = (bf16[128,384]{1,0:T(8,128)(2,1)}, bf16[8,512,128]{2,1,0:T(8,128)(2,1)}, bf16[384,512]{1,0:T(8,128)(2,1)}, f32[8,384]{1,0:T(8,128)}) custom-call(s32[8]{0:T(128)} %rows_ref.1, bf16[32,512,128]{2,1,0:T(8,128)(2,1)} %pair_ref.1, s32[1,512]{1,0:T(1,128)} %bitcast.17, s32[1,512]{1,0:T(1,128)} %bitcast.22, f32[1,128]{1,0:T(1,128)} %bitcast.32, ...), custom_call_target="tpu_custom_call" | custom-call | bytes 22140000 | tf_op jit(solution)/shard_map/pallas_call | solution.py:243
  6.6 0.0 copy-start.7
  6.6 0.0 copy-start.8
  6.7 0.0 copy-start.9
  6.7 0.0 copy-start.10
  6.7 0.5 collective-permute-start.2
  7.2 2.6 %collective-permute-start.5 = (bf16[128,384]{1,0:T(8,128)(2,1)}, bf16[128,384]{1,0:T(8,128)(2,1)S(1)}, u32[]{:S(2)}, u32[]{:S(2)}) collective-permute-start(bf16[128,384]{1,0:T(8,128)(2,1)} %get-tuple-element.21.refs_0_), channel_id=1, source_target_pairs={{0,2},{1,3},{2,0},{3,1},{4,6},{5,7},{6,4},{7,5},{8,10},{9,11},{10,... | collective-permute-start | bytes 294920 | tf_op jit(solution)/shard_map/ppermute | solution.py:240
  9.8 2.6 %collective-permute-start.3 = (bf16[128,384]{1,0:T(8,128)(2,1)}, bf16[128,384]{1,0:T(8,128)(2,1)S(1)}, u32[]{:S(2)}, u32[]{:S(2)}) collective-permute-start(bf16[128,384]{1,0:T(8,128)(2,1)} %get-tuple-element.21.refs_0_), channel_id=1, source_target_pairs={{0,8},{1,9},{2,10},{3,11},{4,12},{5,13},{6,14},{7,15},{8,0},{9,1},... | collective-permute-start | bytes 294920 | tf_op jit(solution)/shard_map/ppermute | solution.py:240
  12.4 1.3 %collective-permute-start.4 = (bf16[128,384]{1,0:T(8,128)(2,1)}, bf16[128,384]{1,0:T(8,128)(2,1)S(1)}, u32[]{:S(2)}, u32[]{:S(2)}) collective-permute-start(bf16[128,384]{1,0:T(8,128)(2,1)} %get-tuple-element.21.refs_0_), channel_id=1, source_target_pairs={{0,12},{1,13},{2,14},{3,15},{4,8},{5,9},{6,10},{7,11},{8,4},{9,5},... | collective-permute-start | bytes 294920 | tf_op jit(solution)/shard_map/ppermute | solution.py:240
  13.7 0.2 collective-permute-start
  14.0 0.0 collective-permute-done.2.other_ref
  14.0 1.7 %collective-permute-start.1 = (bf16[128,384]{1,0:T(8,128)(2,1)}, bf16[128,384]{1,0:T(8,128)(2,1)S(1)}, u32[]{:S(2)}, u32[]{:S(2)}) collective-permute-start(bf16[128,384]{1,0:T(8,128)(2,1)} %get-tuple-element.21.refs_0_), channel_id=1, source_target_pairs={{0,6},{1,7},{2,4},{3,5},{4,2},{5,3},{6,0},{7,1},{8,14},{9,15},{10,... | collective-permute-start | bytes 294920 | tf_op jit(solution)/shard_map/ppermute | solution.py:240
  15.7 0.0 copy-done.2
  15.7 0.0 copy-start
  15.7 1.2 %copy-done = bf16[8,512,128]{2,1,0:T(8,128)(2,1)S(1)} copy-done((bf16[8,512,128]{2,1,0:T(8,128)(2,1)S(1)}, bf16[8,512,128]{2,1,0:T(8,128)(2,1)}, u32[]{:S(2)}) %copy-start) | copy-done | bytes 1048600
  16.9 0.0 copy-start.4
  16.9 1.0 %copy-done.4 = bf16[384,512]{1,0:T(8,128)(2,1)S(1)} copy-done((bf16[384,512]{1,0:T(8,128)(2,1)S(1)}, bf16[384,512]{1,0:T(8,128)(2,1)}, u32[]{:S(2)}) %copy-start.4) | copy-done | bytes 393240
  17.9 0.0 copy-start.1
  17.9 0.0 copy-start.5
  17.9 0.0 copy-start.6
  17.9 2.3 %shard_map.110 = (bf16[16,128,384]{2,1,0:T(8,128)(2,1)S(1)}, bf16[16,384,128]{2,1,0:T(8,128)(2,1)S(1)}) custom-call(bf16[8,512,128]{2,1,0:T(8,128)(2,1)S(1)} %copy-done, bf16[8,512,128]{2,1,0:T(8,128)(2,1)S(1)} %collective-permute-done.2.other_ref, bf16[384,512]{1,0:T(8,128)(2,1)S(1)} %copy-done.4, bf16[128,512]{1,0:T(8,128)(2,1)S(1)} %copy-done.2), custom_call_target="tpu_custom_call" | custom-call | bytes 7380000 | tf_op jit(solution)/shard_map/pallas_call | solution.py:283
  20.2 0.0 collective-permute-done.5.refs_1_
  20.2 0.0 copy-done.3
  20.2 0.0 copy-done.7
  20.2 0.0 copy-done.8
  20.3 0.0 copy-done.9
  20.3 0.0 copy-done.10
  20.3 0.0 copy-done.1
  20.3 0.0 copy-done.5
  20.3 0.0 copy-done.6
  20.3 4.0 %shard_map.111 = (bf16[16,32,128]{2,1,0:T(8,128)(2,1)S(1)}, bf16[16,32,128]{2,1,0:T(8,128)(2,1)S(1)}) custom-call(s32[1]{0:T(128)} %bitcast.me_ref, f32[4]{0:T(128)S(1)} %copy-done.9, bf16[128,384]{1,0:T(8,128)(2,1)S(1)} %copy-done.6, bf16[128,384]{1,0:T(8,128)(2,1)S(1)} %collective-permute-done.5.refs_1_, bf16[8,8,2,32,128]{4,3,2,1,0:T(8,128)(2,1)S(1)} %bitcast.9, ...), custom_call_target="tpu_custom_call" | custom-call | bytes 16236000 | tf_op jit(solution)/shard_map/pallas_call | solution.py:311
  24.3 0.0 collective-permute-done.3.refs_0_
  24.3 0.0 collective-permute-done.4.refs_1_
  24.4 1.6 %collective-permute-start.6 = (bf16[256,384]{1,0:T(8,128)(2,1)S(1)}, bf16[256,384]{1,0:T(8,128)(2,1)S(1)}, u32[]{:S(2)}, u32[]{:S(2)}) collective-permute-start(bf16[256,384]{1,0:T(8,128)(2,1)S(1)} %pad_maximum_fusion), channel_id=1, source_target_pairs={{0,2},{1,3},{2,0},{3,1},{4,6},{5,7},{6,4},{7,5},{8,10},{9,11},{10,... | collective-permute-start | bytes 589832 | tf_op jit(solution)/shard_map/ppermute | solution.py:240
  26.0 0.0 collective-permute-done.refs_13_.refs_0_
  26.0 0.0 collective-permute-done.1.refs_14_.refs_1_
  26.0 4.0 %shard_map.112 = (bf16[16,32,128]{2,1,0:T(8,128)(2,1)S(1)}, bf16[16,32,128]{2,1,0:T(8,128)(2,1)S(1)}) custom-call(s32[1]{0:T(128)} %bitcast.me_ref, f32[4]{0:T(128)S(1)} %copy-done.9, bf16[128,384]{1,0:T(8,128)(2,1)S(1)} %collective-permute-done.3.refs_0_, bf16[128,384]{1,0:T(8,128)(2,1)S(1)} %collective-permute-done.4.refs_1_, ...), custom_call_target="tpu_custom_call" | custom-call | bytes 16236000 | tf_op jit(solution)/shard_map/pallas_call | solution.py:311
  30.0 1.7 %collective-permute-start.7 = (bf16[16,32,128]{2,1,0:T(8,128)(2,1)S(1)}, bf16[16,32,128]{2,1,0:T(8,128)(2,1)S(1)}, u32[]{:S(2)}, u32[]{:S(2)}) collective-permute-start(bf16[16,32,128]{2,1,0:T(8,128)(2,1)S(1)} %get-tuple-element.30.refs_12_), channel_id=1, source_target_pairs={{0,8},{1,9},{2,10},{3,11},{4,12},{5,13},{6,14},{7,15},{8,0},{9,1},... | collective-permute-start | bytes 393224 | tf_op jit(solution)/shard_map/ppermute | solution.py:240
  31.7 0.9 %collective-permute-start.8 = (bf16[16,32,128]{2,1,0:T(8,128)(2,1)S(1)}, bf16[16,32,128]{2,1,0:T(8,128)(2,1)S(1)}, u32[]{:S(2)}, u32[]{:S(2)}) collective-permute-start(bf16[16,32,128]{2,1,0:T(8,128)(2,1)S(1)} %get-tuple-element.32), channel_id=1, source_target_pairs={{0,12},{1,13},{2,14},{3,15},{4,8},{5,9},{6,10},{7,11},{8,4},{9,5},... | collective-permute-start | bytes 393224 | tf_op jit(solution)/shard_map/ppermute | solution.py:240
  32.6 0.5 collective-permute-start.11
  33.1 0.0 collective-permute-done.6.refs_0_.refs_1_
  33.1 4.0 %shard_map.113 = (bf16[16,32,128]{2,1,0:T(8,128)(2,1)S(1)}, bf16[16,32,128]{2,1,0:T(8,128)(2,1)S(1)}) custom-call(s32[1]{0:T(128)} %bitcast.me_ref, f32[4]{0:T(128)S(1)} %copy-done.9, bf16[256,384]{1,0:T(8,128)(2,1)S(1)} %collective-permute-done.6.refs_0_.refs_1_, bf16[256,384]{1,0:T(8,128)(2,1)S(1)} %collective-permute-done.6.refs_0_.refs_1_, ...), custom_call_target="tpu_custom_call" | custom-call | bytes 16236000 | tf_op jit(solution)/shard_map/pallas_call | solution.py:311
  37.1 2.9 %collective-permute-start.12 = (bf16[16,32,128]{2,1,0:T(8,128)(2,1)S(1)}, bf16[16,32,128]{2,1,0:T(8,128)(2,1)S(1)}, u32[]{:S(2)}, u32[]{:S(2)}) collective-permute-start(bf16[16,32,128]{2,1,0:T(8,128)(2,1)S(1)} %get-tuple-element.31.refs_12_), channel_id=1, source_target_pairs={{0,10},{1,11},{2,8},{3,9},{4,14},{5,15},{6,12},{7,13},{8,2},{9,3},... | collective-permute-start | bytes 393224 | tf_op jit(solution)/shard_map/ppermute | solution.py:240
  40.1 1.3 %collective-permute-start.13 = (bf16[16,32,128]{2,1,0:T(8,128)(2,1)S(1)}, bf16[16,32,128]{2,1,0:T(8,128)(2,1)S(1)}, u32[]{:S(2)}, u32[]{:S(2)}) collective-permute-start(bf16[16,32,128]{2,1,0:T(8,128)(2,1)S(1)} %get-tuple-element.36), channel_id=1, source_target_pairs={{0,14},{1,15},{2,12},{3,13},{4,10},{5,11},{6,8},{7,9},{8,6},{9,7},... | collective-permute-start | bytes 393224 | tf_op jit(solution)/shard_map/ppermute | solution.py:240
  41.4 5.5 %collective-permute-done.7.refs_13_.refs_2_ = bf16[16,32,128]{2,1,0:T(8,128)(2,1)S(1)} collective-permute-done((bf16[16,32,128]{2,1,0:T(8,128)(2,1)S(1)}, bf16[16,32,128]{2,1,0:T(8,128)(2,1)S(1)}, u32[]{:S(2)}, u32[]{:S(2)}) %collective-permute-start.7) | collective-permute-done | bytes 131104 | tf_op jit(solution)/shard_map/ppermute | solution.py:240
  46.9 0.0 collective-permute-done.8.refs_14_.refs_3_
  46.9 4.0 %shard_map.114 = (bf16[16,32,128]{2,1,0:T(8,128)(2,1)S(1)}, bf16[16,32,128]{2,1,0:T(8,128)(2,1)S(1)}) custom-call(s32[1]{0:T(128)} %bitcast.me_ref, f32[4]{0:T(128)S(1)} %copy-done.9, bf16[128,384]{1,0:T(8,128)(2,1)S(1)} %collective-permute-done.refs_13_.refs_0_, bf16[128,384]{1,0:T(8,128)(2,1)S(1)} %collective-permute-done.1.refs_14_.refs_1_, ...), custom_call_target="tpu_custom_call" | custom-call | bytes 16236000 | tf_op jit(solution)/shard_map/pallas_call | solution.py:311
  50.9 3.4 %collective-permute-start.9 = (bf16[16,32,128]{2,1,0:T(8,128)(2,1)S(1)}, bf16[16,32,128]{2,1,0:T(8,128)(2,1)S(1)}, u32[]{:S(2)}, u32[]{:S(2)}) collective-permute-start(bf16[16,32,128]{2,1,0:T(8,128)(2,1)S(1)} %get-tuple-element.33), channel_id=1, source_target_pairs={{0,4},{1,5},{2,6},{3,7},{4,0},{5,1},{6,2},{7,3},{8,12},{9,13},{10,... | collective-permute-start | bytes 393224 | tf_op jit(solution)/shard_map/ppermute | solution.py:240
  54.3 0.0 collective-permute-start.10
  54.3 0.0 collective-permute-done.11.refs_1_
  54.3 0.0 collective-permute-done.12.refs_4_
  54.3 0.0 collective-permute-done.13.refs_5_
  54.3 0.9 %shard_map.115.refs_2_ = bf16[128,32,128]{2,1,0:T(8,128)(2,1)} custom-call(s32[1]{0:T(128)} %bitcast.me_ref, bf16[16,32,128]{2,1,0:T(8,128)(2,1)S(1)} %get-tuple-element.27.refs_12_.refs_0_, bf16[16,32,128]{2,1,0:T(8,128)(2,1)S(1)} %collective-permute-done.11.refs_1_, bf16[16,32,128]{2,1,0:T(8,128)(2,1)S(1)} %collective-permute-done.7.refs_13_.refs_2_, ...), custom_call_target="tpu_custom_call" | custom-call | bytes 3690000 | tf_op jit(solution)/shard_map/pallas_call | solution.py:354
  55.3 3.0 %collective-permute-done.9.refs_0_ = bf16[16,32,128]{2,1,0:T(8,128)(2,1)S(1)} collective-permute-done((bf16[16,32,128]{2,1,0:T(8,128)(2,1)S(1)}, bf16[16,32,128]{2,1,0:T(8,128)(2,1)S(1)}, u32[]{:S(2)}, u32[]{:S(2)}) %collective-permute-start.9) | collective-permute-done | bytes 131104 | tf_op jit(solution)/shard_map/ppermute | solution.py:240
  58.3 1.9 %collective-permute-done.10.refs_1_ = bf16[16,32,128]{2,1,0:T(8,128)(2,1)S(1)} collective-permute-done((bf16[16,32,128]{2,1,0:T(8,128)(2,1)S(1)}, bf16[16,32,128]{2,1,0:T(8,128)(2,1)S(1)}, u32[]{:S(2)}, u32[]{:S(2)}) %collective-permute-start.10) | collective-permute-done | bytes 131104 | tf_op jit(solution)/shard_map/ppermute | solution.py:240
  60.2 0.7 %shard_map.116 = bf16[128,32,128]{2,1,0:T(8,128)(2,1)} custom-call(s32[1]{0:T(128)} %bitcast.me_ref, bf16[16,32,128]{2,1,0:T(8,128)(2,1)S(1)} %collective-permute-done.9.refs_0_, bf16[16,32,128]{2,1,0:T(8,128)(2,1)S(1)} %collective-permute-done.10.refs_1_, bf16[128,32,128]{2,1,0:T(8,128)(2,1)} %shard_map.115.refs_2_), custom_call_target="tpu_custom_call", output_to_operand_aliasing={{}: (3, {})} | custom-call | bytes 3690000 | tf_op jit(solution)/shard_map/pallas_call | solution.py:354
  (1 shorter events, 0.0 us)
Async XLA Ops:
  0.0 15.7 %copy-start.2 = (bf16[128,512]{1,0:T(8,128)(2,1)S(1)}, bf16[128,512]{1,0:T(8,128)(2,1)}, u32[]{:S(2)}) copy-start(bf16[128,512]{1,0:T(8,128)(2,1)} %refs_9_.7) | copy-start | bytes 393220
  0.0 20.2 %copy-start.3 = (bf16[128,128]{1,0:T(8,128)(2,1)S(1)}, bf16[128,128]{1,0:T(8,128)(2,1)}, u32[]{:S(2)}) copy-start(bf16[128,128]{1,0:T(8,128)(2,1)} %refs_11_.7) | copy-start | bytes 98308
  6.6 13.6 %copy-start.7 = (s32[512]{0:T(512)S(1)}, s32[512]{0:T(512)}, u32[]{:S(2)}) copy-start(s32[512]{0:T(512)} %param.13) | copy-start | bytes 6148
  6.6 13.6 %copy-start.8 = (s32[512]{0:T(512)S(1)}, s32[512]{0:T(512)}, u32[]{:S(2)}) copy-start(s32[512]{0:T(512)} %param.14) | copy-start | bytes 6148
  6.7 13.6 %copy-start.9 = (f32[4]{0:T(128)S(1)}, f32[4]{0:T(128)}, u32[]{:S(2)}) copy-start(f32[4]{0:T(128)} %chain_bias_ref.7) | copy-start | bytes 52
  6.7 13.6 %copy-start.10 = (f32[128]{0:T(128)S(1)}, f32[128]{0:T(128)}, u32[]{:S(2)}) copy-start(f32[128]{0:T(128)} %param.18) | copy-start | bytes 1540
  6.7 7.3 %collective-permute-start.2 = (bf16[8,512,128]{2,1,0:T(8,128)(2,1)}, bf16[8,512,128]{2,1,0:T(8,128)(2,1)S(1)}, u32[]{:S(2)}, u32[]{:S(2)}) collective-permute-start(bf16[8,512,128]{2,1,0:T(8,128)(2,1)} %get-tuple-element.22.own_ref), channel_id=1, source_target_pairs={{0,1},{1,0},{2,3},{3,2},{4,5},{5,4},{6,7},{7,6},{8,9},{9,8},{10,11... | collective-permute-start | bytes 3145736 | tf_op jit(solution)/shard_map/ppermute | solution.py:240
  7.2 13.0 %collective-permute-start.5 = (bf16[128,384]{1,0:T(8,128)(2,1)}, bf16[128,384]{1,0:T(8,128)(2,1)S(1)}, u32[]{:S(2)}, u32[]{:S(2)}) collective-permute-start(bf16[128,384]{1,0:T(8,128)(2,1)} %get-tuple-element.21.refs_0_), channel_id=1, source_target_pairs={{0,2},{1,3},{2,0},{3,1},{4,6},{5,7},{6,4},{7,5},{8,10},{9,11},{10,... | collective-permute-start | bytes 294920 | tf_op jit(solution)/shard_map/ppermute | solution.py:240
  9.8 14.5 %collective-permute-start.3 = (bf16[128,384]{1,0:T(8,128)(2,1)}, bf16[128,384]{1,0:T(8,128)(2,1)S(1)}, u32[]{:S(2)}, u32[]{:S(2)}) collective-permute-start(bf16[128,384]{1,0:T(8,128)(2,1)} %get-tuple-element.21.refs_0_), channel_id=1, source_target_pairs={{0,8},{1,9},{2,10},{3,11},{4,12},{5,13},{6,14},{7,15},{8,0},{9,1},... | collective-permute-start | bytes 294920 | tf_op jit(solution)/shard_map/ppermute | solution.py:240
  12.4 11.9 %collective-permute-start.4 = (bf16[128,384]{1,0:T(8,128)(2,1)}, bf16[128,384]{1,0:T(8,128)(2,1)S(1)}, u32[]{:S(2)}, u32[]{:S(2)}) collective-permute-start(bf16[128,384]{1,0:T(8,128)(2,1)} %get-tuple-element.21.refs_0_), channel_id=1, source_target_pairs={{0,12},{1,13},{2,14},{3,15},{4,8},{5,9},{6,10},{7,11},{8,4},{9,5},... | collective-permute-start | bytes 294920 | tf_op jit(solution)/shard_map/ppermute | solution.py:240
  13.7 12.2 %collective-permute-start = (bf16[128,384]{1,0:T(8,128)(2,1)}, bf16[128,384]{1,0:T(8,128)(2,1)S(1)}, u32[]{:S(2)}, u32[]{:S(2)}) collective-permute-start(bf16[128,384]{1,0:T(8,128)(2,1)} %get-tuple-element.21.refs_0_), channel_id=1, source_target_pairs={{0,4},{1,5},{2,6},{3,7},{4,0},{5,1},{6,2},{7,3},{8,12},{9,13},{10,... | collective-permute-start | bytes 294920 | tf_op jit(solution)/shard_map/ppermute | solution.py:240
  14.0 12.0 %collective-permute-start.1 = (bf16[128,384]{1,0:T(8,128)(2,1)}, bf16[128,384]{1,0:T(8,128)(2,1)S(1)}, u32[]{:S(2)}, u32[]{:S(2)}) collective-permute-start(bf16[128,384]{1,0:T(8,128)(2,1)} %get-tuple-element.21.refs_0_), channel_id=1, source_target_pairs={{0,6},{1,7},{2,4},{3,5},{4,2},{5,3},{6,0},{7,1},{8,14},{9,15},{10,... | collective-permute-start | bytes 294920 | tf_op jit(solution)/shard_map/ppermute | solution.py:240
  15.7 1.2 %copy-start = (bf16[8,512,128]{2,1,0:T(8,128)(2,1)S(1)}, bf16[8,512,128]{2,1,0:T(8,128)(2,1)}, u32[]{:S(2)}) copy-start(bf16[8,512,128]{2,1,0:T(8,128)(2,1)} %get-tuple-element.22.own_ref) | copy-start | bytes 3145732
  16.9 1.0 %copy-start.4 = (bf16[384,512]{1,0:T(8,128)(2,1)S(1)}, bf16[384,512]{1,0:T(8,128)(2,1)}, u32[]{:S(2)}) copy-start(bf16[384,512]{1,0:T(8,128)(2,1)} %get-tuple-element.23.pick_ref) | copy-start | bytes 1179652
  17.9 2.3 %copy-start.1 = (bf16[8,512,128]{2,1,0:T(8,128)(2,1)S(1)}, bf16[8,512,128]{2,1,0:T(8,128)(2,1)}, u32[]{:S(2)}) copy-start(bf16[8,512,128]{2,1,0:T(8,128)(2,1)} %get-tuple-element.22.own_ref) | copy-start | bytes 3145732
  17.9 2.4 %copy-start.5 = (f32[8,384]{1,0:T(8,128)S(1)}, f32[8,384]{1,0:T(8,128)}, u32[]{:S(2)}) copy-start(f32[8,384]{1,0:T(8,128)} %get-tuple-element.26.refs_8_) | copy-start | bytes 36868
  17.9 2.4 %copy-start.6 = (bf16[128,384]{1,0:T(8,128)(2,1)S(1)}, bf16[128,384]{1,0:T(8,128)(2,1)}, u32[]{:S(2)}) copy-start(bf16[128,384]{1,0:T(8,128)(2,1)} %get-tuple-element.21.refs_0_) | copy-start | bytes 294916
  24.4 8.8 %collective-permute-start.6 = (bf16[256,384]{1,0:T(8,128)(2,1)S(1)}, bf16[256,384]{1,0:T(8,128)(2,1)S(1)}, u32[]{:S(2)}, u32[]{:S(2)}) collective-permute-start(bf16[256,384]{1,0:T(8,128)(2,1)S(1)} %pad_maximum_fusion), channel_id=1, source_target_pairs={{0,2},{1,3},{2,0},{3,1},{4,6},{5,7},{6,4},{7,5},{8,10},{9,11},{10,... | collective-permute-start | bytes 589832 | tf_op jit(solution)/shard_map/ppermute | solution.py:240
  30.0 16.9 %collective-permute-start.7 = (bf16[16,32,128]{2,1,0:T(8,128)(2,1)S(1)}, bf16[16,32,128]{2,1,0:T(8,128)(2,1)S(1)}, u32[]{:S(2)}, u32[]{:S(2)}) collective-permute-start(bf16[16,32,128]{2,1,0:T(8,128)(2,1)S(1)} %get-tuple-element.30.refs_12_), channel_id=1, source_target_pairs={{0,8},{1,9},{2,10},{3,11},{4,12},{5,13},{6,14},{7,15},{8,0},{9,1},... | collective-permute-start | bytes 393224 | tf_op jit(solution)/shard_map/ppermute | solution.py:240
  31.7 15.2 %collective-permute-start.8 = (bf16[16,32,128]{2,1,0:T(8,128)(2,1)S(1)}, bf16[16,32,128]{2,1,0:T(8,128)(2,1)S(1)}, u32[]{:S(2)}, u32[]{:S(2)}) collective-permute-start(bf16[16,32,128]{2,1,0:T(8,128)(2,1)S(1)} %get-tuple-element.32), channel_id=1, source_target_pairs={{0,12},{1,13},{2,14},{3,15},{4,8},{5,9},{6,10},{7,11},{8,4},{9,5},... | collective-permute-start | bytes 393224 | tf_op jit(solution)/shard_map/ppermute | solution.py:240
  32.6 21.7 %collective-permute-start.11 = (bf16[16,32,128]{2,1,0:T(8,128)(2,1)S(1)}, bf16[16,32,128]{2,1,0:T(8,128)(2,1)S(1)}, u32[]{:S(2)}, u32[]{:S(2)}) collective-permute-start(bf16[16,32,128]{2,1,0:T(8,128)(2,1)S(1)} %get-tuple-element.35), channel_id=1, source_target_pairs={{0,2},{1,3},{2,0},{3,1},{4,6},{5,7},{6,4},{7,5},{8,10},{9,11},{10,... | collective-permute-start | bytes 393224 | tf_op jit(solution)/shard_map/ppermute | solution.py:240
  37.1 17.2 %collective-permute-start.12 = (bf16[16,32,128]{2,1,0:T(8,128)(2,1)S(1)}, bf16[16,32,128]{2,1,0:T(8,128)(2,1)S(1)}, u32[]{:S(2)}, u32[]{:S(2)}) collective-permute-start(bf16[16,32,128]{2,1,0:T(8,128)(2,1)S(1)} %get-tuple-element.31.refs_12_), channel_id=1, source_target_pairs={{0,10},{1,11},{2,8},{3,9},{4,14},{5,15},{6,12},{7,13},{8,2},{9,3},... | collective-permute-start | bytes 393224 | tf_op jit(solution)/shard_map/ppermute | solution.py:240
  40.1 14.3 %collective-permute-start.13 = (bf16[16,32,128]{2,1,0:T(8,128)(2,1)S(1)}, bf16[16,32,128]{2,1,0:T(8,128)(2,1)S(1)}, u32[]{:S(2)}, u32[]{:S(2)}) collective-permute-start(bf16[16,32,128]{2,1,0:T(8,128)(2,1)S(1)} %get-tuple-element.36), channel_id=1, source_target_pairs={{0,14},{1,15},{2,12},{3,13},{4,10},{5,11},{6,8},{7,9},{8,6},{9,7},... | collective-permute-start | bytes 393224 | tf_op jit(solution)/shard_map/ppermute | solution.py:240
  50.9 7.4 %collective-permute-start.9 = (bf16[16,32,128]{2,1,0:T(8,128)(2,1)S(1)}, bf16[16,32,128]{2,1,0:T(8,128)(2,1)S(1)}, u32[]{:S(2)}, u32[]{:S(2)}) collective-permute-start(bf16[16,32,128]{2,1,0:T(8,128)(2,1)S(1)} %get-tuple-element.33), channel_id=1, source_target_pairs={{0,4},{1,5},{2,6},{3,7},{4,0},{5,1},{6,2},{7,3},{8,12},{9,13},{10,... | collective-permute-start | bytes 393224 | tf_op jit(solution)/shard_map/ppermute | solution.py:240
  54.3 5.9 %collective-permute-start.10 = (bf16[16,32,128]{2,1,0:T(8,128)(2,1)S(1)}, bf16[16,32,128]{2,1,0:T(8,128)(2,1)S(1)}, u32[]{:S(2)}, u32[]{:S(2)}) collective-permute-start(bf16[16,32,128]{2,1,0:T(8,128)(2,1)S(1)} %get-tuple-element.34), channel_id=1, source_target_pairs={{0,6},{1,7},{2,4},{3,5},{4,2},{5,3},{6,0},{7,1},{8,14},{9,15},{10,... | collective-permute-start | bytes 393224 | tf_op jit(solution)/shard_map/ppermute | solution.py:240

commit v5 on v4

--- a/solution.py
+++ b/solution.py
@@ -268,9 +268,9 @@
             pltpu.VMEM((tokens, heads * rows_held), F32),
             pltpu.VMEM((rows_held, tokens, channels), BF16),
         ],
-        compiler_params=pltpu.CompilerParams(vmem_limit_bytes=60 * 1024 * 1024),
+        compiler_params=PARAMS,
         cost_estimate=measured(6),
-    )(window_rows, pair, mask_row, chain_row, gain, shift, w_bias.T)
+    )(window_rows, pltpu.with_memory_space_constraint(pair, pltpu.HBM), mask_row, chain_row, gain, shift, w_bias.T)
 
     far = [m for m in range(owners // 2, owners) if m % 2 == 0]
     passed = [m + 1 for m in far]
@@ -295,16 +295,20 @@
     split = (count, owners, 2, rows_held, channels)
     own, other = own.reshape(split), other.reshape(split)
     updates = {}
+    *straight, _ = lax.optimization_barrier((*[biases[m] for m in far], keys))
+    straight = swap(jnp.concatenate(straight), 2)
+    for m in passed:
+        biases[m] = straight
     sent = {}
-    for ms in ([0] + near[:1], far, passed, near[1:]):
+    for ms in (far, [0] + near[:1], passed, near[1:]):
         if ms == far:
-            after = [updates[0]] + [biases[m] for m in near[1:]]
-        elif ms == passed:
-            after = [updates[far[0]]]
+            after = []
         elif ms == near[1:]:
             after = [updates[passed[0]]] + [sent[m] for m in far]
         else:
-            after = []
+            after = [updates[far[0] if 0 in ms else 0]]
+            if ms == passed:
+                after += [biases[m] for m in near[1:]]
         blocks = len(ms)
         first = [i * heads * rows_held if ms == passed else 0 for i in range(blocks)]
         rows = 2 * count * rows_held
@@ -339,11 +343,6 @@
         )
         for m, out in zip(ms, outs):
             updates[m] = out
-        if 0 in ms:
-            *straight, _ = lax.optimization_barrier((*[biases[m] for m in far], outs[0]))
-            straight = swap(jnp.concatenate(straight), 2)
-            for i, m in enumerate(passed):
-                biases[m] = straight
         for m, out in zip(ms, outs):
             sent[m] = out if m == 0 else swap(out, 2 * m)
 

time: 61.1 us -> 68.7 us (1.12)
  local copies, waits for them, and re-layouts: 2.26 us -> 9.16 us
  starting transfers between devices: 21.4 us -> 22.9 us
    unnamed x22 -> x34, local copies, waits for them, and re-layouts: 2.26 us -> 9.16 us
    ppermute x14, starting transfers between devices: 21.4 us -> 22.9 us  [swap(): return lax.ppermute(x, 'row', [(i, i ^ bits) for i in range(devices)])]
    pallas_call x1, Pallas kernels: 6.64 us -> 5.51 us  [local(): pl.pallas_call(bias_kernel, grid=(rows_held // step_rows,), out_shape=[ja...]
  transfers between devices with their start and end apart: 14 -> 14, of which waited for: 3 -> 6; matrix products, arithmetic and copies ran while one was open for 0% -> 0% of each run, Pallas kernels for 32% -> 29%
where the time goes in v5:
time: 68.7 us; the launch traced here: 68.5 us
  Pallas kernels  26 us (38%)
  starting transfers between devices  22.9 us (33%)
  waiting for transfers between devices  10.2 us (15%)
  local copies, waits for them, and re-layouts  9.16 us (13%)
    ppermute x14, starting transfers between devices, swap(): return lax.ppermute(x, 'row', [(i, i ^ bits) for i in range(devices)])  22.9 us
    pallas_call x4, Pallas kernels, local(): pl.pallas_call(functools.partial(attention_kernel, heads, ms, first), out...  16.6 us
    ppermute x14, waiting for transfers between devices, swap(): return lax.ppermute(x, 'row', [(i, i ^ bits) for i in range(devices)])  10.2 us
    unnamed x34, local copies, waits for them, and re-layouts  9.16 us
    pallas_call x1, Pallas kernels, local(): pl.pallas_call(bias_kernel, grid=(rows_held // step_rows,), out_shape=[ja...  5.51 us
    pallas_call x1, Pallas kernels, local(): pl.pallas_call(key_value_kernel, out_shape=[jax.ShapeDtypeStruct((2 * cou...  2.28 us
    pallas_call x2, Pallas kernels, local(): pl.pallas_call(functools.partial(gather_kernel, order), out_shape=jax.Sha...  1.64 us
  transfers between devices with their start and end apart: 14, of which 6 were waited for; matrix products, arithmetic and copies ran while one was open for 0% of the time, Pallas kernels for 29%

profile of v5, /device:TPU:0, one launch (start us, length us, event | category | flops | bytes accessed | tf_op | source)
XLA Modules:
  0.0 68.5 jit_solution(14909315905345230429)
XLA Ops:
  0.0 0.0 copy-start.7
  0.0 0.7 copy-done.7
  0.7 0.0 copy-start.9
  0.7 0.7 copy-done.9
  1.4 0.0 copy-start.13
  1.4 0.7 copy-done.13
  2.0 0.7 copy-done.14
  2.7 0.0 copy-start.15
  2.7 0.7 copy-done.15
  3.4 0.7 copy-done.16
  4.0 5.5 %shard_map.109 = (bf16[128,384]{1,0:T(8,128)(2,1)S(1)}, bf16[8,512,128]{2,1,0:T(8,128)(2,1)S(1)}, bf16[384,512]{1,0:T(8,128)(2,1)S(1)}, f32[8,384]{1,0:T(8,128)S(1)}) custom-call(s32[8]{0:T(128)S(1)} %copy-done.14, bf16[32,512,128]{2,1,0:T(8,128)(2,1)} %pair_ref.1, s32[1,512]{1,0:T(1,128)S(1)} %bitcast.17, s32[1,512]{1,0:T(1,128)S(1)} %bitcast.22, ...), custom_call_target="tpu_custom_call" | custom-call | bytes 22140000 | tf_op jit(solution)/shard_map/pallas_call | solution.py:243
  9.5 0.0 copy-start.6
  9.5 0.0 copy-start.8
  9.6 0.0 copy-start.10
  9.6 0.0 copy-start.11
  9.6 0.0 copy-start.12
  9.6 0.5 collective-permute-start.2
  10.1 3.7 %collective-permute-start.3 = (bf16[128,384]{1,0:T(8,128)(2,1)S(1)}, bf16[128,384]{1,0:T(8,128)(2,1)S(1)}, u32[]{:S(2)}, u32[]{:S(2)}) collective-permute-start(bf16[128,384]{1,0:T(8,128)(2,1)S(1)} %get-tuple-element.21.refs_0_), channel_id=1, source_target_pairs={{0,8},{1,9},{2,10},{3,11},{4,12},{5,13},{6,14},{7,15},{8,0},{9,1},... | collective-permute-start | bytes 294920 | tf_op jit(solution)/shard_map/ppermute | solution.py:240
  13.8 1.3 %collective-permute-start.4 = (bf16[128,384]{1,0:T(8,128)(2,1)S(1)}, bf16[128,384]{1,0:T(8,128)(2,1)S(1)}, u32[]{:S(2)}, u32[]{:S(2)}) collective-permute-start(bf16[128,384]{1,0:T(8,128)(2,1)S(1)} %get-tuple-element.21.refs_0_), channel_id=1, source_target_pairs={{0,12},{1,13},{2,14},{3,15},{4,8},{5,9},{6,10},{7,11},{8,4},{9,5},... | collective-permute-start | bytes 294920 | tf_op jit(solution)/shard_map/ppermute | solution.py:240
  15.1 1.5 %collective-permute-start.6 = (bf16[128,384]{1,0:T(8,128)(2,1)S(1)}, bf16[128,384]{1,0:T(8,128)(2,1)S(1)}, u32[]{:S(2)}, u32[]{:S(2)}) collective-permute-start(bf16[128,384]{1,0:T(8,128)(2,1)S(1)} %get-tuple-element.21.refs_0_), channel_id=1, source_target_pairs={{0,2},{1,3},{2,0},{3,1},{4,6},{5,7},{6,4},{7,5},{8,10},{9,11},{10,... | collective-permute-start | bytes 294920 | tf_op jit(solution)/shard_map/ppermute | solution.py:240
  16.6 0.0 collective-permute-done.2.other_ref
  16.6 0.0 copy-done.5
  16.7 2.3 %shard_map.110 = (bf16[16,128,384]{2,1,0:T(8,128)(2,1)S(1)}, bf16[16,384,128]{2,1,0:T(8,128)(2,1)S(1)}) custom-call(bf16[8,512,128]{2,1,0:T(8,128)(2,1)S(1)} %get-tuple-element.22.own_ref, bf16[8,512,128]{2,1,0:T(8,128)(2,1)S(1)} %collective-permute-done.2.other_ref, bf16[384,512]{1,0:T(8,128)(2,1)S(1)} %get-tuple-element.23.pick_ref, ...), custom_call_target="tpu_custom_call" | custom-call | bytes 7380000 | tf_op jit(solution)/shard_map/pallas_call | solution.py:283
  18.9 0.0 copy-start
  18.9 1.2 %copy-done = bf16[16,128,384]{2,1,0:T(8,128)(2,1)} copy-done((bf16[16,128,384]{2,1,0:T(8,128)(2,1)}, bf16[16,128,384]{2,1,0:T(8,128)(2,1)S(1)}, u32[]{:S(2)}) %copy-start) | copy-done | bytes 1572888
  20.1 1.1 %copy-done.3 = bf16[16,384,128]{2,1,0:T(8,128)(2,1)} copy-done((bf16[16,384,128]{2,1,0:T(8,128)(2,1)}, bf16[16,384,128]{2,1,0:T(8,128)(2,1)S(1)}, u32[]{:S(2)}) %copy-start.3) | copy-done | bytes 1572888
  21.3 0.4 collective-permute-done.3.refs_0_
  21.6 0.0 collective-permute-done.4.refs_1_
  21.7 1.8 %collective-permute-start.5 = (bf16[256,384]{1,0:T(8,128)(2,1)S(1)}, bf16[256,384]{1,0:T(8,128)(2,1)S(1)}, u32[]{:S(2)}, u32[]{:S(2)}) collective-permute-start(bf16[256,384]{1,0:T(8,128)(2,1)S(1)} %pad_maximum_fusion), channel_id=1, source_target_pairs={{0,2},{1,3},{2,0},{3,1},{4,6},{5,7},{6,4},{7,5},{8,10},{9,11},{10,... | collective-permute-start | bytes 589832 | tf_op jit(solution)/shard_map/ppermute | solution.py:240
  23.5 0.0 copy-done.6
  23.5 0.0 copy-done.8
  23.5 0.0 copy-done.10
  23.5 0.0 copy-done.11
  23.5 0.0 copy-done.12
  23.5 0.0 copy-start.1
  23.5 1.4 %copy-done.1 = bf16[16,128,384]{2,1,0:T(8,128)(2,1)S(1)} copy-done((bf16[16,128,384]{2,1,0:T(8,128)(2,1)S(1)}, bf16[16,128,384]{2,1,0:T(8,128)(2,1)}, u32[]{:S(2)}) %copy-start.1) | copy-done | bytes 1572888
  24.9 1.4 %copy-done.4 = bf16[16,384,128]{2,1,0:T(8,128)(2,1)S(1)} copy-done((bf16[16,384,128]{2,1,0:T(8,128)(2,1)S(1)}, bf16[16,384,128]{2,1,0:T(8,128)(2,1)}, u32[]{:S(2)}) %copy-start.4) | copy-done | bytes 1572888
  26.3 4.2 %shard_map.111 = (bf16[16,32,128]{2,1,0:T(8,128)(2,1)S(1)}, bf16[16,32,128]{2,1,0:T(8,128)(2,1)S(1)}) custom-call(s32[1]{0:T(128)} %bitcast.me_ref, f32[4]{0:T(128)S(1)} %copy-done.11, bf16[128,384]{1,0:T(8,128)(2,1)S(1)} %collective-permute-done.3.refs_0_, bf16[128,384]{1,0:T(8,128)(2,1)S(1)} %collective-permute-done.4.refs_1_, ...), custom_call_target="tpu_custom_call" | custom-call | bytes 16236000 | tf_op jit(solution)/shard_map/pallas_call | solution.py:315
  30.5 4.3 %collective-permute-start.7 = (bf16[16,32,128]{2,1,0:T(8,128)(2,1)S(1)}, bf16[16,32,128]{2,1,0:T(8,128)(2,1)S(1)}, u32[]{:S(2)}, u32[]{:S(2)}) collective-permute-start(bf16[16,32,128]{2,1,0:T(8,128)(2,1)S(1)} %get-tuple-element.29.refs_12_), channel_id=1, source_target_pairs={{0,8},{1,9},{2,10},{3,11},{4,12},{5,13},{6,14},{7,15},{8,0},{9,1},... | collective-permute-start | bytes 393224 | tf_op jit(solution)/shard_map/ppermute | solution.py:240
  34.9 0.4 collective-permute-start.8
  35.3 0.2 collective-permute-start
  35.5 0.0 collective-permute-done.6.refs_1_
  35.5 1.8 %collective-permute-start.1 = (bf16[128,384]{1,0:T(8,128)(2,1)S(1)}, bf16[128,384]{1,0:T(8,128)(2,1)S(1)}, u32[]{:S(2)}, u32[]{:S(2)}) collective-permute-start(bf16[128,384]{1,0:T(8,128)(2,1)S(1)} %get-tuple-element.21.refs_0_), channel_id=1, source_target_pairs={{0,6},{1,7},{2,4},{3,5},{4,2},{5,3},{6,0},{7,1},{8,14},{9,15},{10,... | collective-permute-start | bytes 294920 | tf_op jit(solution)/shard_map/ppermute | solution.py:240
  37.3 0.0 copy-done.2
  37.3 4.1 %shard_map.112 = (bf16[16,32,128]{2,1,0:T(8,128)(2,1)S(1)}, bf16[16,32,128]{2,1,0:T(8,128)(2,1)S(1)}) custom-call(s32[1]{0:T(128)} %bitcast.me_ref, f32[4]{0:T(128)S(1)} %copy-done.11, bf16[128,384]{1,0:T(8,128)(2,1)S(1)} %get-tuple-element.21.refs_0_, bf16[128,384]{1,0:T(8,128)(2,1)S(1)} %collective-permute-done.6.refs_1_, ...), custom_call_target="tpu_custom_call" | custom-call | bytes 16236000 | tf_op jit(solution)/shard_map/pallas_call | solution.py:315
  41.4 4.2 %collective-permute-done.refs_13_.refs_0_ = bf16[128,384]{1,0:T(8,128)(2,1)S(1)} collective-permute-done((bf16[128,384]{1,0:T(8,128)(2,1)S(1)}, bf16[128,384]{1,0:T(8,128)(2,1)S(1)}, u32[]{:S(2)}, u32[]{:S(2)}) %collective-permute-start) | collective-permute-done | bytes 98336 | tf_op jit(solution)/shard_map/ppermute | solution.py:240
  45.6 0.6 collective-permute-start.11
  46.2 0.6 collective-permute-done.1.refs_14_.refs_1_
  46.8 0.0 collective-permute-done.5.refs_0_.refs_1_
  46.8 4.1 %shard_map.113 = (bf16[16,32,128]{2,1,0:T(8,128)(2,1)S(1)}, bf16[16,32,128]{2,1,0:T(8,128)(2,1)S(1)}) custom-call(s32[1]{0:T(128)} %bitcast.me_ref, f32[4]{0:T(128)S(1)} %copy-done.11, bf16[256,384]{1,0:T(8,128)(2,1)S(1)} %collective-permute-done.5.refs_0_.refs_1_, bf16[256,384]{1,0:T(8,128)(2,1)S(1)} %collective-permute-done.5.refs_0_.refs_1_, ...), custom_call_target="tpu_custom_call" | custom-call | bytes 16236000 | tf_op jit(solution)/shard_map/pallas_call | solution.py:315
  51.0 0.6 collective-permute-start.12
  51.6 3.1 %collective-permute-start.13 = (bf16[16,32,128]{2,1,0:T(8,128)(2,1)S(1)}, bf16[16,32,128]{2,1,0:T(8,128)(2,1)S(1)}, u32[]{:S(2)}, u32[]{:S(2)}) collective-permute-start(bf16[16,32,128]{2,1,0:T(8,128)(2,1)S(1)} %get-tuple-element.36), channel_id=1, source_target_pairs={{0,14},{1,15},{2,12},{3,13},{4,10},{5,11},{6,8},{7,9},{8,6},{9,7},... | collective-permute-start | bytes 393224 | tf_op jit(solution)/shard_map/ppermute | solution.py:240
  54.6 0.0 collective-permute-done.7.refs_13_.refs_2_
  54.6 0.0 collective-permute-done.8.refs_14_.refs_3_
  54.6 4.1 %shard_map.114 = (bf16[16,32,128]{2,1,0:T(8,128)(2,1)S(1)}, bf16[16,32,128]{2,1,0:T(8,128)(2,1)S(1)}) custom-call(s32[1]{0:T(128)} %bitcast.me_ref, f32[4]{0:T(128)S(1)} %copy-done.11, bf16[128,384]{1,0:T(8,128)(2,1)S(1)} %collective-permute-done.refs_13_.refs_0_, bf16[128,384]{1,0:T(8,128)(2,1)S(1)} %collective-permute-done.1.refs_14_.refs_1_, ...), custom_call_target="tpu_custom_call" | custom-call | bytes 16236000 | tf_op jit(solution)/shard_map/pallas_call | solution.py:315
  58.8 0.9 %collective-permute-start.9 = (bf16[16,32,128]{2,1,0:T(8,128)(2,1)S(1)}, bf16[16,32,128]{2,1,0:T(8,128)(2,1)S(1)}, u32[]{:S(2)}, u32[]{:S(2)}) collective-permute-start(bf16[16,32,128]{2,1,0:T(8,128)(2,1)S(1)} %get-tuple-element.33), channel_id=1, source_target_pairs={{0,4},{1,5},{2,6},{3,7},{4,0},{5,1},{6,2},{7,3},{8,12},{9,13},{10,... | collective-permute-start | bytes 393224 | tf_op jit(solution)/shard_map/ppermute | solution.py:240
  59.7 2.2 %collective-permute-start.10 = (bf16[16,32,128]{2,1,0:T(8,128)(2,1)S(1)}, bf16[16,32,128]{2,1,0:T(8,128)(2,1)S(1)}, u32[]{:S(2)}, u32[]{:S(2)}) collective-permute-start(bf16[16,32,128]{2,1,0:T(8,128)(2,1)S(1)} %get-tuple-element.34), channel_id=1, source_target_pairs={{0,6},{1,7},{2,4},{3,5},{4,2},{5,3},{6,0},{7,1},{8,14},{9,15},{10,... | collective-permute-start | bytes 393224 | tf_op jit(solution)/shard_map/ppermute | solution.py:240
  61.8 0.0 collective-permute-done.11.refs_1_
  61.8 0.4 collective-permute-done.12.refs_4_
  62.3 0.0 collective-permute-done.13.refs_5_
  62.3 0.9 %shard_map.115.refs_2_ = bf16[128,32,128]{2,1,0:T(8,128)(2,1)} custom-call(s32[1]{0:T(128)} %bitcast.me_ref, bf16[16,32,128]{2,1,0:T(8,128)(2,1)S(1)} %get-tuple-element.30.refs_12_.refs_0_, bf16[16,32,128]{2,1,0:T(8,128)(2,1)S(1)} %collective-permute-done.11.refs_1_, bf16[16,32,128]{2,1,0:T(8,128)(2,1)S(1)} %collective-permute-done.7.refs_13_.refs_2_, ...), custom_call_target="tpu_custom_call" | custom-call | bytes 3690000 | tf_op jit(solution)/shard_map/pallas_call | solution.py:353
  63.2 2.1 %collective-permute-done.9.refs_0_ = bf16[16,32,128]{2,1,0:T(8,128)(2,1)S(1)} collective-permute-done((bf16[16,32,128]{2,1,0:T(8,128)(2,1)S(1)}, bf16[16,32,128]{2,1,0:T(8,128)(2,1)S(1)}, u32[]{:S(2)}, u32[]{:S(2)}) %collective-permute-start.9) | collective-permute-done | bytes 131104 | tf_op jit(solution)/shard_map/ppermute | solution.py:240
  65.3 2.5 %collective-permute-done.10.refs_1_ = bf16[16,32,128]{2,1,0:T(8,128)(2,1)S(1)} collective-permute-done((bf16[16,32,128]{2,1,0:T(8,128)(2,1)S(1)}, bf16[16,32,128]{2,1,0:T(8,128)(2,1)S(1)}, u32[]{:S(2)}, u32[]{:S(2)}) %collective-permute-start.10) | collective-permute-done | bytes 131104 | tf_op jit(solution)/shard_map/ppermute | solution.py:240
  67.8 0.7 %shard_map.116 = bf16[128,32,128]{2,1,0:T(8,128)(2,1)} custom-call(s32[1]{0:T(128)} %bitcast.me_ref, bf16[16,32,128]{2,1,0:T(8,128)(2,1)S(1)} %collective-permute-done.9.refs_0_, bf16[16,32,128]{2,1,0:T(8,128)(2,1)S(1)} %collective-permute-done.10.refs_1_, bf16[128,32,128]{2,1,0:T(8,128)(2,1)} %shard_map.115.refs_2_), custom_call_target="tpu_custom_call", output_to_operand_aliasing={{}: (3, {})} | custom-call | bytes 3690000 | tf_op jit(solution)/shard_map/pallas_call | solution.py:353
  (7 shorter events, 0.0 us)
Async XLA Ops:
  0.0 0.7 copy-start.7
  0.7 0.7 copy-start.9
  1.4 0.7 copy-start.13
  2.0 0.7 copy-start.14
  2.7 0.7 copy-start.15
  3.4 0.7 copy-start.16
  4.0 12.6 %copy-start.5 = (bf16[128,512]{1,0:T(8,128)(2,1)S(1)}, bf16[128,512]{1,0:T(8,128)(2,1)}, u32[]{:S(2)}) copy-start(bf16[128,512]{1,0:T(8,128)(2,1)} %refs_9_.7) | copy-start | bytes 393220
  9.5 14.0 %copy-start.6 = (bf16[128,128]{1,0:T(8,128)(2,1)S(1)}, bf16[128,128]{1,0:T(8,128)(2,1)}, u32[]{:S(2)}) copy-start(bf16[128,128]{1,0:T(8,128)(2,1)} %refs_11_.7) | copy-start | bytes 98308
  9.5 14.0 %copy-start.8 = (s32[512]{0:T(512)S(1)}, s32[512]{0:T(512)}, u32[]{:S(2)}) copy-start(s32[512]{0:T(512)} %param.13) | copy-start | bytes 6148
  9.6 14.0 %copy-start.10 = (s32[512]{0:T(512)S(1)}, s32[512]{0:T(512)}, u32[]{:S(2)}) copy-start(s32[512]{0:T(512)} %param.14) | copy-start | bytes 6148
  9.6 13.9 %copy-start.11 = (f32[4]{0:T(128)S(1)}, f32[4]{0:T(128)}, u32[]{:S(2)}) copy-start(f32[4]{0:T(128)} %chain_bias_ref.7) | copy-start | bytes 52
  9.6 13.9 %copy-start.12 = (f32[128]{0:T(128)S(1)}, f32[128]{0:T(128)}, u32[]{:S(2)}) copy-start(f32[128]{0:T(128)} %param.18) | copy-start | bytes 1540
  9.6 7.1 %collective-permute-start.2 = (bf16[8,512,128]{2,1,0:T(8,128)(2,1)S(1)}, bf16[8,512,128]{2,1,0:T(8,128)(2,1)S(1)}, u32[]{:S(2)}, u32[]{:S(2)}) collective-permute-start(bf16[8,512,128]{2,1,0:T(8,128)(2,1)S(1)} %get-tuple-element.22.own_ref), channel_id=1, source_target_pairs={{0,1},{1,0},{2,3},{3,2},{4,5},{5,4},{6,7},{7,6},{8,9},{9,8},{10,11... | collective-permute-start | bytes 3145736 | tf_op jit(solution)/shard_map/ppermute | solution.py:240
  10.1 11.5 %collective-permute-start.3 = (bf16[128,384]{1,0:T(8,128)(2,1)S(1)}, bf16[128,384]{1,0:T(8,128)(2,1)S(1)}, u32[]{:S(2)}, u32[]{:S(2)}) collective-permute-start(bf16[128,384]{1,0:T(8,128)(2,1)S(1)} %get-tuple-element.21.refs_0_), channel_id=1, source_target_pairs={{0,8},{1,9},{2,10},{3,11},{4,12},{5,13},{6,14},{7,15},{8,0},{9,1},... | collective-permute-start | bytes 294920 | tf_op jit(solution)/shard_map/ppermute | solution.py:240
  13.8 7.9 %collective-permute-start.4 = (bf16[128,384]{1,0:T(8,128)(2,1)S(1)}, bf16[128,384]{1,0:T(8,128)(2,1)S(1)}, u32[]{:S(2)}, u32[]{:S(2)}) collective-permute-start(bf16[128,384]{1,0:T(8,128)(2,1)S(1)} %get-tuple-element.21.refs_0_), channel_id=1, source_target_pairs={{0,12},{1,13},{2,14},{3,15},{4,8},{5,9},{6,10},{7,11},{8,4},{9,5},... | collective-permute-start | bytes 294920 | tf_op jit(solution)/shard_map/ppermute | solution.py:240
  15.1 20.4 %collective-permute-start.6 = (bf16[128,384]{1,0:T(8,128)(2,1)S(1)}, bf16[128,384]{1,0:T(8,128)(2,1)S(1)}, u32[]{:S(2)}, u32[]{:S(2)}) collective-permute-start(bf16[128,384]{1,0:T(8,128)(2,1)S(1)} %get-tuple-element.21.refs_0_), channel_id=1, source_target_pairs={{0,2},{1,3},{2,0},{3,1},{4,6},{5,7},{6,4},{7,5},{8,10},{9,11},{10,... | collective-permute-start | bytes 294920 | tf_op jit(solution)/shard_map/ppermute | solution.py:240
  18.9 1.2 %copy-start = (bf16[16,128,384]{2,1,0:T(8,128)(2,1)}, bf16[16,128,384]{2,1,0:T(8,128)(2,1)S(1)}, u32[]{:S(2)}) copy-start(bf16[16,128,384]{2,1,0:T(8,128)(2,1)S(1)} %get-tuple-element.24.refs_4_) | copy-start | bytes 4718596
  20.1 1.1 %copy-start.3 = (bf16[16,384,128]{2,1,0:T(8,128)(2,1)}, bf16[16,384,128]{2,1,0:T(8,128)(2,1)S(1)}, u32[]{:S(2)}) copy-start(bf16[16,384,128]{2,1,0:T(8,128)(2,1)S(1)} %get-tuple-element.25.refs_5_) | copy-start | bytes 4718596
  21.7 25.2 %collective-permute-start.5 = (bf16[256,384]{1,0:T(8,128)(2,1)S(1)}, bf16[256,384]{1,0:T(8,128)(2,1)S(1)}, u32[]{:S(2)}, u32[]{:S(2)}) collective-permute-start(bf16[256,384]{1,0:T(8,128)(2,1)S(1)} %pad_maximum_fusion), channel_id=1, source_target_pairs={{0,2},{1,3},{2,0},{3,1},{4,6},{5,7},{6,4},{7,5},{8,10},{9,11},{10,... | collective-permute-start | bytes 589832 | tf_op jit(solution)/shard_map/ppermute | solution.py:240
  23.5 1.4 %copy-start.1 = (bf16[16,128,384]{2,1,0:T(8,128)(2,1)S(1)}, bf16[16,128,384]{2,1,0:T(8,128)(2,1)}, u32[]{:S(2)}) copy-start(bf16[16,128,384]{2,1,0:T(8,128)(2,1)} %copy-done) | copy-start | bytes 4718596
  24.9 1.4 %copy-start.4 = (bf16[16,384,128]{2,1,0:T(8,128)(2,1)S(1)}, bf16[16,384,128]{2,1,0:T(8,128)(2,1)}, u32[]{:S(2)}) copy-start(bf16[16,384,128]{2,1,0:T(8,128)(2,1)} %copy-done.3) | copy-start | bytes 4718596
  26.3 10.9 %copy-start.2 = (bf16[16,128,384]{2,1,0:T(8,128)(2,1)S(1)}, bf16[16,128,384]{2,1,0:T(8,128)(2,1)}, u32[]{:S(2)}) copy-start(bf16[16,128,384]{2,1,0:T(8,128)(2,1)} %copy-done) | copy-start | bytes 4718596
  30.5 24.1 %collective-permute-start.7 = (bf16[16,32,128]{2,1,0:T(8,128)(2,1)S(1)}, bf16[16,32,128]{2,1,0:T(8,128)(2,1)S(1)}, u32[]{:S(2)}, u32[]{:S(2)}) collective-permute-start(bf16[16,32,128]{2,1,0:T(8,128)(2,1)S(1)} %get-tuple-element.29.refs_12_), channel_id=1, source_target_pairs={{0,8},{1,9},{2,10},{3,11},{4,12},{5,13},{6,14},{7,15},{8,0},{9,1},... | collective-permute-start | bytes 393224 | tf_op jit(solution)/shard_map/ppermute | solution.py:240
  34.9 19.8 %collective-permute-start.8 = (bf16[16,32,128]{2,1,0:T(8,128)(2,1)S(1)}, bf16[16,32,128]{2,1,0:T(8,128)(2,1)S(1)}, u32[]{:S(2)}, u32[]{:S(2)}) collective-permute-start(bf16[16,32,128]{2,1,0:T(8,128)(2,1)S(1)} %get-tuple-element.32), channel_id=1, source_target_pairs={{0,12},{1,13},{2,14},{3,15},{4,8},{5,9},{6,10},{7,11},{8,4},{9,5},... | collective-permute-start | bytes 393224 | tf_op jit(solution)/shard_map/ppermute | solution.py:240
  35.3 10.3 %collective-permute-start = (bf16[128,384]{1,0:T(8,128)(2,1)S(1)}, bf16[128,384]{1,0:T(8,128)(2,1)S(1)}, u32[]{:S(2)}, u32[]{:S(2)}) collective-permute-start(bf16[128,384]{1,0:T(8,128)(2,1)S(1)} %get-tuple-element.21.refs_0_), channel_id=1, source_target_pairs={{0,4},{1,5},{2,6},{3,7},{4,0},{5,1},{6,2},{7,3},{8,12},{9,13},{10,... | collective-permute-start | bytes 294920 | tf_op jit(solution)/shard_map/ppermute | solution.py:240
  35.5 11.3 %collective-permute-start.1 = (bf16[128,384]{1,0:T(8,128)(2,1)S(1)}, bf16[128,384]{1,0:T(8,128)(2,1)S(1)}, u32[]{:S(2)}, u32[]{:S(2)}) collective-permute-start(bf16[128,384]{1,0:T(8,128)(2,1)S(1)} %get-tuple-element.21.refs_0_), channel_id=1, source_target_pairs={{0,6},{1,7},{2,4},{3,5},{4,2},{5,3},{6,0},{7,1},{8,14},{9,15},{10,... | collective-permute-start | bytes 294920 | tf_op jit(solution)/shard_map/ppermute | solution.py:240
  45.6 16.2 %collective-permute-start.11 = (bf16[16,32,128]{2,1,0:T(8,128)(2,1)S(1)}, bf16[16,32,128]{2,1,0:T(8,128)(2,1)S(1)}, u32[]{:S(2)}, u32[]{:S(2)}) collective-permute-start(bf16[16,32,128]{2,1,0:T(8,128)(2,1)S(1)} %get-tuple-element.35), channel_id=1, source_target_pairs={{0,2},{1,3},{2,0},{3,1},{4,6},{5,7},{6,4},{7,5},{8,10},{9,11},{10,... | collective-permute-start | bytes 393224 | tf_op jit(solution)/shard_map/ppermute | solution.py:240
  51.0 11.3 %collective-permute-start.12 = (bf16[16,32,128]{2,1,0:T(8,128)(2,1)S(1)}, bf16[16,32,128]{2,1,0:T(8,128)(2,1)S(1)}, u32[]{:S(2)}, u32[]{:S(2)}) collective-permute-start(bf16[16,32,128]{2,1,0:T(8,128)(2,1)S(1)} %get-tuple-element.31.refs_12_), channel_id=1, source_target_pairs={{0,10},{1,11},{2,8},{3,9},{4,14},{5,15},{6,12},{7,13},{8,2},{9,3},... | collective-permute-start | bytes 393224 | tf_op jit(solution)/shard_map/ppermute | solution.py:240
  51.6 10.7 %collective-permute-start.13 = (bf16[16,32,128]{2,1,0:T(8,128)(2,1)S(1)}, bf16[16,32,128]{2,1,0:T(8,128)(2,1)S(1)}, u32[]{:S(2)}, u32[]{:S(2)}) collective-permute-start(bf16[16,32,128]{2,1,0:T(8,128)(2,1)S(1)} %get-tuple-element.36), channel_id=1, source_target_pairs={{0,14},{1,15},{2,12},{3,13},{4,10},{5,11},{6,8},{7,9},{8,6},{9,7},... | collective-permute-start | bytes 393224 | tf_op jit(solution)/shard_map/ppermute | solution.py:240
  58.8 6.5 %collective-permute-start.9 = (bf16[16,32,128]{2,1,0:T(8,128)(2,1)S(1)}, bf16[16,32,128]{2,1,0:T(8,128)(2,1)S(1)}, u32[]{:S(2)}, u32[]{:S(2)}) collective-permute-start(bf16[16,32,128]{2,1,0:T(8,128)(2,1)S(1)} %get-tuple-element.33), channel_id=1, source_target_pairs={{0,4},{1,5},{2,6},{3,7},{4,0},{5,1},{6,2},{7,3},{8,12},{9,13},{10,... | collective-permute-start | bytes 393224 | tf_op jit(solution)/shard_map/ppermute | solution.py:240
  59.7 8.1 %collective-permute-start.10 = (bf16[16,32,128]{2,1,0:T(8,128)(2,1)S(1)}, bf16[16,32,128]{2,1,0:T(8,128)(2,1)S(1)}, u32[]{:S(2)}, u32[]{:S(2)}) collective-permute-start(bf16[16,32,128]{2,1,0:T(8,128)(2,1)S(1)} %get-tuple-element.34), channel_id=1, source_target_pairs={{0,6},{1,7},{2,4},{3,5},{4,2},{5,3},{6,0},{7,1},{8,14},{9,15},{10,... | collective-permute-start | bytes 393224 | tf_op jit(solution)/shard_map/ppermute | solution.py:240

commit v6 on v5

--- a/solution.py
+++ b/solution.py
@@ -63,6 +63,8 @@
     chain_live_ref,
     acc,
     normed,
+    rows_s,
+    rows_sem,
 ):
     step = pl.program_id(0)
     rows, tokens, channels = pair_ref.shape
@@ -87,6 +89,7 @@
 
     @pl.when(step == 0)
     def _():
+        pltpu.make_async_copy(rows_ref, rows_s, rows_sem).start()
         acc[...] = part
         pick = picking(mask_ref[...], live)
         pick_ref[...] = pick
@@ -102,11 +105,13 @@
         full = acc[...].astype(BF16)
         taken = jnp.dot(pick_ref[...], full, preferred_element_type=F32)
         out_ref[...] = taken.T.astype(BF16)
+        pltpu.make_async_copy(rows_ref, rows_s, rows_sem).wait()
         for i in range(window_ref.shape[0]):
-            window_ref[i] = normed[lax.rem(rows_ref[i], held)]
-
-
-def key_value_kernel(own_ref, other_ref, pick_ref, w_ref, k_ref, v_ref):
+            window_ref[i] = normed[lax.rem(rows_s[i], held)]
+
+
+def key_value_kernel(own_ref, other_ref, pick_ref, w_ref, after_ref, k_ref, v_ref, done_ref):
+    done_ref[...] = jnp.zeros_like(done_ref)
     count = own_ref.shape[0]
     live, inner = v_ref.shape[1:]
     for i in range(count):
@@ -250,7 +255,7 @@
             jax.ShapeDtypeStruct((8, live), F32),
         ],
         in_specs=[
-            SMEM,
+            ANY,
             pl.BlockSpec((step_rows, tokens, channels), lambda i: (i, 0, 0)),
             pl.BlockSpec((1, tokens), lambda i: (0, 0)),
             pl.BlockSpec((1, tokens), lambda i: (0, 0)),
@@ -267,10 +272,17 @@
         scratch_shapes=[
             pltpu.VMEM((tokens, heads * rows_held), F32),
             pltpu.VMEM((rows_held, tokens, channels), BF16),
+            pltpu.SMEM((count,), jnp.int32),
+            pltpu.SemaphoreType.DMA(()),
         ],
         compiler_params=PARAMS,
         cost_estimate=measured(6),
-    )(window_rows, pltpu.with_memory_space_constraint(pair, pltpu.HBM), mask_row, chain_row, gain, shift, w_bias.T)
+    )(
+        *[
+            pltpu.with_memory_space_constraint(x, pltpu.HBM)
+            for x in (window_rows, pair, mask_row, chain_row, gain, shift, w_bias.T)
+        ]
+    )
 
     far = [m for m in range(owners // 2, owners) if m % 2 == 0]
     passed = [m + 1 for m in far]
@@ -280,35 +292,34 @@
         biases[m] = swap(bias, 2 * m)
     other = swap(own, 1)
 
-    keys, values = pl.pallas_call(
+    keys, values, done = pl.pallas_call(
         key_value_kernel,
         out_shape=[
             jax.ShapeDtypeStruct((2 * count, inner, live), BF16),
             jax.ShapeDtypeStruct((2 * count, live, inner), BF16),
-        ],
-        in_specs=[VMEM] * 4,
-        out_specs=[VMEM] * 2,
+            jax.ShapeDtypeStruct((8, channels), F32),
+        ],
+        in_specs=[VMEM] * 4 + [ANY],
+        out_specs=[VMEM] * 3,
         compiler_params=PARAMS,
         cost_estimate=measured(2),
-    )(own, other, pick, w_project)
+    )(own, other, pick, w_project, biases[near[0]])
 
     split = (count, owners, 2, rows_held, channels)
     own, other = own.reshape(split), other.reshape(split)
     updates = {}
-    *straight, _ = lax.optimization_barrier((*[biases[m] for m in far], keys))
-    straight = swap(jnp.concatenate(straight), 2)
+    straight = jnp.concatenate([biases[m] for m in far]) + done[:1, :1].astype(BF16)
+    straight = swap(straight, 2)
     for m in passed:
         biases[m] = straight
     sent = {}
     for ms in (far, [0] + near[:1], passed, near[1:]):
         if ms == far:
-            after = []
+            after = [biases[near[1]]]
         elif ms == near[1:]:
             after = [updates[passed[0]]] + [sent[m] for m in far]
         else:
             after = [updates[far[0] if 0 in ms else 0]]
-            if ms == passed:
-                after += [biases[m] for m in near[1:]]
         blocks = len(ms)
         first = [i * heads * rows_held if ms == passed else 0 for i in range(blocks)]
         rows = 2 * count * rows_held

time: 68.7 us -> 61.5 us (0.90)
  local copies, waits for them, and re-layouts: 9.16 us -> 5.69 us
  starting transfers between devices: 22.9 us -> 20.5 us
  waiting for transfers between devices: 10.2 us -> 8.19 us
    unnamed x34 -> x22, local copies, waits for them, and re-layouts: 9.16 us -> 5.18 us
    ppermute x14, starting transfers between devices: 22.9 us -> 20.5 us  [swap(): return lax.ppermute(x, 'row', [(i, i ^ bits) for i in range(devices)])]
    ppermute x14, waiting for transfers between devices: 10.2 us -> 8.19 us  [swap(): return lax.ppermute(x, 'row', [(i, i ^ bits) for i in range(devices)])]
  transfers between devices with their start and end apart: 14 -> 14, of which waited for: 6 -> 4; matrix products, arithmetic and copies ran while one was open for 0% -> 2% of each run, Pallas kernels for 29% -> 32%
where the time goes in v6:
time: 61.5 us; the launch traced here: 61.3 us
  Pallas kernels  26.1 us (42%)
  starting transfers between devices  20.5 us (33%)
  waiting for transfers between devices  8.19 us (13%)
  local copies, waits for them, and re-layouts  5.69 us (9%)
  other arithmetic  0.69 us (1%)
    ppermute x14, starting transfers between devices, swap(): return lax.ppermute(x, 'row', [(i, i ^ bits) for i in range(devices)])  20.5 us
    pallas_call x4, Pallas kernels, local(): pl.pallas_call(functools.partial(attention_kernel, heads, ms, first), out...  16.6 us
    ppermute x14, waiting for transfers between devices, swap(): return lax.ppermute(x, 'row', [(i, i ^ bits) for i in range(devices)])  8.19 us
    pallas_call x1, Pallas kernels, local(): pl.pallas_call(bias_kernel, grid=(rows_held // step_rows,), out_shape=[ja...  5.57 us
    unnamed x22, local copies, waits for them, and re-layouts  5.18 us
    pallas_call x1, Pallas kernels, local(): pl.pallas_call(key_value_kernel, out_shape=[jax.ShapeDtypeStruct((2 * cou...  2.29 us
    pallas_call x2, Pallas kernels, local(): pl.pallas_call(functools.partial(gather_kernel, order), out_shape=jax.Sha...  1.63 us
  transfers between devices with their start and end apart: 14, of which 4 were waited for; matrix products, arithmetic and copies ran while one was open for 2% of the time, Pallas kernels for 32%

profile of v6, /device:TPU:0, one launch (start us, length us, event | category | flops | bytes accessed | tf_op | source)
XLA Modules:
  0.0 61.3 jit_solution(14263305237817375961)
XLA Ops:
  0.0 0.0 copy-start.5
  0.0 5.6 %shard_map.109 = (bf16[128,384]{1,0:T(8,128)(2,1)S(1)}, bf16[8,512,128]{2,1,0:T(8,128)(2,1)S(1)}, bf16[384,512]{1,0:T(8,128)(2,1)S(1)}, f32[8,384]{1,0:T(8,128)S(1)}) custom-call(s32[8]{0:T(128)} %rows_ref.1, bf16[32,512,128]{2,1,0:T(8,128)(2,1)} %pair_ref.1, s32[1,512]{1,0:T(1,128)} %bitcast.18, s32[1,512]{1,0:T(1,128)} %bitcast.23, f32[1,128]{1,0:T(1,128)} %bitcast.33, ...), custom_call_target="tpu_custom_call" | custom-call | bytes 22140000 | tf_op jit(solution)/shard_map/pallas_call | solution.py:248
  5.6 0.5 collective-permute-start.2
  6.1 2.6 %collective-permute-start.3 = (bf16[128,384]{1,0:T(8,128)(2,1)S(1)}, bf16[128,384]{1,0:T(8,128)(2,1)S(1)}, u32[]{:S(2)}, u32[]{:S(2)}) collective-permute-start(bf16[128,384]{1,0:T(8,128)(2,1)S(1)} %get-tuple-element.20.refs_0_), channel_id=1, source_target_pairs={{0,2},{1,3},{2,0},{3,1},{4,6},{5,7},{6,4},{7,5},{8,10},{9,11},{10,... | collective-permute-start | bytes 294920 | tf_op jit(solution)/shard_map/ppermute | solution.py:245
  8.7 3.6 %collective-permute-start.5 = (bf16[128,384]{1,0:T(8,128)(2,1)S(1)}, bf16[128,384]{1,0:T(8,128)(2,1)S(1)}, u32[]{:S(2)}, u32[]{:S(2)}) collective-permute-start(bf16[128,384]{1,0:T(8,128)(2,1)S(1)} %get-tuple-element.20.refs_0_), channel_id=1, source_target_pairs={{0,12},{1,13},{2,14},{3,15},{4,8},{5,9},{6,10},{7,11},{8,4},{9,5},... | collective-permute-start | bytes 294920 | tf_op jit(solution)/shard_map/ppermute | solution.py:245
  12.3 0.0 collective-permute-start.4
  12.3 0.8 %collective-permute-start = (bf16[128,384]{1,0:T(8,128)(2,1)S(1)}, bf16[128,384]{1,0:T(8,128)(2,1)S(1)}, u32[]{:S(2)}, u32[]{:S(2)}) collective-permute-start(bf16[128,384]{1,0:T(8,128)(2,1)S(1)} %get-tuple-element.20.refs_0_), channel_id=1, source_target_pairs={{0,4},{1,5},{2,6},{3,7},{4,0},{5,1},{6,2},{7,3},{8,12},{9,13},{10,... | collective-permute-start | bytes 294920 | tf_op jit(solution)/shard_map/ppermute | solution.py:245
  13.1 0.0 collective-permute-done.3.after_ref.refs_1_
  13.1 0.0 collective-permute-done.2.other_ref
  13.1 0.0 copy-done.5
  13.1 0.0 copy-start.6
  13.1 0.0 copy-start.7
  13.1 0.0 copy-start.8
  13.1 0.0 copy-start.9
  13.1 0.0 copy-start.10
  13.2 2.3 %shard_map.110 = (bf16[16,128,384]{2,1,0:T(8,128)(2,1)S(1)}, bf16[16,384,128]{2,1,0:T(8,128)(2,1)S(1)}, f32[8,128]{1,0:T(8,128)S(1)}) custom-call(bf16[8,512,128]{2,1,0:T(8,128)(2,1)S(1)} %get-tuple-element.21.own_ref, bf16[8,512,128]{2,1,0:T(8,128)(2,1)S(1)} %collective-permute-done.2.other_ref, bf16[384,512]{1,0:T(8,128)(2,1)S(1)} %get-tuple-element.22.pick_ref, ...), custom_call_target="tpu_custom_call" | custom-call | bytes 7380000 | tf_op jit(solution)/shard_map/pallas_call | solution.py:295
  15.4 0.0 copy-start
  15.5 1.2 %copy-done = bf16[16,128,384]{2,1,0:T(8,128)(2,1)} copy-done((bf16[16,128,384]{2,1,0:T(8,128)(2,1)}, bf16[16,128,384]{2,1,0:T(8,128)(2,1)S(1)}, u32[]{:S(2)}) %copy-start) | copy-done | bytes 1572888
  16.6 0.0 copy-start.3
  16.6 1.1 %copy-done.3 = bf16[16,384,128]{2,1,0:T(8,128)(2,1)} copy-done((bf16[16,384,128]{2,1,0:T(8,128)(2,1)}, bf16[16,384,128]{2,1,0:T(8,128)(2,1)S(1)}, u32[]{:S(2)}) %copy-start.3) | copy-done | bytes 1572888
  17.8 0.5 slice.4
  18.3 0.0 collective-permute-done.5.refs_1_
  18.3 2.6 %collective-permute-done.4.refs_0_ = bf16[128,384]{1,0:T(8,128)(2,1)S(1)} collective-permute-done((bf16[128,384]{1,0:T(8,128)(2,1)S(1)}, bf16[128,384]{1,0:T(8,128)(2,1)S(1)}, u32[]{:S(2)}, u32[]{:S(2)}) %collective-permute-start.4) | collective-permute-done | bytes 98336 | tf_op jit(solution)/shard_map/ppermute | solution.py:245
  20.9 0.7 %maximum_add_fusion = bf16[256,384]{1,0:T(8,128)(2,1)S(1)} fusion(bf16[128,384]{1,0:T(8,128)(2,1)S(1)} %collective-permute-done.5.refs_1_, bf16[128,384]{1,0:T(8,128)(2,1)S(1)} %collective-permute-done.4.refs_0_, bf16[]{:T(256)} %bitcast.9), kind=kLoop, calls=%fused_computation | loop fusion | flops 589824 | bytes 393218 | tf_op jit(solution)/shard_map/add | solution.py:311
  21.6 0.6 collective-permute-start.6
  22.2 0.0 collective-permute-done.refs_12_.refs_0_
  22.2 0.0 copy-done.6
  22.2 0.0 copy-done.7
  22.2 0.0 copy-done.8
  22.2 0.0 copy-done.9
  22.2 0.0 copy-done.10
  22.2 0.0 copy-start.1
  22.2 1.4 %copy-done.1 = bf16[16,128,384]{2,1,0:T(8,128)(2,1)S(1)} copy-done((bf16[16,128,384]{2,1,0:T(8,128)(2,1)S(1)}, bf16[16,128,384]{2,1,0:T(8,128)(2,1)}, u32[]{:S(2)}) %copy-start.1) | copy-done | bytes 1572888
  23.6 0.0 copy-start.4
  23.6 1.4 %copy-done.4 = bf16[16,384,128]{2,1,0:T(8,128)(2,1)S(1)} copy-done((bf16[16,384,128]{2,1,0:T(8,128)(2,1)S(1)}, bf16[16,384,128]{2,1,0:T(8,128)(2,1)}, u32[]{:S(2)}) %copy-start.4) | copy-done | bytes 1572888
  25.0 0.0 copy-start.2
  25.0 4.2 %shard_map.111 = (bf16[16,32,128]{2,1,0:T(8,128)(2,1)S(1)}, bf16[16,32,128]{2,1,0:T(8,128)(2,1)S(1)}) custom-call(s32[1]{0:T(128)} %bitcast.me_ref, f32[4]{0:T(128)S(1)} %copy-done.9, bf16[128,384]{1,0:T(8,128)(2,1)S(1)} %collective-permute-done.4.refs_0_, bf16[128,384]{1,0:T(8,128)(2,1)S(1)} %collective-permute-done.5.refs_1_, ...), custom_call_target="tpu_custom_call" | custom-call | bytes 16236000 | tf_op jit(solution)/shard_map/pallas_call | solution.py:326
  29.2 2.5 %collective-permute-start.8 = (bf16[16,32,128]{2,1,0:T(8,128)(2,1)S(1)}, bf16[16,32,128]{2,1,0:T(8,128)(2,1)S(1)}, u32[]{:S(2)}, u32[]{:S(2)}) collective-permute-start(bf16[16,32,128]{2,1,0:T(8,128)(2,1)S(1)} %get-tuple-element.30), channel_id=1, source_target_pairs={{0,12},{1,13},{2,14},{3,15},{4,8},{5,9},{6,10},{7,11},{8,4},{9,5},... | collective-permute-start | bytes 393224 | tf_op jit(solution)/shard_map/ppermute | solution.py:245
  31.7 0.0 collective-permute-start.7
  31.7 2.9 %collective-permute-start.1 = (bf16[128,384]{1,0:T(8,128)(2,1)S(1)}, bf16[128,384]{1,0:T(8,128)(2,1)S(1)}, u32[]{:S(2)}, u32[]{:S(2)}) collective-permute-start(bf16[128,384]{1,0:T(8,128)(2,1)S(1)} %get-tuple-element.20.refs_0_), channel_id=1, source_target_pairs={{0,6},{1,7},{2,4},{3,5},{4,2},{5,3},{6,0},{7,1},{8,14},{9,15},{10,... | collective-permute-start | bytes 294920 | tf_op jit(solution)/shard_map/ppermute | solution.py:245
  34.6 0.0 copy-done.2
  34.6 4.1 %shard_map.112 = (bf16[16,32,128]{2,1,0:T(8,128)(2,1)S(1)}, bf16[16,32,128]{2,1,0:T(8,128)(2,1)S(1)}) custom-call(s32[1]{0:T(128)} %bitcast.me_ref, f32[4]{0:T(128)S(1)} %copy-done.9, bf16[128,384]{1,0:T(8,128)(2,1)S(1)} %get-tuple-element.20.refs_0_, bf16[128,384]{1,0:T(8,128)(2,1)S(1)} %collective-permute-done.3.after_ref.refs_1_, ...), custom_call_target="tpu_custom_call" | custom-call | bytes 16236000 | tf_op jit(solution)/shard_map/pallas_call | solution.py:326
  38.8 0.6 collective-permute-start.11
  39.3 0.0 collective-permute-done.6.refs_0_.refs_1_
  39.3 4.1 %shard_map.113 = (bf16[16,32,128]{2,1,0:T(8,128)(2,1)S(1)}, bf16[16,32,128]{2,1,0:T(8,128)(2,1)S(1)}) custom-call(s32[1]{0:T(128)} %bitcast.me_ref, f32[4]{0:T(128)S(1)} %copy-done.9, bf16[256,384]{1,0:T(8,128)(2,1)S(1)} %collective-permute-done.6.refs_0_.refs_1_, bf16[256,384]{1,0:T(8,128)(2,1)S(1)} %collective-permute-done.6.refs_0_.refs_1_, ...), custom_call_target="tpu_custom_call" | custom-call | bytes 16236000 | tf_op jit(solution)/shard_map/pallas_call | solution.py:326
  43.5 3.5 %collective-permute-start.13 = (bf16[16,32,128]{2,1,0:T(8,128)(2,1)S(1)}, bf16[16,32,128]{2,1,0:T(8,128)(2,1)S(1)}, u32[]{:S(2)}, u32[]{:S(2)}) collective-permute-start(bf16[16,32,128]{2,1,0:T(8,128)(2,1)S(1)} %get-tuple-element.34), channel_id=1, source_target_pairs={{0,14},{1,15},{2,12},{3,13},{4,10},{5,11},{6,8},{7,9},{8,6},{9,7},... | collective-permute-start | bytes 393224 | tf_op jit(solution)/shard_map/ppermute | solution.py:245
  47.0 0.0 collective-permute-done.1.refs_1_
  47.0 0.0 collective-permute-start.12
  47.0 0.0 collective-permute-done.8.refs_14_.refs_3_
  47.0 0.0 collective-permute-done.7.refs_13_.refs_2_
  47.0 4.1 %shard_map.114 = (bf16[16,32,128]{2,1,0:T(8,128)(2,1)S(1)}, bf16[16,32,128]{2,1,0:T(8,128)(2,1)S(1)}) custom-call(s32[1]{0:T(128)} %bitcast.me_ref, f32[4]{0:T(128)S(1)} %copy-done.9, bf16[128,384]{1,0:T(8,128)(2,1)S(1)} %collective-permute-done.refs_12_.refs_0_, bf16[128,384]{1,0:T(8,128)(2,1)S(1)} %collective-permute-done.1.refs_1_, ...), custom_call_target="tpu_custom_call" | custom-call | bytes 16236000 | tf_op jit(solution)/shard_map/pallas_call | solution.py:326
  51.1 1.9 %collective-permute-start.9 = (bf16[16,32,128]{2,1,0:T(8,128)(2,1)S(1)}, bf16[16,32,128]{2,1,0:T(8,128)(2,1)S(1)}, u32[]{:S(2)}, u32[]{:S(2)}) collective-permute-start(bf16[16,32,128]{2,1,0:T(8,128)(2,1)S(1)} %get-tuple-element.31), channel_id=1, source_target_pairs={{0,4},{1,5},{2,6},{3,7},{4,0},{5,1},{6,2},{7,3},{8,12},{9,13},{10,... | collective-permute-start | bytes 393224 | tf_op jit(solution)/shard_map/ppermute | solution.py:245
  53.1 1.0 %collective-permute-start.10 = (bf16[16,32,128]{2,1,0:T(8,128)(2,1)S(1)}, bf16[16,32,128]{2,1,0:T(8,128)(2,1)S(1)}, u32[]{:S(2)}, u32[]{:S(2)}) collective-permute-start(bf16[16,32,128]{2,1,0:T(8,128)(2,1)S(1)} %get-tuple-element.32), channel_id=1, source_target_pairs={{0,6},{1,7},{2,4},{3,5},{4,2},{5,3},{6,0},{7,1},{8,14},{9,15},{10,... | collective-permute-start | bytes 393224 | tf_op jit(solution)/shard_map/ppermute | solution.py:245
  54.1 0.0 collective-permute-done.11.refs_1_
  54.1 0.0 collective-permute-done.13.refs_5_
  54.1 2.6 %collective-permute-done.12.refs_4_ = bf16[16,32,128]{2,1,0:T(8,128)(2,1)S(1)} collective-permute-done((bf16[16,32,128]{2,1,0:T(8,128)(2,1)S(1)}, bf16[16,32,128]{2,1,0:T(8,128)(2,1)S(1)}, u32[]{:S(2)}, u32[]{:S(2)}) %collective-permute-start.12) | collective-permute-done | bytes 131104 | tf_op jit(solution)/shard_map/ppermute | solution.py:245
  56.7 0.9 %shard_map.115.refs_2_ = bf16[128,32,128]{2,1,0:T(8,128)(2,1)} custom-call(s32[1]{0:T(128)} %bitcast.me_ref, bf16[16,32,128]{2,1,0:T(8,128)(2,1)S(1)} %get-tuple-element.28.refs_12_.refs_0_, bf16[16,32,128]{2,1,0:T(8,128)(2,1)S(1)} %collective-permute-done.11.refs_1_, bf16[16,32,128]{2,1,0:T(8,128)(2,1)S(1)} %collective-permute-done.7.refs_13_.refs_2_, ...), custom_call_target="tpu_custom_call" | custom-call | bytes 3690000 | tf_op jit(solution)/shard_map/pallas_call | solution.py:364
  57.6 1.1 %collective-permute-done.9.refs_0_ = bf16[16,32,128]{2,1,0:T(8,128)(2,1)S(1)} collective-permute-done((bf16[16,32,128]{2,1,0:T(8,128)(2,1)S(1)}, bf16[16,32,128]{2,1,0:T(8,128)(2,1)S(1)}, u32[]{:S(2)}, u32[]{:S(2)}) %collective-permute-start.9) | collective-permute-done | bytes 131104 | tf_op jit(solution)/shard_map/ppermute | solution.py:245
  58.7 1.9 %collective-permute-done.10.refs_1_ = bf16[16,32,128]{2,1,0:T(8,128)(2,1)S(1)} collective-permute-done((bf16[16,32,128]{2,1,0:T(8,128)(2,1)S(1)}, bf16[16,32,128]{2,1,0:T(8,128)(2,1)S(1)}, u32[]{:S(2)}, u32[]{:S(2)}) %collective-permute-start.10) | collective-permute-done | bytes 131104 | tf_op jit(solution)/shard_map/ppermute | solution.py:245
  60.6 0.7 %shard_map.116 = bf16[128,32,128]{2,1,0:T(8,128)(2,1)} custom-call(s32[1]{0:T(128)} %bitcast.me_ref, bf16[16,32,128]{2,1,0:T(8,128)(2,1)S(1)} %collective-permute-done.9.refs_0_, bf16[16,32,128]{2,1,0:T(8,128)(2,1)S(1)} %collective-permute-done.10.refs_1_, bf16[128,32,128]{2,1,0:T(8,128)(2,1)} %shard_map.115.refs_2_), custom_call_target="tpu_custom_call", output_to_operand_aliasing={{}: (3, {})} | custom-call | bytes 3690000 | tf_op jit(solution)/shard_map/pallas_call | solution.py:364
  (1 shorter events, 0.0 us)
Async XLA Ops:
  0.0 13.1 %copy-start.5 = (bf16[128,512]{1,0:T(8,128)(2,1)S(1)}, bf16[128,512]{1,0:T(8,128)(2,1)}, u32[]{:S(2)}) copy-start(bf16[128,512]{1,0:T(8,128)(2,1)} %refs_9_.7) | copy-start | bytes 393220
  5.6 7.5 %collective-permute-start.2 = (bf16[8,512,128]{2,1,0:T(8,128)(2,1)S(1)}, bf16[8,512,128]{2,1,0:T(8,128)(2,1)S(1)}, u32[]{:S(2)}, u32[]{:S(2)}) collective-permute-start(bf16[8,512,128]{2,1,0:T(8,128)(2,1)S(1)} %get-tuple-element.21.own_ref), channel_id=1, source_target_pairs={{0,1},{1,0},{2,3},{3,2},{4,5},{5,4},{6,7},{7,6},{8,9},{9,8},{10,11... | collective-permute-start | bytes 3145736 | tf_op jit(solution)/shard_map/ppermute | solution.py:245
  6.1 7.0 %collective-permute-start.3 = (bf16[128,384]{1,0:T(8,128)(2,1)S(1)}, bf16[128,384]{1,0:T(8,128)(2,1)S(1)}, u32[]{:S(2)}, u32[]{:S(2)}) collective-permute-start(bf16[128,384]{1,0:T(8,128)(2,1)S(1)} %get-tuple-element.20.refs_0_), channel_id=1, source_target_pairs={{0,2},{1,3},{2,0},{3,1},{4,6},{5,7},{6,4},{7,5},{8,10},{9,11},{10,... | collective-permute-start | bytes 294920 | tf_op jit(solution)/shard_map/ppermute | solution.py:245
  8.7 9.6 %collective-permute-start.5 = (bf16[128,384]{1,0:T(8,128)(2,1)S(1)}, bf16[128,384]{1,0:T(8,128)(2,1)S(1)}, u32[]{:S(2)}, u32[]{:S(2)}) collective-permute-start(bf16[128,384]{1,0:T(8,128)(2,1)S(1)} %get-tuple-element.20.refs_0_), channel_id=1, source_target_pairs={{0,12},{1,13},{2,14},{3,15},{4,8},{5,9},{6,10},{7,11},{8,4},{9,5},... | collective-permute-start | bytes 294920 | tf_op jit(solution)/shard_map/ppermute | solution.py:245
  12.3 8.6 %collective-permute-start.4 = (bf16[128,384]{1,0:T(8,128)(2,1)S(1)}, bf16[128,384]{1,0:T(8,128)(2,1)S(1)}, u32[]{:S(2)}, u32[]{:S(2)}) collective-permute-start(bf16[128,384]{1,0:T(8,128)(2,1)S(1)} %get-tuple-element.20.refs_0_), channel_id=1, source_target_pairs={{0,8},{1,9},{2,10},{3,11},{4,12},{5,13},{6,14},{7,15},{8,0},{9,1},... | collective-permute-start | bytes 294920 | tf_op jit(solution)/shard_map/ppermute | solution.py:245
  12.3 9.9 %collective-permute-start = (bf16[128,384]{1,0:T(8,128)(2,1)S(1)}, bf16[128,384]{1,0:T(8,128)(2,1)S(1)}, u32[]{:S(2)}, u32[]{:S(2)}) collective-permute-start(bf16[128,384]{1,0:T(8,128)(2,1)S(1)} %get-tuple-element.20.refs_0_), channel_id=1, source_target_pairs={{0,4},{1,5},{2,6},{3,7},{4,0},{5,1},{6,2},{7,3},{8,12},{9,13},{10,... | collective-permute-start | bytes 294920 | tf_op jit(solution)/shard_map/ppermute | solution.py:245
  13.1 9.1 %copy-start.6 = (bf16[128,128]{1,0:T(8,128)(2,1)S(1)}, bf16[128,128]{1,0:T(8,128)(2,1)}, u32[]{:S(2)}) copy-start(bf16[128,128]{1,0:T(8,128)(2,1)} %refs_11_.7) | copy-start | bytes 98308
  13.1 9.1 %copy-start.7 = (s32[512]{0:T(512)S(1)}, s32[512]{0:T(512)}, u32[]{:S(2)}) copy-start(s32[512]{0:T(512)} %param.13) | copy-start | bytes 6148
  13.1 9.0 %copy-start.8 = (s32[512]{0:T(512)S(1)}, s32[512]{0:T(512)}, u32[]{:S(2)}) copy-start(s32[512]{0:T(512)} %param.14) | copy-start | bytes 6148
  13.1 9.0 %copy-start.9 = (f32[4]{0:T(128)S(1)}, f32[4]{0:T(128)}, u32[]{:S(2)}) copy-start(f32[4]{0:T(128)} %chain_bias_ref.7) | copy-start | bytes 52
  13.1 9.0 %copy-start.10 = (f32[128]{0:T(128)S(1)}, f32[128]{0:T(128)}, u32[]{:S(2)}) copy-start(f32[128]{0:T(128)} %param.18) | copy-start | bytes 1540
  15.4 1.2 %copy-start = (bf16[16,128,384]{2,1,0:T(8,128)(2,1)}, bf16[16,128,384]{2,1,0:T(8,128)(2,1)S(1)}, u32[]{:S(2)}) copy-start(bf16[16,128,384]{2,1,0:T(8,128)(2,1)S(1)} %get-tuple-element.23.refs_4_) | copy-start | bytes 4718596
  16.6 1.1 %copy-start.3 = (bf16[16,384,128]{2,1,0:T(8,128)(2,1)}, bf16[16,384,128]{2,1,0:T(8,128)(2,1)S(1)}, u32[]{:S(2)}) copy-start(bf16[16,384,128]{2,1,0:T(8,128)(2,1)S(1)} %get-tuple-element.24.refs_5_) | copy-start | bytes 4718596
  21.6 17.7 %collective-permute-start.6 = (bf16[256,384]{1,0:T(8,128)(2,1)S(1)}, bf16[256,384]{1,0:T(8,128)(2,1)S(1)}, u32[]{:S(2)}, u32[]{:S(2)}) collective-permute-start(bf16[256,384]{1,0:T(8,128)(2,1)S(1)} %maximum_add_fusion), channel_id=1, source_target_pairs={{0,2},{1,3},{2,0},{3,1},{4,6},{5,7},{6,4},{7,5},{8,10},{9,11},{10,... | collective-permute-start | bytes 589832 | tf_op jit(solution)/shard_map/ppermute | solution.py:245
  22.2 1.4 %copy-start.1 = (bf16[16,128,384]{2,1,0:T(8,128)(2,1)S(1)}, bf16[16,128,384]{2,1,0:T(8,128)(2,1)}, u32[]{:S(2)}) copy-start(bf16[16,128,384]{2,1,0:T(8,128)(2,1)} %copy-done) | copy-start | bytes 4718596
  23.6 1.4 %copy-start.4 = (bf16[16,384,128]{2,1,0:T(8,128)(2,1)S(1)}, bf16[16,384,128]{2,1,0:T(8,128)(2,1)}, u32[]{:S(2)}) copy-start(bf16[16,384,128]{2,1,0:T(8,128)(2,1)} %copy-done.3) | copy-start | bytes 4718596
  25.0 9.6 %copy-start.2 = (bf16[16,128,384]{2,1,0:T(8,128)(2,1)S(1)}, bf16[16,128,384]{2,1,0:T(8,128)(2,1)}, u32[]{:S(2)}) copy-start(bf16[16,128,384]{2,1,0:T(8,128)(2,1)} %copy-done) | copy-start | bytes 4718596
  29.2 17.8 %collective-permute-start.8 = (bf16[16,32,128]{2,1,0:T(8,128)(2,1)S(1)}, bf16[16,32,128]{2,1,0:T(8,128)(2,1)S(1)}, u32[]{:S(2)}, u32[]{:S(2)}) collective-permute-start(bf16[16,32,128]{2,1,0:T(8,128)(2,1)S(1)} %get-tuple-element.30), channel_id=1, source_target_pairs={{0,12},{1,13},{2,14},{3,15},{4,8},{5,9},{6,10},{7,11},{8,4},{9,5},... | collective-permute-start | bytes 393224 | tf_op jit(solution)/shard_map/ppermute | solution.py:245
  31.7 15.2 %collective-permute-start.7 = (bf16[16,32,128]{2,1,0:T(8,128)(2,1)S(1)}, bf16[16,32,128]{2,1,0:T(8,128)(2,1)S(1)}, u32[]{:S(2)}, u32[]{:S(2)}) collective-permute-start(bf16[16,32,128]{2,1,0:T(8,128)(2,1)S(1)} %get-tuple-element.27.refs_12_), channel_id=1, source_target_pairs={{0,8},{1,9},{2,10},{3,11},{4,12},{5,13},{6,14},{7,15},{8,0},{9,1},... | collective-permute-start | bytes 393224 | tf_op jit(solution)/shard_map/ppermute | solution.py:245
  31.7 15.2 %collective-permute-start.1 = (bf16[128,384]{1,0:T(8,128)(2,1)S(1)}, bf16[128,384]{1,0:T(8,128)(2,1)S(1)}, u32[]{:S(2)}, u32[]{:S(2)}) collective-permute-start(bf16[128,384]{1,0:T(8,128)(2,1)S(1)} %get-tuple-element.20.refs_0_), channel_id=1, source_target_pairs={{0,6},{1,7},{2,4},{3,5},{4,2},{5,3},{6,0},{7,1},{8,14},{9,15},{10,... | collective-permute-start | bytes 294920 | tf_op jit(solution)/shard_map/ppermute | solution.py:245
  38.8 15.3 %collective-permute-start.11 = (bf16[16,32,128]{2,1,0:T(8,128)(2,1)S(1)}, bf16[16,32,128]{2,1,0:T(8,128)(2,1)S(1)}, u32[]{:S(2)}, u32[]{:S(2)}) collective-permute-start(bf16[16,32,128]{2,1,0:T(8,128)(2,1)S(1)} %get-tuple-element.33), channel_id=1, source_target_pairs={{0,2},{1,3},{2,0},{3,1},{4,6},{5,7},{6,4},{7,5},{8,10},{9,11},{10,... | collective-permute-start | bytes 393224 | tf_op jit(solution)/shard_map/ppermute | solution.py:245
  43.5 10.6 %collective-permute-start.13 = (bf16[16,32,128]{2,1,0:T(8,128)(2,1)S(1)}, bf16[16,32,128]{2,1,0:T(8,128)(2,1)S(1)}, u32[]{:S(2)}, u32[]{:S(2)}) collective-permute-start(bf16[16,32,128]{2,1,0:T(8,128)(2,1)S(1)} %get-tuple-element.34), channel_id=1, source_target_pairs={{0,14},{1,15},{2,12},{3,13},{4,10},{5,11},{6,8},{7,9},{8,6},{9,7},... | collective-permute-start | bytes 393224 | tf_op jit(solution)/shard_map/ppermute | solution.py:245
  47.0 9.7 %collective-permute-start.12 = (bf16[16,32,128]{2,1,0:T(8,128)(2,1)S(1)}, bf16[16,32,128]{2,1,0:T(8,128)(2,1)S(1)}, u32[]{:S(2)}, u32[]{:S(2)}) collective-permute-start(bf16[16,32,128]{2,1,0:T(8,128)(2,1)S(1)} %get-tuple-element.29.refs_12_), channel_id=1, source_target_pairs={{0,10},{1,11},{2,8},{3,9},{4,14},{5,15},{6,12},{7,13},{8,2},{9,3},... | collective-permute-start | bytes 393224 | tf_op jit(solution)/shard_map/ppermute | solution.py:245
  51.1 7.6 %collective-permute-start.9 = (bf16[16,32,128]{2,1,0:T(8,128)(2,1)S(1)}, bf16[16,32,128]{2,1,0:T(8,128)(2,1)S(1)}, u32[]{:S(2)}, u32[]{:S(2)}) collective-permute-start(bf16[16,32,128]{2,1,0:T(8,128)(2,1)S(1)} %get-tuple-element.31), channel_id=1, source_target_pairs={{0,4},{1,5},{2,6},{3,7},{4,0},{5,1},{6,2},{7,3},{8,12},{9,13},{10,... | collective-permute-start | bytes 393224 | tf_op jit(solution)/shard_map/ppermute | solution.py:245
  53.1 7.5 %collective-permute-start.10 = (bf16[16,32,128]{2,1,0:T(8,128)(2,1)S(1)}, bf16[16,32,128]{2,1,0:T(8,128)(2,1)S(1)}, u32[]{:S(2)}, u32[]{:S(2)}) collective-permute-start(bf16[16,32,128]{2,1,0:T(8,128)(2,1)S(1)} %get-tuple-element.32), channel_id=1, source_target_pairs={{0,6},{1,7},{2,4},{3,5},{4,2},{5,3},{6,0},{7,1},{8,14},{9,15},{10,... | collective-permute-start | bytes 393224 | tf_op jit(solution)/shard_map/ppermute | solution.py:245

commit v7 on v6

--- a/solution.py
+++ b/solution.py
@@ -110,8 +110,7 @@
             window_ref[i] = normed[lax.rem(rows_s[i], held)]
 
 
-def key_value_kernel(own_ref, other_ref, pick_ref, w_ref, after_ref, k_ref, v_ref, done_ref):
-    done_ref[...] = jnp.zeros_like(done_ref)
+def key_value_kernel(own_ref, other_ref, pick_ref, w_ref, k_ref, v_ref):
     count = own_ref.shape[0]
     live, inner = v_ref.shape[1:]
     for i in range(count):
@@ -202,6 +201,13 @@
         out_refs[b][pl.ds((1 - core) * half, half)] = result[half:]
 
 
+def join_kernel(*refs):
+    parts, out_ref = refs[:-2], refs[-1]
+    rows = parts[0].shape[0]
+    for i, part in enumerate(parts):
+        out_ref[i * rows : (i + 1) * rows, :] = part[...]
+
+
 def gather_kernel(order, me_ref, *refs):
     parts, out_ref, sems = refs[: len(order)], refs[-2], refs[-1]
     count = parts[0].shape[0]
@@ -292,30 +298,36 @@
         biases[m] = swap(bias, 2 * m)
     other = swap(own, 1)
 
-    keys, values, done = pl.pallas_call(
+    keys, values = pl.pallas_call(
         key_value_kernel,
         out_shape=[
             jax.ShapeDtypeStruct((2 * count, inner, live), BF16),
             jax.ShapeDtypeStruct((2 * count, live, inner), BF16),
-            jax.ShapeDtypeStruct((8, channels), F32),
         ],
-        in_specs=[VMEM] * 4 + [ANY],
-        out_specs=[VMEM] * 3,
+        in_specs=[VMEM] * 4,
+        out_specs=[VMEM] * 2,
         compiler_params=PARAMS,
         cost_estimate=measured(2),
-    )(own, other, pick, w_project, biases[near[0]])
+    )(own, other, pick, w_project)
 
     split = (count, owners, 2, rows_held, channels)
     own, other = own.reshape(split), other.reshape(split)
     updates = {}
-    straight = jnp.concatenate([biases[m] for m in far]) + done[:1, :1].astype(BF16)
+    straight = pl.pallas_call(
+        join_kernel,
+        out_shape=jax.ShapeDtypeStruct((len(far) * heads * rows_held, live), BF16),
+        in_specs=[VMEM] * len(far) + [ANY],
+        out_specs=VMEM,
+        compiler_params=PARAMS,
+        cost_estimate=measured(0.5),
+    )(*[biases[m] for m in far], keys)
     straight = swap(straight, 2)
     for m in passed:
         biases[m] = straight
     sent = {}
     for ms in (far, [0] + near[:1], passed, near[1:]):
         if ms == far:
-            after = [biases[near[1]]]
+            after = [biases[m] for m in near]
         elif ms == near[1:]:
             after = [updates[passed[0]]] + [sent[m] for m in far]
         else:

time: 61.5 us -> 60.8 us (0.989)
  local copies, waits for them, and re-layouts: 5.69 us -> 2.67 us
  Pallas kernels: 26.1 us -> 27.7 us
  waiting for transfers between devices: 8.19 us -> 9.29 us
  other arithmetic: 0.69 us -> 0 us
    unnamed x22, local copies, waits for them, and re-layouts: 5.18 us -> 2.67 us
    ppermute x14, waiting for transfers between devices: 8.19 us -> 9.29 us  [swap(): return lax.ppermute(x, 'row', [(i, i ^ bits) for i in range(devices)])]
    pallas_call x0 -> x1, Pallas kernels: none -> 0.72 us  [local(): pl.pallas_call(join_kernel, out_shape=jax.ShapeDtypeStruct((len(far) * he...]
    add x1 -> x0, other arithmetic: 0.68 us -> none  [local(): jnp.concatenate([biases[m] for m in far]) + done[:1, :1].astype(BF16)]
  transfers between devices with their start and end apart: 14 -> 14, of which waited for: 4 -> 4; matrix products, arithmetic and copies ran while one was open for 2% -> 0% of each run, Pallas kernels for 32% -> 34%
where the time goes in v7:
time: 60.8 us; the launch traced here: 60.6 us
  Pallas kernels  27.7 us (46%)
  starting transfers between devices  20.7 us (34%)
  waiting for transfers between devices  9.29 us (15%)
  local copies, waits for them, and re-layouts  2.67 us (4%)
    ppermute x14, starting transfers between devices, swap(): return lax.ppermute(x, 'row', [(i, i ^ bits) for i in range(devices)])  20.7 us
    pallas_call x4, Pallas kernels, local(): pl.pallas_call(functools.partial(attention_kernel, heads, ms, first), out...  16.9 us
    ppermute x14, waiting for transfers between devices, swap(): return lax.ppermute(x, 'row', [(i, i ^ bits) for i in range(devices)])  9.29 us
    pallas_call x1, Pallas kernels, local(): pl.pallas_call(bias_kernel, grid=(rows_held // step_rows,), out_shape=[ja...  6.18 us
    unnamed x22, local copies, waits for them, and re-layouts  2.67 us
    pallas_call x1, Pallas kernels, local(): pl.pallas_call(key_value_kernel, out_shape=[jax.ShapeDtypeStruct((2 * cou...  2.27 us
    pallas_call x2, Pallas kernels, local(): pl.pallas_call(functools.partial(gather_kernel, order), out_shape=jax.Sha...  1.63 us
  transfers between devices with their start and end apart: 14, of which 4 were waited for; matrix products, arithmetic and copies ran while one was open for 0% of the time, Pallas kernels for 34%

profile of v7, /device:TPU:0, one launch (start us, length us, event | category | flops | bytes accessed | tf_op | source)
XLA Modules:
  0.0 60.6 jit_solution(2834556864108627287)
XLA Ops:
  0.0 0.0 copy-start.5
  0.0 6.2 %shard_map.109 = (bf16[128,384]{1,0:T(8,128)(2,1)}, bf16[8,512,128]{2,1,0:T(8,128)(2,1)S(1)}, bf16[384,512]{1,0:T(8,128)(2,1)S(1)}, f32[8,384]{1,0:T(8,128)S(1)}) custom-call(s32[8]{0:T(128)} %rows_ref.1, bf16[32,512,128]{2,1,0:T(8,128)(2,1)} %pair_ref.1, s32[1,512]{1,0:T(1,128)} %bitcast.17, s32[1,512]{1,0:T(1,128)} %bitcast.22, f32[1,128]{1,0:T(1,128)} %bitcast.32, ...), custom_call_target="tpu_custom_call" | custom-call | bytes 22140000 | tf_op jit(solution)/shard_map/pallas_call | solution.py:254
  6.2 0.5 collective-permute-start.2
  6.7 4.7 %collective-permute-start.4 = (bf16[128,384]{1,0:T(8,128)(2,1)}, bf16[128,384]{1,0:T(8,128)(2,1)S(1)}, u32[]{:S(2)}, u32[]{:S(2)}) collective-permute-start(bf16[128,384]{1,0:T(8,128)(2,1)} %get-tuple-element.19.refs_0_), channel_id=1, source_target_pairs={{0,12},{1,13},{2,14},{3,15},{4,8},{5,9},{6,10},{7,11},{8,4},{9,5},... | collective-permute-start | bytes 294920 | tf_op jit(solution)/shard_map/ppermute | solution.py:251
  11.4 0.0 collective-permute-start.3
  11.4 1.5 %collective-permute-start.6 = (bf16[128,384]{1,0:T(8,128)(2,1)}, bf16[128,384]{1,0:T(8,128)(2,1)S(1)}, u32[]{:S(2)}, u32[]{:S(2)}) collective-permute-start(bf16[128,384]{1,0:T(8,128)(2,1)} %get-tuple-element.19.refs_0_), channel_id=1, source_target_pairs={{0,2},{1,3},{2,0},{3,1},{4,6},{5,7},{6,4},{7,5},{8,10},{9,11},{10,... | collective-permute-start | bytes 294920 | tf_op jit(solution)/shard_map/ppermute | solution.py:251
  12.9 0.6 collective-permute-start.1
  13.5 0.0 collective-permute-done.2.other_ref
  13.5 0.0 copy-start
  13.5 1.4 %collective-permute-start = (bf16[128,384]{1,0:T(8,128)(2,1)}, bf16[128,384]{1,0:T(8,128)(2,1)S(1)}, u32[]{:S(2)}, u32[]{:S(2)}) collective-permute-start(bf16[128,384]{1,0:T(8,128)(2,1)} %get-tuple-element.19.refs_0_), channel_id=1, source_target_pairs={{0,4},{1,5},{2,6},{3,7},{4,0},{5,1},{6,2},{7,3},{8,12},{9,13},{10,... | collective-permute-start | bytes 294920 | tf_op jit(solution)/shard_map/ppermute | solution.py:251
  14.9 0.0 copy-done.5
  14.9 2.3 %shard_map.110 = (bf16[16,128,384]{2,1,0:T(8,128)(2,1)S(1)}, bf16[16,384,128]{2,1,0:T(8,128)(2,1)S(1)}) custom-call(bf16[8,512,128]{2,1,0:T(8,128)(2,1)S(1)} %get-tuple-element.20.own_ref, bf16[8,512,128]{2,1,0:T(8,128)(2,1)S(1)} %collective-permute-done.2.other_ref, bf16[384,512]{1,0:T(8,128)(2,1)S(1)} %get-tuple-element.21.pick_ref, ...), custom_call_target="tpu_custom_call" | custom-call | bytes 7380000 | tf_op jit(solution)/shard_map/pallas_call | solution.py:301
  17.2 0.0 copy-start.3
  17.2 0.0 copy-start.6
  17.2 0.0 copy-start.7
  17.2 0.0 copy-start.8
  17.2 0.0 copy-start.9
  17.2 0.0 copy-start.10
  17.2 0.0 collective-permute-done.4.refs_1_
  17.2 3.3 %collective-permute-done.3.refs_0_ = bf16[128,384]{1,0:T(8,128)(2,1)S(1)} collective-permute-done((bf16[128,384]{1,0:T(8,128)(2,1)}, bf16[128,384]{1,0:T(8,128)(2,1)S(1)}, u32[]{:S(2)}, u32[]{:S(2)}) %collective-permute-start.3) | collective-permute-done | bytes 98336 | tf_op jit(solution)/shard_map/ppermute | solution.py:251
  20.6 0.7 %shard_map.111 = bf16[256,384]{1,0:T(8,128)(2,1)} custom-call(bf16[128,384]{1,0:T(8,128)(2,1)S(1)} %collective-permute-done.3.refs_0_, bf16[128,384]{1,0:T(8,128)(2,1)S(1)} %collective-permute-done.4.refs_1_, bf16[16,128,384]{2,1,0:T(8,128)(2,1)S(1)} %get-tuple-element.22.refs_2_.refs_4_), custom_call_target="tpu_custom_call" | custom-call | bytes 1845000 | tf_op jit(solution)/shard_map/pallas_call | solution.py:316
  21.3 0.0 copy-done
  21.3 1.5 %collective-permute-start.5 = (bf16[256,384]{1,0:T(8,128)(2,1)}, bf16[256,384]{1,0:T(8,128)(2,1)S(1)}, u32[]{:S(2)}, u32[]{:S(2)}) collective-permute-start(bf16[256,384]{1,0:T(8,128)(2,1)} %shard_map.111), channel_id=1, source_target_pairs={{0,2},{1,3},{2,0},{3,1},{4,6},{5,7},{6,4},{7,5},{8,10},{9,11},{10,... | collective-permute-start | bytes 589832 | tf_op jit(solution)/shard_map/ppermute | solution.py:251
  22.8 0.0 copy-done.3
  22.8 0.0 collective-permute-done.6.refs_12_.refs_1_
  22.8 0.0 collective-permute-done.1.refs_14_.refs_1_
  22.8 0.0 collective-permute-done.refs_13_.refs_0_
  22.9 0.0 copy-done.6
  22.9 0.0 copy-done.7
  22.9 0.0 copy-done.8
  22.9 0.0 copy-done.9
  22.9 0.0 copy-done.10
  22.9 0.0 copy-start.1
  22.9 1.2 %copy-done.1 = bf16[8,512,128]{2,1,0:T(8,128)(2,1)S(1)} copy-done((bf16[8,512,128]{2,1,0:T(8,128)(2,1)S(1)}, bf16[8,512,128]{2,1,0:T(8,128)(2,1)}, u32[]{:S(2)}) %copy-start.1) | copy-done | bytes 1048600
  24.1 0.0 copy-start.4
  24.1 1.4 %copy-done.4 = bf16[16,384,128]{2,1,0:T(8,128)(2,1)S(1)} copy-done((bf16[16,384,128]{2,1,0:T(8,128)(2,1)S(1)}, bf16[16,384,128]{2,1,0:T(8,128)(2,1)}, u32[]{:S(2)}) %copy-start.4) | copy-done | bytes 1572888
  25.5 0.0 copy-start.2
  25.5 4.1 %shard_map.112 = (bf16[16,32,128]{2,1,0:T(8,128)(2,1)S(1)}, bf16[16,32,128]{2,1,0:T(8,128)(2,1)S(1)}) custom-call(s32[1]{0:T(128)} %bitcast.me_ref, f32[4]{0:T(128)S(1)} %copy-done.9, bf16[128,384]{1,0:T(8,128)(2,1)S(1)} %collective-permute-done.3.refs_0_, bf16[128,384]{1,0:T(8,128)(2,1)S(1)} %collective-permute-done.4.refs_1_, ...), custom_call_target="tpu_custom_call" | custom-call | bytes 16236000 | tf_op jit(solution)/shard_map/pallas_call | solution.py:338
  29.7 2.5 %collective-permute-start.8 = (bf16[16,32,128]{2,1,0:T(8,128)(2,1)S(1)}, bf16[16,32,128]{2,1,0:T(8,128)(2,1)S(1)}, u32[]{:S(2)}, u32[]{:S(2)}) collective-permute-start(bf16[16,32,128]{2,1,0:T(8,128)(2,1)S(1)} %get-tuple-element.28), channel_id=1, source_target_pairs={{0,12},{1,13},{2,14},{3,15},{4,8},{5,9},{6,10},{7,11},{8,4},{9,5},... | collective-permute-start | bytes 393224 | tf_op jit(solution)/shard_map/ppermute | solution.py:251
  32.2 0.0 collective-permute-start.7
  32.2 0.0 copy-done.2
  32.2 4.5 %shard_map.113 = (bf16[16,32,128]{2,1,0:T(8,128)(2,1)S(1)}, bf16[16,32,128]{2,1,0:T(8,128)(2,1)S(1)}) custom-call(s32[1]{0:T(128)} %bitcast.me_ref, f32[4]{0:T(128)S(1)} %copy-done.9, bf16[128,384]{1,0:T(8,128)(2,1)} %get-tuple-element.19.refs_0_, bf16[128,384]{1,0:T(8,128)(2,1)S(1)} %collective-permute-done.6.refs_12_.refs_1_, ...), custom_call_target="tpu_custom_call" | custom-call | bytes 16236000 | tf_op jit(solution)/shard_map/pallas_call | solution.py:338
  36.7 1.0 %collective-permute-start.11 = (bf16[16,32,128]{2,1,0:T(8,128)(2,1)S(1)}, bf16[16,32,128]{2,1,0:T(8,128)(2,1)S(1)}, u32[]{:S(2)}, u32[]{:S(2)}) collective-permute-start(bf16[16,32,128]{2,1,0:T(8,128)(2,1)S(1)} %get-tuple-element.31), channel_id=1, source_target_pairs={{0,2},{1,3},{2,0},{3,1},{4,6},{5,7},{6,4},{7,5},{8,10},{9,11},{10,... | collective-permute-start | bytes 393224 | tf_op jit(solution)/shard_map/ppermute | solution.py:251
  37.8 0.0 collective-permute-done.5.refs_0_.refs_1_
  37.8 4.1 %shard_map.114 = (bf16[16,32,128]{2,1,0:T(8,128)(2,1)S(1)}, bf16[16,32,128]{2,1,0:T(8,128)(2,1)S(1)}) custom-call(s32[1]{0:T(128)} %bitcast.me_ref, f32[4]{0:T(128)S(1)} %copy-done.9, bf16[256,384]{1,0:T(8,128)(2,1)S(1)} %collective-permute-done.5.refs_0_.refs_1_, bf16[256,384]{1,0:T(8,128)(2,1)S(1)} %collective-permute-done.5.refs_0_.refs_1_, ...), custom_call_target="tpu_custom_call" | custom-call | bytes 16236000 | tf_op jit(solution)/shard_map/pallas_call | solution.py:338
  41.9 1.9 %collective-permute-start.13 = (bf16[16,32,128]{2,1,0:T(8,128)(2,1)S(1)}, bf16[16,32,128]{2,1,0:T(8,128)(2,1)S(1)}, u32[]{:S(2)}, u32[]{:S(2)}) collective-permute-start(bf16[16,32,128]{2,1,0:T(8,128)(2,1)S(1)} %get-tuple-element.32), channel_id=1, source_target_pairs={{0,14},{1,15},{2,12},{3,13},{4,10},{5,11},{6,8},{7,9},{8,6},{9,7},... | collective-permute-start | bytes 393224 | tf_op jit(solution)/shard_map/ppermute | solution.py:251
  43.8 2.0 %collective-permute-start.12 = (bf16[16,32,128]{2,1,0:T(8,128)(2,1)S(1)}, bf16[16,32,128]{2,1,0:T(8,128)(2,1)S(1)}, u32[]{:S(2)}, u32[]{:S(2)}) collective-permute-start(bf16[16,32,128]{2,1,0:T(8,128)(2,1)S(1)} %get-tuple-element.27.refs_12_), channel_id=1, source_target_pairs={{0,10},{1,11},{2,8},{3,9},{4,14},{5,15},{6,12},{7,13},{8,2},{9,3},... | collective-permute-start | bytes 393224 | tf_op jit(solution)/shard_map/ppermute | solution.py:251
  45.8 0.0 collective-permute-done.8.refs_14_.refs_3_
  45.8 0.0 collective-permute-done.7.refs_13_.refs_2_
  45.8 4.1 %shard_map.115 = (bf16[16,32,128]{2,1,0:T(8,128)(2,1)S(1)}, bf16[16,32,128]{2,1,0:T(8,128)(2,1)S(1)}) custom-call(s32[1]{0:T(128)} %bitcast.me_ref, f32[4]{0:T(128)S(1)} %copy-done.9, bf16[128,384]{1,0:T(8,128)(2,1)S(1)} %collective-permute-done.refs_13_.refs_0_, bf16[128,384]{1,0:T(8,128)(2,1)S(1)} %collective-permute-done.1.refs_14_.refs_1_, ...), custom_call_target="tpu_custom_call" | custom-call | bytes 16236000 | tf_op jit(solution)/shard_map/pallas_call | solution.py:338
  50.0 1.5 %collective-permute-start.9 = (bf16[16,32,128]{2,1,0:T(8,128)(2,1)S(1)}, bf16[16,32,128]{2,1,0:T(8,128)(2,1)S(1)}, u32[]{:S(2)}, u32[]{:S(2)}) collective-permute-start(bf16[16,32,128]{2,1,0:T(8,128)(2,1)S(1)} %get-tuple-element.29), channel_id=1, source_target_pairs={{0,4},{1,5},{2,6},{3,7},{4,0},{5,1},{6,2},{7,3},{8,12},{9,13},{10,... | collective-permute-start | bytes 393224 | tf_op jit(solution)/shard_map/ppermute | solution.py:251
  51.5 1.5 %collective-permute-start.10 = (bf16[16,32,128]{2,1,0:T(8,128)(2,1)S(1)}, bf16[16,32,128]{2,1,0:T(8,128)(2,1)S(1)}, u32[]{:S(2)}, u32[]{:S(2)}) collective-permute-start(bf16[16,32,128]{2,1,0:T(8,128)(2,1)S(1)} %get-tuple-element.30), channel_id=1, source_target_pairs={{0,6},{1,7},{2,4},{3,5},{4,2},{5,3},{6,0},{7,1},{8,14},{9,15},{10,... | collective-permute-start | bytes 393224 | tf_op jit(solution)/shard_map/ppermute | solution.py:251
  53.0 0.0 collective-permute-done.11.refs_1_
  53.0 0.0 collective-permute-done.13.refs_5_
  53.0 3.6 %collective-permute-done.12.refs_4_ = bf16[16,32,128]{2,1,0:T(8,128)(2,1)S(1)} collective-permute-done((bf16[16,32,128]{2,1,0:T(8,128)(2,1)S(1)}, bf16[16,32,128]{2,1,0:T(8,128)(2,1)S(1)}, u32[]{:S(2)}, u32[]{:S(2)}) %collective-permute-start.12) | collective-permute-done | bytes 131104 | tf_op jit(solution)/shard_map/ppermute | solution.py:251
  56.6 0.9 %shard_map.116.refs_2_ = bf16[128,32,128]{2,1,0:T(8,128)(2,1)} custom-call(s32[1]{0:T(128)} %bitcast.me_ref, bf16[16,32,128]{2,1,0:T(8,128)(2,1)S(1)} %get-tuple-element.26.refs_12_.refs_0_, bf16[16,32,128]{2,1,0:T(8,128)(2,1)S(1)} %collective-permute-done.11.refs_1_, bf16[16,32,128]{2,1,0:T(8,128)(2,1)S(1)} %collective-permute-done.7.refs_13_.refs_2_, ...), custom_call_target="tpu_custom_call" | custom-call | bytes 3690000 | tf_op jit(solution)/shard_map/pallas_call | solution.py:376
  57.5 0.7 %collective-permute-done.9.refs_0_ = bf16[16,32,128]{2,1,0:T(8,128)(2,1)S(1)} collective-permute-done((bf16[16,32,128]{2,1,0:T(8,128)(2,1)S(1)}, bf16[16,32,128]{2,1,0:T(8,128)(2,1)S(1)}, u32[]{:S(2)}, u32[]{:S(2)}) %collective-permute-start.9) | collective-permute-done | bytes 131104 | tf_op jit(solution)/shard_map/ppermute | solution.py:251
  58.2 1.7 %collective-permute-done.10.refs_1_ = bf16[16,32,128]{2,1,0:T(8,128)(2,1)S(1)} collective-permute-done((bf16[16,32,128]{2,1,0:T(8,128)(2,1)S(1)}, bf16[16,32,128]{2,1,0:T(8,128)(2,1)S(1)}, u32[]{:S(2)}, u32[]{:S(2)}) %collective-permute-start.10) | collective-permute-done | bytes 131104 | tf_op jit(solution)/shard_map/ppermute | solution.py:251
  59.9 0.7 %shard_map.117 = bf16[128,32,128]{2,1,0:T(8,128)(2,1)} custom-call(s32[1]{0:T(128)} %bitcast.me_ref, bf16[16,32,128]{2,1,0:T(8,128)(2,1)S(1)} %collective-permute-done.9.refs_0_, bf16[16,32,128]{2,1,0:T(8,128)(2,1)S(1)} %collective-permute-done.10.refs_1_, bf16[128,32,128]{2,1,0:T(8,128)(2,1)} %shard_map.116.refs_2_), custom_call_target="tpu_custom_call", output_to_operand_aliasing={{}: (3, {})} | custom-call | bytes 3690000 | tf_op jit(solution)/shard_map/pallas_call | solution.py:376
Async XLA Ops:
  0.0 14.9 %copy-start.5 = (bf16[128,512]{1,0:T(8,128)(2,1)S(1)}, bf16[128,512]{1,0:T(8,128)(2,1)}, u32[]{:S(2)}) copy-start(bf16[128,512]{1,0:T(8,128)(2,1)} %refs_9_.7) | copy-start | bytes 393220
  6.2 7.3 %collective-permute-start.2 = (bf16[8,512,128]{2,1,0:T(8,128)(2,1)S(1)}, bf16[8,512,128]{2,1,0:T(8,128)(2,1)S(1)}, u32[]{:S(2)}, u32[]{:S(2)}) collective-permute-start(bf16[8,512,128]{2,1,0:T(8,128)(2,1)S(1)} %get-tuple-element.20.own_ref), channel_id=1, source_target_pairs={{0,1},{1,0},{2,3},{3,2},{4,5},{5,4},{6,7},{7,6},{8,9},{9,8},{10,11... | collective-permute-start | bytes 3145736 | tf_op jit(solution)/shard_map/ppermute | solution.py:251
  6.7 10.5 %collective-permute-start.4 = (bf16[128,384]{1,0:T(8,128)(2,1)}, bf16[128,384]{1,0:T(8,128)(2,1)S(1)}, u32[]{:S(2)}, u32[]{:S(2)}) collective-permute-start(bf16[128,384]{1,0:T(8,128)(2,1)} %get-tuple-element.19.refs_0_), channel_id=1, source_target_pairs={{0,12},{1,13},{2,14},{3,15},{4,8},{5,9},{6,10},{7,11},{8,4},{9,5},... | collective-permute-start | bytes 294920 | tf_op jit(solution)/shard_map/ppermute | solution.py:251
  11.4 9.2 %collective-permute-start.3 = (bf16[128,384]{1,0:T(8,128)(2,1)}, bf16[128,384]{1,0:T(8,128)(2,1)S(1)}, u32[]{:S(2)}, u32[]{:S(2)}) collective-permute-start(bf16[128,384]{1,0:T(8,128)(2,1)} %get-tuple-element.19.refs_0_), channel_id=1, source_target_pairs={{0,8},{1,9},{2,10},{3,11},{4,12},{5,13},{6,14},{7,15},{8,0},{9,1},... | collective-permute-start | bytes 294920 | tf_op jit(solution)/shard_map/ppermute | solution.py:251
  11.4 11.4 %collective-permute-start.6 = (bf16[128,384]{1,0:T(8,128)(2,1)}, bf16[128,384]{1,0:T(8,128)(2,1)S(1)}, u32[]{:S(2)}, u32[]{:S(2)}) collective-permute-start(bf16[128,384]{1,0:T(8,128)(2,1)} %get-tuple-element.19.refs_0_), channel_id=1, source_target_pairs={{0,2},{1,3},{2,0},{3,1},{4,6},{5,7},{6,4},{7,5},{8,10},{9,11},{10,... | collective-permute-start | bytes 294920 | tf_op jit(solution)/shard_map/ppermute | solution.py:251
  12.9 9.9 %collective-permute-start.1 = (bf16[128,384]{1,0:T(8,128)(2,1)}, bf16[128,384]{1,0:T(8,128)(2,1)S(1)}, u32[]{:S(2)}, u32[]{:S(2)}) collective-permute-start(bf16[128,384]{1,0:T(8,128)(2,1)} %get-tuple-element.19.refs_0_), channel_id=1, source_target_pairs={{0,6},{1,7},{2,4},{3,5},{4,2},{5,3},{6,0},{7,1},{8,14},{9,15},{10,... | collective-permute-start | bytes 294920 | tf_op jit(solution)/shard_map/ppermute | solution.py:251
  13.5 7.8 %copy-start = (bf16[8,512,128]{2,1,0:T(8,128)(2,1)}, bf16[8,512,128]{2,1,0:T(8,128)(2,1)S(1)}, u32[]{:S(2)}) copy-start(bf16[8,512,128]{2,1,0:T(8,128)(2,1)S(1)} %collective-permute-done.2.other_ref) | copy-start | bytes 3145732
  13.5 9.3 %collective-permute-start = (bf16[128,384]{1,0:T(8,128)(2,1)}, bf16[128,384]{1,0:T(8,128)(2,1)S(1)}, u32[]{:S(2)}, u32[]{:S(2)}) collective-permute-start(bf16[128,384]{1,0:T(8,128)(2,1)} %get-tuple-element.19.refs_0_), channel_id=1, source_target_pairs={{0,4},{1,5},{2,6},{3,7},{4,0},{5,1},{6,2},{7,3},{8,12},{9,13},{10,... | collective-permute-start | bytes 294920 | tf_op jit(solution)/shard_map/ppermute | solution.py:251
  17.2 5.7 %copy-start.3 = (bf16[16,384,128]{2,1,0:T(8,128)(2,1)}, bf16[16,384,128]{2,1,0:T(8,128)(2,1)S(1)}, u32[]{:S(2)}) copy-start(bf16[16,384,128]{2,1,0:T(8,128)(2,1)S(1)} %get-tuple-element.23.refs_5_) | copy-start | bytes 4718596
  17.2 5.7 %copy-start.6 = (bf16[128,128]{1,0:T(8,128)(2,1)S(1)}, bf16[128,128]{1,0:T(8,128)(2,1)}, u32[]{:S(2)}) copy-start(bf16[128,128]{1,0:T(8,128)(2,1)} %refs_11_.7) | copy-start | bytes 98308
  17.2 5.7 %copy-start.7 = (s32[512]{0:T(512)S(1)}, s32[512]{0:T(512)}, u32[]{:S(2)}) copy-start(s32[512]{0:T(512)} %param.13) | copy-start | bytes 6148
  17.2 5.7 %copy-start.8 = (s32[512]{0:T(512)S(1)}, s32[512]{0:T(512)}, u32[]{:S(2)}) copy-start(s32[512]{0:T(512)} %param.14) | copy-start | bytes 6148
  17.2 5.7 %copy-start.9 = (f32[4]{0:T(128)S(1)}, f32[4]{0:T(128)}, u32[]{:S(2)}) copy-start(f32[4]{0:T(128)} %chain_bias_ref.7) | copy-start | bytes 52
  17.2 5.7 %copy-start.10 = (f32[128]{0:T(128)S(1)}, f32[128]{0:T(128)}, u32[]{:S(2)}) copy-start(f32[128]{0:T(128)} %param.18) | copy-start | bytes 1540
  21.3 16.5 %collective-permute-start.5 = (bf16[256,384]{1,0:T(8,128)(2,1)}, bf16[256,384]{1,0:T(8,128)(2,1)S(1)}, u32[]{:S(2)}, u32[]{:S(2)}) collective-permute-start(bf16[256,384]{1,0:T(8,128)(2,1)} %shard_map.111), channel_id=1, source_target_pairs={{0,2},{1,3},{2,0},{3,1},{4,6},{5,7},{6,4},{7,5},{8,10},{9,11},{10,... | collective-permute-start | bytes 589832 | tf_op jit(solution)/shard_map/ppermute | solution.py:251
  22.9 1.2 %copy-start.1 = (bf16[8,512,128]{2,1,0:T(8,128)(2,1)S(1)}, bf16[8,512,128]{2,1,0:T(8,128)(2,1)}, u32[]{:S(2)}) copy-start(bf16[8,512,128]{2,1,0:T(8,128)(2,1)} %copy-done) | copy-start | bytes 3145732
  24.1 1.4 %copy-start.4 = (bf16[16,384,128]{2,1,0:T(8,128)(2,1)S(1)}, bf16[16,384,128]{2,1,0:T(8,128)(2,1)}, u32[]{:S(2)}) copy-start(bf16[16,384,128]{2,1,0:T(8,128)(2,1)} %copy-done.3) | copy-start | bytes 4718596
  25.5 6.7 %copy-start.2 = (bf16[8,512,128]{2,1,0:T(8,128)(2,1)S(1)}, bf16[8,512,128]{2,1,0:T(8,128)(2,1)}, u32[]{:S(2)}) copy-start(bf16[8,512,128]{2,1,0:T(8,128)(2,1)} %copy-done) | copy-start | bytes 3145732
  29.7 16.1 %collective-permute-start.8 = (bf16[16,32,128]{2,1,0:T(8,128)(2,1)S(1)}, bf16[16,32,128]{2,1,0:T(8,128)(2,1)S(1)}, u32[]{:S(2)}, u32[]{:S(2)}) collective-permute-start(bf16[16,32,128]{2,1,0:T(8,128)(2,1)S(1)} %get-tuple-element.28), channel_id=1, source_target_pairs={{0,12},{1,13},{2,14},{3,15},{4,8},{5,9},{6,10},{7,11},{8,4},{9,5},... | collective-permute-start | bytes 393224 | tf_op jit(solution)/shard_map/ppermute | solution.py:251
  32.2 13.6 %collective-permute-start.7 = (bf16[16,32,128]{2,1,0:T(8,128)(2,1)S(1)}, bf16[16,32,128]{2,1,0:T(8,128)(2,1)S(1)}, u32[]{:S(2)}, u32[]{:S(2)}) collective-permute-start(bf16[16,32,128]{2,1,0:T(8,128)(2,1)S(1)} %get-tuple-element.25.refs_12_), channel_id=1, source_target_pairs={{0,8},{1,9},{2,10},{3,11},{4,12},{5,13},{6,14},{7,15},{8,0},{9,1},... | collective-permute-start | bytes 393224 | tf_op jit(solution)/shard_map/ppermute | solution.py:251
  36.7 16.3 %collective-permute-start.11 = (bf16[16,32,128]{2,1,0:T(8,128)(2,1)S(1)}, bf16[16,32,128]{2,1,0:T(8,128)(2,1)S(1)}, u32[]{:S(2)}, u32[]{:S(2)}) collective-permute-start(bf16[16,32,128]{2,1,0:T(8,128)(2,1)S(1)} %get-tuple-element.31), channel_id=1, source_target_pairs={{0,2},{1,3},{2,0},{3,1},{4,6},{5,7},{6,4},{7,5},{8,10},{9,11},{10,... | collective-permute-start | bytes 393224 | tf_op jit(solution)/shard_map/ppermute | solution.py:251
  41.9 11.1 %collective-permute-start.13 = (bf16[16,32,128]{2,1,0:T(8,128)(2,1)S(1)}, bf16[16,32,128]{2,1,0:T(8,128)(2,1)S(1)}, u32[]{:S(2)}, u32[]{:S(2)}) collective-permute-start(bf16[16,32,128]{2,1,0:T(8,128)(2,1)S(1)} %get-tuple-element.32), channel_id=1, source_target_pairs={{0,14},{1,15},{2,12},{3,13},{4,10},{5,11},{6,8},{7,9},{8,6},{9,7},... | collective-permute-start | bytes 393224 | tf_op jit(solution)/shard_map/ppermute | solution.py:251
  43.8 12.7 %collective-permute-start.12 = (bf16[16,32,128]{2,1,0:T(8,128)(2,1)S(1)}, bf16[16,32,128]{2,1,0:T(8,128)(2,1)S(1)}, u32[]{:S(2)}, u32[]{:S(2)}) collective-permute-start(bf16[16,32,128]{2,1,0:T(8,128)(2,1)S(1)} %get-tuple-element.27.refs_12_), channel_id=1, source_target_pairs={{0,10},{1,11},{2,8},{3,9},{4,14},{5,15},{6,12},{7,13},{8,2},{9,3},... | collective-permute-start | bytes 393224 | tf_op jit(solution)/shard_map/ppermute | solution.py:251
  50.0 8.2 %collective-permute-start.9 = (bf16[16,32,128]{2,1,0:T(8,128)(2,1)S(1)}, bf16[16,32,128]{2,1,0:T(8,128)(2,1)S(1)}, u32[]{:S(2)}, u32[]{:S(2)}) collective-permute-start(bf16[16,32,128]{2,1,0:T(8,128)(2,1)S(1)} %get-tuple-element.29), channel_id=1, source_target_pairs={{0,4},{1,5},{2,6},{3,7},{4,0},{5,1},{6,2},{7,3},{8,12},{9,13},{10,... | collective-permute-start | bytes 393224 | tf_op jit(solution)/shard_map/ppermute | solution.py:251
  51.5 8.4 %collective-permute-start.10 = (bf16[16,32,128]{2,1,0:T(8,128)(2,1)S(1)}, bf16[16,32,128]{2,1,0:T(8,128)(2,1)S(1)}, u32[]{:S(2)}, u32[]{:S(2)}) collective-permute-start(bf16[16,32,128]{2,1,0:T(8,128)(2,1)S(1)} %get-tuple-element.30), channel_id=1, source_target_pairs={{0,6},{1,7},{2,4},{3,5},{4,2},{5,3},{6,0},{7,1},{8,14},{9,15},{10,... | collective-permute-start | bytes 393224 | tf_op jit(solution)/shard_map/ppermute | solution.py:251

commit v8 on v7

--- a/solution.py
+++ b/solution.py
@@ -50,6 +50,7 @@
 
 
 def bias_kernel(
+    me_ref,
     rows_ref,
     pair_ref,
     mask_ref,
@@ -262,6 +263,7 @@
         ],
         in_specs=[
             ANY,
+            ANY,
             pl.BlockSpec((step_rows, tokens, channels), lambda i: (i, 0, 0)),
             pl.BlockSpec((1, tokens), lambda i: (0, 0)),
             pl.BlockSpec((1, tokens), lambda i: (0, 0)),
@@ -284,6 +286,7 @@
         compiler_params=PARAMS,
         cost_estimate=measured(6),
     )(
+        me,
         *[
             pltpu.with_memory_space_constraint(x, pltpu.HBM)
             for x in (window_rows, pair, mask_row, chain_row, gain, shift, w_bias.T)

time: 60.8 us -> 56.1 us (0.923)
  local copies, waits for them, and re-layouts: 2.67 us -> 0.04 us
  Pallas kernels: 27.7 us -> 25.5 us
    unnamed x22 -> x12, local copies, waits for them, and re-layouts: 2.67 us -> 0.04 us
    pallas_call x4, Pallas kernels: 16.9 us -> 16 us  [local(): pl.pallas_call(functools.partial(attention_kernel, heads, ms, first), out...]
    pallas_call x1, Pallas kernels: 0.72 us -> 0.02 us  [local(): pl.pallas_call(join_kernel, out_shape=jax.ShapeDtypeStruct((len(far) * he...]
    pallas_call x1, Pallas kernels: 6.18 us -> 5.57 us  [local(): pl.pallas_call(bias_kernel, grid=(rows_held // step_rows,), out_shape=[ja...]
where the time goes in v8:
time: 56.1 us; the launch traced here: 55.9 us
  Pallas kernels  25.5 us (45%)
  starting transfers between devices  20.8 us (37%)
  waiting for transfers between devices  9.47 us (17%)
    ppermute x14, starting transfers between devices, swap(): return lax.ppermute(x, 'row', [(i, i ^ bits) for i in range(devices)])  20.8 us
    pallas_call x4, Pallas kernels, local(): pl.pallas_call(functools.partial(attention_kernel, heads, ms, first), out...  16 us
    ppermute x14, waiting for transfers between devices, swap(): return lax.ppermute(x, 'row', [(i, i ^ bits) for i in range(devices)])  9.47 us
    pallas_call x1, Pallas kernels, local(): pl.pallas_call(bias_kernel, grid=(rows_held // step_rows,), out_shape=[ja...  5.57 us
    pallas_call x1, Pallas kernels, local(): pl.pallas_call(key_value_kernel, out_shape=[jax.ShapeDtypeStruct((2 * cou...  2.27 us
    pallas_call x2, Pallas kernels, local(): pl.pallas_call(functools.partial(gather_kernel, order), out_shape=jax.Sha...  1.63 us
  transfers between devices with their start and end apart: 14, of which 4 were waited for; matrix products, arithmetic and copies ran while one was open for 0% of the time, Pallas kernels for 34%

profile of v8, /device:TPU:0, one launch (start us, length us, event | category | flops | bytes accessed | tf_op | source)
XLA Modules:
  0.0 55.9 jit_solution(10902952217134240954)
XLA Ops:
  0.0 0.0 copy-start
  0.0 5.6 %shard_map.109 = (bf16[128,384]{1,0:T(8,128)(2,1)S(1)}, bf16[8,512,128]{2,1,0:T(8,128)(2,1)S(1)}, bf16[384,512]{1,0:T(8,128)(2,1)S(1)}, f32[8,384]{1,0:T(8,128)S(1)}) custom-call(s32[1]{0:T(128)} %bitcast.me_ref, s32[8]{0:T(128)} %rows_ref.1, bf16[32,512,128]{2,1,0:T(8,128)(2,1)} %pair_ref.1, s32[1,512]{1,0:T(1,128)} %bitcast.17, s32[1,512]{1,0:T(1,128)} %bitcast.22, ...), custom_call_target="tpu_custom_call" | custom-call | bytes 22140000 | tf_op jit(solution)/shard_map/pallas_call | solution.py:255
  5.6 0.5 collective-permute-start.2
  6.1 4.7 %collective-permute-start.4 = (bf16[128,384]{1,0:T(8,128)(2,1)S(1)}, bf16[128,384]{1,0:T(8,128)(2,1)S(1)}, u32[]{:S(2)}, u32[]{:S(2)}) collective-permute-start(bf16[128,384]{1,0:T(8,128)(2,1)S(1)} %get-tuple-element.19.refs_0_), channel_id=1, source_target_pairs={{0,12},{1,13},{2,14},{3,15},{4,8},{5,9},{6,10},{7,11},{8,4},{9,5},... | collective-permute-start | bytes 294920 | tf_op jit(solution)/shard_map/ppermute | solution.py:252
  10.8 0.0 collective-permute-start.3
  10.8 1.5 %collective-permute-start.6 = (bf16[128,384]{1,0:T(8,128)(2,1)S(1)}, bf16[128,384]{1,0:T(8,128)(2,1)S(1)}, u32[]{:S(2)}, u32[]{:S(2)}) collective-permute-start(bf16[128,384]{1,0:T(8,128)(2,1)S(1)} %get-tuple-element.19.refs_0_), channel_id=1, source_target_pairs={{0,2},{1,3},{2,0},{3,1},{4,6},{5,7},{6,4},{7,5},{8,10},{9,11},{10,... | collective-permute-start | bytes 294920 | tf_op jit(solution)/shard_map/ppermute | solution.py:252
  12.3 0.6 %collective-permute-start.1 = (bf16[128,384]{1,0:T(8,128)(2,1)S(1)}, bf16[128,384]{1,0:T(8,128)(2,1)S(1)}, u32[]{:S(2)}, u32[]{:S(2)}) collective-permute-start(bf16[128,384]{1,0:T(8,128)(2,1)S(1)} %get-tuple-element.19.refs_0_), channel_id=1, source_target_pairs={{0,6},{1,7},{2,4},{3,5},{4,2},{5,3},{6,0},{7,1},{8,14},{9,15},{10,... | collective-permute-start | bytes 294920 | tf_op jit(solution)/shard_map/ppermute | solution.py:252
  12.9 0.0 collective-permute-done.2.other_ref
  12.9 1.4 %collective-permute-start = (bf16[128,384]{1,0:T(8,128)(2,1)S(1)}, bf16[128,384]{1,0:T(8,128)(2,1)S(1)}, u32[]{:S(2)}, u32[]{:S(2)}) collective-permute-start(bf16[128,384]{1,0:T(8,128)(2,1)S(1)} %get-tuple-element.19.refs_0_), channel_id=1, source_target_pairs={{0,4},{1,5},{2,6},{3,7},{4,0},{5,1},{6,2},{7,3},{8,12},{9,13},{10,... | collective-permute-start | bytes 294920 | tf_op jit(solution)/shard_map/ppermute | solution.py:252
  14.3 0.0 copy-done
  14.3 2.3 %shard_map.110 = (bf16[16,128,384]{2,1,0:T(8,128)(2,1)S(1)}, bf16[16,384,128]{2,1,0:T(8,128)(2,1)S(1)}) custom-call(bf16[8,512,128]{2,1,0:T(8,128)(2,1)S(1)} %get-tuple-element.20.own_ref, bf16[8,512,128]{2,1,0:T(8,128)(2,1)S(1)} %collective-permute-done.2.other_ref, bf16[384,512]{1,0:T(8,128)(2,1)S(1)} %get-tuple-element.21.pick_ref, ...), custom_call_target="tpu_custom_call" | custom-call | bytes 7380000 | tf_op jit(solution)/shard_map/pallas_call | solution.py:304
  16.5 0.0 copy-start.1
  16.6 0.0 copy-start.2
  16.6 0.0 copy-start.3
  16.6 0.0 copy-start.4
  16.6 0.0 copy-start.5
  16.6 0.0 collective-permute-done.4.refs_1_
  16.6 3.1 %collective-permute-done.3.refs_0_ = bf16[128,384]{1,0:T(8,128)(2,1)S(1)} collective-permute-done((bf16[128,384]{1,0:T(8,128)(2,1)S(1)}, bf16[128,384]{1,0:T(8,128)(2,1)S(1)}, u32[]{:S(2)}, u32[]{:S(2)}) %collective-permute-start.3) | collective-permute-done | bytes 98336 | tf_op jit(solution)/shard_map/ppermute | solution.py:252
  19.8 1.6 %collective-permute-start.5 = (bf16[256,384]{1,0:T(8,128)(2,1)S(1)}, bf16[256,384]{1,0:T(8,128)(2,1)S(1)}, u32[]{:S(2)}, u32[]{:S(2)}) collective-permute-start(bf16[256,384]{1,0:T(8,128)(2,1)S(1)} %shard_map.111), channel_id=1, source_target_pairs={{0,2},{1,3},{2,0},{3,1},{4,6},{5,7},{6,4},{7,5},{8,10},{9,11},{10,... | collective-permute-start | bytes 589832 | tf_op jit(solution)/shard_map/ppermute | solution.py:252
  21.4 0.0 collective-permute-done.6.refs_12_.refs_1_
  21.4 0.0 collective-permute-done.1.refs_14_.refs_1_
  21.4 0.0 collective-permute-done.refs_13_.refs_0_
  21.4 0.0 copy-done.1
  21.4 0.0 copy-done.2
  21.4 0.0 copy-done.3
  21.4 0.0 copy-done.4
  21.4 0.0 copy-done.5
  21.4 4.0 %shard_map.112 = (bf16[16,32,128]{2,1,0:T(8,128)(2,1)S(1)}, bf16[16,32,128]{2,1,0:T(8,128)(2,1)S(1)}) custom-call(s32[1]{0:T(128)} %bitcast.me_ref, f32[4]{0:T(128)S(1)} %copy-done.4, bf16[128,384]{1,0:T(8,128)(2,1)S(1)} %collective-permute-done.3.refs_0_, bf16[128,384]{1,0:T(8,128)(2,1)S(1)} %collective-permute-done.4.refs_1_, ...), custom_call_target="tpu_custom_call" | custom-call | bytes 16236000 | tf_op jit(solution)/shard_map/pallas_call | solution.py:341
  25.4 2.6 %collective-permute-start.8 = (bf16[16,32,128]{2,1,0:T(8,128)(2,1)S(1)}, bf16[16,32,128]{2,1,0:T(8,128)(2,1)S(1)}, u32[]{:S(2)}, u32[]{:S(2)}) collective-permute-start(bf16[16,32,128]{2,1,0:T(8,128)(2,1)S(1)} %get-tuple-element.28), channel_id=1, source_target_pairs={{0,12},{1,13},{2,14},{3,15},{4,8},{5,9},{6,10},{7,11},{8,4},{9,5},... | collective-permute-start | bytes 393224 | tf_op jit(solution)/shard_map/ppermute | solution.py:252
  28.1 0.0 collective-permute-start.7
  28.1 4.0 %shard_map.113 = (bf16[16,32,128]{2,1,0:T(8,128)(2,1)S(1)}, bf16[16,32,128]{2,1,0:T(8,128)(2,1)S(1)}) custom-call(s32[1]{0:T(128)} %bitcast.me_ref, f32[4]{0:T(128)S(1)} %copy-done.4, bf16[128,384]{1,0:T(8,128)(2,1)S(1)} %get-tuple-element.19.refs_0_, bf16[128,384]{1,0:T(8,128)(2,1)S(1)} %collective-permute-done.6.refs_12_.refs_1_, ...), custom_call_target="tpu_custom_call" | custom-call | bytes 16236000 | tf_op jit(solution)/shard_map/pallas_call | solution.py:341
  32.1 1.6 %collective-permute-start.11 = (bf16[16,32,128]{2,1,0:T(8,128)(2,1)S(1)}, bf16[16,32,128]{2,1,0:T(8,128)(2,1)S(1)}, u32[]{:S(2)}, u32[]{:S(2)}) collective-permute-start(bf16[16,32,128]{2,1,0:T(8,128)(2,1)S(1)} %get-tuple-element.31), channel_id=1, source_target_pairs={{0,2},{1,3},{2,0},{3,1},{4,6},{5,7},{6,4},{7,5},{8,10},{9,11},{10,... | collective-permute-start | bytes 393224 | tf_op jit(solution)/shard_map/ppermute | solution.py:252
  33.7 0.0 collective-permute-done.5.refs_0_.refs_1_
  33.7 4.0 %shard_map.114 = (bf16[16,32,128]{2,1,0:T(8,128)(2,1)S(1)}, bf16[16,32,128]{2,1,0:T(8,128)(2,1)S(1)}) custom-call(s32[1]{0:T(128)} %bitcast.me_ref, f32[4]{0:T(128)S(1)} %copy-done.4, bf16[256,384]{1,0:T(8,128)(2,1)S(1)} %collective-permute-done.5.refs_0_.refs_1_, bf16[256,384]{1,0:T(8,128)(2,1)S(1)} %collective-permute-done.5.refs_0_.refs_1_, ...), custom_call_target="tpu_custom_call" | custom-call | bytes 16236000 | tf_op jit(solution)/shard_map/pallas_call | solution.py:341
  37.7 1.3 %collective-permute-start.13 = (bf16[16,32,128]{2,1,0:T(8,128)(2,1)S(1)}, bf16[16,32,128]{2,1,0:T(8,128)(2,1)S(1)}, u32[]{:S(2)}, u32[]{:S(2)}) collective-permute-start(bf16[16,32,128]{2,1,0:T(8,128)(2,1)S(1)} %get-tuple-element.32), channel_id=1, source_target_pairs={{0,14},{1,15},{2,12},{3,13},{4,10},{5,11},{6,8},{7,9},{8,6},{9,7},... | collective-permute-start | bytes 393224 | tf_op jit(solution)/shard_map/ppermute | solution.py:252
  38.9 2.6 %collective-permute-start.12 = (bf16[16,32,128]{2,1,0:T(8,128)(2,1)S(1)}, bf16[16,32,128]{2,1,0:T(8,128)(2,1)S(1)}, u32[]{:S(2)}, u32[]{:S(2)}) collective-permute-start(bf16[16,32,128]{2,1,0:T(8,128)(2,1)S(1)} %get-tuple-element.27.refs_12_), channel_id=1, source_target_pairs={{0,10},{1,11},{2,8},{3,9},{4,14},{5,15},{6,12},{7,13},{8,2},{9,3},... | collective-permute-start | bytes 393224 | tf_op jit(solution)/shard_map/ppermute | solution.py:252
  41.6 0.0 collective-permute-done.8.refs_14_.refs_3_
  41.6 0.0 collective-permute-done.7.refs_13_.refs_2_
  41.6 4.0 %shard_map.115 = (bf16[16,32,128]{2,1,0:T(8,128)(2,1)S(1)}, bf16[16,32,128]{2,1,0:T(8,128)(2,1)S(1)}) custom-call(s32[1]{0:T(128)} %bitcast.me_ref, f32[4]{0:T(128)S(1)} %copy-done.4, bf16[128,384]{1,0:T(8,128)(2,1)S(1)} %collective-permute-done.refs_13_.refs_0_, bf16[128,384]{1,0:T(8,128)(2,1)S(1)} %collective-permute-done.1.refs_14_.refs_1_, ...), custom_call_target="tpu_custom_call" | custom-call | bytes 16236000 | tf_op jit(solution)/shard_map/pallas_call | solution.py:341
  45.6 1.5 %collective-permute-start.9 = (bf16[16,32,128]{2,1,0:T(8,128)(2,1)S(1)}, bf16[16,32,128]{2,1,0:T(8,128)(2,1)S(1)}, u32[]{:S(2)}, u32[]{:S(2)}) collective-permute-start(bf16[16,32,128]{2,1,0:T(8,128)(2,1)S(1)} %get-tuple-element.29), channel_id=1, source_target_pairs={{0,4},{1,5},{2,6},{3,7},{4,0},{5,1},{6,2},{7,3},{8,12},{9,13},{10,... | collective-permute-start | bytes 393224 | tf_op jit(solution)/shard_map/ppermute | solution.py:252
  47.1 0.9 %collective-permute-start.10 = (bf16[16,32,128]{2,1,0:T(8,128)(2,1)S(1)}, bf16[16,32,128]{2,1,0:T(8,128)(2,1)S(1)}, u32[]{:S(2)}, u32[]{:S(2)}) collective-permute-start(bf16[16,32,128]{2,1,0:T(8,128)(2,1)S(1)} %get-tuple-element.30), channel_id=1, source_target_pairs={{0,6},{1,7},{2,4},{3,5},{4,2},{5,3},{6,0},{7,1},{8,14},{9,15},{10,... | collective-permute-start | bytes 393224 | tf_op jit(solution)/shard_map/ppermute | solution.py:252
  48.0 0.0 collective-permute-done.11.refs_1_
  48.0 0.0 collective-permute-done.13.refs_5_
  48.0 4.1 %collective-permute-done.12.refs_4_ = bf16[16,32,128]{2,1,0:T(8,128)(2,1)S(1)} collective-permute-done((bf16[16,32,128]{2,1,0:T(8,128)(2,1)S(1)}, bf16[16,32,128]{2,1,0:T(8,128)(2,1)S(1)}, u32[]{:S(2)}, u32[]{:S(2)}) %collective-permute-start.12) | collective-permute-done | bytes 131104 | tf_op jit(solution)/shard_map/ppermute | solution.py:252
  52.0 0.9 %shard_map.116.refs_2_ = bf16[128,32,128]{2,1,0:T(8,128)(2,1)} custom-call(s32[1]{0:T(128)} %bitcast.me_ref, bf16[16,32,128]{2,1,0:T(8,128)(2,1)S(1)} %get-tuple-element.26.refs_12_.refs_0_, bf16[16,32,128]{2,1,0:T(8,128)(2,1)S(1)} %collective-permute-done.11.refs_1_, bf16[16,32,128]{2,1,0:T(8,128)(2,1)S(1)} %collective-permute-done.7.refs_13_.refs_2_, ...), custom_call_target="tpu_custom_call" | custom-call | bytes 3690000 | tf_op jit(solution)/shard_map/pallas_call | solution.py:379
  53.0 0.9 %collective-permute-done.9.refs_0_ = bf16[16,32,128]{2,1,0:T(8,128)(2,1)S(1)} collective-permute-done((bf16[16,32,128]{2,1,0:T(8,128)(2,1)S(1)}, bf16[16,32,128]{2,1,0:T(8,128)(2,1)S(1)}, u32[]{:S(2)}, u32[]{:S(2)}) %collective-permute-start.9) | collective-permute-done | bytes 131104 | tf_op jit(solution)/shard_map/ppermute | solution.py:252
  53.8 1.4 %collective-permute-done.10.refs_1_ = bf16[16,32,128]{2,1,0:T(8,128)(2,1)S(1)} collective-permute-done((bf16[16,32,128]{2,1,0:T(8,128)(2,1)S(1)}, bf16[16,32,128]{2,1,0:T(8,128)(2,1)S(1)}, u32[]{:S(2)}, u32[]{:S(2)}) %collective-permute-start.10) | collective-permute-done | bytes 131104 | tf_op jit(solution)/shard_map/ppermute | solution.py:252
  55.2 0.7 %shard_map.117 = bf16[128,32,128]{2,1,0:T(8,128)(2,1)} custom-call(s32[1]{0:T(128)} %bitcast.me_ref, bf16[16,32,128]{2,1,0:T(8,128)(2,1)S(1)} %collective-permute-done.9.refs_0_, bf16[16,32,128]{2,1,0:T(8,128)(2,1)S(1)} %collective-permute-done.10.refs_1_, bf16[128,32,128]{2,1,0:T(8,128)(2,1)} %shard_map.116.refs_2_), custom_call_target="tpu_custom_call", output_to_operand_aliasing={{}: (3, {})} | custom-call | bytes 3690000 | tf_op jit(solution)/shard_map/pallas_call | solution.py:379
  (1 shorter events, 0.0 us)
Async XLA Ops:
  0.0 14.3 %copy-start = (bf16[128,512]{1,0:T(8,128)(2,1)S(1)}, bf16[128,512]{1,0:T(8,128)(2,1)}, u32[]{:S(2)}) copy-start(bf16[128,512]{1,0:T(8,128)(2,1)} %refs_9_.7) | copy-start | bytes 393220
  5.6 7.3 %collective-permute-start.2 = (bf16[8,512,128]{2,1,0:T(8,128)(2,1)S(1)}, bf16[8,512,128]{2,1,0:T(8,128)(2,1)S(1)}, u32[]{:S(2)}, u32[]{:S(2)}) collective-permute-start(bf16[8,512,128]{2,1,0:T(8,128)(2,1)S(1)} %get-tuple-element.20.own_ref), channel_id=1, source_target_pairs={{0,1},{1,0},{2,3},{3,2},{4,5},{5,4},{6,7},{7,6},{8,9},{9,8},{10,11... | collective-permute-start | bytes 3145736 | tf_op jit(solution)/shard_map/ppermute | solution.py:252
  6.1 10.5 %collective-permute-start.4 = (bf16[128,384]{1,0:T(8,128)(2,1)S(1)}, bf16[128,384]{1,0:T(8,128)(2,1)S(1)}, u32[]{:S(2)}, u32[]{:S(2)}) collective-permute-start(bf16[128,384]{1,0:T(8,128)(2,1)S(1)} %get-tuple-element.19.refs_0_), channel_id=1, source_target_pairs={{0,12},{1,13},{2,14},{3,15},{4,8},{5,9},{6,10},{7,11},{8,4},{9,5},... | collective-permute-start | bytes 294920 | tf_op jit(solution)/shard_map/ppermute | solution.py:252
  10.8 9.0 %collective-permute-start.3 = (bf16[128,384]{1,0:T(8,128)(2,1)S(1)}, bf16[128,384]{1,0:T(8,128)(2,1)S(1)}, u32[]{:S(2)}, u32[]{:S(2)}) collective-permute-start(bf16[128,384]{1,0:T(8,128)(2,1)S(1)} %get-tuple-element.19.refs_0_), channel_id=1, source_target_pairs={{0,8},{1,9},{2,10},{3,11},{4,12},{5,13},{6,14},{7,15},{8,0},{9,1},... | collective-permute-start | bytes 294920 | tf_op jit(solution)/shard_map/ppermute | solution.py:252
  10.8 10.6 %collective-permute-start.6 = (bf16[128,384]{1,0:T(8,128)(2,1)S(1)}, bf16[128,384]{1,0:T(8,128)(2,1)S(1)}, u32[]{:S(2)}, u32[]{:S(2)}) collective-permute-start(bf16[128,384]{1,0:T(8,128)(2,1)S(1)} %get-tuple-element.19.refs_0_), channel_id=1, source_target_pairs={{0,2},{1,3},{2,0},{3,1},{4,6},{5,7},{6,4},{7,5},{8,10},{9,11},{10,... | collective-permute-start | bytes 294920 | tf_op jit(solution)/shard_map/ppermute | solution.py:252
  12.3 9.1 %collective-permute-start.1 = (bf16[128,384]{1,0:T(8,128)(2,1)S(1)}, bf16[128,384]{1,0:T(8,128)(2,1)S(1)}, u32[]{:S(2)}, u32[]{:S(2)}) collective-permute-start(bf16[128,384]{1,0:T(8,128)(2,1)S(1)} %get-tuple-element.19.refs_0_), channel_id=1, source_target_pairs={{0,6},{1,7},{2,4},{3,5},{4,2},{5,3},{6,0},{7,1},{8,14},{9,15},{10,... | collective-permute-start | bytes 294920 | tf_op jit(solution)/shard_map/ppermute | solution.py:252
  12.9 8.5 %collective-permute-start = (bf16[128,384]{1,0:T(8,128)(2,1)S(1)}, bf16[128,384]{1,0:T(8,128)(2,1)S(1)}, u32[]{:S(2)}, u32[]{:S(2)}) collective-permute-start(bf16[128,384]{1,0:T(8,128)(2,1)S(1)} %get-tuple-element.19.refs_0_), channel_id=1, source_target_pairs={{0,4},{1,5},{2,6},{3,7},{4,0},{5,1},{6,2},{7,3},{8,12},{9,13},{10,... | collective-permute-start | bytes 294920 | tf_op jit(solution)/shard_map/ppermute | solution.py:252
  16.5 4.8 %copy-start.1 = (bf16[128,128]{1,0:T(8,128)(2,1)S(1)}, bf16[128,128]{1,0:T(8,128)(2,1)}, u32[]{:S(2)}) copy-start(bf16[128,128]{1,0:T(8,128)(2,1)} %refs_11_.7) | copy-start | bytes 98308
  16.6 4.8 %copy-start.2 = (s32[512]{0:T(512)S(1)}, s32[512]{0:T(512)}, u32[]{:S(2)}) copy-start(s32[512]{0:T(512)} %param.13) | copy-start | bytes 6148
  16.6 4.8 %copy-start.3 = (s32[512]{0:T(512)S(1)}, s32[512]{0:T(512)}, u32[]{:S(2)}) copy-start(s32[512]{0:T(512)} %param.14) | copy-start | bytes 6148
  16.6 4.8 %copy-start.4 = (f32[4]{0:T(128)S(1)}, f32[4]{0:T(128)}, u32[]{:S(2)}) copy-start(f32[4]{0:T(128)} %chain_bias_ref.7) | copy-start | bytes 52
  16.6 4.8 %copy-start.5 = (f32[128]{0:T(128)S(1)}, f32[128]{0:T(128)}, u32[]{:S(2)}) copy-start(f32[128]{0:T(128)} %param.18) | copy-start | bytes 1540
  19.8 13.9 %collective-permute-start.5 = (bf16[256,384]{1,0:T(8,128)(2,1)S(1)}, bf16[256,384]{1,0:T(8,128)(2,1)S(1)}, u32[]{:S(2)}, u32[]{:S(2)}) collective-permute-start(bf16[256,384]{1,0:T(8,128)(2,1)S(1)} %shard_map.111), channel_id=1, source_target_pairs={{0,2},{1,3},{2,0},{3,1},{4,6},{5,7},{6,4},{7,5},{8,10},{9,11},{10,... | collective-permute-start | bytes 589832 | tf_op jit(solution)/shard_map/ppermute | solution.py:252
  25.4 16.1 %collective-permute-start.8 = (bf16[16,32,128]{2,1,0:T(8,128)(2,1)S(1)}, bf16[16,32,128]{2,1,0:T(8,128)(2,1)S(1)}, u32[]{:S(2)}, u32[]{:S(2)}) collective-permute-start(bf16[16,32,128]{2,1,0:T(8,128)(2,1)S(1)} %get-tuple-element.28), channel_id=1, source_target_pairs={{0,12},{1,13},{2,14},{3,15},{4,8},{5,9},{6,10},{7,11},{8,4},{9,5},... | collective-permute-start | bytes 393224 | tf_op jit(solution)/shard_map/ppermute | solution.py:252
  28.1 13.5 %collective-permute-start.7 = (bf16[16,32,128]{2,1,0:T(8,128)(2,1)S(1)}, bf16[16,32,128]{2,1,0:T(8,128)(2,1)S(1)}, u32[]{:S(2)}, u32[]{:S(2)}) collective-permute-start(bf16[16,32,128]{2,1,0:T(8,128)(2,1)S(1)} %get-tuple-element.25.refs_12_), channel_id=1, source_target_pairs={{0,8},{1,9},{2,10},{3,11},{4,12},{5,13},{6,14},{7,15},{8,0},{9,1},... | collective-permute-start | bytes 393224 | tf_op jit(solution)/shard_map/ppermute | solution.py:252
  32.1 15.9 %collective-permute-start.11 = (bf16[16,32,128]{2,1,0:T(8,128)(2,1)S(1)}, bf16[16,32,128]{2,1,0:T(8,128)(2,1)S(1)}, u32[]{:S(2)}, u32[]{:S(2)}) collective-permute-start(bf16[16,32,128]{2,1,0:T(8,128)(2,1)S(1)} %get-tuple-element.31), channel_id=1, source_target_pairs={{0,2},{1,3},{2,0},{3,1},{4,6},{5,7},{6,4},{7,5},{8,10},{9,11},{10,... | collective-permute-start | bytes 393224 | tf_op jit(solution)/shard_map/ppermute | solution.py:252
  37.7 10.3 %collective-permute-start.13 = (bf16[16,32,128]{2,1,0:T(8,128)(2,1)S(1)}, bf16[16,32,128]{2,1,0:T(8,128)(2,1)S(1)}, u32[]{:S(2)}, u32[]{:S(2)}) collective-permute-start(bf16[16,32,128]{2,1,0:T(8,128)(2,1)S(1)} %get-tuple-element.32), channel_id=1, source_target_pairs={{0,14},{1,15},{2,12},{3,13},{4,10},{5,11},{6,8},{7,9},{8,6},{9,7},... | collective-permute-start | bytes 393224 | tf_op jit(solution)/shard_map/ppermute | solution.py:252
  38.9 13.1 %collective-permute-start.12 = (bf16[16,32,128]{2,1,0:T(8,128)(2,1)S(1)}, bf16[16,32,128]{2,1,0:T(8,128)(2,1)S(1)}, u32[]{:S(2)}, u32[]{:S(2)}) collective-permute-start(bf16[16,32,128]{2,1,0:T(8,128)(2,1)S(1)} %get-tuple-element.27.refs_12_), channel_id=1, source_target_pairs={{0,10},{1,11},{2,8},{3,9},{4,14},{5,15},{6,12},{7,13},{8,2},{9,3},... | collective-permute-start | bytes 393224 | tf_op jit(solution)/shard_map/ppermute | solution.py:252
  45.6 8.3 %collective-permute-start.9 = (bf16[16,32,128]{2,1,0:T(8,128)(2,1)S(1)}, bf16[16,32,128]{2,1,0:T(8,128)(2,1)S(1)}, u32[]{:S(2)}, u32[]{:S(2)}) collective-permute-start(bf16[16,32,128]{2,1,0:T(8,128)(2,1)S(1)} %get-tuple-element.29), channel_id=1, source_target_pairs={{0,4},{1,5},{2,6},{3,7},{4,0},{5,1},{6,2},{7,3},{8,12},{9,13},{10,... | collective-permute-start | bytes 393224 | tf_op jit(solution)/shard_map/ppermute | solution.py:252
  47.1 8.1 %collective-permute-start.10 = (bf16[16,32,128]{2,1,0:T(8,128)(2,1)S(1)}, bf16[16,32,128]{2,1,0:T(8,128)(2,1)S(1)}, u32[]{:S(2)}, u32[]{:S(2)}) collective-permute-start(bf16[16,32,128]{2,1,0:T(8,128)(2,1)S(1)} %get-tuple-element.30), channel_id=1, source_target_pairs={{0,6},{1,7},{2,4},{3,5},{4,2},{5,3},{6,0},{7,1},{8,14},{9,15},{10,... | collective-permute-start | bytes 393224 | tf_op jit(solution)/shard_map/ppermute | solution.py:252

commit v9 on v8

--- a/solution.py
+++ b/solution.py
@@ -328,13 +328,15 @@
     for m in passed:
         biases[m] = straight
     sent = {}
-    for ms in (far, [0] + near[:1], passed, near[1:]):
+    for ms in (far, passed, near[1:], [0] + near[:1]):
         if ms == far:
-            after = [biases[m] for m in near]
+            after = [biases[near[0]]]
+        elif ms == passed:
+            after = [updates[far[0]]]
         elif ms == near[1:]:
-            after = [updates[passed[0]]] + [sent[m] for m in far]
+            after = [updates[m] for m in passed]
         else:
-            after = [updates[far[0] if 0 in ms else 0]]
+            after = [updates[near[1]], sent[far[0]]]
         blocks = len(ms)
         first = [i * heads * rows_held if ms == passed else 0 for i in range(blocks)]
         rows = 2 * count * rows_held
@@ -373,7 +375,7 @@
             sent[m] = out if m == 0 else swap(out, 2 * m)
 
     whole = []
-    for order in ([0] + near[:1] + far + passed, near[1:]):
+    for order in (near[1:] + far + passed, [0] + near[:1]):
         placed = len(order)
         whole = [
             pl.pallas_call(

time: 56.1 us -> 57 us (1.016)
  starting transfers between devices: 20.8 us -> 21.4 us
    ppermute x14, starting transfers between devices: 20.8 us -> 21.4 us  [swap(): return lax.ppermute(x, 'row', [(i, i ^ bits) for i in range(devices)])]
where the time goes in v9:
time: 57 us; the launch traced here: 56.9 us
  Pallas kernels  25.5 us (45%)
  starting transfers between devices  21.4 us (38%)
  waiting for transfers between devices  9.77 us (17%)
    ppermute x14, starting transfers between devices, swap(): return lax.ppermute(x, 'row', [(i, i ^ bits) for i in range(devices)])  21.4 us
    pallas_call x4, Pallas kernels, local(): pl.pallas_call(functools.partial(attention_kernel, heads, ms, first), out...  16 us
    ppermute x14, waiting for transfers between devices, swap(): return lax.ppermute(x, 'row', [(i, i ^ bits) for i in range(devices)])  9.77 us
    pallas_call x1, Pallas kernels, local(): pl.pallas_call(bias_kernel, grid=(rows_held // step_rows,), out_shape=[ja...  5.57 us
    pallas_call x1, Pallas kernels, local(): pl.pallas_call(key_value_kernel, out_shape=[jax.ShapeDtypeStruct((2 * cou...  2.27 us
    pallas_call x2, Pallas kernels, local(): pl.pallas_call(functools.partial(gather_kernel, order), out_shape=jax.Sha...  1.64 us
  transfers between devices with their start and end apart: 14, of which 4 were waited for; matrix products, arithmetic and copies ran while one was open for 0% of the time, Pallas kernels for 34%

profile of v9, /device:TPU:0, one launch (start us, length us, event | category | flops | bytes accessed | tf_op | source)
XLA Modules:
  0.0 56.9 jit_solution(6941352318952577967)
XLA Ops:
  0.0 0.0 copy-start
  0.0 5.6 %shard_map.109 = (bf16[128,384]{1,0:T(8,128)(2,1)S(1)}, bf16[8,512,128]{2,1,0:T(8,128)(2,1)S(1)}, bf16[384,512]{1,0:T(8,128)(2,1)S(1)}, f32[8,384]{1,0:T(8,128)S(1)}) custom-call(s32[1]{0:T(128)} %bitcast.me_ref, s32[8]{0:T(128)} %rows_ref.1, bf16[32,512,128]{2,1,0:T(8,128)(2,1)} %pair_ref.1, s32[1,512]{1,0:T(1,128)} %bitcast.17, s32[1,512]{1,0:T(1,128)} %bitcast.22, ...), custom_call_target="tpu_custom_call" | custom-call | bytes 22140000 | tf_op jit(solution)/shard_map/pallas_call | solution.py:255
  5.6 0.5 collective-permute-start.1
  6.1 4.7 %collective-permute-start.5 = (bf16[128,384]{1,0:T(8,128)(2,1)S(1)}, bf16[128,384]{1,0:T(8,128)(2,1)S(1)}, u32[]{:S(2)}, u32[]{:S(2)}) collective-permute-start(bf16[128,384]{1,0:T(8,128)(2,1)S(1)} %get-tuple-element.19.refs_0_), channel_id=1, source_target_pairs={{0,12},{1,13},{2,14},{3,15},{4,8},{5,9},{6,10},{7,11},{8,4},{9,5},... | collective-permute-start | bytes 294920 | tf_op jit(solution)/shard_map/ppermute | solution.py:252
  10.8 0.0 collective-permute-start.4
  10.8 1.5 %collective-permute-start = (bf16[128,384]{1,0:T(8,128)(2,1)S(1)}, bf16[128,384]{1,0:T(8,128)(2,1)S(1)}, u32[]{:S(2)}, u32[]{:S(2)}) collective-permute-start(bf16[128,384]{1,0:T(8,128)(2,1)S(1)} %get-tuple-element.19.refs_0_), channel_id=1, source_target_pairs={{0,2},{1,3},{2,0},{3,1},{4,6},{5,7},{6,4},{7,5},{8,10},{9,11},{10,... | collective-permute-start | bytes 294920 | tf_op jit(solution)/shard_map/ppermute | solution.py:252
  12.3 0.0 collective-permute-done.1.other_ref
  12.3 0.0 copy-done
  12.3 2.3 %shard_map.110 = (bf16[16,128,384]{2,1,0:T(8,128)(2,1)S(1)}, bf16[16,384,128]{2,1,0:T(8,128)(2,1)S(1)}) custom-call(bf16[8,512,128]{2,1,0:T(8,128)(2,1)S(1)} %get-tuple-element.20.own_ref, bf16[8,512,128]{2,1,0:T(8,128)(2,1)S(1)} %collective-permute-done.1.other_ref, bf16[384,512]{1,0:T(8,128)(2,1)S(1)} %get-tuple-element.21.pick_ref, ...), custom_call_target="tpu_custom_call" | custom-call | bytes 7380000 | tf_op jit(solution)/shard_map/pallas_call | solution.py:304
  14.6 0.0 copy-start.1
  14.6 0.0 copy-start.2
  14.6 0.0 copy-start.3
  14.6 0.0 copy-start.4
  14.6 0.0 copy-start.5
  14.6 0.0 collective-permute-done.5.refs_1_
  14.6 5.0 %collective-permute-done.4.refs_0_ = bf16[128,384]{1,0:T(8,128)(2,1)S(1)} collective-permute-done((bf16[128,384]{1,0:T(8,128)(2,1)S(1)}, bf16[128,384]{1,0:T(8,128)(2,1)S(1)}, u32[]{:S(2)}, u32[]{:S(2)}) %collective-permute-start.4) | collective-permute-done | bytes 98336 | tf_op jit(solution)/shard_map/ppermute | solution.py:252
  19.7 1.6 %collective-permute-start.6 = (bf16[256,384]{1,0:T(8,128)(2,1)S(1)}, bf16[256,384]{1,0:T(8,128)(2,1)S(1)}, u32[]{:S(2)}, u32[]{:S(2)}) collective-permute-start(bf16[256,384]{1,0:T(8,128)(2,1)S(1)} %shard_map.111), channel_id=1, source_target_pairs={{0,2},{1,3},{2,0},{3,1},{4,6},{5,7},{6,4},{7,5},{8,10},{9,11},{10,... | collective-permute-start | bytes 589832 | tf_op jit(solution)/shard_map/ppermute | solution.py:252
  21.3 0.0 collective-permute-done.refs_12_.refs_1_
  21.3 0.0 copy-done.1
  21.3 0.0 copy-done.2
  21.3 0.0 copy-done.3
  21.3 0.0 copy-done.4
  21.3 0.0 copy-done.5
  21.3 4.0 %shard_map.112 = (bf16[16,32,128]{2,1,0:T(8,128)(2,1)S(1)}, bf16[16,32,128]{2,1,0:T(8,128)(2,1)S(1)}) custom-call(s32[1]{0:T(128)} %bitcast.me_ref, f32[4]{0:T(128)S(1)} %copy-done.4, bf16[128,384]{1,0:T(8,128)(2,1)S(1)} %collective-permute-done.4.refs_0_, bf16[128,384]{1,0:T(8,128)(2,1)S(1)} %collective-permute-done.5.refs_1_, ...), custom_call_target="tpu_custom_call" | custom-call | bytes 16236000 | tf_op jit(solution)/shard_map/pallas_call | solution.py:343
  25.3 0.1 collective-permute-start.7
  25.4 2.5 %collective-permute-start.11 = (bf16[16,32,128]{2,1,0:T(8,128)(2,1)S(1)}, bf16[16,32,128]{2,1,0:T(8,128)(2,1)S(1)}, u32[]{:S(2)}, u32[]{:S(2)}) collective-permute-start(bf16[16,32,128]{2,1,0:T(8,128)(2,1)S(1)} %get-tuple-element.32), channel_id=1, source_target_pairs={{0,12},{1,13},{2,14},{3,15},{4,8},{5,9},{6,10},{7,11},{8,4},{9,5},... | collective-permute-start | bytes 393224 | tf_op jit(solution)/shard_map/ppermute | solution.py:252
  27.9 0.9 %collective-permute-start.3 = (bf16[128,384]{1,0:T(8,128)(2,1)S(1)}, bf16[128,384]{1,0:T(8,128)(2,1)S(1)}, u32[]{:S(2)}, u32[]{:S(2)}) collective-permute-start(bf16[128,384]{1,0:T(8,128)(2,1)S(1)} %get-tuple-element.19.refs_0_), channel_id=1, source_target_pairs={{0,6},{1,7},{2,4},{3,5},{4,2},{5,3},{6,0},{7,1},{8,14},{9,15},{10,... | collective-permute-start | bytes 294920 | tf_op jit(solution)/shard_map/ppermute | solution.py:252
  28.8 1.1 %collective-permute-start.2 = (bf16[128,384]{1,0:T(8,128)(2,1)S(1)}, bf16[128,384]{1,0:T(8,128)(2,1)S(1)}, u32[]{:S(2)}, u32[]{:S(2)}) collective-permute-start(bf16[128,384]{1,0:T(8,128)(2,1)S(1)} %get-tuple-element.19.refs_0_), channel_id=1, source_target_pairs={{0,4},{1,5},{2,6},{3,7},{4,0},{5,1},{6,2},{7,3},{8,12},{9,13},{10,... | collective-permute-start | bytes 294920 | tf_op jit(solution)/shard_map/ppermute | solution.py:252
  29.9 0.0 collective-permute-done.6.refs_0_.refs_1_
  29.9 4.0 %shard_map.113 = (bf16[16,32,128]{2,1,0:T(8,128)(2,1)S(1)}, bf16[16,32,128]{2,1,0:T(8,128)(2,1)S(1)}) custom-call(s32[1]{0:T(128)} %bitcast.me_ref, f32[4]{0:T(128)S(1)} %copy-done.4, bf16[256,384]{1,0:T(8,128)(2,1)S(1)} %collective-permute-done.6.refs_0_.refs_1_, bf16[256,384]{1,0:T(8,128)(2,1)S(1)} %collective-permute-done.6.refs_0_.refs_1_, ...), custom_call_target="tpu_custom_call" | custom-call | bytes 16236000 | tf_op jit(solution)/shard_map/pallas_call | solution.py:343
  33.9 3.0 %collective-permute-start.12 = (bf16[16,32,128]{2,1,0:T(8,128)(2,1)S(1)}, bf16[16,32,128]{2,1,0:T(8,128)(2,1)S(1)}, u32[]{:S(2)}, u32[]{:S(2)}) collective-permute-start(bf16[16,32,128]{2,1,0:T(8,128)(2,1)S(1)} %get-tuple-element.26.refs_12_), channel_id=1, source_target_pairs={{0,10},{1,11},{2,8},{3,9},{4,14},{5,15},{6,12},{7,13},{8,2},{9,3},... | collective-permute-start | bytes 393224 | tf_op jit(solution)/shard_map/ppermute | solution.py:252
  36.9 1.8 %collective-permute-done.3.refs_1_ = bf16[128,384]{1,0:T(8,128)(2,1)S(1)} collective-permute-done((bf16[128,384]{1,0:T(8,128)(2,1)S(1)}, bf16[128,384]{1,0:T(8,128)(2,1)S(1)}, u32[]{:S(2)}, u32[]{:S(2)}) %collective-permute-start.3) | collective-permute-done | bytes 98336 | tf_op jit(solution)/shard_map/ppermute | solution.py:252
  38.7 1.9 %collective-permute-start.13 = (bf16[16,32,128]{2,1,0:T(8,128)(2,1)S(1)}, bf16[16,32,128]{2,1,0:T(8,128)(2,1)S(1)}, u32[]{:S(2)}, u32[]{:S(2)}) collective-permute-start(bf16[16,32,128]{2,1,0:T(8,128)(2,1)S(1)} %get-tuple-element.27.refs_13_), channel_id=1, source_target_pairs={{0,14},{1,15},{2,12},{3,13},{4,10},{5,11},{6,8},{7,9},{8,6},{9,7},... | collective-permute-start | bytes 393224 | tf_op jit(solution)/shard_map/ppermute | solution.py:252
  40.7 0.0 collective-permute-done.2.refs_0_
  40.7 4.0 %shard_map.114 = (bf16[16,32,128]{2,1,0:T(8,128)(2,1)S(1)}, bf16[16,32,128]{2,1,0:T(8,128)(2,1)S(1)}) custom-call(s32[1]{0:T(128)} %bitcast.me_ref, f32[4]{0:T(128)S(1)} %copy-done.4, bf16[128,384]{1,0:T(8,128)(2,1)S(1)} %collective-permute-done.2.refs_0_, bf16[128,384]{1,0:T(8,128)(2,1)S(1)} %collective-permute-done.3.refs_1_, ...), custom_call_target="tpu_custom_call" | custom-call | bytes 16236000 | tf_op jit(solution)/shard_map/pallas_call | solution.py:343
  44.7 0.1 collective-permute-start.10
  44.7 0.0 collective-permute-done.7.refs_13_.refs_2_
  44.8 2.3 %collective-permute-start.9 = (bf16[16,32,128]{2,1,0:T(8,128)(2,1)S(1)}, bf16[16,32,128]{2,1,0:T(8,128)(2,1)S(1)}, u32[]{:S(2)}, u32[]{:S(2)}) collective-permute-start(bf16[16,32,128]{2,1,0:T(8,128)(2,1)S(1)} %get-tuple-element.28.refs_12_), channel_id=1, source_target_pairs={{0,4},{1,5},{2,6},{3,7},{4,0},{5,1},{6,2},{7,3},{8,12},{9,13},{10,... | collective-permute-start | bytes 393224 | tf_op jit(solution)/shard_map/ppermute | solution.py:252
  47.1 4.0 %shard_map.115 = (bf16[16,32,128]{2,1,0:T(8,128)(2,1)S(1)}, bf16[16,32,128]{2,1,0:T(8,128)(2,1)S(1)}) custom-call(s32[1]{0:T(128)} %bitcast.me_ref, f32[4]{0:T(128)S(1)} %copy-done.4, bf16[128,384]{1,0:T(8,128)(2,1)S(1)} %get-tuple-element.19.refs_0_, bf16[128,384]{1,0:T(8,128)(2,1)S(1)} %collective-permute-done.refs_12_.refs_1_, ...), custom_call_target="tpu_custom_call" | custom-call | bytes 16236000 | tf_op jit(solution)/shard_map/pallas_call | solution.py:343
  51.1 0.0 collective-permute-done.11.refs_3_
  51.1 1.2 %collective-permute-start.8 = (bf16[16,32,128]{2,1,0:T(8,128)(2,1)S(1)}, bf16[16,32,128]{2,1,0:T(8,128)(2,1)S(1)}, u32[]{:S(2)}, u32[]{:S(2)}) collective-permute-start(bf16[16,32,128]{2,1,0:T(8,128)(2,1)S(1)} %get-tuple-element.30), channel_id=1, source_target_pairs={{0,2},{1,3},{2,0},{3,1},{4,6},{5,7},{6,4},{7,5},{8,10},{9,11},{10,... | collective-permute-start | bytes 393224 | tf_op jit(solution)/shard_map/ppermute | solution.py:252
  52.3 0.0 collective-permute-done.10.refs_1_
  52.3 1.1 %collective-permute-done.9.refs_0_ = bf16[16,32,128]{2,1,0:T(8,128)(2,1)S(1)} collective-permute-done((bf16[16,32,128]{2,1,0:T(8,128)(2,1)S(1)}, bf16[16,32,128]{2,1,0:T(8,128)(2,1)S(1)}, u32[]{:S(2)}, u32[]{:S(2)}) %collective-permute-start.9) | collective-permute-done | bytes 131104 | tf_op jit(solution)/shard_map/ppermute | solution.py:252
  53.4 0.0 collective-permute-done.12.refs_4_
  53.4 0.0 collective-permute-done.13.refs_5_
  53.4 0.9 %shard_map.116.refs_2_ = bf16[128,32,128]{2,1,0:T(8,128)(2,1)} custom-call(s32[1]{0:T(128)} %bitcast.me_ref, bf16[16,32,128]{2,1,0:T(8,128)(2,1)S(1)} %collective-permute-done.9.refs_0_, bf16[16,32,128]{2,1,0:T(8,128)(2,1)S(1)} %collective-permute-done.10.refs_1_, bf16[16,32,128]{2,1,0:T(8,128)(2,1)S(1)} %collective-permute-done.7.refs_13_.refs_2_, ...), custom_call_target="tpu_custom_call" | custom-call | bytes 3690000 | tf_op jit(solution)/shard_map/pallas_call | solution.py:381
  54.4 1.8 %collective-permute-done.8.refs_1_ = bf16[16,32,128]{2,1,0:T(8,128)(2,1)S(1)} collective-permute-done((bf16[16,32,128]{2,1,0:T(8,128)(2,1)S(1)}, bf16[16,32,128]{2,1,0:T(8,128)(2,1)S(1)}, u32[]{:S(2)}, u32[]{:S(2)}) %collective-permute-start.8) | collective-permute-done | bytes 131104 | tf_op jit(solution)/shard_map/ppermute | solution.py:252
  56.1 0.7 %shard_map.117 = bf16[128,32,128]{2,1,0:T(8,128)(2,1)} custom-call(s32[1]{0:T(128)} %bitcast.me_ref, bf16[16,32,128]{2,1,0:T(8,128)(2,1)S(1)} %get-tuple-element.29.refs_0_, bf16[16,32,128]{2,1,0:T(8,128)(2,1)S(1)} %collective-permute-done.8.refs_1_, bf16[128,32,128]{2,1,0:T(8,128)(2,1)} %shard_map.116.refs_2_), custom_call_target="tpu_custom_call", output_to_operand_aliasing={{}: (3, {})} | custom-call | bytes 3690000 | tf_op jit(solution)/shard_map/pallas_call | solution.py:381
  (1 shorter events, 0.0 us)
Async XLA Ops:
  0.0 12.3 %copy-start = (bf16[128,512]{1,0:T(8,128)(2,1)S(1)}, bf16[128,512]{1,0:T(8,128)(2,1)}, u32[]{:S(2)}) copy-start(bf16[128,512]{1,0:T(8,128)(2,1)} %refs_9_.7) | copy-start | bytes 393220
  5.6 6.7 %collective-permute-start.1 = (bf16[8,512,128]{2,1,0:T(8,128)(2,1)S(1)}, bf16[8,512,128]{2,1,0:T(8,128)(2,1)S(1)}, u32[]{:S(2)}, u32[]{:S(2)}) collective-permute-start(bf16[8,512,128]{2,1,0:T(8,128)(2,1)S(1)} %get-tuple-element.20.own_ref), channel_id=1, source_target_pairs={{0,1},{1,0},{2,3},{3,2},{4,5},{5,4},{6,7},{7,6},{8,9},{9,8},{10,11... | collective-permute-start | bytes 3145736 | tf_op jit(solution)/shard_map/ppermute | solution.py:252
  6.1 8.5 %collective-permute-start.5 = (bf16[128,384]{1,0:T(8,128)(2,1)S(1)}, bf16[128,384]{1,0:T(8,128)(2,1)S(1)}, u32[]{:S(2)}, u32[]{:S(2)}) collective-permute-start(bf16[128,384]{1,0:T(8,128)(2,1)S(1)} %get-tuple-element.19.refs_0_), channel_id=1, source_target_pairs={{0,12},{1,13},{2,14},{3,15},{4,8},{5,9},{6,10},{7,11},{8,4},{9,5},... | collective-permute-start | bytes 294920 | tf_op jit(solution)/shard_map/ppermute | solution.py:252
  10.8 8.9 %collective-permute-start.4 = (bf16[128,384]{1,0:T(8,128)(2,1)S(1)}, bf16[128,384]{1,0:T(8,128)(2,1)S(1)}, u32[]{:S(2)}, u32[]{:S(2)}) collective-permute-start(bf16[128,384]{1,0:T(8,128)(2,1)S(1)} %get-tuple-element.19.refs_0_), channel_id=1, source_target_pairs={{0,8},{1,9},{2,10},{3,11},{4,12},{5,13},{6,14},{7,15},{8,0},{9,1},... | collective-permute-start | bytes 294920 | tf_op jit(solution)/shard_map/ppermute | solution.py:252
  10.8 10.5 %collective-permute-start = (bf16[128,384]{1,0:T(8,128)(2,1)S(1)}, bf16[128,384]{1,0:T(8,128)(2,1)S(1)}, u32[]{:S(2)}, u32[]{:S(2)}) collective-permute-start(bf16[128,384]{1,0:T(8,128)(2,1)S(1)} %get-tuple-element.19.refs_0_), channel_id=1, source_target_pairs={{0,2},{1,3},{2,0},{3,1},{4,6},{5,7},{6,4},{7,5},{8,10},{9,11},{10,... | collective-permute-start | bytes 294920 | tf_op jit(solution)/shard_map/ppermute | solution.py:252
  14.6 6.7 %copy-start.1 = (bf16[128,128]{1,0:T(8,128)(2,1)S(1)}, bf16[128,128]{1,0:T(8,128)(2,1)}, u32[]{:S(2)}) copy-start(bf16[128,128]{1,0:T(8,128)(2,1)} %refs_11_.7) | copy-start | bytes 98308
  14.6 6.7 %copy-start.2 = (s32[512]{0:T(512)S(1)}, s32[512]{0:T(512)}, u32[]{:S(2)}) copy-start(s32[512]{0:T(512)} %param.13) | copy-start | bytes 6148
  14.6 6.7 %copy-start.3 = (s32[512]{0:T(512)S(1)}, s32[512]{0:T(512)}, u32[]{:S(2)}) copy-start(s32[512]{0:T(512)} %param.14) | copy-start | bytes 6148
  14.6 6.7 %copy-start.4 = (f32[4]{0:T(128)S(1)}, f32[4]{0:T(128)}, u32[]{:S(2)}) copy-start(f32[4]{0:T(128)} %chain_bias_ref.7) | copy-start | bytes 52
  14.6 6.7 %copy-start.5 = (f32[128]{0:T(128)S(1)}, f32[128]{0:T(128)}, u32[]{:S(2)}) copy-start(f32[128]{0:T(128)} %param.18) | copy-start | bytes 1540
  19.7 10.2 %collective-permute-start.6 = (bf16[256,384]{1,0:T(8,128)(2,1)S(1)}, bf16[256,384]{1,0:T(8,128)(2,1)S(1)}, u32[]{:S(2)}, u32[]{:S(2)}) collective-permute-start(bf16[256,384]{1,0:T(8,128)(2,1)S(1)} %shard_map.111), channel_id=1, source_target_pairs={{0,2},{1,3},{2,0},{3,1},{4,6},{5,7},{6,4},{7,5},{8,10},{9,11},{10,... | collective-permute-start | bytes 589832 | tf_op jit(solution)/shard_map/ppermute | solution.py:252
  25.3 19.4 %collective-permute-start.7 = (bf16[16,32,128]{2,1,0:T(8,128)(2,1)S(1)}, bf16[16,32,128]{2,1,0:T(8,128)(2,1)S(1)}, u32[]{:S(2)}, u32[]{:S(2)}) collective-permute-start(bf16[16,32,128]{2,1,0:T(8,128)(2,1)S(1)} %get-tuple-element.25.refs_12_), channel_id=1, source_target_pairs={{0,8},{1,9},{2,10},{3,11},{4,12},{5,13},{6,14},{7,15},{8,0},{9,1},... | collective-permute-start | bytes 393224 | tf_op jit(solution)/shard_map/ppermute | solution.py:252
  25.4 25.7 %collective-permute-start.11 = (bf16[16,32,128]{2,1,0:T(8,128)(2,1)S(1)}, bf16[16,32,128]{2,1,0:T(8,128)(2,1)S(1)}, u32[]{:S(2)}, u32[]{:S(2)}) collective-permute-start(bf16[16,32,128]{2,1,0:T(8,128)(2,1)S(1)} %get-tuple-element.32), channel_id=1, source_target_pairs={{0,12},{1,13},{2,14},{3,15},{4,8},{5,9},{6,10},{7,11},{8,4},{9,5},... | collective-permute-start | bytes 393224 | tf_op jit(solution)/shard_map/ppermute | solution.py:252
  27.9 10.8 %collective-permute-start.3 = (bf16[128,384]{1,0:T(8,128)(2,1)S(1)}, bf16[128,384]{1,0:T(8,128)(2,1)S(1)}, u32[]{:S(2)}, u32[]{:S(2)}) collective-permute-start(bf16[128,384]{1,0:T(8,128)(2,1)S(1)} %get-tuple-element.19.refs_0_), channel_id=1, source_target_pairs={{0,6},{1,7},{2,4},{3,5},{4,2},{5,3},{6,0},{7,1},{8,14},{9,15},{10,... | collective-permute-start | bytes 294920 | tf_op jit(solution)/shard_map/ppermute | solution.py:252
  28.8 11.9 %collective-permute-start.2 = (bf16[128,384]{1,0:T(8,128)(2,1)S(1)}, bf16[128,384]{1,0:T(8,128)(2,1)S(1)}, u32[]{:S(2)}, u32[]{:S(2)}) collective-permute-start(bf16[128,384]{1,0:T(8,128)(2,1)S(1)} %get-tuple-element.19.refs_0_), channel_id=1, source_target_pairs={{0,4},{1,5},{2,6},{3,7},{4,0},{5,1},{6,2},{7,3},{8,12},{9,13},{10,... | collective-permute-start | bytes 294920 | tf_op jit(solution)/shard_map/ppermute | solution.py:252
  33.9 19.5 %collective-permute-start.12 = (bf16[16,32,128]{2,1,0:T(8,128)(2,1)S(1)}, bf16[16,32,128]{2,1,0:T(8,128)(2,1)S(1)}, u32[]{:S(2)}, u32[]{:S(2)}) collective-permute-start(bf16[16,32,128]{2,1,0:T(8,128)(2,1)S(1)} %get-tuple-element.26.refs_12_), channel_id=1, source_target_pairs={{0,10},{1,11},{2,8},{3,9},{4,14},{5,15},{6,12},{7,13},{8,2},{9,3},... | collective-permute-start | bytes 393224 | tf_op jit(solution)/shard_map/ppermute | solution.py:252
  38.7 14.7 %collective-permute-start.13 = (bf16[16,32,128]{2,1,0:T(8,128)(2,1)S(1)}, bf16[16,32,128]{2,1,0:T(8,128)(2,1)S(1)}, u32[]{:S(2)}, u32[]{:S(2)}) collective-permute-start(bf16[16,32,128]{2,1,0:T(8,128)(2,1)S(1)} %get-tuple-element.27.refs_13_), channel_id=1, source_target_pairs={{0,14},{1,15},{2,12},{3,13},{4,10},{5,11},{6,8},{7,9},{8,6},{9,7},... | collective-permute-start | bytes 393224 | tf_op jit(solution)/shard_map/ppermute | solution.py:252
  44.7 7.6 %collective-permute-start.10 = (bf16[16,32,128]{2,1,0:T(8,128)(2,1)S(1)}, bf16[16,32,128]{2,1,0:T(8,128)(2,1)S(1)}, u32[]{:S(2)}, u32[]{:S(2)}) collective-permute-start(bf16[16,32,128]{2,1,0:T(8,128)(2,1)S(1)} %get-tuple-element.31), channel_id=1, source_target_pairs={{0,6},{1,7},{2,4},{3,5},{4,2},{5,3},{6,0},{7,1},{8,14},{9,15},{10,... | collective-permute-start | bytes 393224 | tf_op jit(solution)/shard_map/ppermute | solution.py:252
  44.8 8.7 %collective-permute-start.9 = (bf16[16,32,128]{2,1,0:T(8,128)(2,1)S(1)}, bf16[16,32,128]{2,1,0:T(8,128)(2,1)S(1)}, u32[]{:S(2)}, u32[]{:S(2)}) collective-permute-start(bf16[16,32,128]{2,1,0:T(8,128)(2,1)S(1)} %get-tuple-element.28.refs_12_), channel_id=1, source_target_pairs={{0,4},{1,5},{2,6},{3,7},{4,0},{5,1},{6,2},{7,3},{8,12},{9,13},{10,... | collective-permute-start | bytes 393224 | tf_op jit(solution)/shard_map/ppermute | solution.py:252
  51.1 5.0 %collective-permute-start.8 = (bf16[16,32,128]{2,1,0:T(8,128)(2,1)S(1)}, bf16[16,32,128]{2,1,0:T(8,128)(2,1)S(1)}, u32[]{:S(2)}, u32[]{:S(2)}) collective-permute-start(bf16[16,32,128]{2,1,0:T(8,128)(2,1)S(1)} %get-tuple-element.30), channel_id=1, source_target_pairs={{0,2},{1,3},{2,0},{3,1},{4,6},{5,7},{6,4},{7,5},{8,10},{9,11},{10,... | collective-permute-start | bytes 393224 | tf_op jit(solution)/shard_map/ppermute | solution.py:252

commit v10 on v9

--- a/solution.py
+++ b/solution.py
@@ -330,7 +330,7 @@
     sent = {}
     for ms in (far, passed, near[1:], [0] + near[:1]):
         if ms == far:
-            after = [biases[near[0]]]
+            after = [biases[m] for m in near]
         elif ms == passed:
             after = [updates[far[0]]]
         elif ms == near[1:]:

time: 57 us -> 53.5 us (0.939)
  waiting for transfers between devices: 9.77 us -> 6.94 us
  starting transfers between devices: 21.4 us -> 20.7 us
    ppermute x14, waiting for transfers between devices: 9.77 us -> 6.94 us  [swap(): return lax.ppermute(x, 'row', [(i, i ^ bits) for i in range(devices)])]
    ppermute x14, starting transfers between devices: 21.4 us -> 20.7 us  [swap(): return lax.ppermute(x, 'row', [(i, i ^ bits) for i in range(devices)])]
  transfers between devices with their start and end apart: 14 -> 14, of which waited for: 4 -> 5; matrix products, arithmetic and copies ran while one was open for 0% -> 0% of each run, Pallas kernels for 34% -> 36%
where the time goes in v10:
time: 53.5 us; the launch traced here: 53.3 us
  Pallas kernels  25.5 us (48%)
  starting transfers between devices  20.7 us (39%)
  waiting for transfers between devices  6.94 us (13%)
    ppermute x14, starting transfers between devices, swap(): return lax.ppermute(x, 'row', [(i, i ^ bits) for i in range(devices)])  20.7 us
    pallas_call x4, Pallas kernels, local(): pl.pallas_call(functools.partial(attention_kernel, heads, ms, first), out...  16 us
    ppermute x14, waiting for transfers between devices, swap(): return lax.ppermute(x, 'row', [(i, i ^ bits) for i in range(devices)])  6.94 us
    pallas_call x1, Pallas kernels, local(): pl.pallas_call(bias_kernel, grid=(rows_held // step_rows,), out_shape=[ja...  5.57 us
    pallas_call x1, Pallas kernels, local(): pl.pallas_call(key_value_kernel, out_shape=[jax.ShapeDtypeStruct((2 * cou...  2.27 us
    pallas_call x2, Pallas kernels, local(): pl.pallas_call(functools.partial(gather_kernel, order), out_shape=jax.Sha...  1.64 us
  transfers between devices with their start and end apart: 14, of which 5 were waited for; matrix products, arithmetic and copies ran while one was open for 0% of the time, Pallas kernels for 36%

profile of v10, /device:TPU:0, one launch (start us, length us, event | category | flops | bytes accessed | tf_op | source)
XLA Modules:
  0.0 53.3 jit_solution(15200050885176517171)
XLA Ops:
  0.0 0.0 copy-start
  0.0 5.6 %shard_map.109 = (bf16[128,384]{1,0:T(8,128)(2,1)S(1)}, bf16[8,512,128]{2,1,0:T(8,128)(2,1)S(1)}, bf16[384,512]{1,0:T(8,128)(2,1)S(1)}, f32[8,384]{1,0:T(8,128)S(1)}) custom-call(s32[1]{0:T(128)} %bitcast.me_ref, s32[8]{0:T(128)} %rows_ref.1, bf16[32,512,128]{2,1,0:T(8,128)(2,1)} %pair_ref.1, s32[1,512]{1,0:T(1,128)} %bitcast.17, s32[1,512]{1,0:T(1,128)} %bitcast.22, ...), custom_call_target="tpu_custom_call" | custom-call | bytes 22140000 | tf_op jit(solution)/shard_map/pallas_call | solution.py:255
  5.6 0.5 collective-permute-start.1
  6.1 4.7 %collective-permute-start.5 = (bf16[128,384]{1,0:T(8,128)(2,1)S(1)}, bf16[128,384]{1,0:T(8,128)(2,1)S(1)}, u32[]{:S(2)}, u32[]{:S(2)}) collective-permute-start(bf16[128,384]{1,0:T(8,128)(2,1)S(1)} %get-tuple-element.19.refs_0_), channel_id=1, source_target_pairs={{0,12},{1,13},{2,14},{3,15},{4,8},{5,9},{6,10},{7,11},{8,4},{9,5},... | collective-permute-start | bytes 294920 | tf_op jit(solution)/shard_map/ppermute | solution.py:252
  10.8 0.0 collective-permute-start.4
  10.8 1.7 %collective-permute-start.3 = (bf16[128,384]{1,0:T(8,128)(2,1)S(1)}, bf16[128,384]{1,0:T(8,128)(2,1)S(1)}, u32[]{:S(2)}, u32[]{:S(2)}) collective-permute-start(bf16[128,384]{1,0:T(8,128)(2,1)S(1)} %get-tuple-element.19.refs_0_), channel_id=1, source_target_pairs={{0,6},{1,7},{2,4},{3,5},{4,2},{5,3},{6,0},{7,1},{8,14},{9,15},{10,... | collective-permute-start | bytes 294920 | tf_op jit(solution)/shard_map/ppermute | solution.py:252
  12.5 1.2 %collective-permute-start.2 = (bf16[128,384]{1,0:T(8,128)(2,1)S(1)}, bf16[128,384]{1,0:T(8,128)(2,1)S(1)}, u32[]{:S(2)}, u32[]{:S(2)}) collective-permute-start(bf16[128,384]{1,0:T(8,128)(2,1)S(1)} %get-tuple-element.19.refs_0_), channel_id=1, source_target_pairs={{0,4},{1,5},{2,6},{3,7},{4,0},{5,1},{6,2},{7,3},{8,12},{9,13},{10,... | collective-permute-start | bytes 294920 | tf_op jit(solution)/shard_map/ppermute | solution.py:252
  13.8 0.0 collective-permute-done.1.other_ref
  13.8 0.5 collective-permute-start
  14.3 0.0 copy-done
  14.3 2.3 %shard_map.110 = (bf16[16,128,384]{2,1,0:T(8,128)(2,1)S(1)}, bf16[16,384,128]{2,1,0:T(8,128)(2,1)S(1)}) custom-call(bf16[8,512,128]{2,1,0:T(8,128)(2,1)S(1)} %get-tuple-element.20.own_ref, bf16[8,512,128]{2,1,0:T(8,128)(2,1)S(1)} %collective-permute-done.1.other_ref, bf16[384,512]{1,0:T(8,128)(2,1)S(1)} %get-tuple-element.21.pick_ref, ...), custom_call_target="tpu_custom_call" | custom-call | bytes 7380000 | tf_op jit(solution)/shard_map/pallas_call | solution.py:304
  16.5 0.0 copy-start.1
  16.6 0.0 copy-start.2
  16.6 0.0 copy-start.3
  16.6 0.0 copy-start.4
  16.6 0.0 copy-start.5
  16.6 0.0 collective-permute-done.5.refs_1_
  16.6 3.1 %collective-permute-done.4.refs_0_ = bf16[128,384]{1,0:T(8,128)(2,1)S(1)} collective-permute-done((bf16[128,384]{1,0:T(8,128)(2,1)S(1)}, bf16[128,384]{1,0:T(8,128)(2,1)S(1)}, u32[]{:S(2)}, u32[]{:S(2)}) %collective-permute-start.4) | collective-permute-done | bytes 98336 | tf_op jit(solution)/shard_map/ppermute | solution.py:252
  19.8 1.6 %collective-permute-start.6 = (bf16[256,384]{1,0:T(8,128)(2,1)S(1)}, bf16[256,384]{1,0:T(8,128)(2,1)S(1)}, u32[]{:S(2)}, u32[]{:S(2)}) collective-permute-start(bf16[256,384]{1,0:T(8,128)(2,1)S(1)} %shard_map.111), channel_id=1, source_target_pairs={{0,2},{1,3},{2,0},{3,1},{4,6},{5,7},{6,4},{7,5},{8,10},{9,11},{10,... | collective-permute-start | bytes 589832 | tf_op jit(solution)/shard_map/ppermute | solution.py:252
  21.4 0.0 collective-permute-done.3.refs_14_.refs_1_
  21.4 0.0 collective-permute-done.2.refs_13_.refs_0_
  21.4 0.0 collective-permute-done.refs_12_.refs_1_
  21.4 0.0 copy-done.1
  21.4 0.0 copy-done.2
  21.4 0.0 copy-done.3
  21.4 0.0 copy-done.4
  21.4 0.0 copy-done.5
  21.4 4.0 %shard_map.112 = (bf16[16,32,128]{2,1,0:T(8,128)(2,1)S(1)}, bf16[16,32,128]{2,1,0:T(8,128)(2,1)S(1)}) custom-call(s32[1]{0:T(128)} %bitcast.me_ref, f32[4]{0:T(128)S(1)} %copy-done.4, bf16[128,384]{1,0:T(8,128)(2,1)S(1)} %collective-permute-done.4.refs_0_, bf16[128,384]{1,0:T(8,128)(2,1)S(1)} %collective-permute-done.5.refs_1_, ...), custom_call_target="tpu_custom_call" | custom-call | bytes 16236000 | tf_op jit(solution)/shard_map/pallas_call | solution.py:343
  25.4 1.1 %collective-permute-start.7 = (bf16[16,32,128]{2,1,0:T(8,128)(2,1)S(1)}, bf16[16,32,128]{2,1,0:T(8,128)(2,1)S(1)}, u32[]{:S(2)}, u32[]{:S(2)}) collective-permute-start(bf16[16,32,128]{2,1,0:T(8,128)(2,1)S(1)} %get-tuple-element.25.refs_12_), channel_id=1, source_target_pairs={{0,8},{1,9},{2,10},{3,11},{4,12},{5,13},{6,14},{7,15},{8,0},{9,1},... | collective-permute-start | bytes 393224 | tf_op jit(solution)/shard_map/ppermute | solution.py:252
  26.6 2.2 %collective-permute-start.11 = (bf16[16,32,128]{2,1,0:T(8,128)(2,1)S(1)}, bf16[16,32,128]{2,1,0:T(8,128)(2,1)S(1)}, u32[]{:S(2)}, u32[]{:S(2)}) collective-permute-start(bf16[16,32,128]{2,1,0:T(8,128)(2,1)S(1)} %get-tuple-element.32), channel_id=1, source_target_pairs={{0,12},{1,13},{2,14},{3,15},{4,8},{5,9},{6,10},{7,11},{8,4},{9,5},... | collective-permute-start | bytes 393224 | tf_op jit(solution)/shard_map/ppermute | solution.py:252
  28.8 0.0 collective-permute-done.6.refs_0_.refs_1_
  28.8 4.0 %shard_map.113 = (bf16[16,32,128]{2,1,0:T(8,128)(2,1)S(1)}, bf16[16,32,128]{2,1,0:T(8,128)(2,1)S(1)}) custom-call(s32[1]{0:T(128)} %bitcast.me_ref, f32[4]{0:T(128)S(1)} %copy-done.4, bf16[256,384]{1,0:T(8,128)(2,1)S(1)} %collective-permute-done.6.refs_0_.refs_1_, bf16[256,384]{1,0:T(8,128)(2,1)S(1)} %collective-permute-done.6.refs_0_.refs_1_, ...), custom_call_target="tpu_custom_call" | custom-call | bytes 16236000 | tf_op jit(solution)/shard_map/pallas_call | solution.py:343
  32.8 2.4 %collective-permute-start.12 = (bf16[16,32,128]{2,1,0:T(8,128)(2,1)S(1)}, bf16[16,32,128]{2,1,0:T(8,128)(2,1)S(1)}, u32[]{:S(2)}, u32[]{:S(2)}) collective-permute-start(bf16[16,32,128]{2,1,0:T(8,128)(2,1)S(1)} %get-tuple-element.26.refs_12_), channel_id=1, source_target_pairs={{0,10},{1,11},{2,8},{3,9},{4,14},{5,15},{6,12},{7,13},{8,2},{9,3},... | collective-permute-start | bytes 393224 | tf_op jit(solution)/shard_map/ppermute | solution.py:252
  35.2 1.1 %collective-permute-start.13 = (bf16[16,32,128]{2,1,0:T(8,128)(2,1)S(1)}, bf16[16,32,128]{2,1,0:T(8,128)(2,1)S(1)}, u32[]{:S(2)}, u32[]{:S(2)}) collective-permute-start(bf16[16,32,128]{2,1,0:T(8,128)(2,1)S(1)} %get-tuple-element.27.refs_13_), channel_id=1, source_target_pairs={{0,14},{1,15},{2,12},{3,13},{4,10},{5,11},{6,8},{7,9},{8,6},{9,7},... | collective-permute-start | bytes 393224 | tf_op jit(solution)/shard_map/ppermute | solution.py:252
  36.3 4.0 %shard_map.114 = (bf16[16,32,128]{2,1,0:T(8,128)(2,1)S(1)}, bf16[16,32,128]{2,1,0:T(8,128)(2,1)S(1)}) custom-call(s32[1]{0:T(128)} %bitcast.me_ref, f32[4]{0:T(128)S(1)} %copy-done.4, bf16[128,384]{1,0:T(8,128)(2,1)S(1)} %collective-permute-done.2.refs_13_.refs_0_, bf16[128,384]{1,0:T(8,128)(2,1)S(1)} %collective-permute-done.3.refs_14_.refs_1_, ...), custom_call_target="tpu_custom_call" | custom-call | bytes 16236000 | tf_op jit(solution)/shard_map/pallas_call | solution.py:343
  40.3 2.0 %collective-permute-start.10 = (bf16[16,32,128]{2,1,0:T(8,128)(2,1)S(1)}, bf16[16,32,128]{2,1,0:T(8,128)(2,1)S(1)}, u32[]{:S(2)}, u32[]{:S(2)}) collective-permute-start(bf16[16,32,128]{2,1,0:T(8,128)(2,1)S(1)} %get-tuple-element.31), channel_id=1, source_target_pairs={{0,6},{1,7},{2,4},{3,5},{4,2},{5,3},{6,0},{7,1},{8,14},{9,15},{10,... | collective-permute-start | bytes 393224 | tf_op jit(solution)/shard_map/ppermute | solution.py:252
  42.3 0.9 %collective-permute-done.7.refs_13_.refs_2_ = bf16[16,32,128]{2,1,0:T(8,128)(2,1)S(1)} collective-permute-done((bf16[16,32,128]{2,1,0:T(8,128)(2,1)S(1)}, bf16[16,32,128]{2,1,0:T(8,128)(2,1)S(1)}, u32[]{:S(2)}, u32[]{:S(2)}) %collective-permute-start.7) | collective-permute-done | bytes 131104 | tf_op jit(solution)/shard_map/ppermute | solution.py:252
  43.2 0.0 collective-permute-start.9
  43.2 4.0 %shard_map.115 = (bf16[16,32,128]{2,1,0:T(8,128)(2,1)S(1)}, bf16[16,32,128]{2,1,0:T(8,128)(2,1)S(1)}) custom-call(s32[1]{0:T(128)} %bitcast.me_ref, f32[4]{0:T(128)S(1)} %copy-done.4, bf16[128,384]{1,0:T(8,128)(2,1)S(1)} %get-tuple-element.19.refs_0_, bf16[128,384]{1,0:T(8,128)(2,1)S(1)} %collective-permute-done.refs_12_.refs_1_, ...), custom_call_target="tpu_custom_call" | custom-call | bytes 16236000 | tf_op jit(solution)/shard_map/pallas_call | solution.py:343
  47.2 0.0 collective-permute-done.11.refs_3_
  47.2 1.6 %collective-permute-start.8 = (bf16[16,32,128]{2,1,0:T(8,128)(2,1)S(1)}, bf16[16,32,128]{2,1,0:T(8,128)(2,1)S(1)}, u32[]{:S(2)}, u32[]{:S(2)}) collective-permute-start(bf16[16,32,128]{2,1,0:T(8,128)(2,1)S(1)} %get-tuple-element.30), channel_id=1, source_target_pairs={{0,2},{1,3},{2,0},{3,1},{4,6},{5,7},{6,4},{7,5},{8,10},{9,11},{10,... | collective-permute-start | bytes 393224 | tf_op jit(solution)/shard_map/ppermute | solution.py:252
  48.8 1.7 %collective-permute-done.10.refs_1_ = bf16[16,32,128]{2,1,0:T(8,128)(2,1)S(1)} collective-permute-done((bf16[16,32,128]{2,1,0:T(8,128)(2,1)S(1)}, bf16[16,32,128]{2,1,0:T(8,128)(2,1)S(1)}, u32[]{:S(2)}, u32[]{:S(2)}) %collective-permute-start.10) | collective-permute-done | bytes 131104 | tf_op jit(solution)/shard_map/ppermute | solution.py:252
  50.5 0.9 %collective-permute-done.9.refs_0_ = bf16[16,32,128]{2,1,0:T(8,128)(2,1)S(1)} collective-permute-done((bf16[16,32,128]{2,1,0:T(8,128)(2,1)S(1)}, bf16[16,32,128]{2,1,0:T(8,128)(2,1)S(1)}, u32[]{:S(2)}, u32[]{:S(2)}) %collective-permute-start.9) | collective-permute-done | bytes 131104 | tf_op jit(solution)/shard_map/ppermute | solution.py:252
  51.5 0.0 collective-permute-done.12.refs_4_
  51.5 0.0 collective-permute-done.13.refs_5_
  51.5 0.9 %shard_map.116.refs_2_ = bf16[128,32,128]{2,1,0:T(8,128)(2,1)} custom-call(s32[1]{0:T(128)} %bitcast.me_ref, bf16[16,32,128]{2,1,0:T(8,128)(2,1)S(1)} %collective-permute-done.9.refs_0_, bf16[16,32,128]{2,1,0:T(8,128)(2,1)S(1)} %collective-permute-done.10.refs_1_, bf16[16,32,128]{2,1,0:T(8,128)(2,1)S(1)} %collective-permute-done.7.refs_13_.refs_2_, ...), custom_call_target="tpu_custom_call" | custom-call | bytes 3690000 | tf_op jit(solution)/shard_map/pallas_call | solution.py:381
  52.4 0.2 collective-permute-done.8.refs_1_
  52.6 0.7 %shard_map.117 = bf16[128,32,128]{2,1,0:T(8,128)(2,1)} custom-call(s32[1]{0:T(128)} %bitcast.me_ref, bf16[16,32,128]{2,1,0:T(8,128)(2,1)S(1)} %get-tuple-element.29.refs_0_, bf16[16,32,128]{2,1,0:T(8,128)(2,1)S(1)} %collective-permute-done.8.refs_1_, bf16[128,32,128]{2,1,0:T(8,128)(2,1)} %shard_map.116.refs_2_), custom_call_target="tpu_custom_call", output_to_operand_aliasing={{}: (3, {})} | custom-call | bytes 3690000 | tf_op jit(solution)/shard_map/pallas_call | solution.py:381
  (1 shorter events, 0.0 us)
Async XLA Ops:
  0.0 14.3 %copy-start = (bf16[128,512]{1,0:T(8,128)(2,1)S(1)}, bf16[128,512]{1,0:T(8,128)(2,1)}, u32[]{:S(2)}) copy-start(bf16[128,512]{1,0:T(8,128)(2,1)} %refs_9_.7) | copy-start | bytes 393220
  5.6 8.2 %collective-permute-start.1 = (bf16[8,512,128]{2,1,0:T(8,128)(2,1)S(1)}, bf16[8,512,128]{2,1,0:T(8,128)(2,1)S(1)}, u32[]{:S(2)}, u32[]{:S(2)}) collective-permute-start(bf16[8,512,128]{2,1,0:T(8,128)(2,1)S(1)} %get-tuple-element.20.own_ref), channel_id=1, source_target_pairs={{0,1},{1,0},{2,3},{3,2},{4,5},{5,4},{6,7},{7,6},{8,9},{9,8},{10,11... | collective-permute-start | bytes 3145736 | tf_op jit(solution)/shard_map/ppermute | solution.py:252
  6.1 10.5 %collective-permute-start.5 = (bf16[128,384]{1,0:T(8,128)(2,1)S(1)}, bf16[128,384]{1,0:T(8,128)(2,1)S(1)}, u32[]{:S(2)}, u32[]{:S(2)}) collective-permute-start(bf16[128,384]{1,0:T(8,128)(2,1)S(1)} %get-tuple-element.19.refs_0_), channel_id=1, source_target_pairs={{0,12},{1,13},{2,14},{3,15},{4,8},{5,9},{6,10},{7,11},{8,4},{9,5},... | collective-permute-start | bytes 294920 | tf_op jit(solution)/shard_map/ppermute | solution.py:252
  10.8 9.0 %collective-permute-start.4 = (bf16[128,384]{1,0:T(8,128)(2,1)S(1)}, bf16[128,384]{1,0:T(8,128)(2,1)S(1)}, u32[]{:S(2)}, u32[]{:S(2)}) collective-permute-start(bf16[128,384]{1,0:T(8,128)(2,1)S(1)} %get-tuple-element.19.refs_0_), channel_id=1, source_target_pairs={{0,8},{1,9},{2,10},{3,11},{4,12},{5,13},{6,14},{7,15},{8,0},{9,1},... | collective-permute-start | bytes 294920 | tf_op jit(solution)/shard_map/ppermute | solution.py:252
  10.8 10.6 %collective-permute-start.3 = (bf16[128,384]{1,0:T(8,128)(2,1)S(1)}, bf16[128,384]{1,0:T(8,128)(2,1)S(1)}, u32[]{:S(2)}, u32[]{:S(2)}) collective-permute-start(bf16[128,384]{1,0:T(8,128)(2,1)S(1)} %get-tuple-element.19.refs_0_), channel_id=1, source_target_pairs={{0,6},{1,7},{2,4},{3,5},{4,2},{5,3},{6,0},{7,1},{8,14},{9,15},{10,... | collective-permute-start | bytes 294920 | tf_op jit(solution)/shard_map/ppermute | solution.py:252
  12.5 8.9 %collective-permute-start.2 = (bf16[128,384]{1,0:T(8,128)(2,1)S(1)}, bf16[128,384]{1,0:T(8,128)(2,1)S(1)}, u32[]{:S(2)}, u32[]{:S(2)}) collective-permute-start(bf16[128,384]{1,0:T(8,128)(2,1)S(1)} %get-tuple-element.19.refs_0_), channel_id=1, source_target_pairs={{0,4},{1,5},{2,6},{3,7},{4,0},{5,1},{6,2},{7,3},{8,12},{9,13},{10,... | collective-permute-start | bytes 294920 | tf_op jit(solution)/shard_map/ppermute | solution.py:252
  13.8 7.6 %collective-permute-start = (bf16[128,384]{1,0:T(8,128)(2,1)S(1)}, bf16[128,384]{1,0:T(8,128)(2,1)S(1)}, u32[]{:S(2)}, u32[]{:S(2)}) collective-permute-start(bf16[128,384]{1,0:T(8,128)(2,1)S(1)} %get-tuple-element.19.refs_0_), channel_id=1, source_target_pairs={{0,2},{1,3},{2,0},{3,1},{4,6},{5,7},{6,4},{7,5},{8,10},{9,11},{10,... | collective-permute-start | bytes 294920 | tf_op jit(solution)/shard_map/ppermute | solution.py:252
  16.5 4.8 %copy-start.1 = (bf16[128,128]{1,0:T(8,128)(2,1)S(1)}, bf16[128,128]{1,0:T(8,128)(2,1)}, u32[]{:S(2)}) copy-start(bf16[128,128]{1,0:T(8,128)(2,1)} %refs_11_.7) | copy-start | bytes 98308
  16.6 4.8 %copy-start.2 = (s32[512]{0:T(512)S(1)}, s32[512]{0:T(512)}, u32[]{:S(2)}) copy-start(s32[512]{0:T(512)} %param.13) | copy-start | bytes 6148
  16.6 4.8 %copy-start.3 = (s32[512]{0:T(512)S(1)}, s32[512]{0:T(512)}, u32[]{:S(2)}) copy-start(s32[512]{0:T(512)} %param.14) | copy-start | bytes 6148
  16.6 4.8 %copy-start.4 = (f32[4]{0:T(128)S(1)}, f32[4]{0:T(128)}, u32[]{:S(2)}) copy-start(f32[4]{0:T(128)} %chain_bias_ref.7) | copy-start | bytes 52
  16.6 4.8 %copy-start.5 = (f32[128]{0:T(128)S(1)}, f32[128]{0:T(128)}, u32[]{:S(2)}) copy-start(f32[128]{0:T(128)} %param.18) | copy-start | bytes 1540
  19.8 9.0 %collective-permute-start.6 = (bf16[256,384]{1,0:T(8,128)(2,1)S(1)}, bf16[256,384]{1,0:T(8,128)(2,1)S(1)}, u32[]{:S(2)}, u32[]{:S(2)}) collective-permute-start(bf16[256,384]{1,0:T(8,128)(2,1)S(1)} %shard_map.111), channel_id=1, source_target_pairs={{0,2},{1,3},{2,0},{3,1},{4,6},{5,7},{6,4},{7,5},{8,10},{9,11},{10,... | collective-permute-start | bytes 589832 | tf_op jit(solution)/shard_map/ppermute | solution.py:252
  25.4 17.8 %collective-permute-start.7 = (bf16[16,32,128]{2,1,0:T(8,128)(2,1)S(1)}, bf16[16,32,128]{2,1,0:T(8,128)(2,1)S(1)}, u32[]{:S(2)}, u32[]{:S(2)}) collective-permute-start(bf16[16,32,128]{2,1,0:T(8,128)(2,1)S(1)} %get-tuple-element.25.refs_12_), channel_id=1, source_target_pairs={{0,8},{1,9},{2,10},{3,11},{4,12},{5,13},{6,14},{7,15},{8,0},{9,1},... | collective-permute-start | bytes 393224 | tf_op jit(solution)/shard_map/ppermute | solution.py:252
  26.6 20.6 %collective-permute-start.11 = (bf16[16,32,128]{2,1,0:T(8,128)(2,1)S(1)}, bf16[16,32,128]{2,1,0:T(8,128)(2,1)S(1)}, u32[]{:S(2)}, u32[]{:S(2)}) collective-permute-start(bf16[16,32,128]{2,1,0:T(8,128)(2,1)S(1)} %get-tuple-element.32), channel_id=1, source_target_pairs={{0,12},{1,13},{2,14},{3,15},{4,8},{5,9},{6,10},{7,11},{8,4},{9,5},... | collective-permute-start | bytes 393224 | tf_op jit(solution)/shard_map/ppermute | solution.py:252
  32.8 18.7 %collective-permute-start.12 = (bf16[16,32,128]{2,1,0:T(8,128)(2,1)S(1)}, bf16[16,32,128]{2,1,0:T(8,128)(2,1)S(1)}, u32[]{:S(2)}, u32[]{:S(2)}) collective-permute-start(bf16[16,32,128]{2,1,0:T(8,128)(2,1)S(1)} %get-tuple-element.26.refs_12_), channel_id=1, source_target_pairs={{0,10},{1,11},{2,8},{3,9},{4,14},{5,15},{6,12},{7,13},{8,2},{9,3},... | collective-permute-start | bytes 393224 | tf_op jit(solution)/shard_map/ppermute | solution.py:252
  35.2 16.3 %collective-permute-start.13 = (bf16[16,32,128]{2,1,0:T(8,128)(2,1)S(1)}, bf16[16,32,128]{2,1,0:T(8,128)(2,1)S(1)}, u32[]{:S(2)}, u32[]{:S(2)}) collective-permute-start(bf16[16,32,128]{2,1,0:T(8,128)(2,1)S(1)} %get-tuple-element.27.refs_13_), channel_id=1, source_target_pairs={{0,14},{1,15},{2,12},{3,13},{4,10},{5,11},{6,8},{7,9},{8,6},{9,7},... | collective-permute-start | bytes 393224 | tf_op jit(solution)/shard_map/ppermute | solution.py:252
  40.3 10.2 %collective-permute-start.10 = (bf16[16,32,128]{2,1,0:T(8,128)(2,1)S(1)}, bf16[16,32,128]{2,1,0:T(8,128)(2,1)S(1)}, u32[]{:S(2)}, u32[]{:S(2)}) collective-permute-start(bf16[16,32,128]{2,1,0:T(8,128)(2,1)S(1)} %get-tuple-element.31), channel_id=1, source_target_pairs={{0,6},{1,7},{2,4},{3,5},{4,2},{5,3},{6,0},{7,1},{8,14},{9,15},{10,... | collective-permute-start | bytes 393224 | tf_op jit(solution)/shard_map/ppermute | solution.py:252
  43.2 8.3 %collective-permute-start.9 = (bf16[16,32,128]{2,1,0:T(8,128)(2,1)S(1)}, bf16[16,32,128]{2,1,0:T(8,128)(2,1)S(1)}, u32[]{:S(2)}, u32[]{:S(2)}) collective-permute-start(bf16[16,32,128]{2,1,0:T(8,128)(2,1)S(1)} %get-tuple-element.28.refs_12_), channel_id=1, source_target_pairs={{0,4},{1,5},{2,6},{3,7},{4,0},{5,1},{6,2},{7,3},{8,12},{9,13},{10,... | collective-permute-start | bytes 393224 | tf_op jit(solution)/shard_map/ppermute | solution.py:252
  47.2 5.4 %collective-permute-start.8 = (bf16[16,32,128]{2,1,0:T(8,128)(2,1)S(1)}, bf16[16,32,128]{2,1,0:T(8,128)(2,1)S(1)}, u32[]{:S(2)}, u32[]{:S(2)}) collective-permute-start(bf16[16,32,128]{2,1,0:T(8,128)(2,1)S(1)} %get-tuple-element.30), channel_id=1, source_target_pairs={{0,2},{1,3},{2,0},{3,1},{4,6},{5,7},{6,4},{7,5},{8,10},{9,11},{10,... | collective-permute-start | bytes 393224 | tf_op jit(solution)/shard_map/ppermute | solution.py:252

commit v11 on v10

--- a/solution.py
+++ b/solution.py
@@ -316,27 +316,30 @@
     split = (count, owners, 2, rows_held, channels)
     own, other = own.reshape(split), other.reshape(split)
     updates = {}
-    straight = pl.pallas_call(
-        join_kernel,
-        out_shape=jax.ShapeDtypeStruct((len(far) * heads * rows_held, live), BF16),
-        in_specs=[VMEM] * len(far) + [ANY],
-        out_specs=VMEM,
-        compiler_params=PARAMS,
-        cost_estimate=measured(0.5),
-    )(*[biases[m] for m in far], keys)
-    straight = swap(straight, 2)
-    for m in passed:
-        biases[m] = straight
     sent = {}
-    for ms in (far, passed, near[1:], [0] + near[:1]):
-        if ms == far:
-            after = [biases[m] for m in near]
+    head, rest = far[-1:], far[:-1]
+    for ms in (head, rest, passed, near[1:], [0] + near[:1]):
+        if ms == head:
+            after = []
+        elif ms == rest:
+            straight = pl.pallas_call(
+                join_kernel,
+                out_shape=jax.ShapeDtypeStruct((len(far) * heads * rows_held, live), BF16),
+                in_specs=[VMEM] * len(far) + [ANY],
+                out_specs=VMEM,
+                compiler_params=PARAMS,
+                cost_estimate=measured(0.5),
+            )(*[biases[m] for m in far], updates[head[0]])
+            straight = swap(straight, 2)
+            for m in passed:
+                biases[m] = straight
+            after = [updates[head[0]]] + [biases[m] for m in near]
         elif ms == passed:
-            after = [updates[far[0]]]
+            after = [updates[rest[0]]]
         elif ms == near[1:]:
             after = [updates[m] for m in passed]
         else:
-            after = [updates[near[1]], sent[far[0]]]
+            after = [updates[near[1]]] + [sent[m] for m in head]
         blocks = len(ms)
         first = [i * heads * rows_held if ms == passed else 0 for i in range(blocks)]
         rows = 2 * count * rows_held

time: 53.5 us -> 51.5 us (0.963)
  waiting for transfers between devices: 6.94 us -> 3.31 us
  starting transfers between devices: 20.7 us -> 21.7 us
  Pallas kernels: 25.5 us -> 26.2 us
    ppermute x14, waiting for transfers between devices: 6.94 us -> 3.31 us  [swap(): return lax.ppermute(x, 'row', [(i, i ^ bits) for i in range(devices)])]
    ppermute x14, starting transfers between devices: 20.7 us -> 21.7 us  [swap(): return lax.ppermute(x, 'row', [(i, i ^ bits) for i in range(devices)])]
    pallas_call x4 -> x5, Pallas kernels: 16 us -> 16.7 us  [local(): pl.pallas_call(functools.partial(attention_kernel, heads, ms, first), out...]
  transfers between devices with their start and end apart: 14 -> 14, of which waited for: 5 -> 3; matrix products, arithmetic and copies ran while one was open for 0% -> 0% of each run, Pallas kernels for 36% -> 39%
where the time goes in v11:
time: 51.5 us; the launch traced here: 51.4 us
  Pallas kernels  26.2 us (51%)
  starting transfers between devices  21.7 us (42%)
  waiting for transfers between devices  3.31 us (6%)
    ppermute x14, starting transfers between devices, swap(): return lax.ppermute(x, 'row', [(i, i ^ bits) for i in range(devices)])  21.7 us
    pallas_call x5, Pallas kernels, local(): pl.pallas_call(functools.partial(attention_kernel, heads, ms, first), out...  16.7 us
    pallas_call x1, Pallas kernels, local(): pl.pallas_call(bias_kernel, grid=(rows_held // step_rows,), out_shape=[ja...  5.57 us
    ppermute x14, waiting for transfers between devices, swap(): return lax.ppermute(x, 'row', [(i, i ^ bits) for i in range(devices)])  3.31 us
    pallas_call x1, Pallas kernels, local(): pl.pallas_call(key_value_kernel, out_shape=[jax.ShapeDtypeStruct((2 * cou...  2.27 us
    pallas_call x2, Pallas kernels, local(): pl.pallas_call(functools.partial(gather_kernel, order), out_shape=jax.Sha...  1.64 us
  transfers between devices with their start and end apart: 14, of which 3 were waited for; matrix products, arithmetic and copies ran while one was open for 0% of the time, Pallas kernels for 39%

profile of v11, /device:TPU:0, one launch (start us, length us, event | category | flops | bytes accessed | tf_op | source)
XLA Modules:
  0.0 51.4 jit_solution(4800985550692883007)
XLA Ops:
  0.0 0.0 copy-start
  0.0 5.6 %shard_map.109 = (bf16[128,384]{1,0:T(8,128)(2,1)S(1)}, bf16[8,512,128]{2,1,0:T(8,128)(2,1)S(1)}, bf16[384,512]{1,0:T(8,128)(2,1)S(1)}, f32[8,384]{1,0:T(8,128)S(1)}) custom-call(s32[1]{0:T(128)} %bitcast.me_ref, s32[8]{0:T(128)} %rows_ref.1, bf16[32,512,128]{2,1,0:T(8,128)(2,1)} %pair_ref.1, s32[1,512]{1,0:T(1,128)} %bitcast.19, s32[1,512]{1,0:T(1,128)} %bitcast.25, ...), custom_call_target="tpu_custom_call" | custom-call | bytes 22140000 | tf_op jit(solution)/shard_map/pallas_call | solution.py:255
  5.6 0.0 copy-start.1
  5.6 0.0 copy-start.2
  5.6 0.0 copy-start.3
  5.6 0.0 copy-start.4
  5.6 0.0 copy-start.5
  5.6 0.5 %collective-permute-start.1 = (bf16[8,512,128]{2,1,0:T(8,128)(2,1)S(1)}, bf16[8,512,128]{2,1,0:T(8,128)(2,1)S(1)}, u32[]{:S(2)}, u32[]{:S(2)}) collective-permute-start(bf16[8,512,128]{2,1,0:T(8,128)(2,1)S(1)} %get-tuple-element.18.own_ref), channel_id=1, source_target_pairs={{0,1},{1,0},{2,3},{3,2},{4,5},{5,4},{6,7},{7,6},{8,9},{9,8},{10,11... | collective-permute-start | bytes 3145736 | tf_op jit(solution)/shard_map/ppermute | solution.py:252
  6.2 4.7 %collective-permute-start.5 = (bf16[128,384]{1,0:T(8,128)(2,1)S(1)}, bf16[128,384]{1,0:T(8,128)(2,1)S(1)}, u32[]{:S(2)}, u32[]{:S(2)}) collective-permute-start(bf16[128,384]{1,0:T(8,128)(2,1)S(1)} %get-tuple-element.17.refs_0_), channel_id=1, source_target_pairs={{0,12},{1,13},{2,14},{3,15},{4,8},{5,9},{6,10},{7,11},{8,4},{9,5},... | collective-permute-start | bytes 294920 | tf_op jit(solution)/shard_map/ppermute | solution.py:252
  10.8 0.0 collective-permute-start.4
  10.8 1.7 %collective-permute-start.3 = (bf16[128,384]{1,0:T(8,128)(2,1)S(1)}, bf16[128,384]{1,0:T(8,128)(2,1)S(1)}, u32[]{:S(2)}, u32[]{:S(2)}) collective-permute-start(bf16[128,384]{1,0:T(8,128)(2,1)S(1)} %get-tuple-element.17.refs_0_), channel_id=1, source_target_pairs={{0,6},{1,7},{2,4},{3,5},{4,2},{5,3},{6,0},{7,1},{8,14},{9,15},{10,... | collective-permute-start | bytes 294920 | tf_op jit(solution)/shard_map/ppermute | solution.py:252
  12.6 1.2 %collective-permute-start.2 = (bf16[128,384]{1,0:T(8,128)(2,1)S(1)}, bf16[128,384]{1,0:T(8,128)(2,1)S(1)}, u32[]{:S(2)}, u32[]{:S(2)}) collective-permute-start(bf16[128,384]{1,0:T(8,128)(2,1)S(1)} %get-tuple-element.17.refs_0_), channel_id=1, source_target_pairs={{0,4},{1,5},{2,6},{3,7},{4,0},{5,1},{6,2},{7,3},{8,12},{9,13},{10,... | collective-permute-start | bytes 294920 | tf_op jit(solution)/shard_map/ppermute | solution.py:252
  13.8 0.0 collective-permute-done.1.other_ref
  13.8 0.5 collective-permute-start
  14.3 0.0 copy-done
  14.3 2.3 %shard_map.110 = (bf16[16,128,384]{2,1,0:T(8,128)(2,1)S(1)}, bf16[16,384,128]{2,1,0:T(8,128)(2,1)S(1)}) custom-call(bf16[8,512,128]{2,1,0:T(8,128)(2,1)S(1)} %get-tuple-element.18.own_ref, bf16[8,512,128]{2,1,0:T(8,128)(2,1)S(1)} %collective-permute-done.1.other_ref, bf16[384,512]{1,0:T(8,128)(2,1)S(1)} %get-tuple-element.19.pick_ref, ...), custom_call_target="tpu_custom_call" | custom-call | bytes 7380000 | tf_op jit(solution)/shard_map/pallas_call | solution.py:304
  16.6 0.0 collective-permute-done.5.refs_0_.refs_1_
  16.6 0.0 copy-done.1
  16.6 0.0 copy-done.2
  16.6 0.0 copy-done.3
  16.6 0.0 copy-done.4
  16.7 0.0 copy-done.5
  16.7 2.3 %shard_map.111.refs_2_.refs_11_ = bf16[16,32,128]{2,1,0:T(8,128)(2,1)S(1)} custom-call(s32[1]{0:T(128)} %bitcast.me_ref, f32[4]{0:T(128)S(1)} %copy-done.4, bf16[128,384]{1,0:T(8,128)(2,1)S(1)} %collective-permute-done.5.refs_0_.refs_1_, bf16[8,8,2,32,128]{4,3,2,1,0:T(8,128)(2,1)S(1)} %bitcast.9, bf16[8,8,2,32,128]{4,3,2,1,0:T(8,128)(2,1)S(1)} %bitcast.14, ...), custom_call_target="tpu_custom_call" | custom-call | bytes 8118000 | tf_op jit(solution)/shard_map/pallas_call | solution.py:346
  19.0 0.8 %collective-permute-done.4.refs_0_ = bf16[128,384]{1,0:T(8,128)(2,1)S(1)} collective-permute-done((bf16[128,384]{1,0:T(8,128)(2,1)S(1)}, bf16[128,384]{1,0:T(8,128)(2,1)S(1)}, u32[]{:S(2)}, u32[]{:S(2)}) %collective-permute-start.4) | collective-permute-done | bytes 98336 | tf_op jit(solution)/shard_map/ppermute | solution.py:252
  19.8 1.6 %collective-permute-start.6 = (bf16[256,384]{1,0:T(8,128)(2,1)S(1)}, bf16[256,384]{1,0:T(8,128)(2,1)S(1)}, u32[]{:S(2)}, u32[]{:S(2)}) collective-permute-start(bf16[256,384]{1,0:T(8,128)(2,1)S(1)} %shard_map.112), channel_id=1, source_target_pairs={{0,2},{1,3},{2,0},{3,1},{4,6},{5,7},{6,4},{7,5},{8,10},{9,11},{10,... | collective-permute-start | bytes 589832 | tf_op jit(solution)/shard_map/ppermute | solution.py:252
  21.4 2.5 %collective-permute-start.7 = (bf16[16,32,128]{2,1,0:T(8,128)(2,1)S(1)}, bf16[16,32,128]{2,1,0:T(8,128)(2,1)S(1)}, u32[]{:S(2)}, u32[]{:S(2)}) collective-permute-start(bf16[16,32,128]{2,1,0:T(8,128)(2,1)S(1)} %shard_map.111.refs_2_.refs_11_), channel_id=1, source_target_pairs={{0,12},{1,13},{2,14},{3,15},{4,8},{5,9},{6,10},{7,11},{8,4},{9,5},... | collective-permute-start | bytes 393224 | tf_op jit(solution)/shard_map/ppermute | solution.py:252
  23.9 0.0 collective-permute-done.3.refs_14_.refs_1_
  23.9 0.0 collective-permute-done.2.refs_13_.refs_0_
  23.9 0.0 collective-permute-done.refs_12_.refs_1_
  23.9 2.4 %shard_map.113.refs_12_ = bf16[16,32,128]{2,1,0:T(8,128)(2,1)S(1)} custom-call(s32[1]{0:T(128)} %bitcast.me_ref, f32[4]{0:T(128)S(1)} %copy-done.4, bf16[128,384]{1,0:T(8,128)(2,1)S(1)} %collective-permute-done.4.refs_0_, bf16[8,8,2,32,128]{4,3,2,1,0:T(8,128)(2,1)S(1)} %bitcast.10, bf16[8,8,2,32,128]{4,3,2,1,0:T(8,128)(2,1)S(1)} %bitcast.15, ...), custom_call_target="tpu_custom_call" | custom-call | bytes 8118000 | tf_op jit(solution)/shard_map/pallas_call | solution.py:346
  26.3 0.2 collective-permute-start.11
  26.5 0.0 collective-permute-done.6.refs_0_.refs_1_
  26.5 4.0 %shard_map.114 = (bf16[16,32,128]{2,1,0:T(8,128)(2,1)S(1)}, bf16[16,32,128]{2,1,0:T(8,128)(2,1)S(1)}) custom-call(s32[1]{0:T(128)} %bitcast.me_ref, f32[4]{0:T(128)S(1)} %copy-done.4, bf16[256,384]{1,0:T(8,128)(2,1)S(1)} %collective-permute-done.6.refs_0_.refs_1_, bf16[256,384]{1,0:T(8,128)(2,1)S(1)} %collective-permute-done.6.refs_0_.refs_1_, ...), custom_call_target="tpu_custom_call" | custom-call | bytes 16236000 | tf_op jit(solution)/shard_map/pallas_call | solution.py:346
  30.5 2.7 %collective-permute-start.12 = (bf16[16,32,128]{2,1,0:T(8,128)(2,1)S(1)}, bf16[16,32,128]{2,1,0:T(8,128)(2,1)S(1)}, u32[]{:S(2)}, u32[]{:S(2)}) collective-permute-start(bf16[16,32,128]{2,1,0:T(8,128)(2,1)S(1)} %get-tuple-element.23.refs_12_), channel_id=1, source_target_pairs={{0,10},{1,11},{2,8},{3,9},{4,14},{5,15},{6,12},{7,13},{8,2},{9,3},... | collective-permute-start | bytes 393224 | tf_op jit(solution)/shard_map/ppermute | solution.py:252
  33.3 2.3 %collective-permute-start.13 = (bf16[16,32,128]{2,1,0:T(8,128)(2,1)S(1)}, bf16[16,32,128]{2,1,0:T(8,128)(2,1)S(1)}, u32[]{:S(2)}, u32[]{:S(2)}) collective-permute-start(bf16[16,32,128]{2,1,0:T(8,128)(2,1)S(1)} %get-tuple-element.24.refs_13_), channel_id=1, source_target_pairs={{0,14},{1,15},{2,12},{3,13},{4,10},{5,11},{6,8},{7,9},{8,6},{9,7},... | collective-permute-start | bytes 393224 | tf_op jit(solution)/shard_map/ppermute | solution.py:252
  35.6 4.0 %shard_map.115 = (bf16[16,32,128]{2,1,0:T(8,128)(2,1)S(1)}, bf16[16,32,128]{2,1,0:T(8,128)(2,1)S(1)}) custom-call(s32[1]{0:T(128)} %bitcast.me_ref, f32[4]{0:T(128)S(1)} %copy-done.4, bf16[128,384]{1,0:T(8,128)(2,1)S(1)} %collective-permute-done.2.refs_13_.refs_0_, bf16[128,384]{1,0:T(8,128)(2,1)S(1)} %collective-permute-done.3.refs_14_.refs_1_, ...), custom_call_target="tpu_custom_call" | custom-call | bytes 16236000 | tf_op jit(solution)/shard_map/pallas_call | solution.py:346
  39.6 0.2 collective-permute-start.10
  39.8 0.0 collective-permute-done.7.refs_13_.refs_3_
  39.8 1.8 %collective-permute-start.9 = (bf16[16,32,128]{2,1,0:T(8,128)(2,1)S(1)}, bf16[16,32,128]{2,1,0:T(8,128)(2,1)S(1)}, u32[]{:S(2)}, u32[]{:S(2)}) collective-permute-start(bf16[16,32,128]{2,1,0:T(8,128)(2,1)S(1)} %get-tuple-element.25.refs_12_), channel_id=1, source_target_pairs={{0,4},{1,5},{2,6},{3,7},{4,0},{5,1},{6,2},{7,3},{8,12},{9,13},{10,... | collective-permute-start | bytes 393224 | tf_op jit(solution)/shard_map/ppermute | solution.py:252
  41.6 4.0 %shard_map.116 = (bf16[16,32,128]{2,1,0:T(8,128)(2,1)S(1)}, bf16[16,32,128]{2,1,0:T(8,128)(2,1)S(1)}) custom-call(s32[1]{0:T(128)} %bitcast.me_ref, f32[4]{0:T(128)S(1)} %copy-done.4, bf16[128,384]{1,0:T(8,128)(2,1)S(1)} %get-tuple-element.17.refs_0_, bf16[128,384]{1,0:T(8,128)(2,1)S(1)} %collective-permute-done.refs_12_.refs_1_, ...), custom_call_target="tpu_custom_call" | custom-call | bytes 16236000 | tf_op jit(solution)/shard_map/pallas_call | solution.py:346
  45.6 0.0 collective-permute-done.11.refs_2_
  45.6 1.6 %collective-permute-start.8 = (bf16[16,32,128]{2,1,0:T(8,128)(2,1)S(1)}, bf16[16,32,128]{2,1,0:T(8,128)(2,1)S(1)}, u32[]{:S(2)}, u32[]{:S(2)}) collective-permute-start(bf16[16,32,128]{2,1,0:T(8,128)(2,1)S(1)} %get-tuple-element.27), channel_id=1, source_target_pairs={{0,2},{1,3},{2,0},{3,1},{4,6},{5,7},{6,4},{7,5},{8,10},{9,11},{10,... | collective-permute-start | bytes 393224 | tf_op jit(solution)/shard_map/ppermute | solution.py:252
  47.2 0.0 collective-permute-done.10.refs_1_
  47.2 1.8 %collective-permute-done.9.refs_0_ = bf16[16,32,128]{2,1,0:T(8,128)(2,1)S(1)} collective-permute-done((bf16[16,32,128]{2,1,0:T(8,128)(2,1)S(1)}, bf16[16,32,128]{2,1,0:T(8,128)(2,1)S(1)}, u32[]{:S(2)}, u32[]{:S(2)}) %collective-permute-start.9) | collective-permute-done | bytes 131104 | tf_op jit(solution)/shard_map/ppermute | solution.py:252
  49.0 0.0 collective-permute-done.12.refs_4_
  49.0 0.0 collective-permute-done.13.refs_5_
  49.0 0.9 %shard_map.117.refs_2_ = bf16[128,32,128]{2,1,0:T(8,128)(2,1)} custom-call(s32[1]{0:T(128)} %bitcast.me_ref, bf16[16,32,128]{2,1,0:T(8,128)(2,1)S(1)} %collective-permute-done.9.refs_0_, bf16[16,32,128]{2,1,0:T(8,128)(2,1)S(1)} %collective-permute-done.10.refs_1_, bf16[16,32,128]{2,1,0:T(8,128)(2,1)S(1)} %collective-permute-done.11.refs_2_, ...), custom_call_target="tpu_custom_call" | custom-call | bytes 3690000 | tf_op jit(solution)/shard_map/pallas_call | solution.py:384
  49.9 0.7 %collective-permute-done.8.refs_1_ = bf16[16,32,128]{2,1,0:T(8,128)(2,1)S(1)} collective-permute-done((bf16[16,32,128]{2,1,0:T(8,128)(2,1)S(1)}, bf16[16,32,128]{2,1,0:T(8,128)(2,1)S(1)}, u32[]{:S(2)}, u32[]{:S(2)}) %collective-permute-start.8) | collective-permute-done | bytes 131104 | tf_op jit(solution)/shard_map/ppermute | solution.py:252
  50.7 0.7 %shard_map.118 = bf16[128,32,128]{2,1,0:T(8,128)(2,1)} custom-call(s32[1]{0:T(128)} %bitcast.me_ref, bf16[16,32,128]{2,1,0:T(8,128)(2,1)S(1)} %get-tuple-element.26.refs_0_, bf16[16,32,128]{2,1,0:T(8,128)(2,1)S(1)} %collective-permute-done.8.refs_1_, bf16[128,32,128]{2,1,0:T(8,128)(2,1)} %shard_map.117.refs_2_), custom_call_target="tpu_custom_call", output_to_operand_aliasing={{}: (3, {})} | custom-call | bytes 3690000 | tf_op jit(solution)/shard_map/pallas_call | solution.py:384
  (1 shorter events, 0.0 us)
Async XLA Ops:
  0.0 14.3 %copy-start = (bf16[128,512]{1,0:T(8,128)(2,1)S(1)}, bf16[128,512]{1,0:T(8,128)(2,1)}, u32[]{:S(2)}) copy-start(bf16[128,512]{1,0:T(8,128)(2,1)} %refs_9_.5) | copy-start | bytes 393220
  5.6 11.0 %copy-start.1 = (bf16[128,128]{1,0:T(8,128)(2,1)S(1)}, bf16[128,128]{1,0:T(8,128)(2,1)}, u32[]{:S(2)}) copy-start(bf16[128,128]{1,0:T(8,128)(2,1)} %refs_11_.5) | copy-start | bytes 98308
  5.6 11.0 %copy-start.2 = (s32[512]{0:T(512)S(1)}, s32[512]{0:T(512)}, u32[]{:S(2)}) copy-start(s32[512]{0:T(512)} %param.13) | copy-start | bytes 6148
  5.6 11.0 %copy-start.3 = (s32[512]{0:T(512)S(1)}, s32[512]{0:T(512)}, u32[]{:S(2)}) copy-start(s32[512]{0:T(512)} %param.14) | copy-start | bytes 6148
  5.6 11.0 %copy-start.4 = (f32[4]{0:T(128)S(1)}, f32[4]{0:T(128)}, u32[]{:S(2)}) copy-start(f32[4]{0:T(128)} %chain_bias_ref.9) | copy-start | bytes 52
  5.6 11.0 %copy-start.5 = (f32[128]{0:T(128)S(1)}, f32[128]{0:T(128)}, u32[]{:S(2)}) copy-start(f32[128]{0:T(128)} %param.18) | copy-start | bytes 1540
  5.6 8.2 %collective-permute-start.1 = (bf16[8,512,128]{2,1,0:T(8,128)(2,1)S(1)}, bf16[8,512,128]{2,1,0:T(8,128)(2,1)S(1)}, u32[]{:S(2)}, u32[]{:S(2)}) collective-permute-start(bf16[8,512,128]{2,1,0:T(8,128)(2,1)S(1)} %get-tuple-element.18.own_ref), channel_id=1, source_target_pairs={{0,1},{1,0},{2,3},{3,2},{4,5},{5,4},{6,7},{7,6},{8,9},{9,8},{10,11... | collective-permute-start | bytes 3145736 | tf_op jit(solution)/shard_map/ppermute | solution.py:252
  6.2 10.5 %collective-permute-start.5 = (bf16[128,384]{1,0:T(8,128)(2,1)S(1)}, bf16[128,384]{1,0:T(8,128)(2,1)S(1)}, u32[]{:S(2)}, u32[]{:S(2)}) collective-permute-start(bf16[128,384]{1,0:T(8,128)(2,1)S(1)} %get-tuple-element.17.refs_0_), channel_id=1, source_target_pairs={{0,12},{1,13},{2,14},{3,15},{4,8},{5,9},{6,10},{7,11},{8,4},{9,5},... | collective-permute-start | bytes 294920 | tf_op jit(solution)/shard_map/ppermute | solution.py:252
  10.8 9.0 %collective-permute-start.4 = (bf16[128,384]{1,0:T(8,128)(2,1)S(1)}, bf16[128,384]{1,0:T(8,128)(2,1)S(1)}, u32[]{:S(2)}, u32[]{:S(2)}) collective-permute-start(bf16[128,384]{1,0:T(8,128)(2,1)S(1)} %get-tuple-element.17.refs_0_), channel_id=1, source_target_pairs={{0,8},{1,9},{2,10},{3,11},{4,12},{5,13},{6,14},{7,15},{8,0},{9,1},... | collective-permute-start | bytes 294920 | tf_op jit(solution)/shard_map/ppermute | solution.py:252
  10.8 13.1 %collective-permute-start.3 = (bf16[128,384]{1,0:T(8,128)(2,1)S(1)}, bf16[128,384]{1,0:T(8,128)(2,1)S(1)}, u32[]{:S(2)}, u32[]{:S(2)}) collective-permute-start(bf16[128,384]{1,0:T(8,128)(2,1)S(1)} %get-tuple-element.17.refs_0_), channel_id=1, source_target_pairs={{0,6},{1,7},{2,4},{3,5},{4,2},{5,3},{6,0},{7,1},{8,14},{9,15},{10,... | collective-permute-start | bytes 294920 | tf_op jit(solution)/shard_map/ppermute | solution.py:252
  12.6 11.3 %collective-permute-start.2 = (bf16[128,384]{1,0:T(8,128)(2,1)S(1)}, bf16[128,384]{1,0:T(8,128)(2,1)S(1)}, u32[]{:S(2)}, u32[]{:S(2)}) collective-permute-start(bf16[128,384]{1,0:T(8,128)(2,1)S(1)} %get-tuple-element.17.refs_0_), channel_id=1, source_target_pairs={{0,4},{1,5},{2,6},{3,7},{4,0},{5,1},{6,2},{7,3},{8,12},{9,13},{10,... | collective-permute-start | bytes 294920 | tf_op jit(solution)/shard_map/ppermute | solution.py:252
  13.8 10.1 %collective-permute-start = (bf16[128,384]{1,0:T(8,128)(2,1)S(1)}, bf16[128,384]{1,0:T(8,128)(2,1)S(1)}, u32[]{:S(2)}, u32[]{:S(2)}) collective-permute-start(bf16[128,384]{1,0:T(8,128)(2,1)S(1)} %get-tuple-element.17.refs_0_), channel_id=1, source_target_pairs={{0,2},{1,3},{2,0},{3,1},{4,6},{5,7},{6,4},{7,5},{8,10},{9,11},{10,... | collective-permute-start | bytes 294920 | tf_op jit(solution)/shard_map/ppermute | solution.py:252
  19.8 6.7 %collective-permute-start.6 = (bf16[256,384]{1,0:T(8,128)(2,1)S(1)}, bf16[256,384]{1,0:T(8,128)(2,1)S(1)}, u32[]{:S(2)}, u32[]{:S(2)}) collective-permute-start(bf16[256,384]{1,0:T(8,128)(2,1)S(1)} %shard_map.112), channel_id=1, source_target_pairs={{0,2},{1,3},{2,0},{3,1},{4,6},{5,7},{6,4},{7,5},{8,10},{9,11},{10,... | collective-permute-start | bytes 589832 | tf_op jit(solution)/shard_map/ppermute | solution.py:252
  21.4 18.4 %collective-permute-start.7 = (bf16[16,32,128]{2,1,0:T(8,128)(2,1)S(1)}, bf16[16,32,128]{2,1,0:T(8,128)(2,1)S(1)}, u32[]{:S(2)}, u32[]{:S(2)}) collective-permute-start(bf16[16,32,128]{2,1,0:T(8,128)(2,1)S(1)} %shard_map.111.refs_2_.refs_11_), channel_id=1, source_target_pairs={{0,12},{1,13},{2,14},{3,15},{4,8},{5,9},{6,10},{7,11},{8,4},{9,5},... | collective-permute-start | bytes 393224 | tf_op jit(solution)/shard_map/ppermute | solution.py:252
  26.3 19.4 %collective-permute-start.11 = (bf16[16,32,128]{2,1,0:T(8,128)(2,1)S(1)}, bf16[16,32,128]{2,1,0:T(8,128)(2,1)S(1)}, u32[]{:S(2)}, u32[]{:S(2)}) collective-permute-start(bf16[16,32,128]{2,1,0:T(8,128)(2,1)S(1)} %shard_map.113.refs_12_), channel_id=1, source_target_pairs={{0,8},{1,9},{2,10},{3,11},{4,12},{5,13},{6,14},{7,15},{8,0},{9,1},... | collective-permute-start | bytes 393224 | tf_op jit(solution)/shard_map/ppermute | solution.py:252
  30.5 18.5 %collective-permute-start.12 = (bf16[16,32,128]{2,1,0:T(8,128)(2,1)S(1)}, bf16[16,32,128]{2,1,0:T(8,128)(2,1)S(1)}, u32[]{:S(2)}, u32[]{:S(2)}) collective-permute-start(bf16[16,32,128]{2,1,0:T(8,128)(2,1)S(1)} %get-tuple-element.23.refs_12_), channel_id=1, source_target_pairs={{0,10},{1,11},{2,8},{3,9},{4,14},{5,15},{6,12},{7,13},{8,2},{9,3},... | collective-permute-start | bytes 393224 | tf_op jit(solution)/shard_map/ppermute | solution.py:252
  33.3 15.7 %collective-permute-start.13 = (bf16[16,32,128]{2,1,0:T(8,128)(2,1)S(1)}, bf16[16,32,128]{2,1,0:T(8,128)(2,1)S(1)}, u32[]{:S(2)}, u32[]{:S(2)}) collective-permute-start(bf16[16,32,128]{2,1,0:T(8,128)(2,1)S(1)} %get-tuple-element.24.refs_13_), channel_id=1, source_target_pairs={{0,14},{1,15},{2,12},{3,13},{4,10},{5,11},{6,8},{7,9},{8,6},{9,7},... | collective-permute-start | bytes 393224 | tf_op jit(solution)/shard_map/ppermute | solution.py:252
  39.6 7.6 %collective-permute-start.10 = (bf16[16,32,128]{2,1,0:T(8,128)(2,1)S(1)}, bf16[16,32,128]{2,1,0:T(8,128)(2,1)S(1)}, u32[]{:S(2)}, u32[]{:S(2)}) collective-permute-start(bf16[16,32,128]{2,1,0:T(8,128)(2,1)S(1)} %get-tuple-element.28), channel_id=1, source_target_pairs={{0,6},{1,7},{2,4},{3,5},{4,2},{5,3},{6,0},{7,1},{8,14},{9,15},{10,... | collective-permute-start | bytes 393224 | tf_op jit(solution)/shard_map/ppermute | solution.py:252
  39.8 9.2 %collective-permute-start.9 = (bf16[16,32,128]{2,1,0:T(8,128)(2,1)S(1)}, bf16[16,32,128]{2,1,0:T(8,128)(2,1)S(1)}, u32[]{:S(2)}, u32[]{:S(2)}) collective-permute-start(bf16[16,32,128]{2,1,0:T(8,128)(2,1)S(1)} %get-tuple-element.25.refs_12_), channel_id=1, source_target_pairs={{0,4},{1,5},{2,6},{3,7},{4,0},{5,1},{6,2},{7,3},{8,12},{9,13},{10,... | collective-permute-start | bytes 393224 | tf_op jit(solution)/shard_map/ppermute | solution.py:252
  45.6 5.0 %collective-permute-start.8 = (bf16[16,32,128]{2,1,0:T(8,128)(2,1)S(1)}, bf16[16,32,128]{2,1,0:T(8,128)(2,1)S(1)}, u32[]{:S(2)}, u32[]{:S(2)}) collective-permute-start(bf16[16,32,128]{2,1,0:T(8,128)(2,1)S(1)} %get-tuple-element.27), channel_id=1, source_target_pairs={{0,2},{1,3},{2,0},{3,1},{4,6},{5,7},{6,4},{7,5},{8,10},{9,11},{10,... | collective-permute-start | bytes 393224 | tf_op jit(solution)/shard_map/ppermute | solution.py:252

commit v12 on v11

--- a/solution.py
+++ b/solution.py
@@ -167,9 +167,9 @@
                 jnp.dot(x, w_g, preferred_element_type=F32) + gate_bias_ref[...]
             )
 
-        def some_windows(g, carry):
+        def some_windows(g):
             spans = [
-                pl.ds(pl.multiple_of((g * half + i) * block, block), block) for i in range(half)
+                slice((g * half + i) * block, (g * half + i + 1) * block) for i in range(half)
             ]
             scores = []
             for i in range(half):
@@ -193,9 +193,9 @@
                 for h in range(1, heads):
                     attended = jnp.where(lane_head == h, m[h * block : (h + 1) * block], attended)
                 gated_s[spans[i], :] = (gate_s[spans[i], :] * attended).astype(BF16)
-            return carry
-
-        lax.fori_loop(0, 2, some_windows, 0)
+
+        for g in range(2):
+            some_windows(g)
         result = jnp.dot(gated_s[...], w_out_ref[...], preferred_element_type=F32)
         result = (result.reshape(windows, block, inner) * keep[None]).astype(BF16)
         out_refs[b][pl.ds(core * half, half)] = result[:half]

time: 51.5 us -> 51 us (level)
  Pallas kernels: 26.2 us -> 24.4 us
  waiting for transfers between devices: 3.31 us -> 4.65 us
    pallas_call x5, Pallas kernels: 16.7 us -> 14.9 us  [local(): pl.pallas_call(functools.partial(attention_kernel, heads, ms, first), out...]
    ppermute x14, waiting for transfers between devices: 3.31 us -> 4.65 us  [swap(): return lax.ppermute(x, 'row', [(i, i ^ bits) for i in range(devices)])]
  transfers between devices with their start and end apart: 14 -> 14, of which waited for: 3 -> 4; matrix products, arithmetic and copies ran while one was open for 0% -> 0% of each run, Pallas kernels for 39% -> 36%
where the time goes in v12:
time: 51 us; the launch traced here: 50.9 us
  Pallas kernels  24.4 us (48%)
  starting transfers between devices  21.4 us (42%)
  waiting for transfers between devices  4.65 us (9%)
    ppermute x14, starting transfers between devices, swap(): return lax.ppermute(x, 'row', [(i, i ^ bits) for i in range(devices)])  21.4 us
    pallas_call x5, Pallas kernels, local(): pl.pallas_call(functools.partial(attention_kernel, heads, ms, first), out...  14.9 us
    pallas_call x1, Pallas kernels, local(): pl.pallas_call(bias_kernel, grid=(rows_held // step_rows,), out_shape=[ja...  5.57 us
    ppermute x14, waiting for transfers between devices, swap(): return lax.ppermute(x, 'row', [(i, i ^ bits) for i in range(devices)])  4.65 us
    pallas_call x1, Pallas kernels, local(): pl.pallas_call(key_value_kernel, out_shape=[jax.ShapeDtypeStruct((2 * cou...  2.27 us
    pallas_call x2, Pallas kernels, local(): pl.pallas_call(functools.partial(gather_kernel, order), out_shape=jax.Sha...  1.65 us
  transfers between devices with their start and end apart: 14, of which 4 were waited for; matrix products, arithmetic and copies ran while one was open for 0% of the time, Pallas kernels for 36%

profile of v12, /device:TPU:0, one launch (start us, length us, event | category | flops | bytes accessed | tf_op | source)
XLA Modules:
  0.0 50.9 jit_solution(10322571160401586167)
XLA Ops:
  0.0 0.0 copy-start
  0.0 5.6 %shard_map.109 = (bf16[128,384]{1,0:T(8,128)(2,1)S(1)}, bf16[8,512,128]{2,1,0:T(8,128)(2,1)S(1)}, bf16[384,512]{1,0:T(8,128)(2,1)S(1)}, f32[8,384]{1,0:T(8,128)S(1)}) custom-call(s32[1]{0:T(128)} %bitcast.me_ref, s32[8]{0:T(128)} %rows_ref.1, bf16[32,512,128]{2,1,0:T(8,128)(2,1)} %pair_ref.1, s32[1,512]{1,0:T(1,128)} %bitcast.19, s32[1,512]{1,0:T(1,128)} %bitcast.25, ...), custom_call_target="tpu_custom_call" | custom-call | bytes 22140000 | tf_op jit(solution)/shard_map/pallas_call | solution.py:255
  5.6 0.0 copy-start.1
  5.6 0.0 copy-start.2
  5.6 0.0 copy-start.3
  5.6 0.0 copy-start.4
  5.6 0.0 copy-start.5
  5.6 0.5 %collective-permute-start.1 = (bf16[8,512,128]{2,1,0:T(8,128)(2,1)S(1)}, bf16[8,512,128]{2,1,0:T(8,128)(2,1)S(1)}, u32[]{:S(2)}, u32[]{:S(2)}) collective-permute-start(bf16[8,512,128]{2,1,0:T(8,128)(2,1)S(1)} %get-tuple-element.18.own_ref), channel_id=1, source_target_pairs={{0,1},{1,0},{2,3},{3,2},{4,5},{5,4},{6,7},{7,6},{8,9},{9,8},{10,11... | collective-permute-start | bytes 3145736 | tf_op jit(solution)/shard_map/ppermute | solution.py:252
  6.2 4.7 %collective-permute-start.5 = (bf16[128,384]{1,0:T(8,128)(2,1)S(1)}, bf16[128,384]{1,0:T(8,128)(2,1)S(1)}, u32[]{:S(2)}, u32[]{:S(2)}) collective-permute-start(bf16[128,384]{1,0:T(8,128)(2,1)S(1)} %get-tuple-element.17.refs_0_), channel_id=1, source_target_pairs={{0,12},{1,13},{2,14},{3,15},{4,8},{5,9},{6,10},{7,11},{8,4},{9,5},... | collective-permute-start | bytes 294920 | tf_op jit(solution)/shard_map/ppermute | solution.py:252
  10.8 0.0 collective-permute-start.4
  10.8 1.7 %collective-permute-start.3 = (bf16[128,384]{1,0:T(8,128)(2,1)S(1)}, bf16[128,384]{1,0:T(8,128)(2,1)S(1)}, u32[]{:S(2)}, u32[]{:S(2)}) collective-permute-start(bf16[128,384]{1,0:T(8,128)(2,1)S(1)} %get-tuple-element.17.refs_0_), channel_id=1, source_target_pairs={{0,6},{1,7},{2,4},{3,5},{4,2},{5,3},{6,0},{7,1},{8,14},{9,15},{10,... | collective-permute-start | bytes 294920 | tf_op jit(solution)/shard_map/ppermute | solution.py:252
  12.6 1.2 %collective-permute-start.2 = (bf16[128,384]{1,0:T(8,128)(2,1)S(1)}, bf16[128,384]{1,0:T(8,128)(2,1)S(1)}, u32[]{:S(2)}, u32[]{:S(2)}) collective-permute-start(bf16[128,384]{1,0:T(8,128)(2,1)S(1)} %get-tuple-element.17.refs_0_), channel_id=1, source_target_pairs={{0,4},{1,5},{2,6},{3,7},{4,0},{5,1},{6,2},{7,3},{8,12},{9,13},{10,... | collective-permute-start | bytes 294920 | tf_op jit(solution)/shard_map/ppermute | solution.py:252
  13.8 0.0 collective-permute-done.1.other_ref
  13.8 0.5 collective-permute-start
  14.3 0.0 copy-done
  14.3 2.3 %shard_map.110 = (bf16[16,128,384]{2,1,0:T(8,128)(2,1)S(1)}, bf16[16,384,128]{2,1,0:T(8,128)(2,1)S(1)}) custom-call(bf16[8,512,128]{2,1,0:T(8,128)(2,1)S(1)} %get-tuple-element.18.own_ref, bf16[8,512,128]{2,1,0:T(8,128)(2,1)S(1)} %collective-permute-done.1.other_ref, bf16[384,512]{1,0:T(8,128)(2,1)S(1)} %get-tuple-element.19.pick_ref, ...), custom_call_target="tpu_custom_call" | custom-call | bytes 7380000 | tf_op jit(solution)/shard_map/pallas_call | solution.py:304
  16.6 0.0 collective-permute-done.5.refs_0_.refs_1_
  16.6 0.0 copy-done.1
  16.6 0.0 copy-done.2
  16.6 0.0 copy-done.3
  16.7 0.0 copy-done.4
  16.7 0.0 copy-done.5
  16.7 2.1 %shard_map.111.refs_2_.refs_11_ = bf16[16,32,128]{2,1,0:T(8,128)(2,1)S(1)} custom-call(s32[1]{0:T(128)} %bitcast.me_ref, f32[4]{0:T(128)S(1)} %copy-done.4, bf16[128,384]{1,0:T(8,128)(2,1)S(1)} %collective-permute-done.5.refs_0_.refs_1_, bf16[8,8,2,32,128]{4,3,2,1,0:T(8,128)(2,1)S(1)} %bitcast.9, bf16[8,8,2,32,128]{4,3,2,1,0:T(8,128)(2,1)S(1)} %bitcast.14, ...), custom_call_target="tpu_custom_call" | custom-call | bytes 8118000 | tf_op jit(solution)/shard_map/pallas_call | solution.py:346
  18.8 1.0 %collective-permute-done.4.refs_0_ = bf16[128,384]{1,0:T(8,128)(2,1)S(1)} collective-permute-done((bf16[128,384]{1,0:T(8,128)(2,1)S(1)}, bf16[128,384]{1,0:T(8,128)(2,1)S(1)}, u32[]{:S(2)}, u32[]{:S(2)}) %collective-permute-start.4) | collective-permute-done | bytes 98336 | tf_op jit(solution)/shard_map/ppermute | solution.py:252
  19.8 1.6 %collective-permute-start.6 = (bf16[256,384]{1,0:T(8,128)(2,1)S(1)}, bf16[256,384]{1,0:T(8,128)(2,1)S(1)}, u32[]{:S(2)}, u32[]{:S(2)}) collective-permute-start(bf16[256,384]{1,0:T(8,128)(2,1)S(1)} %shard_map.112), channel_id=1, source_target_pairs={{0,2},{1,3},{2,0},{3,1},{4,6},{5,7},{6,4},{7,5},{8,10},{9,11},{10,... | collective-permute-start | bytes 589832 | tf_op jit(solution)/shard_map/ppermute | solution.py:252
  21.4 2.5 %collective-permute-start.7 = (bf16[16,32,128]{2,1,0:T(8,128)(2,1)S(1)}, bf16[16,32,128]{2,1,0:T(8,128)(2,1)S(1)}, u32[]{:S(2)}, u32[]{:S(2)}) collective-permute-start(bf16[16,32,128]{2,1,0:T(8,128)(2,1)S(1)} %shard_map.111.refs_2_.refs_11_), channel_id=1, source_target_pairs={{0,12},{1,13},{2,14},{3,15},{4,8},{5,9},{6,10},{7,11},{8,4},{9,5},... | collective-permute-start | bytes 393224 | tf_op jit(solution)/shard_map/ppermute | solution.py:252
  23.9 0.0 collective-permute-done.3.refs_14_.refs_1_
  23.9 0.0 collective-permute-done.2.refs_13_.refs_0_
  23.9 0.0 collective-permute-done.refs_12_.refs_1_
  23.9 2.1 %shard_map.113.refs_12_ = bf16[16,32,128]{2,1,0:T(8,128)(2,1)S(1)} custom-call(s32[1]{0:T(128)} %bitcast.me_ref, f32[4]{0:T(128)S(1)} %copy-done.4, bf16[128,384]{1,0:T(8,128)(2,1)S(1)} %collective-permute-done.4.refs_0_, bf16[8,8,2,32,128]{4,3,2,1,0:T(8,128)(2,1)S(1)} %bitcast.10, bf16[8,8,2,32,128]{4,3,2,1,0:T(8,128)(2,1)S(1)} %bitcast.15, ...), custom_call_target="tpu_custom_call" | custom-call | bytes 8118000 | tf_op jit(solution)/shard_map/pallas_call | solution.py:346
  26.1 0.1 collective-permute-start.11
  26.1 0.2 collective-permute-done.6.refs_0_.refs_1_
  26.3 3.5 %shard_map.114 = (bf16[16,32,128]{2,1,0:T(8,128)(2,1)S(1)}, bf16[16,32,128]{2,1,0:T(8,128)(2,1)S(1)}) custom-call(s32[1]{0:T(128)} %bitcast.me_ref, f32[4]{0:T(128)S(1)} %copy-done.4, bf16[256,384]{1,0:T(8,128)(2,1)S(1)} %collective-permute-done.6.refs_0_.refs_1_, bf16[256,384]{1,0:T(8,128)(2,1)S(1)} %collective-permute-done.6.refs_0_.refs_1_, ...), custom_call_target="tpu_custom_call" | custom-call | bytes 16236000 | tf_op jit(solution)/shard_map/pallas_call | solution.py:346
  29.9 2.7 %collective-permute-start.12 = (bf16[16,32,128]{2,1,0:T(8,128)(2,1)S(1)}, bf16[16,32,128]{2,1,0:T(8,128)(2,1)S(1)}, u32[]{:S(2)}, u32[]{:S(2)}) collective-permute-start(bf16[16,32,128]{2,1,0:T(8,128)(2,1)S(1)} %get-tuple-element.23.refs_12_), channel_id=1, source_target_pairs={{0,10},{1,11},{2,8},{3,9},{4,14},{5,15},{6,12},{7,13},{8,2},{9,3},... | collective-permute-start | bytes 393224 | tf_op jit(solution)/shard_map/ppermute | solution.py:252
  32.6 2.3 %collective-permute-start.13 = (bf16[16,32,128]{2,1,0:T(8,128)(2,1)S(1)}, bf16[16,32,128]{2,1,0:T(8,128)(2,1)S(1)}, u32[]{:S(2)}, u32[]{:S(2)}) collective-permute-start(bf16[16,32,128]{2,1,0:T(8,128)(2,1)S(1)} %get-tuple-element.24.refs_13_), channel_id=1, source_target_pairs={{0,14},{1,15},{2,12},{3,13},{4,10},{5,11},{6,8},{7,9},{8,6},{9,7},... | collective-permute-start | bytes 393224 | tf_op jit(solution)/shard_map/ppermute | solution.py:252
  34.9 3.5 %shard_map.115 = (bf16[16,32,128]{2,1,0:T(8,128)(2,1)S(1)}, bf16[16,32,128]{2,1,0:T(8,128)(2,1)S(1)}) custom-call(s32[1]{0:T(128)} %bitcast.me_ref, f32[4]{0:T(128)S(1)} %copy-done.4, bf16[128,384]{1,0:T(8,128)(2,1)S(1)} %collective-permute-done.2.refs_13_.refs_0_, bf16[128,384]{1,0:T(8,128)(2,1)S(1)} %collective-permute-done.3.refs_14_.refs_1_, ...), custom_call_target="tpu_custom_call" | custom-call | bytes 16236000 | tf_op jit(solution)/shard_map/pallas_call | solution.py:346
  38.4 0.4 collective-permute-start.10
  38.8 0.0 collective-permute-done.7.refs_13_.refs_3_
  38.8 1.6 %collective-permute-start.9 = (bf16[16,32,128]{2,1,0:T(8,128)(2,1)S(1)}, bf16[16,32,128]{2,1,0:T(8,128)(2,1)S(1)}, u32[]{:S(2)}, u32[]{:S(2)}) collective-permute-start(bf16[16,32,128]{2,1,0:T(8,128)(2,1)S(1)} %get-tuple-element.25.refs_12_), channel_id=1, source_target_pairs={{0,4},{1,5},{2,6},{3,7},{4,0},{5,1},{6,2},{7,3},{8,12},{9,13},{10,... | collective-permute-start | bytes 393224 | tf_op jit(solution)/shard_map/ppermute | solution.py:252
  40.5 3.6 %shard_map.116 = (bf16[16,32,128]{2,1,0:T(8,128)(2,1)S(1)}, bf16[16,32,128]{2,1,0:T(8,128)(2,1)S(1)}) custom-call(s32[1]{0:T(128)} %bitcast.me_ref, f32[4]{0:T(128)S(1)} %copy-done.4, bf16[128,384]{1,0:T(8,128)(2,1)S(1)} %get-tuple-element.17.refs_0_, bf16[128,384]{1,0:T(8,128)(2,1)S(1)} %collective-permute-done.refs_12_.refs_1_, ...), custom_call_target="tpu_custom_call" | custom-call | bytes 16236000 | tf_op jit(solution)/shard_map/pallas_call | solution.py:346
  44.0 0.0 collective-permute-done.11.refs_2_
  44.0 1.6 %collective-permute-start.8 = (bf16[16,32,128]{2,1,0:T(8,128)(2,1)S(1)}, bf16[16,32,128]{2,1,0:T(8,128)(2,1)S(1)}, u32[]{:S(2)}, u32[]{:S(2)}) collective-permute-start(bf16[16,32,128]{2,1,0:T(8,128)(2,1)S(1)} %get-tuple-element.27), channel_id=1, source_target_pairs={{0,2},{1,3},{2,0},{3,1},{4,6},{5,7},{6,4},{7,5},{8,10},{9,11},{10,... | collective-permute-start | bytes 393224 | tf_op jit(solution)/shard_map/ppermute | solution.py:252
  45.6 1.0 %collective-permute-done.10.refs_1_ = bf16[16,32,128]{2,1,0:T(8,128)(2,1)S(1)} collective-permute-done((bf16[16,32,128]{2,1,0:T(8,128)(2,1)S(1)}, bf16[16,32,128]{2,1,0:T(8,128)(2,1)S(1)}, u32[]{:S(2)}, u32[]{:S(2)}) %collective-permute-start.10) | collective-permute-done | bytes 131104 | tf_op jit(solution)/shard_map/ppermute | solution.py:252
  46.6 2.4 %collective-permute-done.9.refs_0_ = bf16[16,32,128]{2,1,0:T(8,128)(2,1)S(1)} collective-permute-done((bf16[16,32,128]{2,1,0:T(8,128)(2,1)S(1)}, bf16[16,32,128]{2,1,0:T(8,128)(2,1)S(1)}, u32[]{:S(2)}, u32[]{:S(2)}) %collective-permute-start.9) | collective-permute-done | bytes 131104 | tf_op jit(solution)/shard_map/ppermute | solution.py:252
  49.0 0.0 collective-permute-done.12.refs_4_
  49.0 0.0 collective-permute-done.13.refs_5_
  49.0 0.9 %shard_map.117.refs_2_ = bf16[128,32,128]{2,1,0:T(8,128)(2,1)} custom-call(s32[1]{0:T(128)} %bitcast.me_ref, bf16[16,32,128]{2,1,0:T(8,128)(2,1)S(1)} %collective-permute-done.9.refs_0_, bf16[16,32,128]{2,1,0:T(8,128)(2,1)S(1)} %collective-permute-done.10.refs_1_, bf16[16,32,128]{2,1,0:T(8,128)(2,1)S(1)} %collective-permute-done.11.refs_2_, ...), custom_call_target="tpu_custom_call" | custom-call | bytes 3690000 | tf_op jit(solution)/shard_map/pallas_call | solution.py:384
  50.0 0.0 collective-permute-done.8.refs_1_
  50.0 0.7 %shard_map.118 = bf16[128,32,128]{2,1,0:T(8,128)(2,1)} custom-call(s32[1]{0:T(128)} %bitcast.me_ref, bf16[16,32,128]{2,1,0:T(8,128)(2,1)S(1)} %get-tuple-element.26.refs_0_, bf16[16,32,128]{2,1,0:T(8,128)(2,1)S(1)} %collective-permute-done.8.refs_1_, bf16[128,32,128]{2,1,0:T(8,128)(2,1)} %shard_map.117.refs_2_), custom_call_target="tpu_custom_call", output_to_operand_aliasing={{}: (3, {})} | custom-call | bytes 3690000 | tf_op jit(solution)/shard_map/pallas_call | solution.py:384
  (1 shorter events, 0.0 us)
Async XLA Ops:
  0.0 14.3 %copy-start = (bf16[128,512]{1,0:T(8,128)(2,1)S(1)}, bf16[128,512]{1,0:T(8,128)(2,1)}, u32[]{:S(2)}) copy-start(bf16[128,512]{1,0:T(8,128)(2,1)} %refs_9_.5) | copy-start | bytes 393220
  5.6 11.0 %copy-start.1 = (bf16[128,128]{1,0:T(8,128)(2,1)S(1)}, bf16[128,128]{1,0:T(8,128)(2,1)}, u32[]{:S(2)}) copy-start(bf16[128,128]{1,0:T(8,128)(2,1)} %refs_11_.5) | copy-start | bytes 98308
  5.6 11.0 %copy-start.2 = (s32[512]{0:T(512)S(1)}, s32[512]{0:T(512)}, u32[]{:S(2)}) copy-start(s32[512]{0:T(512)} %param.13) | copy-start | bytes 6148
  5.6 11.0 %copy-start.3 = (s32[512]{0:T(512)S(1)}, s32[512]{0:T(512)}, u32[]{:S(2)}) copy-start(s32[512]{0:T(512)} %param.14) | copy-start | bytes 6148
  5.6 11.0 %copy-start.4 = (f32[4]{0:T(128)S(1)}, f32[4]{0:T(128)}, u32[]{:S(2)}) copy-start(f32[4]{0:T(128)} %chain_bias_ref.9) | copy-start | bytes 52
  5.6 11.0 %copy-start.5 = (f32[128]{0:T(128)S(1)}, f32[128]{0:T(128)}, u32[]{:S(2)}) copy-start(f32[128]{0:T(128)} %param.18) | copy-start | bytes 1540
  5.6 8.2 %collective-permute-start.1 = (bf16[8,512,128]{2,1,0:T(8,128)(2,1)S(1)}, bf16[8,512,128]{2,1,0:T(8,128)(2,1)S(1)}, u32[]{:S(2)}, u32[]{:S(2)}) collective-permute-start(bf16[8,512,128]{2,1,0:T(8,128)(2,1)S(1)} %get-tuple-element.18.own_ref), channel_id=1, source_target_pairs={{0,1},{1,0},{2,3},{3,2},{4,5},{5,4},{6,7},{7,6},{8,9},{9,8},{10,11... | collective-permute-start | bytes 3145736 | tf_op jit(solution)/shard_map/ppermute | solution.py:252
  6.2 10.5 %collective-permute-start.5 = (bf16[128,384]{1,0:T(8,128)(2,1)S(1)}, bf16[128,384]{1,0:T(8,128)(2,1)S(1)}, u32[]{:S(2)}, u32[]{:S(2)}) collective-permute-start(bf16[128,384]{1,0:T(8,128)(2,1)S(1)} %get-tuple-element.17.refs_0_), channel_id=1, source_target_pairs={{0,12},{1,13},{2,14},{3,15},{4,8},{5,9},{6,10},{7,11},{8,4},{9,5},... | collective-permute-start | bytes 294920 | tf_op jit(solution)/shard_map/ppermute | solution.py:252
  10.8 9.0 %collective-permute-start.4 = (bf16[128,384]{1,0:T(8,128)(2,1)S(1)}, bf16[128,384]{1,0:T(8,128)(2,1)S(1)}, u32[]{:S(2)}, u32[]{:S(2)}) collective-permute-start(bf16[128,384]{1,0:T(8,128)(2,1)S(1)} %get-tuple-element.17.refs_0_), channel_id=1, source_target_pairs={{0,8},{1,9},{2,10},{3,11},{4,12},{5,13},{6,14},{7,15},{8,0},{9,1},... | collective-permute-start | bytes 294920 | tf_op jit(solution)/shard_map/ppermute | solution.py:252
  10.8 13.1 %collective-permute-start.3 = (bf16[128,384]{1,0:T(8,128)(2,1)S(1)}, bf16[128,384]{1,0:T(8,128)(2,1)S(1)}, u32[]{:S(2)}, u32[]{:S(2)}) collective-permute-start(bf16[128,384]{1,0:T(8,128)(2,1)S(1)} %get-tuple-element.17.refs_0_), channel_id=1, source_target_pairs={{0,6},{1,7},{2,4},{3,5},{4,2},{5,3},{6,0},{7,1},{8,14},{9,15},{10,... | collective-permute-start | bytes 294920 | tf_op jit(solution)/shard_map/ppermute | solution.py:252
  12.6 11.3 %collective-permute-start.2 = (bf16[128,384]{1,0:T(8,128)(2,1)S(1)}, bf16[128,384]{1,0:T(8,128)(2,1)S(1)}, u32[]{:S(2)}, u32[]{:S(2)}) collective-permute-start(bf16[128,384]{1,0:T(8,128)(2,1)S(1)} %get-tuple-element.17.refs_0_), channel_id=1, source_target_pairs={{0,4},{1,5},{2,6},{3,7},{4,0},{5,1},{6,2},{7,3},{8,12},{9,13},{10,... | collective-permute-start | bytes 294920 | tf_op jit(solution)/shard_map/ppermute | solution.py:252
  13.8 10.1 %collective-permute-start = (bf16[128,384]{1,0:T(8,128)(2,1)S(1)}, bf16[128,384]{1,0:T(8,128)(2,1)S(1)}, u32[]{:S(2)}, u32[]{:S(2)}) collective-permute-start(bf16[128,384]{1,0:T(8,128)(2,1)S(1)} %get-tuple-element.17.refs_0_), channel_id=1, source_target_pairs={{0,2},{1,3},{2,0},{3,1},{4,6},{5,7},{6,4},{7,5},{8,10},{9,11},{10,... | collective-permute-start | bytes 294920 | tf_op jit(solution)/shard_map/ppermute | solution.py:252
  19.8 6.5 %collective-permute-start.6 = (bf16[256,384]{1,0:T(8,128)(2,1)S(1)}, bf16[256,384]{1,0:T(8,128)(2,1)S(1)}, u32[]{:S(2)}, u32[]{:S(2)}) collective-permute-start(bf16[256,384]{1,0:T(8,128)(2,1)S(1)} %shard_map.112), channel_id=1, source_target_pairs={{0,2},{1,3},{2,0},{3,1},{4,6},{5,7},{6,4},{7,5},{8,10},{9,11},{10,... | collective-permute-start | bytes 589832 | tf_op jit(solution)/shard_map/ppermute | solution.py:252
  21.4 17.4 %collective-permute-start.7 = (bf16[16,32,128]{2,1,0:T(8,128)(2,1)S(1)}, bf16[16,32,128]{2,1,0:T(8,128)(2,1)S(1)}, u32[]{:S(2)}, u32[]{:S(2)}) collective-permute-start(bf16[16,32,128]{2,1,0:T(8,128)(2,1)S(1)} %shard_map.111.refs_2_.refs_11_), channel_id=1, source_target_pairs={{0,12},{1,13},{2,14},{3,15},{4,8},{5,9},{6,10},{7,11},{8,4},{9,5},... | collective-permute-start | bytes 393224 | tf_op jit(solution)/shard_map/ppermute | solution.py:252
  26.1 18.0 %collective-permute-start.11 = (bf16[16,32,128]{2,1,0:T(8,128)(2,1)S(1)}, bf16[16,32,128]{2,1,0:T(8,128)(2,1)S(1)}, u32[]{:S(2)}, u32[]{:S(2)}) collective-permute-start(bf16[16,32,128]{2,1,0:T(8,128)(2,1)S(1)} %shard_map.113.refs_12_), channel_id=1, source_target_pairs={{0,8},{1,9},{2,10},{3,11},{4,12},{5,13},{6,14},{7,15},{8,0},{9,1},... | collective-permute-start | bytes 393224 | tf_op jit(solution)/shard_map/ppermute | solution.py:252
  29.9 19.2 %collective-permute-start.12 = (bf16[16,32,128]{2,1,0:T(8,128)(2,1)S(1)}, bf16[16,32,128]{2,1,0:T(8,128)(2,1)S(1)}, u32[]{:S(2)}, u32[]{:S(2)}) collective-permute-start(bf16[16,32,128]{2,1,0:T(8,128)(2,1)S(1)} %get-tuple-element.23.refs_12_), channel_id=1, source_target_pairs={{0,10},{1,11},{2,8},{3,9},{4,14},{5,15},{6,12},{7,13},{8,2},{9,3},... | collective-permute-start | bytes 393224 | tf_op jit(solution)/shard_map/ppermute | solution.py:252
  32.6 16.5 %collective-permute-start.13 = (bf16[16,32,128]{2,1,0:T(8,128)(2,1)S(1)}, bf16[16,32,128]{2,1,0:T(8,128)(2,1)S(1)}, u32[]{:S(2)}, u32[]{:S(2)}) collective-permute-start(bf16[16,32,128]{2,1,0:T(8,128)(2,1)S(1)} %get-tuple-element.24.refs_13_), channel_id=1, source_target_pairs={{0,14},{1,15},{2,12},{3,13},{4,10},{5,11},{6,8},{7,9},{8,6},{9,7},... | collective-permute-start | bytes 393224 | tf_op jit(solution)/shard_map/ppermute | solution.py:252
  38.4 8.2 %collective-permute-start.10 = (bf16[16,32,128]{2,1,0:T(8,128)(2,1)S(1)}, bf16[16,32,128]{2,1,0:T(8,128)(2,1)S(1)}, u32[]{:S(2)}, u32[]{:S(2)}) collective-permute-start(bf16[16,32,128]{2,1,0:T(8,128)(2,1)S(1)} %get-tuple-element.28), channel_id=1, source_target_pairs={{0,6},{1,7},{2,4},{3,5},{4,2},{5,3},{6,0},{7,1},{8,14},{9,15},{10,... | collective-permute-start | bytes 393224 | tf_op jit(solution)/shard_map/ppermute | solution.py:252
  38.8 10.2 %collective-permute-start.9 = (bf16[16,32,128]{2,1,0:T(8,128)(2,1)S(1)}, bf16[16,32,128]{2,1,0:T(8,128)(2,1)S(1)}, u32[]{:S(2)}, u32[]{:S(2)}) collective-permute-start(bf16[16,32,128]{2,1,0:T(8,128)(2,1)S(1)} %get-tuple-element.25.refs_12_), channel_id=1, source_target_pairs={{0,4},{1,5},{2,6},{3,7},{4,0},{5,1},{6,2},{7,3},{8,12},{9,13},{10,... | collective-permute-start | bytes 393224 | tf_op jit(solution)/shard_map/ppermute | solution.py:252
  44.0 6.0 %collective-permute-start.8 = (bf16[16,32,128]{2,1,0:T(8,128)(2,1)S(1)}, bf16[16,32,128]{2,1,0:T(8,128)(2,1)S(1)}, u32[]{:S(2)}, u32[]{:S(2)}) collective-permute-start(bf16[16,32,128]{2,1,0:T(8,128)(2,1)S(1)} %get-tuple-element.27), channel_id=1, source_target_pairs={{0,2},{1,3},{2,0},{3,1},{4,6},{5,7},{6,4},{7,5},{8,10},{9,11},{10,... | collective-permute-start | bytes 393224 | tf_op jit(solution)/shard_map/ppermute | solution.py:252

commit v13 on v12

--- a/solution.py
+++ b/solution.py
@@ -318,7 +318,7 @@
     updates = {}
     sent = {}
     head, rest = far[-1:], far[:-1]
-    for ms in (head, rest, passed, near[1:], [0] + near[:1]):
+    for ms in (head, rest, passed[-1:], passed[:-1], near[1:], [0] + near[:1]):
         if ms == head:
             after = []
         elif ms == rest:
@@ -334,14 +334,16 @@
             for m in passed:
                 biases[m] = straight
             after = [updates[head[0]]] + [biases[m] for m in near]
-        elif ms == passed:
+        elif ms == passed[-1:]:
             after = [updates[rest[0]]]
+        elif ms == passed[:-1]:
+            after = [updates[passed[-1]]]
         elif ms == near[1:]:
             after = [updates[m] for m in passed]
         else:
             after = [updates[near[1]]] + [sent[m] for m in head]
         blocks = len(ms)
-        first = [i * heads * rows_held if ms == passed else 0 for i in range(blocks)]
+        first = [passed.index(m) * heads * rows_held if m in passed else 0 for m in ms]
         rows = 2 * count * rows_held
         outs = pl.pallas_call(
             functools.partial(attention_kernel, heads, ms, first),

time: 51 us -> 51.2 us (level)
  Pallas kernels: 24.4 us -> 25.2 us
  starting transfers between devices: 21.4 us -> 20.8 us
    pallas_call x5 -> x6, Pallas kernels: 14.9 us -> 15.7 us  [local(): pl.pallas_call(functools.partial(attention_kernel, heads, ms, first), out...]
    ppermute x14, starting transfers between devices: 21.4 us -> 20.8 us  [swap(): return lax.ppermute(x, 'row', [(i, i ^ bits) for i in range(devices)])]
  transfers between devices with their start and end apart: 14 -> 14, of which waited for: 4 -> 4; matrix products, arithmetic and copies ran while one was open for 0% -> 0% of each run, Pallas kernels for 36% -> 37%
where the time goes in v13:
time: 51.2 us; the launch traced here: 51.1 us
  Pallas kernels  25.2 us (49%)
  starting transfers between devices  20.8 us (41%)
  waiting for transfers between devices  4.79 us (9%)
    ppermute x14, starting transfers between devices, swap(): return lax.ppermute(x, 'row', [(i, i ^ bits) for i in range(devices)])  20.8 us
    pallas_call x6, Pallas kernels, local(): pl.pallas_call(functools.partial(attention_kernel, heads, ms, first), out...  15.7 us
    pallas_call x1, Pallas kernels, local(): pl.pallas_call(bias_kernel, grid=(rows_held // step_rows,), out_shape=[ja...  5.57 us
    ppermute x14, waiting for transfers between devices, swap(): return lax.ppermute(x, 'row', [(i, i ^ bits) for i in range(devices)])  4.79 us
    pallas_call x1, Pallas kernels, local(): pl.pallas_call(key_value_kernel, out_shape=[jax.ShapeDtypeStruct((2 * cou...  2.27 us
    pallas_call x2, Pallas kernels, local(): pl.pallas_call(functools.partial(gather_kernel, order), out_shape=jax.Sha...  1.65 us
  transfers between devices with their start and end apart: 14, of which 4 were waited for; matrix products, arithmetic and copies ran while one was open for 0% of the time, Pallas kernels for 37%

profile of v13, /device:TPU:0, one launch (start us, length us, event | category | flops | bytes accessed | tf_op | source)
XLA Modules:
  0.0 51.1 jit_solution(4358867964310060380)
XLA Ops:
  0.0 0.0 copy-start
  0.0 5.6 %shard_map.109 = (bf16[128,384]{1,0:T(8,128)(2,1)S(1)}, bf16[8,512,128]{2,1,0:T(8,128)(2,1)S(1)}, bf16[384,512]{1,0:T(8,128)(2,1)S(1)}, f32[8,384]{1,0:T(8,128)S(1)}) custom-call(s32[1]{0:T(128)} %bitcast.me_ref, s32[8]{0:T(128)} %rows_ref.1, bf16[32,512,128]{2,1,0:T(8,128)(2,1)} %pair_ref.1, s32[1,512]{1,0:T(1,128)} %bitcast.21, s32[1,512]{1,0:T(1,128)} %bitcast.28, ...), custom_call_target="tpu_custom_call" | custom-call | bytes 22140000 | tf_op jit(solution)/shard_map/pallas_call | solution.py:255
  5.6 0.0 copy-start.1
  5.6 0.0 copy-start.2
  5.6 0.0 copy-start.3
  5.6 0.0 copy-start.4
  5.6 0.0 copy-start.5
  5.6 0.5 %collective-permute-start.1 = (bf16[8,512,128]{2,1,0:T(8,128)(2,1)S(1)}, bf16[8,512,128]{2,1,0:T(8,128)(2,1)S(1)}, u32[]{:S(2)}, u32[]{:S(2)}) collective-permute-start(bf16[8,512,128]{2,1,0:T(8,128)(2,1)S(1)} %get-tuple-element.16.own_ref), channel_id=1, source_target_pairs={{0,1},{1,0},{2,3},{3,2},{4,5},{5,4},{6,7},{7,6},{8,9},{9,8},{10,11... | collective-permute-start | bytes 3145736 | tf_op jit(solution)/shard_map/ppermute | solution.py:252
  6.2 4.7 %collective-permute-start.5 = (bf16[128,384]{1,0:T(8,128)(2,1)S(1)}, bf16[128,384]{1,0:T(8,128)(2,1)S(1)}, u32[]{:S(2)}, u32[]{:S(2)}) collective-permute-start(bf16[128,384]{1,0:T(8,128)(2,1)S(1)} %get-tuple-element.15.refs_0_), channel_id=1, source_target_pairs={{0,12},{1,13},{2,14},{3,15},{4,8},{5,9},{6,10},{7,11},{8,4},{9,5},... | collective-permute-start | bytes 294920 | tf_op jit(solution)/shard_map/ppermute | solution.py:252
  10.8 0.0 collective-permute-start.4
  10.8 1.7 %collective-permute-start.3 = (bf16[128,384]{1,0:T(8,128)(2,1)S(1)}, bf16[128,384]{1,0:T(8,128)(2,1)S(1)}, u32[]{:S(2)}, u32[]{:S(2)}) collective-permute-start(bf16[128,384]{1,0:T(8,128)(2,1)S(1)} %get-tuple-element.15.refs_0_), channel_id=1, source_target_pairs={{0,6},{1,7},{2,4},{3,5},{4,2},{5,3},{6,0},{7,1},{8,14},{9,15},{10,... | collective-permute-start | bytes 294920 | tf_op jit(solution)/shard_map/ppermute | solution.py:252
  12.6 1.2 %collective-permute-start.2 = (bf16[128,384]{1,0:T(8,128)(2,1)S(1)}, bf16[128,384]{1,0:T(8,128)(2,1)S(1)}, u32[]{:S(2)}, u32[]{:S(2)}) collective-permute-start(bf16[128,384]{1,0:T(8,128)(2,1)S(1)} %get-tuple-element.15.refs_0_), channel_id=1, source_target_pairs={{0,4},{1,5},{2,6},{3,7},{4,0},{5,1},{6,2},{7,3},{8,12},{9,13},{10,... | collective-permute-start | bytes 294920 | tf_op jit(solution)/shard_map/ppermute | solution.py:252
  13.8 0.0 collective-permute-done.1.other_ref
  13.8 0.5 collective-permute-start
  14.3 0.0 copy-done
  14.3 2.3 %shard_map.110 = (bf16[16,128,384]{2,1,0:T(8,128)(2,1)S(1)}, bf16[16,384,128]{2,1,0:T(8,128)(2,1)S(1)}) custom-call(bf16[8,512,128]{2,1,0:T(8,128)(2,1)S(1)} %get-tuple-element.16.own_ref, bf16[8,512,128]{2,1,0:T(8,128)(2,1)S(1)} %collective-permute-done.1.other_ref, bf16[384,512]{1,0:T(8,128)(2,1)S(1)} %get-tuple-element.17.pick_ref, ...), custom_call_target="tpu_custom_call" | custom-call | bytes 7380000 | tf_op jit(solution)/shard_map/pallas_call | solution.py:304
  16.6 0.0 collective-permute-done.5.refs_0_.refs_1_
  16.6 0.0 copy-done.1
  16.6 0.0 copy-done.2
  16.6 0.0 copy-done.3
  16.7 0.0 copy-done.4
  16.7 0.0 copy-done.5
  16.7 2.1 %shard_map.111.refs_2_.refs_11_ = bf16[16,32,128]{2,1,0:T(8,128)(2,1)S(1)} custom-call(s32[1]{0:T(128)} %bitcast.me_ref, f32[4]{0:T(128)S(1)} %copy-done.4, bf16[128,384]{1,0:T(8,128)(2,1)S(1)} %collective-permute-done.5.refs_0_.refs_1_, bf16[8,8,2,32,128]{4,3,2,1,0:T(8,128)(2,1)S(1)} %bitcast.9, bf16[8,8,2,32,128]{4,3,2,1,0:T(8,128)(2,1)S(1)} %bitcast.15, ...), custom_call_target="tpu_custom_call" | custom-call | bytes 8118000 | tf_op jit(solution)/shard_map/pallas_call | solution.py:348
  18.8 1.0 %collective-permute-done.4.refs_0_ = bf16[128,384]{1,0:T(8,128)(2,1)S(1)} collective-permute-done((bf16[128,384]{1,0:T(8,128)(2,1)S(1)}, bf16[128,384]{1,0:T(8,128)(2,1)S(1)}, u32[]{:S(2)}, u32[]{:S(2)}) %collective-permute-start.4) | collective-permute-done | bytes 98336 | tf_op jit(solution)/shard_map/ppermute | solution.py:252
  19.8 1.6 %collective-permute-start.6 = (bf16[256,384]{1,0:T(8,128)(2,1)S(1)}, bf16[256,384]{1,0:T(8,128)(2,1)S(1)}, u32[]{:S(2)}, u32[]{:S(2)}) collective-permute-start(bf16[256,384]{1,0:T(8,128)(2,1)S(1)} %shard_map.112), channel_id=1, source_target_pairs={{0,2},{1,3},{2,0},{3,1},{4,6},{5,7},{6,4},{7,5},{8,10},{9,11},{10,... | collective-permute-start | bytes 589832 | tf_op jit(solution)/shard_map/ppermute | solution.py:252
  21.4 2.5 %collective-permute-start.7 = (bf16[16,32,128]{2,1,0:T(8,128)(2,1)S(1)}, bf16[16,32,128]{2,1,0:T(8,128)(2,1)S(1)}, u32[]{:S(2)}, u32[]{:S(2)}) collective-permute-start(bf16[16,32,128]{2,1,0:T(8,128)(2,1)S(1)} %shard_map.111.refs_2_.refs_11_), channel_id=1, source_target_pairs={{0,12},{1,13},{2,14},{3,15},{4,8},{5,9},{6,10},{7,11},{8,4},{9,5},... | collective-permute-start | bytes 393224 | tf_op jit(solution)/shard_map/ppermute | solution.py:252
  23.9 0.0 collective-permute-done.3.refs_14_.refs_1_
  23.9 0.0 collective-permute-done.2.refs_13_.refs_0_
  23.9 0.0 collective-permute-done.refs_12_.refs_1_
  23.9 2.1 %shard_map.113.refs_11_ = bf16[16,32,128]{2,1,0:T(8,128)(2,1)S(1)} custom-call(s32[1]{0:T(128)} %bitcast.me_ref, f32[4]{0:T(128)S(1)} %copy-done.4, bf16[128,384]{1,0:T(8,128)(2,1)S(1)} %collective-permute-done.4.refs_0_, bf16[8,8,2,32,128]{4,3,2,1,0:T(8,128)(2,1)S(1)} %bitcast.10, bf16[8,8,2,32,128]{4,3,2,1,0:T(8,128)(2,1)S(1)} %bitcast.16, ...), custom_call_target="tpu_custom_call" | custom-call | bytes 8118000 | tf_op jit(solution)/shard_map/pallas_call | solution.py:348
  26.1 0.1 collective-permute-start.11
  26.1 0.2 collective-permute-done.6.refs_0_
  26.3 2.1 %shard_map.114.refs_11_.refs_13_ = bf16[16,32,128]{2,1,0:T(8,128)(2,1)S(1)} custom-call(s32[1]{0:T(128)} %bitcast.me_ref, f32[4]{0:T(128)S(1)} %copy-done.4, bf16[256,384]{1,0:T(8,128)(2,1)S(1)} %collective-permute-done.6.refs_0_, bf16[8,8,2,32,128]{4,3,2,1,0:T(8,128)(2,1)S(1)} %bitcast.11, bf16[8,8,2,32,128]{4,3,2,1,0:T(8,128)(2,1)S(1)} %bitcast.17, ...), custom_call_target="tpu_custom_call" | custom-call | bytes 8118000 | tf_op jit(solution)/shard_map/pallas_call | solution.py:348
  28.4 3.5 %collective-permute-start.13 = (bf16[16,32,128]{2,1,0:T(8,128)(2,1)S(1)}, bf16[16,32,128]{2,1,0:T(8,128)(2,1)S(1)}, u32[]{:S(2)}, u32[]{:S(2)}) collective-permute-start(bf16[16,32,128]{2,1,0:T(8,128)(2,1)S(1)} %shard_map.114.refs_11_.refs_13_), channel_id=1, source_target_pairs={{0,14},{1,15},{2,12},{3,13},{4,10},{5,11},{6,8},{7,9},{8,6},{9,7},... | collective-permute-start | bytes 393224 | tf_op jit(solution)/shard_map/ppermute | solution.py:252
  31.9 2.1 %shard_map.115.refs_12_ = bf16[16,32,128]{2,1,0:T(8,128)(2,1)S(1)} custom-call(s32[1]{0:T(128)} %bitcast.me_ref, f32[4]{0:T(128)S(1)} %copy-done.4, bf16[256,384]{1,0:T(8,128)(2,1)S(1)} %collective-permute-done.6.refs_0_, bf16[8,8,2,32,128]{4,3,2,1,0:T(8,128)(2,1)S(1)} %bitcast.12, bf16[8,8,2,32,128]{4,3,2,1,0:T(8,128)(2,1)S(1)} %bitcast.18, ...), custom_call_target="tpu_custom_call" | custom-call | bytes 8118000 | tf_op jit(solution)/shard_map/pallas_call | solution.py:348
  34.1 0.7 %collective-permute-start.12 = (bf16[16,32,128]{2,1,0:T(8,128)(2,1)S(1)}, bf16[16,32,128]{2,1,0:T(8,128)(2,1)S(1)}, u32[]{:S(2)}, u32[]{:S(2)}) collective-permute-start(bf16[16,32,128]{2,1,0:T(8,128)(2,1)S(1)} %shard_map.115.refs_12_), channel_id=1, source_target_pairs={{0,10},{1,11},{2,8},{3,9},{4,14},{5,15},{6,12},{7,13},{8,2},{9,3},... | collective-permute-start | bytes 393224 | tf_op jit(solution)/shard_map/ppermute | solution.py:252
  34.8 3.5 %shard_map.116 = (bf16[16,32,128]{2,1,0:T(8,128)(2,1)S(1)}, bf16[16,32,128]{2,1,0:T(8,128)(2,1)S(1)}) custom-call(s32[1]{0:T(128)} %bitcast.me_ref, f32[4]{0:T(128)S(1)} %copy-done.4, bf16[128,384]{1,0:T(8,128)(2,1)S(1)} %collective-permute-done.2.refs_13_.refs_0_, bf16[128,384]{1,0:T(8,128)(2,1)S(1)} %collective-permute-done.3.refs_14_.refs_1_, ...), custom_call_target="tpu_custom_call" | custom-call | bytes 16236000 | tf_op jit(solution)/shard_map/pallas_call | solution.py:348
  38.3 2.4 %collective-permute-start.10 = (bf16[16,32,128]{2,1,0:T(8,128)(2,1)S(1)}, bf16[16,32,128]{2,1,0:T(8,128)(2,1)S(1)}, u32[]{:S(2)}, u32[]{:S(2)}) collective-permute-start(bf16[16,32,128]{2,1,0:T(8,128)(2,1)S(1)} %get-tuple-element.24), channel_id=1, source_target_pairs={{0,6},{1,7},{2,4},{3,5},{4,2},{5,3},{6,0},{7,1},{8,14},{9,15},{10,... | collective-permute-start | bytes 393224 | tf_op jit(solution)/shard_map/ppermute | solution.py:252
  40.7 0.0 collective-permute-done.7.refs_13_.refs_3_
  40.7 0.0 collective-permute-start.9
  40.7 3.6 %shard_map.117 = (bf16[16,32,128]{2,1,0:T(8,128)(2,1)S(1)}, bf16[16,32,128]{2,1,0:T(8,128)(2,1)S(1)}) custom-call(s32[1]{0:T(128)} %bitcast.me_ref, f32[4]{0:T(128)S(1)} %copy-done.4, bf16[128,384]{1,0:T(8,128)(2,1)S(1)} %get-tuple-element.15.refs_0_, bf16[128,384]{1,0:T(8,128)(2,1)S(1)} %collective-permute-done.refs_12_.refs_1_, ...), custom_call_target="tpu_custom_call" | custom-call | bytes 16236000 | tf_op jit(solution)/shard_map/pallas_call | solution.py:348
  44.3 0.0 collective-permute-done.11.refs_2_
  44.3 1.4 %collective-permute-start.8 = (bf16[16,32,128]{2,1,0:T(8,128)(2,1)S(1)}, bf16[16,32,128]{2,1,0:T(8,128)(2,1)S(1)}, u32[]{:S(2)}, u32[]{:S(2)}) collective-permute-start(bf16[16,32,128]{2,1,0:T(8,128)(2,1)S(1)} %get-tuple-element.23), channel_id=1, source_target_pairs={{0,2},{1,3},{2,0},{3,1},{4,6},{5,7},{6,4},{7,5},{8,10},{9,11},{10,... | collective-permute-start | bytes 393224 | tf_op jit(solution)/shard_map/ppermute | solution.py:252
  45.7 2.3 %collective-permute-done.10.refs_1_ = bf16[16,32,128]{2,1,0:T(8,128)(2,1)S(1)} collective-permute-done((bf16[16,32,128]{2,1,0:T(8,128)(2,1)S(1)}, bf16[16,32,128]{2,1,0:T(8,128)(2,1)S(1)}, u32[]{:S(2)}, u32[]{:S(2)}) %collective-permute-start.10) | collective-permute-done | bytes 131104 | tf_op jit(solution)/shard_map/ppermute | solution.py:252
  48.0 1.2 %collective-permute-done.9.refs_0_ = bf16[16,32,128]{2,1,0:T(8,128)(2,1)S(1)} collective-permute-done((bf16[16,32,128]{2,1,0:T(8,128)(2,1)S(1)}, bf16[16,32,128]{2,1,0:T(8,128)(2,1)S(1)}, u32[]{:S(2)}, u32[]{:S(2)}) %collective-permute-start.9) | collective-permute-done | bytes 131104 | tf_op jit(solution)/shard_map/ppermute | solution.py:252
  49.2 0.0 collective-permute-done.12.refs_4_
  49.2 0.0 collective-permute-done.13.refs_5_
  49.2 0.9 %shard_map.118.refs_2_ = bf16[128,32,128]{2,1,0:T(8,128)(2,1)} custom-call(s32[1]{0:T(128)} %bitcast.me_ref, bf16[16,32,128]{2,1,0:T(8,128)(2,1)S(1)} %collective-permute-done.9.refs_0_, bf16[16,32,128]{2,1,0:T(8,128)(2,1)S(1)} %collective-permute-done.10.refs_1_, bf16[16,32,128]{2,1,0:T(8,128)(2,1)S(1)} %collective-permute-done.11.refs_2_, ...), custom_call_target="tpu_custom_call" | custom-call | bytes 3690000 | tf_op jit(solution)/shard_map/pallas_call | solution.py:386
  50.2 0.0 collective-permute-done.8.refs_1_
  50.2 0.7 %shard_map.119 = bf16[128,32,128]{2,1,0:T(8,128)(2,1)} custom-call(s32[1]{0:T(128)} %bitcast.me_ref, bf16[16,32,128]{2,1,0:T(8,128)(2,1)S(1)} %get-tuple-element.22.refs_0_, bf16[16,32,128]{2,1,0:T(8,128)(2,1)S(1)} %collective-permute-done.8.refs_1_, bf16[128,32,128]{2,1,0:T(8,128)(2,1)} %shard_map.118.refs_2_), custom_call_target="tpu_custom_call", output_to_operand_aliasing={{}: (3, {})} | custom-call | bytes 3690000 | tf_op jit(solution)/shard_map/pallas_call | solution.py:386
  (1 shorter events, 0.0 us)
Async XLA Ops:
  0.0 14.3 %copy-start = (bf16[128,512]{1,0:T(8,128)(2,1)S(1)}, bf16[128,512]{1,0:T(8,128)(2,1)}, u32[]{:S(2)}) copy-start(bf16[128,512]{1,0:T(8,128)(2,1)} %refs_9_.3) | copy-start | bytes 393220
  5.6 11.0 %copy-start.1 = (bf16[128,128]{1,0:T(8,128)(2,1)S(1)}, bf16[128,128]{1,0:T(8,128)(2,1)}, u32[]{:S(2)}) copy-start(bf16[128,128]{1,0:T(8,128)(2,1)} %refs_11_.3) | copy-start | bytes 98308
  5.6 11.0 %copy-start.2 = (s32[512]{0:T(512)S(1)}, s32[512]{0:T(512)}, u32[]{:S(2)}) copy-start(s32[512]{0:T(512)} %param.13) | copy-start | bytes 6148
  5.6 11.0 %copy-start.3 = (s32[512]{0:T(512)S(1)}, s32[512]{0:T(512)}, u32[]{:S(2)}) copy-start(s32[512]{0:T(512)} %param.14) | copy-start | bytes 6148
  5.6 11.0 %copy-start.4 = (f32[4]{0:T(128)S(1)}, f32[4]{0:T(128)}, u32[]{:S(2)}) copy-start(f32[4]{0:T(128)} %chain_bias_ref.11) | copy-start | bytes 52
  5.6 11.0 %copy-start.5 = (f32[128]{0:T(128)S(1)}, f32[128]{0:T(128)}, u32[]{:S(2)}) copy-start(f32[128]{0:T(128)} %param.18) | copy-start | bytes 1540
  5.6 8.2 %collective-permute-start.1 = (bf16[8,512,128]{2,1,0:T(8,128)(2,1)S(1)}, bf16[8,512,128]{2,1,0:T(8,128)(2,1)S(1)}, u32[]{:S(2)}, u32[]{:S(2)}) collective-permute-start(bf16[8,512,128]{2,1,0:T(8,128)(2,1)S(1)} %get-tuple-element.16.own_ref), channel_id=1, source_target_pairs={{0,1},{1,0},{2,3},{3,2},{4,5},{5,4},{6,7},{7,6},{8,9},{9,8},{10,11... | collective-permute-start | bytes 3145736 | tf_op jit(solution)/shard_map/ppermute | solution.py:252
  6.2 10.5 %collective-permute-start.5 = (bf16[128,384]{1,0:T(8,128)(2,1)S(1)}, bf16[128,384]{1,0:T(8,128)(2,1)S(1)}, u32[]{:S(2)}, u32[]{:S(2)}) collective-permute-start(bf16[128,384]{1,0:T(8,128)(2,1)S(1)} %get-tuple-element.15.refs_0_), channel_id=1, source_target_pairs={{0,12},{1,13},{2,14},{3,15},{4,8},{5,9},{6,10},{7,11},{8,4},{9,5},... | collective-permute-start | bytes 294920 | tf_op jit(solution)/shard_map/ppermute | solution.py:252
  10.8 9.0 %collective-permute-start.4 = (bf16[128,384]{1,0:T(8,128)(2,1)S(1)}, bf16[128,384]{1,0:T(8,128)(2,1)S(1)}, u32[]{:S(2)}, u32[]{:S(2)}) collective-permute-start(bf16[128,384]{1,0:T(8,128)(2,1)S(1)} %get-tuple-element.15.refs_0_), channel_id=1, source_target_pairs={{0,8},{1,9},{2,10},{3,11},{4,12},{5,13},{6,14},{7,15},{8,0},{9,1},... | collective-permute-start | bytes 294920 | tf_op jit(solution)/shard_map/ppermute | solution.py:252
  10.8 13.1 %collective-permute-start.3 = (bf16[128,384]{1,0:T(8,128)(2,1)S(1)}, bf16[128,384]{1,0:T(8,128)(2,1)S(1)}, u32[]{:S(2)}, u32[]{:S(2)}) collective-permute-start(bf16[128,384]{1,0:T(8,128)(2,1)S(1)} %get-tuple-element.15.refs_0_), channel_id=1, source_target_pairs={{0,6},{1,7},{2,4},{3,5},{4,2},{5,3},{6,0},{7,1},{8,14},{9,15},{10,... | collective-permute-start | bytes 294920 | tf_op jit(solution)/shard_map/ppermute | solution.py:252
  12.6 11.3 %collective-permute-start.2 = (bf16[128,384]{1,0:T(8,128)(2,1)S(1)}, bf16[128,384]{1,0:T(8,128)(2,1)S(1)}, u32[]{:S(2)}, u32[]{:S(2)}) collective-permute-start(bf16[128,384]{1,0:T(8,128)(2,1)S(1)} %get-tuple-element.15.refs_0_), channel_id=1, source_target_pairs={{0,4},{1,5},{2,6},{3,7},{4,0},{5,1},{6,2},{7,3},{8,12},{9,13},{10,... | collective-permute-start | bytes 294920 | tf_op jit(solution)/shard_map/ppermute | solution.py:252
  13.8 10.1 %collective-permute-start = (bf16[128,384]{1,0:T(8,128)(2,1)S(1)}, bf16[128,384]{1,0:T(8,128)(2,1)S(1)}, u32[]{:S(2)}, u32[]{:S(2)}) collective-permute-start(bf16[128,384]{1,0:T(8,128)(2,1)S(1)} %get-tuple-element.15.refs_0_), channel_id=1, source_target_pairs={{0,2},{1,3},{2,0},{3,1},{4,6},{5,7},{6,4},{7,5},{8,10},{9,11},{10,... | collective-permute-start | bytes 294920 | tf_op jit(solution)/shard_map/ppermute | solution.py:252
  19.8 6.5 %collective-permute-start.6 = (bf16[256,384]{1,0:T(8,128)(2,1)S(1)}, bf16[256,384]{1,0:T(8,128)(2,1)S(1)}, u32[]{:S(2)}, u32[]{:S(2)}) collective-permute-start(bf16[256,384]{1,0:T(8,128)(2,1)S(1)} %shard_map.112), channel_id=1, source_target_pairs={{0,2},{1,3},{2,0},{3,1},{4,6},{5,7},{6,4},{7,5},{8,10},{9,11},{10,... | collective-permute-start | bytes 589832 | tf_op jit(solution)/shard_map/ppermute | solution.py:252
  21.4 19.3 %collective-permute-start.7 = (bf16[16,32,128]{2,1,0:T(8,128)(2,1)S(1)}, bf16[16,32,128]{2,1,0:T(8,128)(2,1)S(1)}, u32[]{:S(2)}, u32[]{:S(2)}) collective-permute-start(bf16[16,32,128]{2,1,0:T(8,128)(2,1)S(1)} %shard_map.111.refs_2_.refs_11_), channel_id=1, source_target_pairs={{0,12},{1,13},{2,14},{3,15},{4,8},{5,9},{6,10},{7,11},{8,4},{9,5},... | collective-permute-start | bytes 393224 | tf_op jit(solution)/shard_map/ppermute | solution.py:252
  26.1 18.2 %collective-permute-start.11 = (bf16[16,32,128]{2,1,0:T(8,128)(2,1)S(1)}, bf16[16,32,128]{2,1,0:T(8,128)(2,1)S(1)}, u32[]{:S(2)}, u32[]{:S(2)}) collective-permute-start(bf16[16,32,128]{2,1,0:T(8,128)(2,1)S(1)} %shard_map.113.refs_11_), channel_id=1, source_target_pairs={{0,8},{1,9},{2,10},{3,11},{4,12},{5,13},{6,14},{7,15},{8,0},{9,1},... | collective-permute-start | bytes 393224 | tf_op jit(solution)/shard_map/ppermute | solution.py:252
  28.4 20.8 %collective-permute-start.13 = (bf16[16,32,128]{2,1,0:T(8,128)(2,1)S(1)}, bf16[16,32,128]{2,1,0:T(8,128)(2,1)S(1)}, u32[]{:S(2)}, u32[]{:S(2)}) collective-permute-start(bf16[16,32,128]{2,1,0:T(8,128)(2,1)S(1)} %shard_map.114.refs_11_.refs_13_), channel_id=1, source_target_pairs={{0,14},{1,15},{2,12},{3,13},{4,10},{5,11},{6,8},{7,9},{8,6},{9,7},... | collective-permute-start | bytes 393224 | tf_op jit(solution)/shard_map/ppermute | solution.py:252
  34.1 15.2 %collective-permute-start.12 = (bf16[16,32,128]{2,1,0:T(8,128)(2,1)S(1)}, bf16[16,32,128]{2,1,0:T(8,128)(2,1)S(1)}, u32[]{:S(2)}, u32[]{:S(2)}) collective-permute-start(bf16[16,32,128]{2,1,0:T(8,128)(2,1)S(1)} %shard_map.115.refs_12_), channel_id=1, source_target_pairs={{0,10},{1,11},{2,8},{3,9},{4,14},{5,15},{6,12},{7,13},{8,2},{9,3},... | collective-permute-start | bytes 393224 | tf_op jit(solution)/shard_map/ppermute | solution.py:252
  38.3 9.7 %collective-permute-start.10 = (bf16[16,32,128]{2,1,0:T(8,128)(2,1)S(1)}, bf16[16,32,128]{2,1,0:T(8,128)(2,1)S(1)}, u32[]{:S(2)}, u32[]{:S(2)}) collective-permute-start(bf16[16,32,128]{2,1,0:T(8,128)(2,1)S(1)} %get-tuple-element.24), channel_id=1, source_target_pairs={{0,6},{1,7},{2,4},{3,5},{4,2},{5,3},{6,0},{7,1},{8,14},{9,15},{10,... | collective-permute-start | bytes 393224 | tf_op jit(solution)/shard_map/ppermute | solution.py:252
  40.7 8.5 %collective-permute-start.9 = (bf16[16,32,128]{2,1,0:T(8,128)(2,1)S(1)}, bf16[16,32,128]{2,1,0:T(8,128)(2,1)S(1)}, u32[]{:S(2)}, u32[]{:S(2)}) collective-permute-start(bf16[16,32,128]{2,1,0:T(8,128)(2,1)S(1)} %get-tuple-element.21.refs_12_), channel_id=1, source_target_pairs={{0,4},{1,5},{2,6},{3,7},{4,0},{5,1},{6,2},{7,3},{8,12},{9,13},{10,... | collective-permute-start | bytes 393224 | tf_op jit(solution)/shard_map/ppermute | solution.py:252
  44.3 5.9 %collective-permute-start.8 = (bf16[16,32,128]{2,1,0:T(8,128)(2,1)S(1)}, bf16[16,32,128]{2,1,0:T(8,128)(2,1)S(1)}, u32[]{:S(2)}, u32[]{:S(2)}) collective-permute-start(bf16[16,32,128]{2,1,0:T(8,128)(2,1)S(1)} %get-tuple-element.23), channel_id=1, source_target_pairs={{0,2},{1,3},{2,0},{3,1},{4,6},{5,7},{6,4},{7,5},{8,10},{9,11},{10,... | collective-permute-start | bytes 393224 | tf_op jit(solution)/shard_map/ppermute | solution.py:252

commit v14 on v12

--- a/solution.py
+++ b/solution.py
@@ -317,7 +317,7 @@
     own, other = own.reshape(split), other.reshape(split)
     updates = {}
     sent = {}
-    head, rest = far[-1:], far[:-1]
+    head, rest = far[:1], far[1:]
     for ms in (head, rest, passed, near[1:], [0] + near[:1]):
         if ms == head:
             after = []

time: 51 us -> 50.8 us (level)
  transfers between devices with their start and end apart: 14 -> 14, of which waited for: 4 -> 3; matrix products, arithmetic and copies ran while one was open for 0% -> 0% of each run, Pallas kernels for 36% -> 36%
where the time goes in v14:
time: 50.8 us; the launch traced here: 50.7 us
  Pallas kernels  24.4 us (48%)
  starting transfers between devices  21.8 us (43%)
  waiting for transfers between devices  4.17 us (8%)
    ppermute x14, starting transfers between devices, swap(): return lax.ppermute(x, 'row', [(i, i ^ bits) for i in range(devices)])  21.8 us
    pallas_call x5, Pallas kernels, local(): pl.pallas_call(functools.partial(attention_kernel, heads, ms, first), out...  14.9 us
    pallas_call x1, Pallas kernels, local(): pl.pallas_call(bias_kernel, grid=(rows_held // step_rows,), out_shape=[ja...  5.57 us
    ppermute x14, waiting for transfers between devices, swap(): return lax.ppermute(x, 'row', [(i, i ^ bits) for i in range(devices)])  4.17 us
    pallas_call x1, Pallas kernels, local(): pl.pallas_call(key_value_kernel, out_shape=[jax.ShapeDtypeStruct((2 * cou...  2.27 us
    pallas_call x2, Pallas kernels, local(): pl.pallas_call(functools.partial(gather_kernel, order), out_shape=jax.Sha...  1.65 us
  transfers between devices with their start and end apart: 14, of which 3 were waited for; matrix products, arithmetic and copies ran while one was open for 0% of the time, Pallas kernels for 36%

profile of v14, /device:TPU:0, one launch (start us, length us, event | category | flops | bytes accessed | tf_op | source)
XLA Modules:
  0.0 50.7 jit_solution(17903549575417720414)
XLA Ops:
  0.0 0.0 copy-start
  0.0 5.6 %shard_map.109 = (bf16[128,384]{1,0:T(8,128)(2,1)S(1)}, bf16[8,512,128]{2,1,0:T(8,128)(2,1)S(1)}, bf16[384,512]{1,0:T(8,128)(2,1)S(1)}, f32[8,384]{1,0:T(8,128)S(1)}) custom-call(s32[1]{0:T(128)} %bitcast.me_ref, s32[8]{0:T(128)} %rows_ref.1, bf16[32,512,128]{2,1,0:T(8,128)(2,1)} %pair_ref.1, s32[1,512]{1,0:T(1,128)} %bitcast.19, s32[1,512]{1,0:T(1,128)} %bitcast.25, ...), custom_call_target="tpu_custom_call" | custom-call | bytes 22140000 | tf_op jit(solution)/shard_map/pallas_call | solution.py:255
  5.6 0.0 copy-start.1
  5.6 0.0 copy-start.2
  5.6 0.0 copy-start.3
  5.6 0.0 copy-start.4
  5.6 0.0 copy-start.5
  5.6 0.5 %collective-permute-start.1 = (bf16[8,512,128]{2,1,0:T(8,128)(2,1)S(1)}, bf16[8,512,128]{2,1,0:T(8,128)(2,1)S(1)}, u32[]{:S(2)}, u32[]{:S(2)}) collective-permute-start(bf16[8,512,128]{2,1,0:T(8,128)(2,1)S(1)} %get-tuple-element.18.own_ref), channel_id=1, source_target_pairs={{0,1},{1,0},{2,3},{3,2},{4,5},{5,4},{6,7},{7,6},{8,9},{9,8},{10,11... | collective-permute-start | bytes 3145736 | tf_op jit(solution)/shard_map/ppermute | solution.py:252
  6.2 3.7 %collective-permute-start.4 = (bf16[128,384]{1,0:T(8,128)(2,1)S(1)}, bf16[128,384]{1,0:T(8,128)(2,1)S(1)}, u32[]{:S(2)}, u32[]{:S(2)}) collective-permute-start(bf16[128,384]{1,0:T(8,128)(2,1)S(1)} %get-tuple-element.17.refs_0_), channel_id=1, source_target_pairs={{0,8},{1,9},{2,10},{3,11},{4,12},{5,13},{6,14},{7,15},{8,0},{9,1},... | collective-permute-start | bytes 294920 | tf_op jit(solution)/shard_map/ppermute | solution.py:252
  9.8 1.3 %collective-permute-start.5 = (bf16[128,384]{1,0:T(8,128)(2,1)S(1)}, bf16[128,384]{1,0:T(8,128)(2,1)S(1)}, u32[]{:S(2)}, u32[]{:S(2)}) collective-permute-start(bf16[128,384]{1,0:T(8,128)(2,1)S(1)} %get-tuple-element.17.refs_0_), channel_id=1, source_target_pairs={{0,12},{1,13},{2,14},{3,15},{4,8},{5,9},{6,10},{7,11},{8,4},{9,5},... | collective-permute-start | bytes 294920 | tf_op jit(solution)/shard_map/ppermute | solution.py:252
  11.2 1.2 %collective-permute-start.3 = (bf16[128,384]{1,0:T(8,128)(2,1)S(1)}, bf16[128,384]{1,0:T(8,128)(2,1)S(1)}, u32[]{:S(2)}, u32[]{:S(2)}) collective-permute-start(bf16[128,384]{1,0:T(8,128)(2,1)S(1)} %get-tuple-element.17.refs_0_), channel_id=1, source_target_pairs={{0,6},{1,7},{2,4},{3,5},{4,2},{5,3},{6,0},{7,1},{8,14},{9,15},{10,... | collective-permute-start | bytes 294920 | tf_op jit(solution)/shard_map/ppermute | solution.py:252
  12.4 1.8 %collective-permute-start.2 = (bf16[128,384]{1,0:T(8,128)(2,1)S(1)}, bf16[128,384]{1,0:T(8,128)(2,1)S(1)}, u32[]{:S(2)}, u32[]{:S(2)}) collective-permute-start(bf16[128,384]{1,0:T(8,128)(2,1)S(1)} %get-tuple-element.17.refs_0_), channel_id=1, source_target_pairs={{0,4},{1,5},{2,6},{3,7},{4,0},{5,1},{6,2},{7,3},{8,12},{9,13},{10,... | collective-permute-start | bytes 294920 | tf_op jit(solution)/shard_map/ppermute | solution.py:252
  14.2 0.0 collective-permute-done.1.other_ref
  14.2 0.5 %collective-permute-start = (bf16[128,384]{1,0:T(8,128)(2,1)S(1)}, bf16[128,384]{1,0:T(8,128)(2,1)S(1)}, u32[]{:S(2)}, u32[]{:S(2)}) collective-permute-start(bf16[128,384]{1,0:T(8,128)(2,1)S(1)} %get-tuple-element.17.refs_0_), channel_id=1, source_target_pairs={{0,2},{1,3},{2,0},{3,1},{4,6},{5,7},{6,4},{7,5},{8,10},{9,11},{10,... | collective-permute-start | bytes 294920 | tf_op jit(solution)/shard_map/ppermute | solution.py:252
  14.7 0.0 copy-done
  14.7 2.3 %shard_map.110 = (bf16[16,128,384]{2,1,0:T(8,128)(2,1)S(1)}, bf16[16,384,128]{2,1,0:T(8,128)(2,1)S(1)}) custom-call(bf16[8,512,128]{2,1,0:T(8,128)(2,1)S(1)} %get-tuple-element.18.own_ref, bf16[8,512,128]{2,1,0:T(8,128)(2,1)S(1)} %collective-permute-done.1.other_ref, bf16[384,512]{1,0:T(8,128)(2,1)S(1)} %get-tuple-element.19.pick_ref, ...), custom_call_target="tpu_custom_call" | custom-call | bytes 7380000 | tf_op jit(solution)/shard_map/pallas_call | solution.py:304
  16.9 0.8 %collective-permute-done.4.refs_0_ = bf16[128,384]{1,0:T(8,128)(2,1)S(1)} collective-permute-done((bf16[128,384]{1,0:T(8,128)(2,1)S(1)}, bf16[128,384]{1,0:T(8,128)(2,1)S(1)}, u32[]{:S(2)}, u32[]{:S(2)}) %collective-permute-start.4) | collective-permute-done | bytes 98336 | tf_op jit(solution)/shard_map/ppermute | solution.py:252
  17.7 0.0 copy-done.1
  17.7 0.0 copy-done.2
  17.7 0.0 copy-done.3
  17.7 0.0 copy-done.4
  17.7 0.0 copy-done.5
  17.8 2.1 %shard_map.111.refs_2_.refs_11_ = bf16[16,32,128]{2,1,0:T(8,128)(2,1)S(1)} custom-call(s32[1]{0:T(128)} %bitcast.me_ref, f32[4]{0:T(128)S(1)} %copy-done.4, bf16[128,384]{1,0:T(8,128)(2,1)S(1)} %collective-permute-done.4.refs_0_, bf16[8,8,2,32,128]{4,3,2,1,0:T(8,128)(2,1)S(1)} %bitcast.9, bf16[8,8,2,32,128]{4,3,2,1,0:T(8,128)(2,1)S(1)} %bitcast.14, ...), custom_call_target="tpu_custom_call" | custom-call | bytes 8118000 | tf_op jit(solution)/shard_map/pallas_call | solution.py:346
  19.9 0.0 collective-permute-done.5.refs_1_.refs_0_
  19.9 1.8 %collective-permute-start.6 = (bf16[256,384]{1,0:T(8,128)(2,1)S(1)}, bf16[256,384]{1,0:T(8,128)(2,1)S(1)}, u32[]{:S(2)}, u32[]{:S(2)}) collective-permute-start(bf16[256,384]{1,0:T(8,128)(2,1)S(1)} %shard_map.112), channel_id=1, source_target_pairs={{0,2},{1,3},{2,0},{3,1},{4,6},{5,7},{6,4},{7,5},{8,10},{9,11},{10,... | collective-permute-start | bytes 589832 | tf_op jit(solution)/shard_map/ppermute | solution.py:252
  21.8 2.1 %collective-permute-start.7 = (bf16[16,32,128]{2,1,0:T(8,128)(2,1)S(1)}, bf16[16,32,128]{2,1,0:T(8,128)(2,1)S(1)}, u32[]{:S(2)}, u32[]{:S(2)}) collective-permute-start(bf16[16,32,128]{2,1,0:T(8,128)(2,1)S(1)} %shard_map.111.refs_2_.refs_11_), channel_id=1, source_target_pairs={{0,8},{1,9},{2,10},{3,11},{4,12},{5,13},{6,14},{7,15},{8,0},{9,1},... | collective-permute-start | bytes 393224 | tf_op jit(solution)/shard_map/ppermute | solution.py:252
  23.8 0.0 collective-permute-done.3.refs_14_.refs_1_
  23.8 0.0 collective-permute-done.2.refs_13_.refs_0_
  23.8 0.0 collective-permute-done.refs_12_.refs_1_
  23.9 2.1 %shard_map.113.refs_12_ = bf16[16,32,128]{2,1,0:T(8,128)(2,1)S(1)} custom-call(s32[1]{0:T(128)} %bitcast.me_ref, f32[4]{0:T(128)S(1)} %copy-done.4, bf16[128,384]{1,0:T(8,128)(2,1)S(1)} %collective-permute-done.5.refs_1_.refs_0_, bf16[8,8,2,32,128]{4,3,2,1,0:T(8,128)(2,1)S(1)} %bitcast.10, bf16[8,8,2,32,128]{4,3,2,1,0:T(8,128)(2,1)S(1)} %bitcast.15, ...), custom_call_target="tpu_custom_call" | custom-call | bytes 8118000 | tf_op jit(solution)/shard_map/pallas_call | solution.py:346
  26.0 1.3 %collective-permute-start.11 = (bf16[16,32,128]{2,1,0:T(8,128)(2,1)S(1)}, bf16[16,32,128]{2,1,0:T(8,128)(2,1)S(1)}, u32[]{:S(2)}, u32[]{:S(2)}) collective-permute-start(bf16[16,32,128]{2,1,0:T(8,128)(2,1)S(1)} %shard_map.113.refs_12_), channel_id=1, source_target_pairs={{0,12},{1,13},{2,14},{3,15},{4,8},{5,9},{6,10},{7,11},{8,4},{9,5},... | collective-permute-start | bytes 393224 | tf_op jit(solution)/shard_map/ppermute | solution.py:252
  27.3 0.0 collective-permute-done.6.refs_0_.refs_1_
  27.3 3.5 %shard_map.114 = (bf16[16,32,128]{2,1,0:T(8,128)(2,1)S(1)}, bf16[16,32,128]{2,1,0:T(8,128)(2,1)S(1)}) custom-call(s32[1]{0:T(128)} %bitcast.me_ref, f32[4]{0:T(128)S(1)} %copy-done.4, bf16[256,384]{1,0:T(8,128)(2,1)S(1)} %collective-permute-done.6.refs_0_.refs_1_, bf16[256,384]{1,0:T(8,128)(2,1)S(1)} %collective-permute-done.6.refs_0_.refs_1_, ...), custom_call_target="tpu_custom_call" | custom-call | bytes 16236000 | tf_op jit(solution)/shard_map/pallas_call | solution.py:346
  30.8 2.9 %collective-permute-start.12 = (bf16[16,32,128]{2,1,0:T(8,128)(2,1)S(1)}, bf16[16,32,128]{2,1,0:T(8,128)(2,1)S(1)}, u32[]{:S(2)}, u32[]{:S(2)}) collective-permute-start(bf16[16,32,128]{2,1,0:T(8,128)(2,1)S(1)} %get-tuple-element.23.refs_12_), channel_id=1, source_target_pairs={{0,10},{1,11},{2,8},{3,9},{4,14},{5,15},{6,12},{7,13},{8,2},{9,3},... | collective-permute-start | bytes 393224 | tf_op jit(solution)/shard_map/ppermute | solution.py:252
  33.7 1.1 %collective-permute-start.13 = (bf16[16,32,128]{2,1,0:T(8,128)(2,1)S(1)}, bf16[16,32,128]{2,1,0:T(8,128)(2,1)S(1)}, u32[]{:S(2)}, u32[]{:S(2)}) collective-permute-start(bf16[16,32,128]{2,1,0:T(8,128)(2,1)S(1)} %get-tuple-element.24.refs_13_), channel_id=1, source_target_pairs={{0,14},{1,15},{2,12},{3,13},{4,10},{5,11},{6,8},{7,9},{8,6},{9,7},... | collective-permute-start | bytes 393224 | tf_op jit(solution)/shard_map/ppermute | solution.py:252
  34.8 3.5 %shard_map.115 = (bf16[16,32,128]{2,1,0:T(8,128)(2,1)S(1)}, bf16[16,32,128]{2,1,0:T(8,128)(2,1)S(1)}) custom-call(s32[1]{0:T(128)} %bitcast.me_ref, f32[4]{0:T(128)S(1)} %copy-done.4, bf16[128,384]{1,0:T(8,128)(2,1)S(1)} %collective-permute-done.2.refs_13_.refs_0_, bf16[128,384]{1,0:T(8,128)(2,1)S(1)} %collective-permute-done.3.refs_14_.refs_1_, ...), custom_call_target="tpu_custom_call" | custom-call | bytes 16236000 | tf_op jit(solution)/shard_map/pallas_call | solution.py:346
  38.3 0.8 %collective-permute-start.10 = (bf16[16,32,128]{2,1,0:T(8,128)(2,1)S(1)}, bf16[16,32,128]{2,1,0:T(8,128)(2,1)S(1)}, u32[]{:S(2)}, u32[]{:S(2)}) collective-permute-start(bf16[16,32,128]{2,1,0:T(8,128)(2,1)S(1)} %get-tuple-element.28), channel_id=1, source_target_pairs={{0,6},{1,7},{2,4},{3,5},{4,2},{5,3},{6,0},{7,1},{8,14},{9,15},{10,... | collective-permute-start | bytes 393224 | tf_op jit(solution)/shard_map/ppermute | solution.py:252
  39.1 0.0 collective-permute-done.7.refs_13_.refs_2_
  39.1 1.6 %collective-permute-start.9 = (bf16[16,32,128]{2,1,0:T(8,128)(2,1)S(1)}, bf16[16,32,128]{2,1,0:T(8,128)(2,1)S(1)}, u32[]{:S(2)}, u32[]{:S(2)}) collective-permute-start(bf16[16,32,128]{2,1,0:T(8,128)(2,1)S(1)} %get-tuple-element.25.refs_12_), channel_id=1, source_target_pairs={{0,4},{1,5},{2,6},{3,7},{4,0},{5,1},{6,2},{7,3},{8,12},{9,13},{10,... | collective-permute-start | bytes 393224 | tf_op jit(solution)/shard_map/ppermute | solution.py:252
  40.8 3.6 %shard_map.116 = (bf16[16,32,128]{2,1,0:T(8,128)(2,1)S(1)}, bf16[16,32,128]{2,1,0:T(8,128)(2,1)S(1)}) custom-call(s32[1]{0:T(128)} %bitcast.me_ref, f32[4]{0:T(128)S(1)} %copy-done.4, bf16[128,384]{1,0:T(8,128)(2,1)S(1)} %get-tuple-element.17.refs_0_, bf16[128,384]{1,0:T(8,128)(2,1)S(1)} %collective-permute-done.refs_12_.refs_1_, ...), custom_call_target="tpu_custom_call" | custom-call | bytes 16236000 | tf_op jit(solution)/shard_map/pallas_call | solution.py:346
  44.3 0.0 collective-permute-done.11.refs_3_
  44.3 1.2 %collective-permute-start.8 = (bf16[16,32,128]{2,1,0:T(8,128)(2,1)S(1)}, bf16[16,32,128]{2,1,0:T(8,128)(2,1)S(1)}, u32[]{:S(2)}, u32[]{:S(2)}) collective-permute-start(bf16[16,32,128]{2,1,0:T(8,128)(2,1)S(1)} %get-tuple-element.27), channel_id=1, source_target_pairs={{0,2},{1,3},{2,0},{3,1},{4,6},{5,7},{6,4},{7,5},{8,10},{9,11},{10,... | collective-permute-start | bytes 393224 | tf_op jit(solution)/shard_map/ppermute | solution.py:252
  45.5 1.4 %collective-permute-done.10.refs_1_ = bf16[16,32,128]{2,1,0:T(8,128)(2,1)S(1)} collective-permute-done((bf16[16,32,128]{2,1,0:T(8,128)(2,1)S(1)}, bf16[16,32,128]{2,1,0:T(8,128)(2,1)S(1)}, u32[]{:S(2)}, u32[]{:S(2)}) %collective-permute-start.10) | collective-permute-done | bytes 131104 | tf_op jit(solution)/shard_map/ppermute | solution.py:252
  46.9 2.0 %collective-permute-done.9.refs_0_ = bf16[16,32,128]{2,1,0:T(8,128)(2,1)S(1)} collective-permute-done((bf16[16,32,128]{2,1,0:T(8,128)(2,1)S(1)}, bf16[16,32,128]{2,1,0:T(8,128)(2,1)S(1)}, u32[]{:S(2)}, u32[]{:S(2)}) %collective-permute-start.9) | collective-permute-done | bytes 131104 | tf_op jit(solution)/shard_map/ppermute | solution.py:252
  48.9 0.0 collective-permute-done.12.refs_4_
  48.9 0.0 collective-permute-done.13.refs_5_
  48.9 0.9 %shard_map.117.refs_2_ = bf16[128,32,128]{2,1,0:T(8,128)(2,1)} custom-call(s32[1]{0:T(128)} %bitcast.me_ref, bf16[16,32,128]{2,1,0:T(8,128)(2,1)S(1)} %collective-permute-done.9.refs_0_, bf16[16,32,128]{2,1,0:T(8,128)(2,1)S(1)} %collective-permute-done.10.refs_1_, bf16[16,32,128]{2,1,0:T(8,128)(2,1)S(1)} %collective-permute-done.7.refs_13_.refs_2_, ...), custom_call_target="tpu_custom_call" | custom-call | bytes 3690000 | tf_op jit(solution)/shard_map/pallas_call | solution.py:384
  49.8 0.0 collective-permute-done.8.refs_1_
  49.8 0.7 %shard_map.118 = bf16[128,32,128]{2,1,0:T(8,128)(2,1)} custom-call(s32[1]{0:T(128)} %bitcast.me_ref, bf16[16,32,128]{2,1,0:T(8,128)(2,1)S(1)} %get-tuple-element.26.refs_0_, bf16[16,32,128]{2,1,0:T(8,128)(2,1)S(1)} %collective-permute-done.8.refs_1_, bf16[128,32,128]{2,1,0:T(8,128)(2,1)} %shard_map.117.refs_2_), custom_call_target="tpu_custom_call", output_to_operand_aliasing={{}: (3, {})} | custom-call | bytes 3690000 | tf_op jit(solution)/shard_map/pallas_call | solution.py:384
  (1 shorter events, 0.0 us)
Async XLA Ops:
  0.0 14.7 %copy-start = (bf16[128,512]{1,0:T(8,128)(2,1)S(1)}, bf16[128,512]{1,0:T(8,128)(2,1)}, u32[]{:S(2)}) copy-start(bf16[128,512]{1,0:T(8,128)(2,1)} %refs_9_.5) | copy-start | bytes 393220
  5.6 12.2 %copy-start.1 = (bf16[128,128]{1,0:T(8,128)(2,1)S(1)}, bf16[128,128]{1,0:T(8,128)(2,1)}, u32[]{:S(2)}) copy-start(bf16[128,128]{1,0:T(8,128)(2,1)} %refs_11_.5) | copy-start | bytes 98308
  5.6 12.1 %copy-start.2 = (s32[512]{0:T(512)S(1)}, s32[512]{0:T(512)}, u32[]{:S(2)}) copy-start(s32[512]{0:T(512)} %param.13) | copy-start | bytes 6148
  5.6 12.1 %copy-start.3 = (s32[512]{0:T(512)S(1)}, s32[512]{0:T(512)}, u32[]{:S(2)}) copy-start(s32[512]{0:T(512)} %param.14) | copy-start | bytes 6148
  5.6 12.1 %copy-start.4 = (f32[4]{0:T(128)S(1)}, f32[4]{0:T(128)}, u32[]{:S(2)}) copy-start(f32[4]{0:T(128)} %chain_bias_ref.9) | copy-start | bytes 52
  5.6 12.1 %copy-start.5 = (f32[128]{0:T(128)S(1)}, f32[128]{0:T(128)}, u32[]{:S(2)}) copy-start(f32[128]{0:T(128)} %param.18) | copy-start | bytes 1540
  5.6 8.5 %collective-permute-start.1 = (bf16[8,512,128]{2,1,0:T(8,128)(2,1)S(1)}, bf16[8,512,128]{2,1,0:T(8,128)(2,1)S(1)}, u32[]{:S(2)}, u32[]{:S(2)}) collective-permute-start(bf16[8,512,128]{2,1,0:T(8,128)(2,1)S(1)} %get-tuple-element.18.own_ref), channel_id=1, source_target_pairs={{0,1},{1,0},{2,3},{3,2},{4,5},{5,4},{6,7},{7,6},{8,9},{9,8},{10,11... | collective-permute-start | bytes 3145736 | tf_op jit(solution)/shard_map/ppermute | solution.py:252
  6.2 11.6 %collective-permute-start.4 = (bf16[128,384]{1,0:T(8,128)(2,1)S(1)}, bf16[128,384]{1,0:T(8,128)(2,1)S(1)}, u32[]{:S(2)}, u32[]{:S(2)}) collective-permute-start(bf16[128,384]{1,0:T(8,128)(2,1)S(1)} %get-tuple-element.17.refs_0_), channel_id=1, source_target_pairs={{0,8},{1,9},{2,10},{3,11},{4,12},{5,13},{6,14},{7,15},{8,0},{9,1},... | collective-permute-start | bytes 294920 | tf_op jit(solution)/shard_map/ppermute | solution.py:252
  9.8 10.1 %collective-permute-start.5 = (bf16[128,384]{1,0:T(8,128)(2,1)S(1)}, bf16[128,384]{1,0:T(8,128)(2,1)S(1)}, u32[]{:S(2)}, u32[]{:S(2)}) collective-permute-start(bf16[128,384]{1,0:T(8,128)(2,1)S(1)} %get-tuple-element.17.refs_0_), channel_id=1, source_target_pairs={{0,12},{1,13},{2,14},{3,15},{4,8},{5,9},{6,10},{7,11},{8,4},{9,5},... | collective-permute-start | bytes 294920 | tf_op jit(solution)/shard_map/ppermute | solution.py:252
  11.2 12.7 %collective-permute-start.3 = (bf16[128,384]{1,0:T(8,128)(2,1)S(1)}, bf16[128,384]{1,0:T(8,128)(2,1)S(1)}, u32[]{:S(2)}, u32[]{:S(2)}) collective-permute-start(bf16[128,384]{1,0:T(8,128)(2,1)S(1)} %get-tuple-element.17.refs_0_), channel_id=1, source_target_pairs={{0,6},{1,7},{2,4},{3,5},{4,2},{5,3},{6,0},{7,1},{8,14},{9,15},{10,... | collective-permute-start | bytes 294920 | tf_op jit(solution)/shard_map/ppermute | solution.py:252
  12.4 11.5 %collective-permute-start.2 = (bf16[128,384]{1,0:T(8,128)(2,1)S(1)}, bf16[128,384]{1,0:T(8,128)(2,1)S(1)}, u32[]{:S(2)}, u32[]{:S(2)}) collective-permute-start(bf16[128,384]{1,0:T(8,128)(2,1)S(1)} %get-tuple-element.17.refs_0_), channel_id=1, source_target_pairs={{0,4},{1,5},{2,6},{3,7},{4,0},{5,1},{6,2},{7,3},{8,12},{9,13},{10,... | collective-permute-start | bytes 294920 | tf_op jit(solution)/shard_map/ppermute | solution.py:252
  14.2 9.7 %collective-permute-start = (bf16[128,384]{1,0:T(8,128)(2,1)S(1)}, bf16[128,384]{1,0:T(8,128)(2,1)S(1)}, u32[]{:S(2)}, u32[]{:S(2)}) collective-permute-start(bf16[128,384]{1,0:T(8,128)(2,1)S(1)} %get-tuple-element.17.refs_0_), channel_id=1, source_target_pairs={{0,2},{1,3},{2,0},{3,1},{4,6},{5,7},{6,4},{7,5},{8,10},{9,11},{10,... | collective-permute-start | bytes 294920 | tf_op jit(solution)/shard_map/ppermute | solution.py:252
  19.9 7.3 %collective-permute-start.6 = (bf16[256,384]{1,0:T(8,128)(2,1)S(1)}, bf16[256,384]{1,0:T(8,128)(2,1)S(1)}, u32[]{:S(2)}, u32[]{:S(2)}) collective-permute-start(bf16[256,384]{1,0:T(8,128)(2,1)S(1)} %shard_map.112), channel_id=1, source_target_pairs={{0,2},{1,3},{2,0},{3,1},{4,6},{5,7},{6,4},{7,5},{8,10},{9,11},{10,... | collective-permute-start | bytes 589832 | tf_op jit(solution)/shard_map/ppermute | solution.py:252
  21.8 17.4 %collective-permute-start.7 = (bf16[16,32,128]{2,1,0:T(8,128)(2,1)S(1)}, bf16[16,32,128]{2,1,0:T(8,128)(2,1)S(1)}, u32[]{:S(2)}, u32[]{:S(2)}) collective-permute-start(bf16[16,32,128]{2,1,0:T(8,128)(2,1)S(1)} %shard_map.111.refs_2_.refs_11_), channel_id=1, source_target_pairs={{0,8},{1,9},{2,10},{3,11},{4,12},{5,13},{6,14},{7,15},{8,0},{9,1},... | collective-permute-start | bytes 393224 | tf_op jit(solution)/shard_map/ppermute | solution.py:252
  26.0 18.3 %collective-permute-start.11 = (bf16[16,32,128]{2,1,0:T(8,128)(2,1)S(1)}, bf16[16,32,128]{2,1,0:T(8,128)(2,1)S(1)}, u32[]{:S(2)}, u32[]{:S(2)}) collective-permute-start(bf16[16,32,128]{2,1,0:T(8,128)(2,1)S(1)} %shard_map.113.refs_12_), channel_id=1, source_target_pairs={{0,12},{1,13},{2,14},{3,15},{4,8},{5,9},{6,10},{7,11},{8,4},{9,5},... | collective-permute-start | bytes 393224 | tf_op jit(solution)/shard_map/ppermute | solution.py:252
  30.8 18.1 %collective-permute-start.12 = (bf16[16,32,128]{2,1,0:T(8,128)(2,1)S(1)}, bf16[16,32,128]{2,1,0:T(8,128)(2,1)S(1)}, u32[]{:S(2)}, u32[]{:S(2)}) collective-permute-start(bf16[16,32,128]{2,1,0:T(8,128)(2,1)S(1)} %get-tuple-element.23.refs_12_), channel_id=1, source_target_pairs={{0,10},{1,11},{2,8},{3,9},{4,14},{5,15},{6,12},{7,13},{8,2},{9,3},... | collective-permute-start | bytes 393224 | tf_op jit(solution)/shard_map/ppermute | solution.py:252
  33.7 15.1 %collective-permute-start.13 = (bf16[16,32,128]{2,1,0:T(8,128)(2,1)S(1)}, bf16[16,32,128]{2,1,0:T(8,128)(2,1)S(1)}, u32[]{:S(2)}, u32[]{:S(2)}) collective-permute-start(bf16[16,32,128]{2,1,0:T(8,128)(2,1)S(1)} %get-tuple-element.24.refs_13_), channel_id=1, source_target_pairs={{0,14},{1,15},{2,12},{3,13},{4,10},{5,11},{6,8},{7,9},{8,6},{9,7},... | collective-permute-start | bytes 393224 | tf_op jit(solution)/shard_map/ppermute | solution.py:252
  38.3 8.5 %collective-permute-start.10 = (bf16[16,32,128]{2,1,0:T(8,128)(2,1)S(1)}, bf16[16,32,128]{2,1,0:T(8,128)(2,1)S(1)}, u32[]{:S(2)}, u32[]{:S(2)}) collective-permute-start(bf16[16,32,128]{2,1,0:T(8,128)(2,1)S(1)} %get-tuple-element.28), channel_id=1, source_target_pairs={{0,6},{1,7},{2,4},{3,5},{4,2},{5,3},{6,0},{7,1},{8,14},{9,15},{10,... | collective-permute-start | bytes 393224 | tf_op jit(solution)/shard_map/ppermute | solution.py:252
  39.1 9.7 %collective-permute-start.9 = (bf16[16,32,128]{2,1,0:T(8,128)(2,1)S(1)}, bf16[16,32,128]{2,1,0:T(8,128)(2,1)S(1)}, u32[]{:S(2)}, u32[]{:S(2)}) collective-permute-start(bf16[16,32,128]{2,1,0:T(8,128)(2,1)S(1)} %get-tuple-element.25.refs_12_), channel_id=1, source_target_pairs={{0,4},{1,5},{2,6},{3,7},{4,0},{5,1},{6,2},{7,3},{8,12},{9,13},{10,... | collective-permute-start | bytes 393224 | tf_op jit(solution)/shard_map/ppermute | solution.py:252
  44.3 5.5 %collective-permute-start.8 = (bf16[16,32,128]{2,1,0:T(8,128)(2,1)S(1)}, bf16[16,32,128]{2,1,0:T(8,128)(2,1)S(1)}, u32[]{:S(2)}, u32[]{:S(2)}) collective-permute-start(bf16[16,32,128]{2,1,0:T(8,128)(2,1)S(1)} %get-tuple-element.27), channel_id=1, source_target_pairs={{0,2},{1,3},{2,0},{3,1},{4,6},{5,7},{6,4},{7,5},{8,10},{9,11},{10,... | collective-permute-start | bytes 393224 | tf_op jit(solution)/shard_map/ppermute | solution.py:252

commit v15 on v12

--- a/solution.py
+++ b/solution.py
@@ -337,7 +337,7 @@
         elif ms == passed:
             after = [updates[rest[0]]]
         elif ms == near[1:]:
-            after = [updates[m] for m in passed]
+            after = [updates[m] for m in passed] + [sent[m] for m in head]
         else:
             after = [updates[near[1]]] + [sent[m] for m in head]
         blocks = len(ms)
@@ -355,7 +355,7 @@
                 pltpu.VMEM((rows, inner), BF16),
             ],
             compiler_params=PARAMS,
-            cost_estimate=measured(2.2 * blocks),
+            cost_estimate=measured(0.2 * blocks),
         )(
             me,
             chain_bias,

time: 51 us -> 51 us (level)
  no operation moved by 1% of the time
where the time goes in v15:
time: 51 us; the launch traced here: 50.9 us
  Pallas kernels  24.4 us (48%)
  starting transfers between devices  21.4 us (42%)
  waiting for transfers between devices  4.66 us (9%)
    ppermute x14, starting transfers between devices, swap(): return lax.ppermute(x, 'row', [(i, i ^ bits) for i in range(devices)])  21.4 us
    pallas_call x5, Pallas kernels, local(): pl.pallas_call(functools.partial(attention_kernel, heads, ms, first), out...  14.9 us
    pallas_call x1, Pallas kernels, local(): pl.pallas_call(bias_kernel, grid=(rows_held // step_rows,), out_shape=[ja...  5.57 us
    ppermute x14, waiting for transfers between devices, swap(): return lax.ppermute(x, 'row', [(i, i ^ bits) for i in range(devices)])  4.66 us
    pallas_call x1, Pallas kernels, local(): pl.pallas_call(key_value_kernel, out_shape=[jax.ShapeDtypeStruct((2 * cou...  2.28 us
    pallas_call x2, Pallas kernels, local(): pl.pallas_call(functools.partial(gather_kernel, order), out_shape=jax.Sha...  1.65 us
  transfers between devices with their start and end apart: 14, of which 4 were waited for; matrix products, arithmetic and copies ran while one was open for 0% of the time, Pallas kernels for 36%

profile of v15, /device:TPU:0, one launch (start us, length us, event | category | flops | bytes accessed | tf_op | source)
XLA Modules:
  0.0 50.9 jit_solution(8972877344451678912)
XLA Ops:
  0.0 0.0 copy-start
  0.0 5.6 %shard_map.109 = (bf16[128,384]{1,0:T(8,128)(2,1)S(1)}, bf16[8,512,128]{2,1,0:T(8,128)(2,1)S(1)}, bf16[384,512]{1,0:T(8,128)(2,1)S(1)}, f32[8,384]{1,0:T(8,128)S(1)}) custom-call(s32[1]{0:T(128)} %bitcast.me_ref, s32[8]{0:T(128)} %rows_ref.1, bf16[32,512,128]{2,1,0:T(8,128)(2,1)} %pair_ref.1, s32[1,512]{1,0:T(1,128)} %bitcast.19, s32[1,512]{1,0:T(1,128)} %bitcast.25, ...), custom_call_target="tpu_custom_call" | custom-call | bytes 22140000 | tf_op jit(solution)/shard_map/pallas_call | solution.py:255
  5.6 0.0 copy-start.1
  5.6 0.0 copy-start.2
  5.6 0.0 copy-start.3
  5.6 0.0 copy-start.4
  5.6 0.0 copy-start.5
  5.6 0.5 %collective-permute-start.1 = (bf16[8,512,128]{2,1,0:T(8,128)(2,1)S(1)}, bf16[8,512,128]{2,1,0:T(8,128)(2,1)S(1)}, u32[]{:S(2)}, u32[]{:S(2)}) collective-permute-start(bf16[8,512,128]{2,1,0:T(8,128)(2,1)S(1)} %get-tuple-element.18.own_ref), channel_id=1, source_target_pairs={{0,1},{1,0},{2,3},{3,2},{4,5},{5,4},{6,7},{7,6},{8,9},{9,8},{10,11... | collective-permute-start | bytes 3145736 | tf_op jit(solution)/shard_map/ppermute | solution.py:252
  6.2 4.7 %collective-permute-start.5 = (bf16[128,384]{1,0:T(8,128)(2,1)S(1)}, bf16[128,384]{1,0:T(8,128)(2,1)S(1)}, u32[]{:S(2)}, u32[]{:S(2)}) collective-permute-start(bf16[128,384]{1,0:T(8,128)(2,1)S(1)} %get-tuple-element.17.refs_0_), channel_id=1, source_target_pairs={{0,12},{1,13},{2,14},{3,15},{4,8},{5,9},{6,10},{7,11},{8,4},{9,5},... | collective-permute-start | bytes 294920 | tf_op jit(solution)/shard_map/ppermute | solution.py:252
  10.8 0.0 collective-permute-start.4
  10.8 1.7 %collective-permute-start.3 = (bf16[128,384]{1,0:T(8,128)(2,1)S(1)}, bf16[128,384]{1,0:T(8,128)(2,1)S(1)}, u32[]{:S(2)}, u32[]{:S(2)}) collective-permute-start(bf16[128,384]{1,0:T(8,128)(2,1)S(1)} %get-tuple-element.17.refs_0_), channel_id=1, source_target_pairs={{0,6},{1,7},{2,4},{3,5},{4,2},{5,3},{6,0},{7,1},{8,14},{9,15},{10,... | collective-permute-start | bytes 294920 | tf_op jit(solution)/shard_map/ppermute | solution.py:252
  12.6 1.2 %collective-permute-start.2 = (bf16[128,384]{1,0:T(8,128)(2,1)S(1)}, bf16[128,384]{1,0:T(8,128)(2,1)S(1)}, u32[]{:S(2)}, u32[]{:S(2)}) collective-permute-start(bf16[128,384]{1,0:T(8,128)(2,1)S(1)} %get-tuple-element.17.refs_0_), channel_id=1, source_target_pairs={{0,4},{1,5},{2,6},{3,7},{4,0},{5,1},{6,2},{7,3},{8,12},{9,13},{10,... | collective-permute-start | bytes 294920 | tf_op jit(solution)/shard_map/ppermute | solution.py:252
  13.8 0.0 collective-permute-done.1.other_ref
  13.8 0.5 collective-permute-start
  14.3 0.0 copy-done
  14.3 2.3 %shard_map.110 = (bf16[16,128,384]{2,1,0:T(8,128)(2,1)S(1)}, bf16[16,384,128]{2,1,0:T(8,128)(2,1)S(1)}) custom-call(bf16[8,512,128]{2,1,0:T(8,128)(2,1)S(1)} %get-tuple-element.18.own_ref, bf16[8,512,128]{2,1,0:T(8,128)(2,1)S(1)} %collective-permute-done.1.other_ref, bf16[384,512]{1,0:T(8,128)(2,1)S(1)} %get-tuple-element.19.pick_ref, ...), custom_call_target="tpu_custom_call" | custom-call | bytes 7380000 | tf_op jit(solution)/shard_map/pallas_call | solution.py:304
  16.6 0.0 collective-permute-done.5.refs_0_.refs_1_
  16.6 0.0 copy-done.1
  16.6 0.0 copy-done.2
  16.7 0.0 copy-done.3
  16.7 0.0 copy-done.4
  16.7 0.0 copy-done.5
  16.7 2.1 %shard_map.111.refs_2_.refs_11_ = bf16[16,32,128]{2,1,0:T(8,128)(2,1)S(1)} custom-call(s32[1]{0:T(128)} %bitcast.me_ref, f32[4]{0:T(128)S(1)} %copy-done.4, bf16[128,384]{1,0:T(8,128)(2,1)S(1)} %collective-permute-done.5.refs_0_.refs_1_, bf16[8,8,2,32,128]{4,3,2,1,0:T(8,128)(2,1)S(1)} %bitcast.9, bf16[8,8,2,32,128]{4,3,2,1,0:T(8,128)(2,1)S(1)} %bitcast.14, ...), custom_call_target="tpu_custom_call" | custom-call | bytes 738000 | tf_op jit(solution)/shard_map/pallas_call | solution.py:346
  18.8 1.0 %collective-permute-done.4.refs_0_ = bf16[128,384]{1,0:T(8,128)(2,1)S(1)} collective-permute-done((bf16[128,384]{1,0:T(8,128)(2,1)S(1)}, bf16[128,384]{1,0:T(8,128)(2,1)S(1)}, u32[]{:S(2)}, u32[]{:S(2)}) %collective-permute-start.4) | collective-permute-done | bytes 98336 | tf_op jit(solution)/shard_map/ppermute | solution.py:252
  19.8 1.6 %collective-permute-start.6 = (bf16[256,384]{1,0:T(8,128)(2,1)S(1)}, bf16[256,384]{1,0:T(8,128)(2,1)S(1)}, u32[]{:S(2)}, u32[]{:S(2)}) collective-permute-start(bf16[256,384]{1,0:T(8,128)(2,1)S(1)} %shard_map.112), channel_id=1, source_target_pairs={{0,2},{1,3},{2,0},{3,1},{4,6},{5,7},{6,4},{7,5},{8,10},{9,11},{10,... | collective-permute-start | bytes 589832 | tf_op jit(solution)/shard_map/ppermute | solution.py:252
  21.4 2.5 %collective-permute-start.7 = (bf16[16,32,128]{2,1,0:T(8,128)(2,1)S(1)}, bf16[16,32,128]{2,1,0:T(8,128)(2,1)S(1)}, u32[]{:S(2)}, u32[]{:S(2)}) collective-permute-start(bf16[16,32,128]{2,1,0:T(8,128)(2,1)S(1)} %shard_map.111.refs_2_.refs_11_), channel_id=1, source_target_pairs={{0,12},{1,13},{2,14},{3,15},{4,8},{5,9},{6,10},{7,11},{8,4},{9,5},... | collective-permute-start | bytes 393224 | tf_op jit(solution)/shard_map/ppermute | solution.py:252
  23.9 0.0 collective-permute-done.3.refs_14_.refs_1_
  23.9 0.0 collective-permute-done.2.refs_13_.refs_0_
  23.9 0.0 collective-permute-done.refs_12_.refs_1_
  23.9 2.1 %shard_map.113.refs_12_ = bf16[16,32,128]{2,1,0:T(8,128)(2,1)S(1)} custom-call(s32[1]{0:T(128)} %bitcast.me_ref, f32[4]{0:T(128)S(1)} %copy-done.4, bf16[128,384]{1,0:T(8,128)(2,1)S(1)} %collective-permute-done.4.refs_0_, bf16[8,8,2,32,128]{4,3,2,1,0:T(8,128)(2,1)S(1)} %bitcast.10, bf16[8,8,2,32,128]{4,3,2,1,0:T(8,128)(2,1)S(1)} %bitcast.15, ...), custom_call_target="tpu_custom_call" | custom-call | bytes 738000 | tf_op jit(solution)/shard_map/pallas_call | solution.py:346
  26.1 0.1 collective-permute-start.11
  26.1 0.2 collective-permute-done.6.refs_0_.refs_1_
  26.3 3.5 %shard_map.114 = (bf16[16,32,128]{2,1,0:T(8,128)(2,1)S(1)}, bf16[16,32,128]{2,1,0:T(8,128)(2,1)S(1)}) custom-call(s32[1]{0:T(128)} %bitcast.me_ref, f32[4]{0:T(128)S(1)} %copy-done.4, bf16[256,384]{1,0:T(8,128)(2,1)S(1)} %collective-permute-done.6.refs_0_.refs_1_, bf16[256,384]{1,0:T(8,128)(2,1)S(1)} %collective-permute-done.6.refs_0_.refs_1_, ...), custom_call_target="tpu_custom_call" | custom-call | bytes 1476000 | tf_op jit(solution)/shard_map/pallas_call | solution.py:346
  29.9 2.7 %collective-permute-start.12 = (bf16[16,32,128]{2,1,0:T(8,128)(2,1)S(1)}, bf16[16,32,128]{2,1,0:T(8,128)(2,1)S(1)}, u32[]{:S(2)}, u32[]{:S(2)}) collective-permute-start(bf16[16,32,128]{2,1,0:T(8,128)(2,1)S(1)} %get-tuple-element.23.refs_12_), channel_id=1, source_target_pairs={{0,10},{1,11},{2,8},{3,9},{4,14},{5,15},{6,12},{7,13},{8,2},{9,3},... | collective-permute-start | bytes 393224 | tf_op jit(solution)/shard_map/ppermute | solution.py:252
  32.6 2.3 %collective-permute-start.13 = (bf16[16,32,128]{2,1,0:T(8,128)(2,1)S(1)}, bf16[16,32,128]{2,1,0:T(8,128)(2,1)S(1)}, u32[]{:S(2)}, u32[]{:S(2)}) collective-permute-start(bf16[16,32,128]{2,1,0:T(8,128)(2,1)S(1)} %get-tuple-element.24.refs_13_), channel_id=1, source_target_pairs={{0,14},{1,15},{2,12},{3,13},{4,10},{5,11},{6,8},{7,9},{8,6},{9,7},... | collective-permute-start | bytes 393224 | tf_op jit(solution)/shard_map/ppermute | solution.py:252
  34.9 0.0 collective-permute-done.7.refs_14_.refs_13_.refs_3_
  34.9 3.5 %shard_map.115 = (bf16[16,32,128]{2,1,0:T(8,128)(2,1)S(1)}, bf16[16,32,128]{2,1,0:T(8,128)(2,1)S(1)}) custom-call(s32[1]{0:T(128)} %bitcast.me_ref, f32[4]{0:T(128)S(1)} %copy-done.4, bf16[128,384]{1,0:T(8,128)(2,1)S(1)} %collective-permute-done.2.refs_13_.refs_0_, bf16[128,384]{1,0:T(8,128)(2,1)S(1)} %collective-permute-done.3.refs_14_.refs_1_, ...), custom_call_target="tpu_custom_call" | custom-call | bytes 1476000 | tf_op jit(solution)/shard_map/pallas_call | solution.py:346
  38.4 0.4 collective-permute-start.10
  38.8 1.6 %collective-permute-start.9 = (bf16[16,32,128]{2,1,0:T(8,128)(2,1)S(1)}, bf16[16,32,128]{2,1,0:T(8,128)(2,1)S(1)}, u32[]{:S(2)}, u32[]{:S(2)}) collective-permute-start(bf16[16,32,128]{2,1,0:T(8,128)(2,1)S(1)} %get-tuple-element.25.refs_12_), channel_id=1, source_target_pairs={{0,4},{1,5},{2,6},{3,7},{4,0},{5,1},{6,2},{7,3},{8,12},{9,13},{10,... | collective-permute-start | bytes 393224 | tf_op jit(solution)/shard_map/ppermute | solution.py:252
  40.5 3.6 %shard_map.116 = (bf16[16,32,128]{2,1,0:T(8,128)(2,1)S(1)}, bf16[16,32,128]{2,1,0:T(8,128)(2,1)S(1)}) custom-call(s32[1]{0:T(128)} %bitcast.me_ref, f32[4]{0:T(128)S(1)} %copy-done.4, bf16[128,384]{1,0:T(8,128)(2,1)S(1)} %get-tuple-element.17.refs_0_, bf16[128,384]{1,0:T(8,128)(2,1)S(1)} %collective-permute-done.refs_12_.refs_1_, ...), custom_call_target="tpu_custom_call" | custom-call | bytes 1476000 | tf_op jit(solution)/shard_map/pallas_call | solution.py:346
  44.0 0.0 collective-permute-done.11.refs_2_
  44.0 1.6 %collective-permute-start.8 = (bf16[16,32,128]{2,1,0:T(8,128)(2,1)S(1)}, bf16[16,32,128]{2,1,0:T(8,128)(2,1)S(1)}, u32[]{:S(2)}, u32[]{:S(2)}) collective-permute-start(bf16[16,32,128]{2,1,0:T(8,128)(2,1)S(1)} %get-tuple-element.27), channel_id=1, source_target_pairs={{0,2},{1,3},{2,0},{3,1},{4,6},{5,7},{6,4},{7,5},{8,10},{9,11},{10,... | collective-permute-start | bytes 393224 | tf_op jit(solution)/shard_map/ppermute | solution.py:252
  45.6 1.0 %collective-permute-done.10.refs_1_ = bf16[16,32,128]{2,1,0:T(8,128)(2,1)S(1)} collective-permute-done((bf16[16,32,128]{2,1,0:T(8,128)(2,1)S(1)}, bf16[16,32,128]{2,1,0:T(8,128)(2,1)S(1)}, u32[]{:S(2)}, u32[]{:S(2)}) %collective-permute-start.10) | collective-permute-done | bytes 131104 | tf_op jit(solution)/shard_map/ppermute | solution.py:252
  46.6 2.4 %collective-permute-done.9.refs_0_ = bf16[16,32,128]{2,1,0:T(8,128)(2,1)S(1)} collective-permute-done((bf16[16,32,128]{2,1,0:T(8,128)(2,1)S(1)}, bf16[16,32,128]{2,1,0:T(8,128)(2,1)S(1)}, u32[]{:S(2)}, u32[]{:S(2)}) %collective-permute-start.9) | collective-permute-done | bytes 131104 | tf_op jit(solution)/shard_map/ppermute | solution.py:252
  49.0 0.0 collective-permute-done.12.refs_4_
  49.0 0.0 collective-permute-done.13.refs_5_
  49.0 0.9 %shard_map.117.refs_2_ = bf16[128,32,128]{2,1,0:T(8,128)(2,1)} custom-call(s32[1]{0:T(128)} %bitcast.me_ref, bf16[16,32,128]{2,1,0:T(8,128)(2,1)S(1)} %collective-permute-done.9.refs_0_, bf16[16,32,128]{2,1,0:T(8,128)(2,1)S(1)} %collective-permute-done.10.refs_1_, bf16[16,32,128]{2,1,0:T(8,128)(2,1)S(1)} %collective-permute-done.11.refs_2_, ...), custom_call_target="tpu_custom_call" | custom-call | bytes 3690000 | tf_op jit(solution)/shard_map/pallas_call | solution.py:384
  50.0 0.0 collective-permute-done.8.refs_1_
  50.0 0.7 %shard_map.118 = bf16[128,32,128]{2,1,0:T(8,128)(2,1)} custom-call(s32[1]{0:T(128)} %bitcast.me_ref, bf16[16,32,128]{2,1,0:T(8,128)(2,1)S(1)} %get-tuple-element.26.refs_0_, bf16[16,32,128]{2,1,0:T(8,128)(2,1)S(1)} %collective-permute-done.8.refs_1_, bf16[128,32,128]{2,1,0:T(8,128)(2,1)} %shard_map.117.refs_2_), custom_call_target="tpu_custom_call", output_to_operand_aliasing={{}: (3, {})} | custom-call | bytes 3690000 | tf_op jit(solution)/shard_map/pallas_call | solution.py:384
  (1 shorter events, 0.0 us)
Async XLA Ops:
  0.0 14.3 %copy-start = (bf16[128,512]{1,0:T(8,128)(2,1)S(1)}, bf16[128,512]{1,0:T(8,128)(2,1)}, u32[]{:S(2)}) copy-start(bf16[128,512]{1,0:T(8,128)(2,1)} %refs_9_.5) | copy-start | bytes 393220
  5.6 11.1 %copy-start.1 = (bf16[128,128]{1,0:T(8,128)(2,1)S(1)}, bf16[128,128]{1,0:T(8,128)(2,1)}, u32[]{:S(2)}) copy-start(bf16[128,128]{1,0:T(8,128)(2,1)} %refs_11_.5) | copy-start | bytes 98308
  5.6 11.1 %copy-start.2 = (s32[512]{0:T(512)S(1)}, s32[512]{0:T(512)}, u32[]{:S(2)}) copy-start(s32[512]{0:T(512)} %param.13) | copy-start | bytes 6148
  5.6 11.1 %copy-start.3 = (s32[512]{0:T(512)S(1)}, s32[512]{0:T(512)}, u32[]{:S(2)}) copy-start(s32[512]{0:T(512)} %param.14) | copy-start | bytes 6148
  5.6 11.1 %copy-start.4 = (f32[4]{0:T(128)S(1)}, f32[4]{0:T(128)}, u32[]{:S(2)}) copy-start(f32[4]{0:T(128)} %chain_bias_ref.9) | copy-start | bytes 52
  5.6 11.0 %copy-start.5 = (f32[128]{0:T(128)S(1)}, f32[128]{0:T(128)}, u32[]{:S(2)}) copy-start(f32[128]{0:T(128)} %param.18) | copy-start | bytes 1540
  5.6 8.2 %collective-permute-start.1 = (bf16[8,512,128]{2,1,0:T(8,128)(2,1)S(1)}, bf16[8,512,128]{2,1,0:T(8,128)(2,1)S(1)}, u32[]{:S(2)}, u32[]{:S(2)}) collective-permute-start(bf16[8,512,128]{2,1,0:T(8,128)(2,1)S(1)} %get-tuple-element.18.own_ref), channel_id=1, source_target_pairs={{0,1},{1,0},{2,3},{3,2},{4,5},{5,4},{6,7},{7,6},{8,9},{9,8},{10,11... | collective-permute-start | bytes 3145736 | tf_op jit(solution)/shard_map/ppermute | solution.py:252
  6.2 10.5 %collective-permute-start.5 = (bf16[128,384]{1,0:T(8,128)(2,1)S(1)}, bf16[128,384]{1,0:T(8,128)(2,1)S(1)}, u32[]{:S(2)}, u32[]{:S(2)}) collective-permute-start(bf16[128,384]{1,0:T(8,128)(2,1)S(1)} %get-tuple-element.17.refs_0_), channel_id=1, source_target_pairs={{0,12},{1,13},{2,14},{3,15},{4,8},{5,9},{6,10},{7,11},{8,4},{9,5},... | collective-permute-start | bytes 294920 | tf_op jit(solution)/shard_map/ppermute | solution.py:252
  10.8 9.0 %collective-permute-start.4 = (bf16[128,384]{1,0:T(8,128)(2,1)S(1)}, bf16[128,384]{1,0:T(8,128)(2,1)S(1)}, u32[]{:S(2)}, u32[]{:S(2)}) collective-permute-start(bf16[128,384]{1,0:T(8,128)(2,1)S(1)} %get-tuple-element.17.refs_0_), channel_id=1, source_target_pairs={{0,8},{1,9},{2,10},{3,11},{4,12},{5,13},{6,14},{7,15},{8,0},{9,1},... | collective-permute-start | bytes 294920 | tf_op jit(solution)/shard_map/ppermute | solution.py:252
  10.8 13.1 %collective-permute-start.3 = (bf16[128,384]{1,0:T(8,128)(2,1)S(1)}, bf16[128,384]{1,0:T(8,128)(2,1)S(1)}, u32[]{:S(2)}, u32[]{:S(2)}) collective-permute-start(bf16[128,384]{1,0:T(8,128)(2,1)S(1)} %get-tuple-element.17.refs_0_), channel_id=1, source_target_pairs={{0,6},{1,7},{2,4},{3,5},{4,2},{5,3},{6,0},{7,1},{8,14},{9,15},{10,... | collective-permute-start | bytes 294920 | tf_op jit(solution)/shard_map/ppermute | solution.py:252
  12.6 11.3 %collective-permute-start.2 = (bf16[128,384]{1,0:T(8,128)(2,1)S(1)}, bf16[128,384]{1,0:T(8,128)(2,1)S(1)}, u32[]{:S(2)}, u32[]{:S(2)}) collective-permute-start(bf16[128,384]{1,0:T(8,128)(2,1)S(1)} %get-tuple-element.17.refs_0_), channel_id=1, source_target_pairs={{0,4},{1,5},{2,6},{3,7},{4,0},{5,1},{6,2},{7,3},{8,12},{9,13},{10,... | collective-permute-start | bytes 294920 | tf_op jit(solution)/shard_map/ppermute | solution.py:252
  13.8 10.1 %collective-permute-start = (bf16[128,384]{1,0:T(8,128)(2,1)S(1)}, bf16[128,384]{1,0:T(8,128)(2,1)S(1)}, u32[]{:S(2)}, u32[]{:S(2)}) collective-permute-start(bf16[128,384]{1,0:T(8,128)(2,1)S(1)} %get-tuple-element.17.refs_0_), channel_id=1, source_target_pairs={{0,2},{1,3},{2,0},{3,1},{4,6},{5,7},{6,4},{7,5},{8,10},{9,11},{10,... | collective-permute-start | bytes 294920 | tf_op jit(solution)/shard_map/ppermute | solution.py:252
  19.8 6.5 %collective-permute-start.6 = (bf16[256,384]{1,0:T(8,128)(2,1)S(1)}, bf16[256,384]{1,0:T(8,128)(2,1)S(1)}, u32[]{:S(2)}, u32[]{:S(2)}) collective-permute-start(bf16[256,384]{1,0:T(8,128)(2,1)S(1)} %shard_map.112), channel_id=1, source_target_pairs={{0,2},{1,3},{2,0},{3,1},{4,6},{5,7},{6,4},{7,5},{8,10},{9,11},{10,... | collective-permute-start | bytes 589832 | tf_op jit(solution)/shard_map/ppermute | solution.py:252
  21.4 13.5 %collective-permute-start.7 = (bf16[16,32,128]{2,1,0:T(8,128)(2,1)S(1)}, bf16[16,32,128]{2,1,0:T(8,128)(2,1)S(1)}, u32[]{:S(2)}, u32[]{:S(2)}) collective-permute-start(bf16[16,32,128]{2,1,0:T(8,128)(2,1)S(1)} %shard_map.111.refs_2_.refs_11_), channel_id=1, source_target_pairs={{0,12},{1,13},{2,14},{3,15},{4,8},{5,9},{6,10},{7,11},{8,4},{9,5},... | collective-permute-start | bytes 393224 | tf_op jit(solution)/shard_map/ppermute | solution.py:252
  26.1 17.9 %collective-permute-start.11 = (bf16[16,32,128]{2,1,0:T(8,128)(2,1)S(1)}, bf16[16,32,128]{2,1,0:T(8,128)(2,1)S(1)}, u32[]{:S(2)}, u32[]{:S(2)}) collective-permute-start(bf16[16,32,128]{2,1,0:T(8,128)(2,1)S(1)} %shard_map.113.refs_12_), channel_id=1, source_target_pairs={{0,8},{1,9},{2,10},{3,11},{4,12},{5,13},{6,14},{7,15},{8,0},{9,1},... | collective-permute-start | bytes 393224 | tf_op jit(solution)/shard_map/ppermute | solution.py:252
  29.9 19.2 %collective-permute-start.12 = (bf16[16,32,128]{2,1,0:T(8,128)(2,1)S(1)}, bf16[16,32,128]{2,1,0:T(8,128)(2,1)S(1)}, u32[]{:S(2)}, u32[]{:S(2)}) collective-permute-start(bf16[16,32,128]{2,1,0:T(8,128)(2,1)S(1)} %get-tuple-element.23.refs_12_), channel_id=1, source_target_pairs={{0,10},{1,11},{2,8},{3,9},{4,14},{5,15},{6,12},{7,13},{8,2},{9,3},... | collective-permute-start | bytes 393224 | tf_op jit(solution)/shard_map/ppermute | solution.py:252
  32.6 16.5 %collective-permute-start.13 = (bf16[16,32,128]{2,1,0:T(8,128)(2,1)S(1)}, bf16[16,32,128]{2,1,0:T(8,128)(2,1)S(1)}, u32[]{:S(2)}, u32[]{:S(2)}) collective-permute-start(bf16[16,32,128]{2,1,0:T(8,128)(2,1)S(1)} %get-tuple-element.24.refs_13_), channel_id=1, source_target_pairs={{0,14},{1,15},{2,12},{3,13},{4,10},{5,11},{6,8},{7,9},{8,6},{9,7},... | collective-permute-start | bytes 393224 | tf_op jit(solution)/shard_map/ppermute | solution.py:252
  38.4 8.2 %collective-permute-start.10 = (bf16[16,32,128]{2,1,0:T(8,128)(2,1)S(1)}, bf16[16,32,128]{2,1,0:T(8,128)(2,1)S(1)}, u32[]{:S(2)}, u32[]{:S(2)}) collective-permute-start(bf16[16,32,128]{2,1,0:T(8,128)(2,1)S(1)} %get-tuple-element.28), channel_id=1, source_target_pairs={{0,6},{1,7},{2,4},{3,5},{4,2},{5,3},{6,0},{7,1},{8,14},{9,15},{10,... | collective-permute-start | bytes 393224 | tf_op jit(solution)/shard_map/ppermute | solution.py:252
  38.8 10.2 %collective-permute-start.9 = (bf16[16,32,128]{2,1,0:T(8,128)(2,1)S(1)}, bf16[16,32,128]{2,1,0:T(8,128)(2,1)S(1)}, u32[]{:S(2)}, u32[]{:S(2)}) collective-permute-start(bf16[16,32,128]{2,1,0:T(8,128)(2,1)S(1)} %get-tuple-element.25.refs_12_), channel_id=1, source_target_pairs={{0,4},{1,5},{2,6},{3,7},{4,0},{5,1},{6,2},{7,3},{8,12},{9,13},{10,... | collective-permute-start | bytes 393224 | tf_op jit(solution)/shard_map/ppermute | solution.py:252
  44.0 6.0 %collective-permute-start.8 = (bf16[16,32,128]{2,1,0:T(8,128)(2,1)S(1)}, bf16[16,32,128]{2,1,0:T(8,128)(2,1)S(1)}, u32[]{:S(2)}, u32[]{:S(2)}) collective-permute-start(bf16[16,32,128]{2,1,0:T(8,128)(2,1)S(1)} %get-tuple-element.27), channel_id=1, source_target_pairs={{0,2},{1,3},{2,0},{3,1},{4,6},{5,7},{6,4},{7,5},{8,10},{9,11},{10,... | collective-permute-start | bytes 393224 | tf_op jit(solution)/shard_map/ppermute | solution.py:252
